TPU v7x, 32 devices: a whole 2x2x4 slice. The times are simulated.
32 devices in a mesh: fsdp: 4 (over y, core), ctx: 4 (over z), tp: 2 (over x).
Axes of the slice: x: 2, y: 2, z: 4, core: 2. Of those that a mesh axis runs over, the one named last changes fastest.
Arguments:
- tokens: bfloat16 [8, 2048, 768], P('fsdp', 'ctx'), may hold values from -6 to 6
- prev_logits: float32 [8, 2048, 12], P('fsdp', 'ctx'), may hold values from -3 to 3
- routes: int32 [8, 2048, 2], P('fsdp', 'ctx'), may hold values from 0 to 11, all different within a row; in each aligned block of 512 rows (0 to 511, 512 to 1023, ..., all dimensions but the last counted through in order) at most 128 rows name the same one
- prefix: int32 [8], P('fsdp'), may hold values from 204 to 1024
- norm_gains: bfloat16 [2, 768], P(None, 'fsdp'), may hold values from 0.099609375 to 1.8984375
- query_key_value_weight: bfloat16 [3, 768, 768], P(None, 'fsdp', 'tp'), may hold values from -0.21875 to 0.21875
- output_projection_weight: bfloat16 [768, 768], P('fsdp', 'tp'), may hold values from -0.875 to 0.875
- router_gate_weight: bfloat16 [768, 16], P('fsdp'), may hold values from -0.15625 to 0.15625
- const_vec: bfloat16 [2, 768], P(None, 'fsdp'), may hold values from -6 to 6
- gate_up: bfloat16 [8, 2, 768, 2048], P(None, None, 'fsdp', 'tp'), may hold values from -0.21875 to 0.21875
- down_weight: bfloat16 [8, 768, 2048], P(None, 'fsdp', 'tp'), may hold values from -0.25 to 0.25
- cotangent: bfloat16 [8, 2048, 768], P('fsdp', 'ctx'), may hold values from -6 to 6
Outputs:
- layer_out: bfloat16 [8, 2048, 768], P('fsdp', 'ctx')
- grad_tokens: float32 [8, 2048, 768], P('fsdp', 'ctx')
- grad_prev: float32 [8, 2048, 12], P('fsdp', 'ctx')
- grad_gains: float32 [2, 768], P(None, 'fsdp')
- grad_qkv: float32 [3, 768, 768], P(None, 'fsdp', 'tp')
- grad_out: float32 [768, 768], P('fsdp', 'tp')
- grad_gate: float32 [768, 16], P('fsdp')
- grad_const: float32 [2, 768], P(None, 'fsdp')
- grad_gate_up: float32 [8, 2, 768, 2048], P(None, None, 'fsdp', 'tp')
- grad_down: float32 [8, 768, 2048], P(None, 'fsdp', 'tp')
Inputs may be any that keep to these rules, and one draw needn't show every extreme that they name: `routes`: each row names 2 different experts; in each aligned block of 512 rows no expert is named by more than 128 rows, a bound that some block reaches.
All inputs are finite; a program needn't handle non-finite values.
Results may differ from a plain program's by a relative error of at most 0.024.
Values may be sent and summed in bfloat16 or wider, within the bound.
A program may use at most 320 MiB of HBM per device.

v0:
```python
import math

import jax
import jax.numpy as jnp
from jax import lax
from jax.sharding import PartitionSpec as P

HEAD_DIM = 64
NFFN = 8
NCONST = 2
TOP = 2
NEXP = 12
CAPACITY = 128


epsilon = 1e-05


def rope_tables(positions):
    half_dim = HEAD_DIM // 2
    frequency = 10000.0 ** (-(jnp.arange(half_dim, dtype=jnp.float32) * 2.0 / HEAD_DIM))
    angles = positions.astype(jnp.float32)[:, None] * frequency[None, :]
    return (jnp.cos(angles)[:, None, :], jnp.sin(angles)[:, None, :])


def rotate(values, cosine, sine):
    first_half, second = jnp.split(values, 2, axis=-1)
    return jnp.concatenate(
        [first_half * cosine - second * sine, second * cosine + first_half * sine], axis=-1
    )


def unrotate(values, cosine, sine):
    first_half, second = jnp.split(values, 2, axis=-1)
    return jnp.concatenate(
        [first_half * cosine + second * sine, second * cosine - first_half * sine], axis=-1
    )


def norm_forward(values, gain_row):
    inverse = lax.rsqrt(jnp.mean(values * values, axis=-1, keepdims=True) + epsilon)
    return (values * inverse * gain_row, inverse)


def norm_backward(values, inverse, gain_row, grad_normed):
    scaled = grad_normed * gain_row
    grad_gain = jnp.sum(grad_normed * values * inverse, axis=0)
    grad_values = inverse * scaled - values * inverse**3 * jnp.mean(
        scaled * values, axis=-1, keepdims=True
    )
    return (grad_values, grad_gain)


def slot_table(block_routes):
    row_count = block_routes.shape[0]
    experts = jnp.arange(NFFN, dtype=jnp.int32)
    matches = block_routes[None, :, :] == experts[:, None, None]
    hit_rows = jnp.any(matches, axis=2).astype(jnp.int32)
    places = jnp.cumsum(hit_rows, axis=1) - 1
    slot_ids = jnp.arange(CAPACITY, dtype=jnp.int32)
    chosen = ((places[:, :, None] == slot_ids[None, None, :]) & (hit_rows[:, :, None] > 0)).astype(
        jnp.int32
    )
    row_ids = jnp.arange(row_count, dtype=jnp.int32)
    slot_rows = jnp.sum(chosen * row_ids[None, :, None], axis=1)
    slot_valid = jnp.sum(chosen, axis=1).astype(jnp.float32)
    second_hit = matches[:, :, 1].astype(jnp.int32)
    slot_which = jnp.sum(chosen * second_hit[:, :, None], axis=1)
    return (slot_rows, slot_which, slot_valid)


def on_device(
    tokens,
    prev_logits,
    routes,
    prefix,
    norm_gains,
    query_key_value_weight,
    output_projection_weight,
    router_gate_weight,
    const_vec,
    gate_up,
    down_weight,
    cotangent,
):
    seq_local, row_count, width = tokens.shape
    flat_rows = seq_local * row_count
    source = tokens.astype(jnp.float32).reshape(flat_rows, width)
    previous = prev_logits.reshape(flat_rows, NEXP)
    route_rows = routes.reshape(flat_rows, TOP)
    grad_y = cotangent.astype(jnp.float32).reshape(flat_rows, width)
    head_cols = query_key_value_weight.shape[2]
    head_count = head_cols // HEAD_DIM
    length = row_count * lax.axis_size("ctx")
    query_pos = lax.axis_index("ctx") * row_count + jnp.arange(row_count, dtype=jnp.int32)
    score_scale = HEAD_DIM ** (-0.5)
    cosine, sine = rope_tables(query_pos)
    qkv_full, out_full, gains_full = (
        lax.all_gather(query_key_value_weight, "fsdp", axis=1, tiled=True),
        lax.all_gather(output_projection_weight, "fsdp", axis=0, tiled=True),
        lax.all_gather(norm_gains, "fsdp", axis=1, tiled=True),
    )
    gain_one = gains_full[0].astype(jnp.float32)
    gain_two = gains_full[1].astype(jnp.float32)
    normed_one, inverse_one = norm_forward(source, gain_one)
    normalized_reduced = normed_one.astype(jnp.bfloat16)
    projected_rows = jnp.einsum(
        "nd,cde->cne", normalized_reduced, qkv_full, preferred_element_type=jnp.float32
    )
    shaped = projected_rows.reshape(3, seq_local, row_count, head_count, HEAD_DIM)
    queries = rotate(shaped[0], cosine, sine).astype(jnp.bfloat16)
    key_flat = (
        rotate(shaped[1], cosine, sine)
        .astype(jnp.bfloat16)
        .reshape(seq_local, row_count, head_cols)
    )
    value_flat = shaped[2].astype(jnp.bfloat16).reshape(seq_local, row_count, head_cols)

    def allowed_mask(key_pos):
        return (key_pos[None, None, :] <= query_pos[None, :, None]) | (
            key_pos[None, None, :] < prefix[:, None, None]
        )

    start_state = (
        jnp.full((seq_local, head_count, row_count), -1e30, jnp.float32),
        jnp.zeros((seq_local, head_count, row_count), jnp.float32),
        jnp.zeros((seq_local, head_count, row_count, HEAD_DIM), jnp.float32),
    )
    key_piece = lax.all_gather(key_flat, "ctx", axis=1, tiled=True)
    value_piece = lax.all_gather(value_flat, "ctx", axis=1, tiled=True)
    piece_rows = key_piece.shape[1]
    fold_key_block = math.gcd(piece_rows, 1024)
    step_count = piece_rows // fold_key_block
    key_parts = jnp.moveaxis(
        key_piece.reshape(seq_local, step_count, fold_key_block, head_count, HEAD_DIM), 1, 0
    )
    value_parts = jnp.moveaxis(
        value_piece.reshape(seq_local, step_count, fold_key_block, head_count, HEAD_DIM), 1, 0
    )
    offsets = jnp.arange(step_count, dtype=jnp.int32) * fold_key_block

    def inner(state, packed):
        key_part, value_part, offset = packed
        run_max, run_sum, run_acc = state
        scores = (
            jnp.einsum("sqhd,skhd->shqk", queries, key_part, preferred_element_type=jnp.float32)
            * score_scale
        )
        key_pos = offset + jnp.arange(fold_key_block, dtype=jnp.int32)
        allowed = allowed_mask(key_pos)[:, None]
        masked = jnp.where(allowed, scores, -1e30)
        new_max = jnp.maximum(run_max, jnp.max(masked, axis=-1))
        expo_terms = jnp.where(allowed, jnp.exp(masked - new_max[..., None]), 0.0)
        decay = jnp.exp(run_max - new_max)
        new_sum = run_sum * decay + jnp.sum(expo_terms, axis=-1)
        new_acc = run_acc * decay[..., None] + jnp.einsum(
            "shqk,skhd->shqd",
            expo_terms.astype(jnp.bfloat16),
            value_part,
            preferred_element_type=jnp.float32,
        )
        return ((new_max, new_sum, new_acc), None)

    result_state, unused = lax.scan(inner, start_state, (key_parts, value_parts, offsets))
    run_max, run_sum, run_acc = result_state
    log_total = run_max + jnp.log(run_sum)
    mixed_three = jnp.transpose(run_acc / run_sum[..., None], (0, 2, 1, 3))
    mixed_reduced = mixed_three.reshape(flat_rows, head_cols).astype(jnp.bfloat16)
    attn_part = lax.dot_general(
        mixed_reduced, out_full, (((1,), (1,)), ((), ())), preferred_element_type=jnp.float32
    )
    attention_result = lax.psum(attn_part.astype(jnp.bfloat16), "tp").astype(jnp.float32)
    hidden = source + attention_result
    gate_full, const_full, gu_full, down_full = (
        lax.all_gather(router_gate_weight, "fsdp", axis=0, tiled=True),
        lax.all_gather(const_vec, "fsdp", axis=1, tiled=True),
        lax.all_gather(gate_up, "fsdp", axis=2, tiled=True),
        lax.all_gather(down_weight, "fsdp", axis=1, tiled=True),
    )
    normed_two, inverse_two = norm_forward(hidden, gain_two)
    second_normalized_reduced = normed_two.astype(jnp.bfloat16)
    combined_logits = jnp.dot(
        second_normalized_reduced, gate_full, preferred_element_type=jnp.float32
    )
    router = combined_logits[:, :NEXP] + previous
    route_hot = (route_rows[:, :, None] == jnp.arange(NEXP, dtype=jnp.int32)).astype(jnp.float32)
    chosen = jnp.sum(route_hot * router[:, None, :], axis=-1)
    gate_probs = jax.nn.softmax(chosen, axis=-1)
    mixing = jax.nn.softmax(combined_logits[:, NEXP:].reshape(flat_rows, NCONST, 2), axis=-1)
    const_vals = const_full.astype(jnp.float32)
    const_out = mixing[:, :, 0:1] * normed_two[:, None, :] + mixing[:, :, 1:2] * const_vals[None]
    copy_flag = (route_rows == NFFN + 1).astype(jnp.float32)
    const_ids = NFFN + 2 + jnp.arange(NCONST, dtype=jnp.int32)
    const_flag = (route_rows[:, :, None] == const_ids).astype(jnp.float32)
    copy_weight = jnp.sum(gate_probs * copy_flag, axis=-1)
    const_weight = jnp.sum(gate_probs[:, :, None] * const_flag, axis=1)
    special = copy_weight[:, None] * normed_two + jnp.sum(
        const_weight[:, :, None] * const_out, axis=1
    )
    block_rows, block_which, block_valid = jax.vmap(slot_table)(routes)
    row_offset = (jnp.arange(seq_local, dtype=jnp.int32) * row_count)[:, None, None]
    slot_rows = jnp.transpose(block_rows + row_offset, (1, 0, 2)).reshape(
        NFFN, seq_local * CAPACITY
    )
    slot_which = jnp.transpose(block_which, (1, 0, 2)).reshape(NFFN, seq_local * CAPACITY)
    slot_valid = jnp.transpose(block_valid, (1, 0, 2)).reshape(NFFN, seq_local * CAPACITY)
    gates_at = gate_probs[slot_rows]
    slot_gate = jnp.where(slot_which == 1, gates_at[..., 1], gates_at[..., 0]) * slot_valid
    inputs = second_normalized_reduced[slot_rows]
    gate_and_up = jnp.einsum("ecd,etdf->etcf", inputs, gu_full, preferred_element_type=jnp.float32)
    gate_pre = gate_and_up[:, 0]
    up_pre = gate_and_up[:, 1]
    active = (jax.nn.silu(gate_pre) * up_pre).astype(jnp.bfloat16)
    result = jnp.einsum("ecf,edf->ecd", active, down_full, preferred_element_type=jnp.float32)
    weighted = result * slot_gate[:, :, None]
    ffn_part = (
        jnp.zeros((flat_rows, width), jnp.float32)
        .at[slot_rows.reshape(-1)]
        .add(weighted.reshape(-1, width))
    )
    ffn_out = lax.psum(ffn_part.astype(jnp.bfloat16), "tp").astype(jnp.float32)
    layer_out = (hidden + ffn_out + special).astype(jnp.bfloat16)
    slot_dy = grad_y[slot_rows]
    d_result = (slot_gate[:, :, None] * slot_dy).astype(jnp.bfloat16)
    d_active = jnp.einsum("ecd,edf->ecf", d_result, down_full, preferred_element_type=jnp.float32)
    grad_down_local = jnp.einsum(
        "ecd,ecf->edf", d_result, active, preferred_element_type=jnp.float32
    )
    sigmoid_pre = jax.nn.sigmoid(gate_pre)
    d_gate_pre = d_active * up_pre * (sigmoid_pre * (1.0 + gate_pre * (1.0 - sigmoid_pre)))
    d_up_pre = d_active * (gate_pre * sigmoid_pre)
    d_both = jnp.stack([d_gate_pre, d_up_pre], axis=1).astype(jnp.bfloat16)
    d_inputs = jnp.einsum("etcf,etdf->ecd", d_both, gu_full, preferred_element_type=jnp.float32)
    grad_gu_local = jnp.einsum("ecd,etcf->etdf", inputs, d_both, preferred_element_type=jnp.float32)
    d_normed_part = (
        jnp.zeros((flat_rows, width), jnp.float32)
        .at[slot_rows.reshape(-1)]
        .add(d_inputs.reshape(-1, width))
    )
    slot_gate_grad = jnp.sum(result * slot_dy, axis=-1) * slot_valid
    d_gate_part = (
        jnp.zeros((flat_rows, TOP), jnp.float32).at[slot_rows, slot_which].add(slot_gate_grad)
    )
    d_normed_ffn, d_gate_ffn = (
        lax.psum(d_normed_part.astype(jnp.bfloat16), "tp").astype(jnp.float32),
        lax.psum(d_gate_part.astype(jnp.bfloat16), "tp").astype(jnp.float32),
    )
    dy_normed = jnp.sum(grad_y * normed_two, axis=-1)
    dy_const = jnp.sum(grad_y[:, None, :] * const_out, axis=-1)
    dy_vec = jnp.sum(grad_y[:, None, :] * const_vals[None], axis=-1)
    d_gates = (
        d_gate_ffn
        + copy_flag * dy_normed[:, None]
        + jnp.sum(const_flag * dy_const[:, None, :], axis=-1)
    )
    d_chosen = gate_probs * (d_gates - jnp.sum(gate_probs * d_gates, axis=-1, keepdims=True))
    grad_prev = jnp.sum(route_hot * d_chosen[:, :, None], axis=1)
    d_mix = jnp.stack([const_weight * dy_normed[:, None], const_weight * dy_vec], axis=-1)
    d_const_logits = mixing * (d_mix - jnp.sum(mixing * d_mix, axis=-1, keepdims=True))
    grad_cvec = jnp.sum((const_weight * mixing[:, :, 1])[:, :, None] * grad_y[:, None, :], axis=0)
    d_logits = jnp.concatenate(
        [grad_prev, d_const_logits.reshape(flat_rows, 2 * NCONST)], axis=1
    ).astype(jnp.bfloat16)
    grad_gate_local = lax.dot_general(
        second_normalized_reduced,
        d_logits,
        (((0,), (0,)), ((), ())),
        preferred_element_type=jnp.float32,
    )
    direct_weight = copy_weight + jnp.sum(const_weight * mixing[:, :, 0], axis=-1)
    d_normed_two = (
        d_normed_ffn
        + direct_weight[:, None] * grad_y
        + lax.dot_general(
            d_logits, gate_full, (((1,), (1,)), ((), ())), preferred_element_type=jnp.float32
        )
    )
    grad_hidden_norm, grad_gain_two = norm_backward(hidden, inverse_two, gain_two, d_normed_two)
    grad_hidden = grad_y + grad_hidden_norm
    expert_owned = (
        lax.psum_scatter(
            grad_gate_local.astype(jnp.bfloat16), "fsdp", scatter_dimension=0, tiled=True
        ).astype(jnp.float32),
        lax.psum_scatter(
            grad_cvec.astype(jnp.bfloat16), "fsdp", scatter_dimension=1, tiled=True
        ).astype(jnp.float32),
        lax.psum_scatter(
            grad_gu_local.astype(jnp.bfloat16), "fsdp", scatter_dimension=2, tiled=True
        ).astype(jnp.float32),
        lax.psum_scatter(
            grad_down_local.astype(jnp.bfloat16), "fsdp", scatter_dimension=1, tiled=True
        ).astype(jnp.float32),
    )
    d_attn = grad_hidden.astype(jnp.bfloat16)
    grad_out_local = lax.dot_general(
        d_attn, mixed_reduced, (((0,), (0,)), ((), ())), preferred_element_type=jnp.float32
    )
    d_mixed = (
        jnp.dot(d_attn, out_full, preferred_element_type=jnp.float32)
        .astype(jnp.bfloat16)
        .reshape(seq_local, row_count, head_count, HEAD_DIM)
    )
    delta = jnp.transpose(jnp.sum(d_mixed.astype(jnp.float32) * mixed_three, axis=-1), (0, 2, 1))
    key_all, value_all = (
        lax.all_gather(key_flat, "ctx", axis=1, tiled=True),
        lax.all_gather(value_flat, "ctx", axis=1, tiled=True),
    )
    key_block = math.gcd(length, 1024)
    block_count = length // key_block
    key_parts = jnp.moveaxis(
        key_all.reshape(seq_local, block_count, key_block, head_count, HEAD_DIM), 1, 0
    )
    value_parts = jnp.moveaxis(
        value_all.reshape(seq_local, block_count, key_block, head_count, HEAD_DIM), 1, 0
    )
    offsets = jnp.arange(block_count, dtype=jnp.int32) * key_block

    def back_step(d_query, packed):
        key_part, value_part, offset = packed
        scores = (
            jnp.einsum("sqhd,skhd->shqk", queries, key_part, preferred_element_type=jnp.float32)
            * score_scale
        )
        key_pos = offset + jnp.arange(key_block, dtype=jnp.int32)
        allowed = allowed_mask(key_pos)[:, None]
        probs = jnp.where(allowed, jnp.exp(scores - log_total[..., None]), 0.0)
        d_probs = jnp.einsum(
            "sqhd,skhd->shqk", d_mixed, value_part, preferred_element_type=jnp.float32
        )
        d_scores = (probs * (d_probs - delta[..., None]) * score_scale).astype(jnp.bfloat16)
        d_query = d_query + jnp.einsum(
            "shqk,skhd->sqhd", d_scores, key_part, preferred_element_type=jnp.float32
        )
        d_key = jnp.einsum("shqk,sqhd->skhd", d_scores, queries, preferred_element_type=jnp.float32)
        d_value = jnp.einsum(
            "shqk,sqhd->skhd",
            probs.astype(jnp.bfloat16),
            d_mixed,
            preferred_element_type=jnp.float32,
        )
        return (
            d_query,
            (
                d_key.reshape(seq_local, key_block, head_cols),
                d_value.reshape(seq_local, key_block, head_cols),
            ),
        )

    d_query, key_terms = lax.scan(
        back_step,
        jnp.zeros((seq_local, row_count, head_count, HEAD_DIM), jnp.float32),
        (key_parts, value_parts, offsets),
    )
    key_term_all = jnp.moveaxis(key_terms[0], 0, 1).reshape(seq_local, length, head_cols)
    value_term_all = jnp.moveaxis(key_terms[1], 0, 1).reshape(seq_local, length, head_cols)
    key_grads, value_grads = (
        lax.psum_scatter(
            key_term_all.astype(jnp.bfloat16), "ctx", scatter_dimension=1, tiled=True
        ).astype(jnp.float32),
        lax.psum_scatter(
            value_term_all.astype(jnp.bfloat16), "ctx", scatter_dimension=1, tiled=True
        ).astype(jnp.float32),
    )
    d_query_raw = unrotate(d_query, cosine, sine).reshape(flat_rows, head_cols)
    d_key_raw = unrotate(
        key_grads.reshape(seq_local, row_count, head_count, HEAD_DIM), cosine, sine
    ).reshape(flat_rows, head_cols)
    d_proj = jnp.stack([d_query_raw, d_key_raw, value_grads.reshape(flat_rows, head_cols)]).astype(
        jnp.bfloat16
    )
    grad_qkv_local = jnp.einsum(
        "nd,cne->cde", normalized_reduced, d_proj, preferred_element_type=jnp.float32
    )
    d_normed_one_part = jnp.einsum(
        "cne,cde->nd", d_proj, qkv_full, preferred_element_type=jnp.float32
    )
    d_normed_one = lax.psum(d_normed_one_part.astype(jnp.bfloat16), "tp").astype(jnp.float32)
    grad_source_norm, grad_gain_one = norm_backward(source, inverse_one, gain_one, d_normed_one)
    grad_tokens = grad_hidden + grad_source_norm
    grad_gains_local = jnp.stack([grad_gain_one, grad_gain_two])
    attention_owned = (
        lax.psum_scatter(
            grad_gains_local.astype(jnp.bfloat16), "fsdp", scatter_dimension=1, tiled=True
        ).astype(jnp.float32),
        lax.psum_scatter(
            grad_qkv_local.astype(jnp.bfloat16), "fsdp", scatter_dimension=1, tiled=True
        ).astype(jnp.float32),
        lax.psum_scatter(
            grad_out_local.astype(jnp.bfloat16), "fsdp", scatter_dimension=0, tiled=True
        ).astype(jnp.float32),
    )
    owned = (
        lax.psum(attention_owned[0].astype(jnp.bfloat16), "ctx").astype(jnp.float32),
        lax.psum(attention_owned[1].astype(jnp.bfloat16), "ctx").astype(jnp.float32),
        lax.psum(attention_owned[2].astype(jnp.bfloat16), "ctx").astype(jnp.float32),
        lax.psum(expert_owned[0].astype(jnp.bfloat16), "ctx").astype(jnp.float32),
        lax.psum(expert_owned[1].astype(jnp.bfloat16), "ctx").astype(jnp.float32),
        lax.psum(expert_owned[2].astype(jnp.bfloat16), "ctx").astype(jnp.float32),
        lax.psum(expert_owned[3].astype(jnp.bfloat16), "ctx").astype(jnp.float32),
    )
    out_shape = (seq_local, row_count, width)
    return (
        layer_out.reshape(out_shape),
        grad_tokens.reshape(out_shape),
        grad_prev.reshape(seq_local, row_count, NEXP),
        owned[0],
        owned[1],
        owned[2],
        owned[3],
        owned[4],
        owned[5],
        owned[6],
    )


def solution(mesh):
    in_specs = (
        P("fsdp", "ctx", None),
        P("fsdp", "ctx", None),
        P("fsdp", "ctx", None),
        P("fsdp"),
        P(None, "fsdp"),
        P(None, "fsdp", "tp"),
        P("fsdp", "tp"),
        P("fsdp", None),
        P(None, "fsdp"),
        P(None, None, "fsdp", "tp"),
        P(None, "fsdp", "tp"),
        P("fsdp", "ctx", None),
    )
    out_specs = (
        P("fsdp", "ctx", None),
        P("fsdp", "ctx", None),
        P("fsdp", "ctx", None),
        P(None, "fsdp"),
        P(None, "fsdp", "tp"),
        P("fsdp", "tp"),
        P("fsdp", None),
        P(None, "fsdp"),
        P(None, None, "fsdp", "tp"),
        P(None, "fsdp", "tp"),
    )
    return jax.shard_map(
        on_device, mesh=mesh, in_specs=in_specs, out_specs=out_specs, check_vma=False
    )
```

profile of v0, /device:TPU:0, one launch (start us, length us, event | category | flops | bytes accessed | tf_op | source)
XLA Modules:
  0.0 1832.8 jit_solution(14684340375510341460)
XLA Ops:
  17.8 15.3 all-gather.9.cloned.1.call-done
  62.7 51.4 %all-gather.11.cloned.1.call-done = bf16[2,2048,384]{1,2,0:T(8,128)(2,1)} async-done(((bf16[2,512,384]{1,2,0:T(8,128)(2,1)}), bf16[2,2048,384]{1,2,0:T(8,128)(2,1)}) %all-gather.11.cloned.1.call-update) | async-done | bytes 3145744 | tf_op jit(solution)/shard_map/all_gather | solution.py:129
  124.9 53.5 %all-gather.13.cloned.1.call-done = bf16[2,2048,384]{1,2,0:T(8,128)(2,1)} async-done(((bf16[2,512,384]{1,2,0:T(8,128)(2,1)}), bf16[2,2048,384]{1,2,0:T(8,128)(2,1)}) %all-gather.13.cloned.1.call-update) | async-done | bytes 3145744 | tf_op jit(solution)/shard_map/all_gather | solution.py:130
  189.1 78.3 %while.30 = (s32[]{:T(128)}, f32[2,6,512]{2,1,0:T(8,128)S(1)}, f32[2,6,512]{2,1,0:T(8,128)S(1)}, f32[2,6,512,64]{2,3,1,0:T(8,128)}, s32[2]{0:T(128)S(1)}, /*inde...) while((s32[]{:T(128)}, f32[2,6,512]{2,1,0:T(8,128)S(1)}, ...), condition=%wide.region_4.5_spmd.clone, body=%wide.region_1.4_spmd.clone.sunk | while | flops 1695188480 | bytes 113414400 | solution.py:164
  191.5 12.0 fusion.150
  203.5 12.0 fusion.151
  215.6 11.3 fusion.153
  230.5 12.0 fusion.150
  242.5 12.0 fusion.151
  254.6 11.3 fusion.153
  295.8 9.4 gather_fusion.2
  305.2 19.5 %all-reduce.8.cloned.1.call-done = bf16[1024,768]{1,0:T(8,128)(2,1)} async-done(((bf16[1024,768]{1,0:T(8,128)(2,1)}), bf16[1024,768]{1,0:T(8,128)(2,1)}) %all-reduce.8.cloned.1.call-update) | async-done | bytes 1572880 | tf_op jit(solution)/shard_map/psum | solution.py:172
  332.1 12.0 gather_fusion
  354.9 8.7 gather_fusion.1
  370.3 110.5 %all-gather.15.cloned.1.call-done = bf16[8,2,768,1024]{3,2,1,0:T(8,128)(2,1)} async-done(((bf16[8,2,192,1024]{3,2,1,0:T(8,128)(2,1)}), bf16[8,2,768,1024]{3,2,1,0:T(8,128)(2,1)}) %all-gather.15.cloned.1.call-update) | async-done | bytes 25165840 | tf_op jit(solution)/shard_map/all_gather | solution.py:177
  480.8 19.7 %convolution_bitcast_fusion = f32[8,2,256,1024]{3,2,1,0:T(8,128)} fusion(bf16[8,256,768,1]{2,1,3,0:T(8,128)(2,1)S(1)} %bitcast.367, bf16[8,2,768,1024]{3,2,1,0:T(8,128)(2,1)} %all-gather.15.cloned.1.call-done), kind=kOutput, calls=%fused_computation.67 | convolution fusion | flops 6442450944 | bytes 45088768 | tf_op jit(solution)/shard_map/ecd,etdf->etcf/dot_general | solution.py:210
  500.5 63.9 %all-gather.17.cloned.1.call-done = bf16[8,768,1024]{2,1,0:T(8,128)(2,1)} async-done(((bf16[8,192,1024]{2,1,0:T(8,128)(2,1)}), bf16[8,768,1024]{2,1,0:T(8,128)(2,1)}) %all-gather.17.cloned.1.call-update) | async-done | bytes 12582928 | tf_op jit(solution)/shard_map/all_gather | solution.py:178
  564.4 19.2 %fusion.53 = (bf16[8,1,256,1024]{3,2,0,1:T(8,128)(2,1)}, bf16[8,1,256,1024]{3,2,0,1:T(8,128)(2,1)}, bf16[8,256,1024]{2,1,0:T(8,128)(2,1)}) fusion(f32[8,2,256,1024]{3,2,1,0:T(8,128)} %convolution_bitcast_fusion, bf16[8,768,1024]{2,1,0:T(8,128)(2,1)} %all-gather.17.cloned.1.call-done, f32[8,256,768]{2,1,0:T(8,128)} %bitcast.363, f32[8,256]{1,0:T(8,128)S(1)} %fusion.81), kind=kOutput, calls=%fused_computation.91 | convolution fusion | flops 3255828480 | bytes 48242688 | tf_op jit(solution)/shard_map/ecd,edf->ecf/dot_general | solution.py:225
  583.6 16.9 fusion.47
  600.5 15.6 scatter_custom_fusion.1
  617.6 14.5 multiply_reduce_fusion.3
  632.2 12.5 scatter_custom_fusion.2
  650.5 18.5 %all-reduce.10.cloned.1.call-done = bf16[1024,768]{1,0:T(8,128)(2,1)} async-done(((bf16[1024,768]{1,0:T(8,128)(2,1)}), bf16[1024,768]{1,0:T(8,128)(2,1)}) %all-reduce.10.cloned.1.call-update) | async-done | bytes 1572880 | tf_op jit(solution)/shard_map/psum | solution.py:245
  686.7 140.9 %while.31 = (s32[]{:T(128)}, f32[2,512,6,64]{1,3,2,0:T(8,128)}, bf16[2,2,1024,384]{3,2,0,1:T(8,128)(2,1)}, bf16[2,2,1024,384]{3,2,0,1:T(8,128)(2,1)}, bf16[2,2,1...) while((s32[]{:T(128)}, f32[2,512,6,64]{1,3,2,0:T(8,128)}, ...), condition=%wide.region_39.40_spmd.clone, body=%wide.region_38.39_spmd.clone.sunk | while | flops 4098100736 | bytes 151613712 | solution.py:349
  687.1 11.2 fusion.164
  701.5 16.5 fusion.165
  726.0 12.2 fusion.166
  740.8 9.8 fusion.167
  757.1 11.2 fusion.164
  771.4 16.5 fusion.165
  796.4 12.2 fusion.166
  811.2 9.8 fusion.167
  828.4 15.6 scatter_custom_fusion
  847.2 40.9 %reduce-scatter.18.cloned.1.call-done = bf16[2,512,384]{2,1,0:T(8,128)(2,1)} async-done(((bf16[2,2048,384]{2,1,0:T(8,128)(2,1)}), bf16[2,512,384]{2,1,0:T(8,128)(2,1)}) %reduce-scatter.18.cloned.1.call-update) | async-done | bytes 786448 | tf_op jit(solution)/shard_map/reduce_scatter | solution.py:357
  896.0 54.6 %reduce-scatter.20.cloned.1.call-done = bf16[2,512,384]{2,1,0:T(8,128)(2,1)} async-done(((bf16[2,2048,384]{2,1,0:T(8,128)(2,1)}), bf16[2,512,384]{2,1,0:T(8,128)(2,1)}) %reduce-scatter.20.cloned.1.call-update) | async-done | bytes 786448 | tf_op jit(solution)/shard_map/reduce_scatter | solution.py:360
  970.7 12.5 convolution_convert_fusion
  985.0 17.6 convert_bitcast_fusion
  1002.7 33.2 %copy.248 = bf16[8,2,768,1024]{3,0,1,2:T(8,128)(2,1)} copy(bf16[8,2,768,1024]{2,3,1,0:T(8,128)(2,1)} %convert_bitcast_fusion) | data formatting | bytes 50331648 | tf_op jit(solution)/shard_map/convert_element_type | solution.py:288
  1045.9 28.2 %reduce-scatter.30.cloned.1.call-done = bf16[192,1152]{1,0:T(8,128)(2,1)} async-done(((bf16[768,1152]{1,0:T(8,128)(2,1)}), bf16[192,1152]{1,0:T(8,128)(2,1)}) %reduce-scatter.30.cloned.1.call-update) | async-done | bytes 442384
  1076.8 21.7 %reduce-scatter.22.cloned.1.call-done = bf16[192,384]{1,0:T(8,128)(2,1)} async-done(((bf16[768,384]{1,0:T(8,128)(2,1)}), bf16[192,384]{1,0:T(8,128)(2,1)}) %reduce-scatter.22.cloned.1.call-update) | async-done | bytes 147472 | tf_op jit(solution)/shard_map/reduce_scatter | solution.py:388
  1098.6 102.2 %reduce-scatter.26.cloned.1.call-done = bf16[8,192,1024]{2,1,0:T(8,128)(2,1)} async-done(((bf16[8,768,1024]{2,1,0:T(8,128)(2,1)}), bf16[8,192,1024]{2,1,0:T(8,128)(2,1)}) %reduce-scatter.26.cloned.1.call-update) | async-done | bytes 3145744 | tf_op jit(solution)/shard_map/reduce_scatter | solution.py:290
  1200.8 182.9 %reduce-scatter.24.cloned.1.call-done = bf16[8,2,192,1024]{3,0,1,2:T(8,128)(2,1)} async-done(((bf16[8,2,768,1024]{3,0,1,2:T(8,128)(2,1)}), bf16[8,2,192,1024]{3,0,1,2:T(8,128)(2,1)}) %reduce-scatter.24.cloned.1.call-update) | async-done | bytes 6291472 | tf_op jit(solution)/shard_map/reduce_scatter | solution.py:287
  1383.8 22.7 %reduce-scatter.34.cloned.1.call-done = bf16[192,2]{1,0:T(8,128)(2,1)} async-done(((bf16[768,2]{1,0:T(8,128)(2,1)}), bf16[192,2]{1,0:T(8,128)(2,1)}) %reduce-scatter.34.cloned.1.call-update) | async-done | bytes 784
  1408.1 21.2 %reduce-scatter.32.cloned.1.call-done = bf16[192,16]{1,0:T(8,128)(2,1)} async-done(((bf16[768,16]{1,0:T(8,128)(2,1)}), bf16[192,16]{1,0:T(8,128)(2,1)}) %reduce-scatter.32.cloned.1.call-update) | async-done | bytes 6160
  1436.3 15.8 reduce-scatter.28.cloned.1.call-done
  1453.0 19.3 %all-reduce = (bf16[2,192]{1,0:T(2,128)(2,1)S(1)}, bf16[192,16]{0,1:T(8,128)(2,1)S(1)}, bf16[2,192]{1,0:T(2,128)(2,1)S(1)}) all-reduce(bf16[2,192]{1,0:T(2,128)(2,1)S(1)} %copy.262, bf16[192,16]{0,1:T(8,128)(2,1)S(1)} %copy.266, bf16[2,192]{1,0:T(2,128)(2,1)S(1)} %copy.268), channel_id=1, replica_groups=mesh['fsdp'=4,'ctx'=4,'tp'=2] {'ctx'}, use_global_device_ids=true, to_apply=%region_47.48 | all-reduce | flops 3840 | bytes 15360 | tf_op jit(solution)/shard_map/psum | solution.py:393
  1474.0 332.9 %all-reduce.12.cloned.1.call-done = (bf16[3,192,384]{1,2,0:T(8,128)(2,1)}, bf16[8,2,192,1024]{3,0,1,2:T(8,128)(2,1)}, bf16[192,384]{1,0:T(8,128)(2,1)}, bf16[8,192,1024]{2,1,0:T(8,128)(2,1)}) async-done(((bf16[3,192,384]{1,2,0:T(8,128)(2,1)}, bf16[8,2,192,1024]{3,0,1,2:T(8,128)(2,1)}, bf16[192,384]{1,0:T(8,128)(2,1)}, bf16[8,192,1024]{2,1,0:T(8,128)(2,1)}), (bf16[3,192,384]{1,2,0:T(8,128)(2,1)}, ...) | async-done | bytes 10027024 | tf_op jit(solution)/shard_map/psum | solution.py:394
  1810.7 11.4 copy.251
  (386 shorter events, 252.0 us)
Async XLA Ops:
  7.2 26.0 %all-gather.9.cloned.1.call-start = ((), (), s32[]{:S(2)}) async-start(), calls=%async_computation.9 | async-start | bytes 2211840 | tf_op jit(solution)/shard_map/all_gather | solution.py:99
  7.9 106.2 %all-gather.11.cloned.1.call-start = ((), (), s32[]{:S(2)}) async-start(), calls=%async_computation.10 | async-start | bytes 3932160 | tf_op jit(solution)/shard_map/all_gather | solution.py:129
  16.2 20.7 %copy-start.42 = (f32[1,4,2,128]{3,1,2,0:T(4,128)}, f32[1,4,2,128]{3,1,2,0:T(4,128)S(1)}, u32[]{:S(2)}) copy-start(f32[1,4,2,128]{3,1,2,0:T(4,128)S(1)} %copy.301) | copy-start | bytes 12292
  17.1 28.6 %copy-start.30 = (f32[512,32]{0,1:T(8,128)}, f32[512,32]{0,1:T(8,128)S(1)}, u32[]{:S(2)}) copy-start(f32[512,32]{0,1:T(8,128)S(1)} %get-tuple-element.488) | copy-start | bytes 196612
  17.1 28.6 %copy-start.32 = (f32[512,32]{0,1:T(8,128)}, f32[512,32]{0,1:T(8,128)S(1)}, u32[]{:S(2)}) copy-start(f32[512,32]{0,1:T(8,128)S(1)} %get-tuple-element.489) | copy-start | bytes 196612
  17.8 15.3 copy-start.23
  50.5 127.9 %all-gather.13.cloned.1.call-start = ((), (), s32[]{:S(2)}) async-start(), calls=%async_computation.11 | async-start | bytes 3932160 | tf_op jit(solution)/shard_map/all_gather | solution.py:130
  53.3 271.4 %all-reduce.8.cloned.1.call-start = ((), (), s32[]{:S(2)}) async-start(), calls=%async_computation.12 | async-start | bytes 3145728 | tf_op jit(solution)/shard_map/psum | solution.py:172
  203.5 12.1 copy-start.18
  203.5 12.1 copy-start.25
  242.5 12.1 copy-start.18
  242.5 12.1 copy-start.25
  274.4 206.4 %all-gather.15.cloned.1.call-start = ((), (), s32[]{:S(2)}) async-start(), calls=%async_computation.13 | async-start | bytes 31457280 | tf_op jit(solution)/shard_map/all_gather | solution.py:177
  275.0 289.4 %all-gather.17.cloned.1.call-start = ((), (), s32[]{:S(2)}) async-start(), calls=%async_computation.14 | async-start | bytes 15728640 | tf_op jit(solution)/shard_map/all_gather | solution.py:178
  275.6 12.3 copy-start.36
  275.6 19.8 %copy-start.63 = (s32[2]{0:T(128)S(1)}, s32[2]{0:T(128)}, u32[]{:S(2)}) copy-start(s32[2]{0:T(128)} %constant.110) | copy-start | bytes 28
  275.6 19.9 %copy-start.62 = (s32[2]{0:T(128)S(1)}, s32[2]{0:T(128)}, u32[]{:S(2)}) copy-start(s32[2]{0:T(128)} %constant.113) | copy-start | bytes 28
  275.6 393.4 %all-reduce.10.cloned.1.call-start = ((), (), s32[]{:S(2)}) async-start(), calls=%async_computation.15 | async-start | bytes 3145728 | tf_op jit(solution)/shard_map/psum | solution.py:245
  305.2 22.2 %copy-start.44 = (f32[768]{0:T(1024)S(1)}, f32[768]{0:T(1024)}, u32[]{:S(2)}) copy-start(f32[768]{0:T(1024)} %get-tuple-element.387) | copy-start | bytes 9220
  305.2 295.3 %copy-start.59 = (s32[2048,1]{0,1:T(1,128)}, s32[2048,1]{0,1:T(1,128)S(1)}, u32[]{:S(2)}) copy-start(s32[2048,1]{0,1:T(1,128)S(1)} %compare_select_fusion) | copy-start | bytes 24580
  327.4 346.0 %copy-start.46 = (f32[1024]{0:T(1024)}, f32[1024]{0:T(1024)S(1)}, u32[]{:S(2)}) copy-start(f32[1024]{0:T(1024)S(1)} %get-tuple-element.487) | copy-start | bytes 12292
  363.6 117.2 %copy-start.10 = (bf16[2048,768]{1,0:T(8,128)(2,1)S(1)}, bf16[2048,768]{1,0:T(8,128)(2,1)}, u32[]{:S(2)}) copy-start(bf16[2048,768]{1,0:T(8,128)(2,1)} %gather_fusion) | copy-start | bytes 9437188
  370.1 130.4 %copy-start.53 = (f32[1,4,2,128]{3,1,2,0:T(4,128)}, f32[1,4,2,128]{3,1,2,0:T(4,128)S(1)}, u32[]{:S(2)}) copy-start(f32[1,4,2,128]{3,1,2,0:T(4,128)S(1)} %copy.305) | copy-start | bytes 12292
  370.2 247.4 %copy-start.37 = (f32[8,256]{1,0:T(8,128)}, f32[8,256]{1,0:T(8,128)S(1)}, u32[]{:S(2)}) copy-start(f32[8,256]{1,0:T(8,128)S(1)} %fusion.81) | copy-start | bytes 24580
  370.3 298.7 %copy-start.55 = (bf16[1024,4]{0,1:T(4,128)(2,1)}, bf16[1024,4]{0,1:T(4,128)(2,1)S(1)}, u32[]{:S(2)}) copy-start(bf16[1024,4]{0,1:T(4,128)(2,1)S(1)} %multiply_convert_fusion.6) | copy-start | bytes 24580
  617.4 270.7 %reduce-scatter.18.cloned.1.call-start = ((), (), s32[]{:S(2)}) async-start(), calls=%async_computation.16 | async-start | bytes 3932160 | tf_op jit(solution)/shard_map/reduce_scatter | solution.py:357
  617.6 51.4 %copy-start.6 = (bf16[2,512,768]{2,1,0:T(8,128)(2,1)S(1)}, bf16[2,512,768]{2,1,0:T(8,128)(2,1)}, u32[]{:S(2)}) copy-start(bf16[2,512,768]{2,1,0:T(8,128)(2,1)} %param.16) | copy-start | bytes 4718596
  617.6 51.4 %copy-start.14 = (bf16[1024,768]{1,0:T(8,128)(2,1)S(1)}, bf16[1024,768]{1,0:T(8,128)(2,1)}, u32[]{:S(2)}) copy-start(bf16[1024,768]{1,0:T(8,128)(2,1)} %all-reduce.8.cloned.1.call-done) | copy-start | bytes 4718596
  650.5 22.8 %copy-start.40 = (bf16[1024,12]{0,1:T(8,128)(2,1)}, bf16[1024,12]{0,1:T(8,128)(2,1)S(1)}, u32[]{:S(2)}) copy-start(bf16[1024,12]{0,1:T(8,128)(2,1)S(1)} %convert.68) | copy-start | bytes 73732
  827.6 123.0 %reduce-scatter.20.cloned.1.call-start = ((), (), s32[]{:S(2)}) async-start(), calls=%async_computation.17 | async-start | bytes 3932160 | tf_op jit(solution)/shard_map/reduce_scatter | solution.py:360
  828.3 213.6 %all-reduce.14.cloned.1.call-start = ((), (), s32[]{:S(2)}) async-start(), calls=%async_computation.26 | async-start | bytes 6291456 | tf_op jit(solution)/shard_map/psum | solution.py:221
  845.3 45.0 %copy-start.31 = (f32[512,32]{0,1:T(8,128)S(1)}, f32[512,32]{0,1:T(8,128)}, u32[]{:S(2)}) copy-start(f32[512,32]{0,1:T(8,128)} %copy-done.30) | copy-start | bytes 196612
  845.3 45.0 %copy-start.33 = (f32[512,32]{0,1:T(8,128)S(1)}, f32[512,32]{0,1:T(8,128)}, u32[]{:S(2)}) copy-start(f32[512,32]{0,1:T(8,128)} %copy-done.32) | copy-start | bytes 196612
  895.0 55.6 %copy-start.28 = (bf16[1,1024,384]{2,1,0:T(8,128)(2,1)}, bf16[1,1024,384]{2,1,0:T(8,128)(2,1)S(1)}, u32[]{:S(2)}) copy-start(bf16[1,1024,384]{2,1,0:T(8,128)(2,1)S(1)} %copy.245) | copy-start | bytes 2359300
  896.0 59.8 %copy-start.29 = (bf16[1,1024,384]{2,1,0:T(8,128)(2,1)}, bf16[1,1024,384]{2,1,0:T(8,128)(2,1)S(1)}, u32[]{:S(2)}) copy-start(bf16[1,1024,384]{2,1,0:T(8,128)(2,1)S(1)} %copy.244) | copy-start | bytes 2359300
  955.8 118.3 %reduce-scatter.30.cloned.1.call-start = ((), (), s32[]{:S(2)}) async-start(), calls=%async_computation.22 | async-start | bytes 2211840
  967.6 131.0 %reduce-scatter.22.cloned.1.call-start = ((), (), s32[]{:S(2)}) async-start(), calls=%async_computation.18 | async-start | bytes 737280 | tf_op jit(solution)/shard_map/reduce_scatter | solution.py:388
  970.6 230.2 %reduce-scatter.26.cloned.1.call-start = ((), (), s32[]{:S(2)}) async-start(), calls=%async_computation.20 | async-start | bytes 15728640 | tf_op jit(solution)/shard_map/reduce_scatter | solution.py:290
  983.2 400.5 %reduce-scatter.24.cloned.1.call-start = ((), (), s32[]{:S(2)}) async-start(), calls=%async_computation.19 | async-start | bytes 31457280 | tf_op jit(solution)/shard_map/reduce_scatter | solution.py:287
  1036.0 370.5 %reduce-scatter.34.cloned.1.call-start = ((), (), s32[]{:S(2)}) async-start(), calls=%async_computation.24 | async-start | bytes 245760
  1037.5 391.8 %reduce-scatter.32.cloned.1.call-start = ((), (), s32[]{:S(2)}) async-start(), calls=%async_computation.23 | async-start | bytes 245760
  1038.7 413.4 %reduce-scatter.28.cloned.1.call-start = ((), (), s32[]{:S(2)}) async-start(), calls=%async_computation.21 | async-start | bytes 245760
  1045.6 761.3 %all-reduce.12.cloned.1.call-start = ((), (), s32[]{:S(2)}) async-start(), calls=%async_computation.25 | async-start | bytes 20348928 | tf_op jit(solution)/shard_map/psum | solution.py:394
  1383.7 23.7 %copy-start.35 = (f32[1024,12]{0,1:T(8,128)S(1)}, f32[1024,12]{0,1:T(8,128)}, u32[]{:S(2)}) copy-start(f32[1024,12]{0,1:T(8,128)} %copy-done.34) | copy-start | bytes 147460
  1383.7 46.4 %copy-start.15 = (bf16[1024,768]{1,0:T(8,128)(2,1)S(1)}, bf16[1024,768]{1,0:T(8,128)(2,1)}, u32[]{:S(2)}) copy-start(bf16[1024,768]{1,0:T(8,128)(2,1)} %all-reduce.8.cloned.1.call-done) | copy-start | bytes 4718596
  1383.7 46.4 %copy-start.45 = (f32[768]{0:T(1024)S(1)}, f32[768]{0:T(1024)}, u32[]{:S(2)}) copy-start(f32[768]{0:T(1024)} %get-tuple-element.387) | copy-start | bytes 9220
  1383.7 46.4 %copy-start.47 = (f32[1024]{0:T(1024)S(1)}, f32[1024]{0:T(1024)}, u32[]{:S(2)}) copy-start(f32[1024]{0:T(1024)} %copy-done.46) | copy-start | bytes 12292
  1383.7 46.4 %copy-start.54 = (f32[1,4,2,128]{3,1,2,0:T(4,128)S(1)}, f32[1,4,2,128]{3,1,2,0:T(4,128)}, u32[]{:S(2)}) copy-start(f32[1,4,2,128]{3,1,2,0:T(4,128)} %copy-done.53) | copy-start | bytes 12292
  (41 other events, 181.2 us)
Sparse Core Ops, SparseCore 0:
  9.6 23.5 all-gather.8
  50.6 63.3 all-gather.10
  116.2 62.1 all-gather.12
  274.5 50.1 all-reduce.7
  326.2 154.4 all-gather.14
  482.3 82.0 all-gather.16
  617.5 51.4 all-reduce.9
  827.7 60.2 reduce-scatter.17
  890.3 60.2 reduce-scatter.19
  955.9 85.9 all-reduce.13
  1044.7 29.3 reduce-scatter.29
  1076.5 22.0 reduce-scatter.21
  1101.7 99.0 reduce-scatter.25
  1203.2 180.4 reduce-scatter.23
  1386.7 19.7 reduce-scatter.33
  1409.5 19.7 reduce-scatter.31
  1432.3 19.7 reduce-scatter.27
  1455.7 351.1 all-reduce.11
where the time goes:
time: 1840 us; the launch traced here: 1830 us
  waiting for transfers between devices  1160 us (63%)
  matrix products  288 us (16%)
  local copies, waits for them, and re-layouts  176 us (10%)
  other arithmetic  139 us (8%)
  blocking collectives  49 us (3%)
    psum x1, waiting for transfers between devices, on_device(): lax.psum(attention_owned[1].astype(jnp.bfloat16), 'ctx').astype(jnp.float32)  333 us
    reduce_scatter x1, waiting for transfers between devices, on_device(): lax.psum_scatter(grad_gu_local.astype(jnp.bfloat16), 'fsdp', scatter_dime...  183 us
    all_gather x1, waiting for transfers between devices, on_device(): lax.all_gather(gate_up, 'fsdp', axis=2, tiled=True)  110 us
    reduce_scatter x1, waiting for transfers between devices, on_device(): lax.psum_scatter(grad_down_local.astype(jnp.bfloat16), 'fsdp', scatter_di...  102 us
    unnamed x22, waiting for transfers between devices  90.6 us
    all_gather x1, waiting for transfers between devices, on_device(): lax.all_gather(down_weight, 'fsdp', axis=1, tiled=True)  63.9 us
    reduce_scatter x1, waiting for transfers between devices, on_device(): lax.psum_scatter(value_term_all.astype(jnp.bfloat16), 'ctx', scatter_dime...  54.6 us
    all_gather x1, waiting for transfers between devices, on_device(): value_piece = lax.all_gather(value_flat, 'ctx', axis=1, tiled=True)  53.5 us
  transfers between devices with their start and end apart: 18, of which 18 were waited for; matrix products, arithmetic and copies ran while one was open for 14% of the time, Pallas kernels for 0%

commit v1 on v0

--- a/solution.py
+++ b/solution.py
@@ -1,8 +1,11 @@
+import functools
 import math
 
 import jax
 import jax.numpy as jnp
 from jax import lax
+from jax.experimental import pallas as pl
+from jax.experimental.pallas import tpu as pltpu
 from jax.sharding import PartitionSpec as P
 
 HEAD_DIM = 64
@@ -56,7 +59,10 @@
     experts = jnp.arange(NFFN, dtype=jnp.int32)
     matches = block_routes[None, :, :] == experts[:, None, None]
     hit_rows = jnp.any(matches, axis=2).astype(jnp.int32)
-    places = jnp.cumsum(hit_rows, axis=1) - 1
+    earlier = jnp.tril(jnp.ones((row_count, row_count), jnp.float32))
+    places = jnp.einsum(
+        "er,sr->es", hit_rows.astype(jnp.float32), earlier, precision=lax.Precision.HIGHEST
+    ).astype(jnp.int32) - 1
     slot_ids = jnp.arange(CAPACITY, dtype=jnp.int32)
     chosen = ((places[:, :, None] == slot_ids[None, None, :]) & (hit_rows[:, :, None] > 0)).astype(
         jnp.int32
@@ -413,6 +419,851 @@
     )
 
 
+MIB = 1 << 20
+F32 = jnp.float32
+BF = jnp.bfloat16
+WHOLE = pl.BlockSpec(memory_space=pltpu.VMEM)
+SCALARS = pl.BlockSpec(memory_space=pltpu.SMEM)
+LOG2E = 1.4426950408889634
+
+
+def mm(a, b):
+    return lax.dot_general(a, b, (((1,), (0,)), ((), ())), preferred_element_type=F32)
+
+
+def mm_nt(a, b):
+    return lax.dot_general(a, b, (((1,), (1,)), ((), ())), preferred_element_type=F32)
+
+
+def mm_tn(a, b):
+    return lax.dot_general(a, b, (((0,), (0,)), ((), ())), preferred_element_type=F32)
+
+
+def out(shape, dtype=BF):
+    return jax.ShapeDtypeStruct(shape, dtype)
+
+
+def run(body, name, scalars, ins, outs, scratch=(), flops=0, vmem=56):
+    moved = sum(math.prod(a.shape) * a.dtype.itemsize for a in (*ins, *outs))
+    return pl.pallas_call(
+        body,
+        out_shape=tuple(outs),
+        in_specs=[SCALARS] + [WHOLE] * len(ins),
+        out_specs=tuple([WHOLE] * len(outs)),
+        scratch_shapes=list(scratch),
+        compiler_params=pltpu.CompilerParams(vmem_limit_bytes=vmem * MIB),
+        cost_estimate=pl.CostEstimate(flops=flops, bytes_accessed=moved, transcendentals=0),
+        name=name,
+    )(scalars, *ins)
+
+
+def pack_kernel(sc, routes_ref, gy_ref, hot_ref, gyt_ref, *g_refs):
+    me = sc[0]
+    rows = gy_ref.shape[0]
+    named = routes_ref[...]
+    named = jnp.where(named < NFFN, jnp.bitwise_xor(named, me), named)
+    first, second = named[0:1], named[1:2]
+    gyt = gy_ref[...].T
+    gyt_ref[...] = gyt
+    ids = lax.broadcasted_iota(jnp.int32, (16, rows), 0)
+    hits = ((ids == first) | (ids == second)).astype(F32)
+    before = lax.broadcasted_iota(jnp.int32, (rows, rows), 0)
+    after = lax.broadcasted_iota(jnp.int32, (rows, rows), 1)
+    upper = (before <= after).astype(F32).astype(BF)
+    places = mm(hits.astype(BF), upper) - 1.0
+    slots = lax.broadcasted_iota(jnp.int32, (CAPACITY, rows), 0).astype(F32)
+    for k in range(NFFN):
+        hot = jnp.where((slots == places[k : k + 1]) & (hits[k : k + 1] > 0.5), 1.0, 0.0)
+        hot = hot.astype(BF)
+        hot_ref[k * CAPACITY : (k + 1) * CAPACITY, :] = hot
+        g_refs[k][...] = mm_nt(gyt, hot).astype(BF)
+
+
+def norm_kernel(sc, tokens_ref, gain_ref, n_ref, nt_ref, xt_ref):
+    for s in range(2):
+        x = tokens_ref[s].astype(F32)
+        inverse = lax.rsqrt(jnp.mean(x * x, axis=-1, keepdims=True) + epsilon)
+        n = (x * inverse * gain_ref[...]).astype(BF)
+        n_ref[s] = n
+        nt_ref[:, s * x.shape[0] : (s + 1) * x.shape[0]] = n.T
+    xt_ref[...] = tokens_ref[sc[2]].T
+
+
+def swap_halves(v):
+    width = v.shape[1]
+    lane = lax.broadcasted_iota(jnp.int32, v.shape, 1)
+    half = HEAD_DIM // 2
+    low = jnp.bitwise_and(lane, HEAD_DIM - 1) < half
+    return jnp.where(low, pltpu.roll(v, width - half, 1), pltpu.roll(v, half, 1))
+
+
+def qkv_kernel(sc, n_ref, p0, p1, p2, p3, cos_ref, sin_ref, o0, o1, o2, o3, w_out, wo_out, st):
+    z, f = sc[1], sc[3]
+    for j, p in enumerate((p0, p1, p2, p3)):
+        src = jnp.bitwise_xor(f, j)
+        rows = pl.multiple_of(src * 192, 192)
+        for c in range(3):
+            w_out[c, pl.ds(rows, 192), :] = p[c * 192 : (c + 1) * 192, :]
+        wo_out[pl.ds(rows, 192), :] = p[576:768, :]
+    cos = jnp.concatenate([cos_ref[...]] * 3, axis=1)
+    sin = jnp.concatenate([sin_ref[...]] * 3, axis=1)
+    half_rows = cos.shape[0] // 2
+    for s in range(2):
+        n = n_ref[s]
+        q = mm(n, w_out[0])
+        k = mm(n, w_out[1])
+        q = (q * cos + swap_halves(q) * sin).astype(BF)
+        k = (k * cos + swap_halves(k) * sin).astype(BF)
+        v = mm(n, w_out[2]).astype(BF)
+        for half in range(2):
+            d = jnp.bitwise_xor(z, 2 * s + half)
+            for j in range(3):
+                col = (half * 3 + j) * HEAD_DIM
+                parts = [
+                    a[r * half_rows : (r + 1) * half_rows, col : col + HEAD_DIM]
+                    for r in range(2)
+                    for a in (q, k, v)
+                ]
+                st[d, j] = jnp.concatenate(parts, axis=1)
+    for d, o in enumerate((o0, o1, o2, o3)):
+        o[...] = st[d]
+
+
+def unpack_qkv(z, blocks, q_s, k_s, v_s):
+    h = HEAD_DIM
+    for d, b in enumerate(blocks):
+        base = pl.multiple_of(jnp.bitwise_xor(z, d) * 512, 512)
+        for j in range(3):
+            blk = b[j]
+            for r in range(2):
+                at = pl.ds(base + r * 256, 256)
+                q_s[j, at, :] = blk[:, r * 192 : r * 192 + h]
+                k_s[j, at, :] = blk[:, r * 192 + h : r * 192 + 2 * h]
+                v_s[j, at, :] = blk[:, r * 192 + 2 * h : r * 192 + 3 * h]
+
+
+def attn_masks(prefix):
+    return [(i, [(t, t >= i) for t in range(max(2, i + 1))]) for i in range(4)]
+
+
+def allowed_tile(key_tile, query_tile, prefix):
+    key = lax.broadcasted_iota(jnp.int32, (512, 512), 0) + key_tile * 512
+    query = lax.broadcasted_iota(jnp.int32, (512, 512), 1) + query_tile * 512
+    return (key <= query) | (key < prefix)
+
+
+def attn_kernel(sc, b0, b1, b2, b3, o0, o1, o2, o3, m_ref, q_s, k_s, v_s, st):
+    z, prefix = sc[1], sc[4]
+    unpack_qkv(z, (b0, b1, b2, b3), q_s, k_s, v_s)
+    scale = HEAD_DIM ** (-0.5) * LOG2E
+
+    def unit(j, carry):
+        vt = v_s[j].T
+        for i, tiles in attn_masks(prefix):
+            q = q_s[j, i * 512 : (i + 1) * 512, :]
+            scores = []
+            for t, masked in tiles:
+                s = mm_nt(k_s[j, t * 512 : (t + 1) * 512, :], q)
+                if masked:
+                    s = jnp.where(allowed_tile(t, i, prefix), s, -1e30)
+                scores.append(s)
+            top = scores[0].max(axis=0, keepdims=True)
+            for s in scores[1:]:
+                top = jnp.maximum(top, s.max(axis=0, keepdims=True))
+            total = jnp.zeros_like(top)
+            acc = jnp.zeros((HEAD_DIM, 512), F32)
+            for (t, masked), s in zip(tiles, scores):
+                p = jnp.exp2((s - top) * scale)
+                total = total + p.sum(axis=0, keepdims=True)
+                acc = acc + mm(vt[:, t * 512 : (t + 1) * 512], p.astype(BF))
+            mixed = acc / total
+            cols = slice(i * 512, (i + 1) * 512)
+            m_ref[j, 0:HEAD_DIM, cols] = mixed
+            m_ref[j, HEAD_DIM : HEAD_DIM + 8, cols] = jnp.broadcast_to(
+                top * scale + jnp.log2(total), (8, 512)
+            )
+            st[i, pl.ds(pl.multiple_of(j * HEAD_DIM, HEAD_DIM), HEAD_DIM), :] = mixed.astype(BF)
+        return carry
+
+    lax.fori_loop(0, 3, unit, 0)
+    for d, o in enumerate((o0, o1, o2, o3)):
+        o[...] = st[jnp.bitwise_xor(z, d)]
+
+
+def outproj_kernel(sc, b0, b1, b2, b3, wo_ref, mixed_ref, own_ref, send_ref, st):
+    z, x = sc[1], sc[2]
+    for d, b in enumerate((b0, b1, b2, b3)):
+        st[d] = b[...]
+    for s in range(2):
+        for half in range(2):
+            mixed_ref[s, half * 192 : (half + 1) * 192, :] = st[jnp.bitwise_xor(z, 2 * s + half)]
+    own_ref[...] = mm(wo_ref[...], mixed_ref[x]).astype(BF)
+    send_ref[...] = mm(wo_ref[...], mixed_ref[1 - x]).astype(BF)
+
+
+def row_state(me, hidden, gain, gate_t, prev, routes):
+    rows = hidden.shape[1]
+    inverse = lax.rsqrt(jnp.mean(hidden * hidden, axis=0, keepdims=True) + epsilon)
+    normed = hidden * inverse * gain
+    normed_b = normed.astype(BF)
+    logits = mm(gate_t, normed_b)
+    router = logits + prev
+    ids = lax.broadcasted_iota(jnp.int32, (16, rows), 0)
+    named = [routes[0:1], routes[1:2]]
+    picks = [jnp.sum(jnp.where(ids == r, router, 0.0), axis=0, keepdims=True) for r in named]
+    top = jnp.maximum(picks[0], picks[1])
+    e = [jnp.exp(p - top) for p in picks]
+    gates = [v / (e[0] + e[1]) for v in e]
+    ks = [jnp.where(r < NFFN, jnp.bitwise_xor(r, me), r) for r in named]
+    copy_w = sum(jnp.where(r == NFFN + 1, g, 0.0) for r, g in zip(named, gates))
+    const_w = [
+        sum(jnp.where(r == NFFN + 2 + c, g, 0.0) for r, g in zip(named, gates))
+        for c in range(NCONST)
+    ]
+    mixing = []
+    for c in range(NCONST):
+        a, b = logits[NEXP + 2 * c : NEXP + 2 * c + 1], logits[NEXP + 2 * c + 1 : NEXP + 2 * c + 2]
+        t = jnp.maximum(a, b)
+        ea, eb = jnp.exp(a - t), jnp.exp(b - t)
+        mixing.append((ea / (ea + eb), eb / (ea + eb)))
+    return dict(
+        inverse=inverse, normed=normed, normed_b=normed_b, ids=ids, named=named, ks=ks,
+        gates=gates, copy_w=copy_w, const_w=const_w, mixing=mixing,
+    )
+
+
+def router_kernel(sc, xt, own, recv, gain, gate_t, prev, routes, hot, hidden_ref, *x_refs):
+    me = sc[0]
+    hidden = xt[...].astype(F32) + (own[...].astype(F32) + recv[...].astype(F32))
+    hidden_ref[...] = hidden
+    s = row_state(me, hidden, gain[...], gate_t[...], prev[...], routes[...])
+    ids = s["ids"][0:8]
+    gate_rows = sum(jnp.where(ids == k, g, 0.0) for k, g in zip(s["ks"], s["gates"]))
+    high = gate_rows.astype(BF).astype(F32)
+    extra = jnp.concatenate([high, gate_rows - high], axis=0).astype(BF)
+    ext = jnp.concatenate([s["normed_b"], extra], axis=0)
+    for k in range(NFFN):
+        x_refs[k][...] = mm_nt(ext, hot[k * CAPACITY : (k + 1) * CAPACITY, :]).astype(BF)
+
+
+def wprep_kernel(sc, *refs):
+    blocks, w_ref, wt_ref = refs[:8], refs[8], refs[9]
+    me = sc[0]
+    for k, b in enumerate(blocks):
+        s = jnp.bitwise_xor(me, k)
+        rows = pl.multiple_of((s // 2) * 192, 192)
+        cols = pl.multiple_of((s % 2) * 1024, 1024)
+        for m in range(3):
+            w_ref[m, pl.ds(rows, 192), pl.ds(cols, 1024)] = b[m]
+    tile = 256
+
+    def step(t, carry):
+        at = pl.ds(pl.multiple_of(t * tile, tile), tile)
+        for m in range(3):
+            wt_ref[m, at, :] = w_ref[m, :, at].T
+        return carry
+
+    lax.fori_loop(0, w_ref.shape[2] // tile, step, 0)
+
+
+def expert_body(first, sc, xs, gs, w, wt, *refs):
+    if first:
+        y_refs, r_refs = refs[0:8], refs[8:16]
+        refs = refs[16:]
+    else:
+        refs = refs[5:]
+    bx, bg, ba, bp, bu = refs[:5]
+    refs = refs[5:]
+    xt, gt, grow = refs[:3]
+    if first:
+        din, res, graw = refs[3:]
+    j = pl.program_id(0)
+
+    @pl.when(j == 0)
+    def _():
+        for k in range(8):
+            cols = slice(k * CAPACITY, (k + 1) * CAPACITY)
+            xt[:, cols] = xs[k, 0:768]
+            pair = xs[k, 768:784].astype(F32)
+            gate = pair[k : k + 1] + pair[8 + k : 9 + k]
+            grow[:, cols] = jnp.broadcast_to(gate, (8, CAPACITY))
+            g = gs[k]
+            if first:
+                graw[:, cols] = g
+            gt[:, cols] = (g.astype(F32) * gate).astype(BF)
+        if first:
+            din[...] = jnp.zeros_like(din)
+            res[...] = jnp.zeros_like(res)
+        bx[0] = xt[...]
+        bg[0] = gt[...]
+
+    x = xt[...]
+    pre = mm(wt[0], x)
+    up = mm(wt[1], x)
+    sig = 1.0 / (1.0 + jnp.exp(-pre))
+    silu = pre * sig
+    act = (silu * up).astype(BF)
+    ba[0] = act
+    da = mm(wt[2], gt[...])
+    dp = (da * up * (sig * (1.0 + pre * (1.0 - sig)))).astype(BF)
+    du = (da * silu).astype(BF)
+    bp[0] = dp
+    bu[0] = du
+    if first:
+        din[...] += mm(w[0], dp) + mm(w[1], du)
+        res[...] += mm(w[2], act)
+
+        @pl.when(j == pl.num_programs(0) - 1)
+        def _():
+            row = lax.broadcasted_iota(jnp.int32, (8, CAPACITY), 0)
+            for k in range(8):
+                cols = slice(k * CAPACITY, (k + 1) * CAPACITY)
+                r = res[:, cols]
+                dg = jnp.sum(graw[:, cols].astype(F32) * r, axis=0, keepdims=True)
+                high = dg.astype(BF).astype(F32)
+                tail = jnp.concatenate(
+                    [jnp.where(row == k, high, 0.0), jnp.where(row == k, dg - high, 0.0)], axis=0
+                )
+                y_refs[k][0:768, :] = din[:, cols].astype(BF)
+                y_refs[k][768:784, :] = tail.astype(BF)
+                r_refs[k][...] = (r * grow[0:1, cols]).astype(BF)
+
+
+def expert_call(first, plane, xs, gs, w, wt, held):
+    tile = 512 if first else 512
+    steps = w.shape[2] // tile
+    slots = 8 * CAPACITY
+    width = w.shape[1]
+    n_ctx = 4
+    buffers = [
+        out((n_ctx, width, slots)), out((n_ctx, width, slots)),
+        out((n_ctx, w.shape[2], slots)), out((n_ctx, w.shape[2], slots)), out((n_ctx, w.shape[2], slots)),
+    ]
+    fixed3 = lambda j, s: (0, 0, 0)
+    specs_in = [
+        pl.BlockSpec(xs.shape, fixed3), pl.BlockSpec(gs.shape, fixed3),
+        pl.BlockSpec((3, width, tile), lambda j, s: (0, 0, j)),
+        pl.BlockSpec((3, tile, width), lambda j, s: (0, j, 0)),
+    ]
+    buffer_specs = [
+        pl.BlockSpec((1, width, slots), lambda j, s: (s[0], 0, 0)),
+        pl.BlockSpec((1, width, slots), lambda j, s: (s[0], 0, 0)),
+    ] + [pl.BlockSpec((1, tile, slots), lambda j, s: (s[0], j, 0))] * 3
+    scratch = [
+        pltpu.VMEM((width, slots), BF), pltpu.VMEM((width, slots), BF), pltpu.VMEM((8, slots), F32),
+    ]
+    outs, specs_out, aliases, extra_in = list(buffers), list(buffer_specs), {}, []
+    if first:
+        packet = [out((width + 16, CAPACITY))] * 8 + [out((width, CAPACITY))] * 8
+        outs = packet + outs
+        specs_out = [pl.BlockSpec(p.shape, lambda j, s: (0, 0)) for p in packet] + specs_out
+        scratch += [pltpu.VMEM((width, slots), F32)] * 2 + [pltpu.VMEM((width, slots), BF)]
+    else:
+        extra_in = list(held)
+        specs_in += [pl.BlockSpec(memory_space=pl.ANY)] * 5
+        aliases = {5 + i: i for i in range(5)}
+    macs = width * w.shape[2] * slots * (6 if first else 3)
+    return pl.pallas_call(
+        functools.partial(expert_body, first),
+        out_shape=tuple(outs),
+        grid_spec=pltpu.PrefetchScalarGridSpec(
+            num_scalar_prefetch=1, grid=(steps,), in_specs=specs_in, out_specs=tuple(specs_out),
+            scratch_shapes=scratch,
+        ),
+        input_output_aliases=aliases,
+        compiler_params=pltpu.CompilerParams(vmem_limit_bytes=58 * MIB),
+        cost_estimate=pl.CostEstimate(flops=2 * macs, bytes_accessed=40 * MIB, transcendentals=0),
+        name="experts_own" if first else "experts_more",
+    )(plane, xs, gs, w, wt, *extra_in)
+
+
+def grads_body(w_cols, sc, bx, bg, ba, bp, bu, *refs):
+    outs, acc = refs[:8], refs[8]
+    p = pl.program_id(0)
+
+    @pl.when(p == 0)
+    def _():
+        acc[...] = jnp.zeros_like(acc)
+
+    for xh in range(2):
+        acc[xh, 0] += mm_nt(bx[0], bp[0, xh])
+        acc[xh, 1] += mm_nt(bx[0], bu[0, xh])
+        acc[xh, 2] += mm_nt(bg[0], ba[0, xh])
+
+    @pl.when(p == pl.num_programs(0) - 1)
+    def _():
+        me = sc[0]
+        for k in range(8):
+            s = jnp.bitwise_xor(me, k)
+            rows = pl.multiple_of((s // 2) * 192, 192)
+            for m in range(3):
+                outs[k][m] = acc[s % 2, m, pl.ds(rows, 192), :].astype(BF)
+
+
+def grads_call(scalars, part, parts, held):
+    bx, bg, ba, bp, bu = held
+    n_ctx, width, slots = bx.shape
+    half = ba.shape[1] // 2
+    cols = half // parts
+    split = lambda a: a.reshape(n_ctx, 2, half, slots)
+    tall = pl.BlockSpec((1, 2, cols, slots), lambda p, s: (p, 0, part, 0))
+    macs = 3 * width * slots * n_ctx * 2 * cols
+    return pl.pallas_call(
+        functools.partial(grads_body, cols),
+        out_shape=tuple([out((3, 192, cols))] * 8),
+        grid_spec=pltpu.PrefetchScalarGridSpec(
+            num_scalar_prefetch=1, grid=(n_ctx,),
+            in_specs=[pl.BlockSpec((1, width, slots), lambda p, s: (p, 0, 0))] * 2 + [tall] * 3,
+            out_specs=tuple([pl.BlockSpec((3, 192, cols), lambda p, s: (0, 0, 0))] * 8),
+            scratch_shapes=[pltpu.VMEM((2, 3, width, cols), F32)],
+        ),
+        compiler_params=pltpu.CompilerParams(vmem_limit_bytes=56 * MIB),
+        cost_estimate=pl.CostEstimate(flops=2 * macs, bytes_accessed=30 * MIB, transcendentals=0),
+        name="expert_grads",
+    )(scalars, bx, bg, split(ba), split(bp), split(bu))
+
+
+def place_body(first, sc, *refs):
+    blocks = refs[:8]
+    gu, dn = refs[8:] if first else refs[10:]
+    at = pl.program_id(0)
+    for k in range(8):
+
+        @pl.when(at == k)
+        def _(k=k):
+            gu[0, 0] = blocks[k][0].astype(F32)
+            gu[0, 1] = blocks[k][1].astype(F32)
+            dn[0] = blocks[k][2].astype(F32)
+
+
+def place_call(scalars, part, parts, blocks, held):
+    cols = blocks[0].shape[2]
+    first = held is None
+    xor = lambda k, s: jnp.bitwise_xor(k, s[0])
+    extra = [] if first else list(held)
+    return pl.pallas_call(
+        functools.partial(place_body, first),
+        out_shape=(out((NFFN, 2, 192, cols * parts), F32), out((NFFN, 192, cols * parts), F32)),
+        grid_spec=pltpu.PrefetchScalarGridSpec(
+            num_scalar_prefetch=1, grid=(NFFN,),
+            in_specs=[pl.BlockSpec((3, 192, cols), lambda k, s: (0, 0, 0))] * 8
+            + [pl.BlockSpec(memory_space=pl.ANY)] * len(extra),
+            out_specs=(
+                pl.BlockSpec((1, 2, 192, cols), lambda k, s: (xor(k, s), 0, 0, part)),
+                pl.BlockSpec((1, 192, cols), lambda k, s: (xor(k, s), 0, part)),
+            ),
+        ),
+        input_output_aliases={} if first else {9: 0, 10: 1},
+        compiler_params=pltpu.CompilerParams(vmem_limit_bytes=40 * MIB),
+        cost_estimate=pl.CostEstimate(flops=0, bytes_accessed=28 * MIB // parts, transcendentals=0),
+        name="place_grads",
+    )(scalars, *blocks, *extra)
+
+
+def combine_kernel(sc, hidden_ref, gain, gate_t, gate, prev, routes, const, gyt, hot, *refs):
+    ys, (dt_ref, gprev_ref, small_ref) = refs[:8], refs[8:]
+    hidden = hidden_ref[...]
+    width, rows = hidden.shape
+    s = row_state(sc[0], hidden, gain[...], gate_t[...], prev[...], routes[...])
+    y = jnp.concatenate([r[...] for r in ys], axis=1)
+    back = mm(y, hot[...])
+    ids, named, gates, mixing = s["ids"], s["named"], s["gates"], s["mixing"]
+    normed, inverse = s["normed"], s["inverse"]
+    d_expert = back[768:776] + back[776:784]
+    gy = gyt[...].astype(F32)
+    dy_normed = jnp.sum(gy * normed, axis=0, keepdims=True)
+    vecs = const[...].astype(F32)
+    dy_vec = [jnp.sum(gy * vecs[:, c : c + 1], axis=0, keepdims=True) for c in range(NCONST)]
+    d_gates = []
+    for j in range(TOP):
+        g = jnp.sum(jnp.where(ids[0:8] == s["ks"][j], d_expert, 0.0), axis=0, keepdims=True)
+        g = g + jnp.where(named[j] == NFFN + 1, dy_normed, 0.0)
+        for c in range(NCONST):
+            dy_const = mixing[c][0] * dy_normed + mixing[c][1] * dy_vec[c]
+            g = g + jnp.where(named[j] == NFFN + 2 + c, dy_const, 0.0)
+        d_gates.append(g)
+    inner = gates[0] * d_gates[0] + gates[1] * d_gates[1]
+    d_chosen = [gates[j] * (d_gates[j] - inner) for j in range(TOP)]
+    d_logits = sum(jnp.where(ids == named[j], d_chosen[j], 0.0) for j in range(TOP))
+    gprev_ref[...] = d_logits
+    coefs = []
+    direct = s["copy_w"]
+    for c in range(NCONST):
+        w, (m0, m1) = s["const_w"][c], mixing[c]
+        d0, d1 = w * dy_normed, w * dy_vec[c]
+        mid = m0 * d0 + m1 * d1
+        d_logits = d_logits + jnp.where(ids == NEXP + 2 * c, m0 * (d0 - mid), 0.0)
+        d_logits = d_logits + jnp.where(ids == NEXP + 2 * c + 1, m1 * (d1 - mid), 0.0)
+        direct = direct + w * m0
+        coefs.append(w * m1)
+    d_logits_b = d_logits.astype(BF)
+    d_normed = back[0:768] + direct * gy + mm(gate[...], d_logits_b)
+    u = gain[...] * d_normed
+    mean = jnp.mean(u * hidden, axis=0, keepdims=True)
+    d_hidden = gy + inverse * u - hidden * (inverse * inverse * inverse * mean)
+    dt_ref[...] = d_hidden.astype(BF)
+    lane = lax.broadcasted_iota(jnp.int32, (width, 128), 1)
+    g_gate = mm_nt(s["normed_b"], jnp.concatenate([d_logits_b] + [jnp.zeros_like(d_logits_b)] * 7, axis=0))
+    g_gain = jnp.sum(d_normed * hidden * inverse, axis=1, keepdims=True)
+    small = jnp.where(lane < 16, g_gate, 0.0)
+    for c in range(NCONST):
+        g_const = jnp.sum(gy * coefs[c], axis=1, keepdims=True)
+        small = jnp.where(lane == 16 + c, g_const, small)
+    small = jnp.where(lane == 18, g_gain, small)
+    small_ref[...] = small
+
+
+def layer_kernel(sc, hidden_ref, gain, gate_t, prev, routes, const, hot, *refs):
+    rs, out_ref = refs[:8], refs[8]
+    hidden = hidden_ref[...]
+    s = row_state(sc[0], hidden, gain[...], gate_t[...], prev[...], routes[...])
+    r = jnp.concatenate([v[...] for v in rs], axis=1)
+    total = hidden + mm(r, hot[...])
+    weight = s["copy_w"]
+    vecs = const[...].astype(F32)
+    for c in range(NCONST):
+        weight = weight + s["const_w"][c] * s["mixing"][c][0]
+        total = total + (s["const_w"][c] * s["mixing"][c][1]) * vecs[:, c : c + 1]
+    total = total + weight * s["normed"]
+    out_ref[...] = total.astype(BF).T
+
+
+def dmixed_kernel(sc, own, other, wo, o0, o1, o2, o3, st):
+    z, x = sc[1], sc[2]
+    for r, d_ref in enumerate((own, other)):
+        s = jnp.bitwise_xor(x, r)
+        dm = mm_tn(wo[...], d_ref[...]).astype(BF)
+        for half in range(2):
+            st[jnp.bitwise_xor(z, 2 * s + half)] = dm[half * 192 : (half + 1) * 192]
+    for d, o in enumerate((o0, o1, o2, o3)):
+        o[...] = st[d]
+
+
+def outgrad_kernel(sc, own, other, mixed, small, o_ref, dh_ref):
+    x = sc[2]
+    g = mm_nt(own[...], mixed[x]) + mm_nt(other[...], mixed[1 - x])
+    for f in range(4):
+        rows = slice(f * 192, (f + 1) * 192)
+        o_ref[f, :, 0:384] = g[rows].astype(BF)
+        o_ref[f, :, 384:512] = small[rows, :].astype(BF)
+    dh_ref[x] = own[...].T
+    dh_ref[1 - x] = other[...].T
+
+
+def attn_back_kernel(sc, b0, b1, b2, b3, m_ref, g0, g1, g2, g3, o0, o1, o2, o3,
+                     q_s, k_s, v_s, g_s, dq_s, dk_s, dv_s, st):
+    z, prefix = sc[1], sc[4]
+    unpack_qkv(z, (b0, b1, b2, b3), q_s, k_s, v_s)
+    h = HEAD_DIM
+    for d, g in enumerate((g0, g1, g2, g3)):
+        base = pl.multiple_of(jnp.bitwise_xor(z, d) * 512, 512)
+        for j in range(3):
+            g_s[j, :, pl.ds(base, 512)] = g[j * h : (j + 1) * h, :]
+    scale = h ** (-0.5)
+
+    def unit(j, carry):
+        kt = k_s[j].T
+        dk_s[...] = jnp.zeros_like(dk_s)
+        dv_s[...] = jnp.zeros_like(dv_s)
+        for i, tiles in attn_masks(prefix):
+            cols = slice(i * 512, (i + 1) * 512)
+            q = q_s[j, cols, :]
+            gt = g_s[j, :, cols]
+            mixed = m_ref[j, 0:h, cols]
+            lse = m_ref[j, h : h + 1, cols]
+            delta = jnp.sum(gt.astype(F32) * mixed, axis=0, keepdims=True)
+            dqt = jnp.zeros((h, 512), F32)
+            for t, masked in tiles:
+                at = slice(t * 512, (t + 1) * 512)
+                s = mm_nt(k_s[j, at, :], q)
+                p = jnp.exp2(s * (scale * LOG2E) - lse)
+                if masked:
+                    p = jnp.where(allowed_tile(t, i, prefix), p, 0.0)
+                dp = mm(v_s[j, at, :], gt)
+                ds = (p * (dp - delta)).astype(BF)
+                dv_s[at, :] += mm_nt(p.astype(BF), gt)
+                dk_s[at, :] += mm(ds, q)
+                dqt = dqt + mm(kt[:, at], ds)
+            dq_s[cols, :] = dqt.T
+        for i in range(4):
+            parts = []
+            for r in range(2):
+                rows = slice(i * 512 + r * 256, i * 512 + (r + 1) * 256)
+                parts += [dq_s[rows, :] * scale, dk_s[rows, :] * scale, dv_s[rows, :]]
+            st[i, j] = jnp.concatenate([v.astype(BF) for v in parts], axis=1)
+        return carry
+
+    lax.fori_loop(0, 3, unit, 0)
+    for d, o in enumerate((o0, o1, o2, o3)):
+        o[...] = st[jnp.bitwise_xor(z, d)]
+
+
+def dproj_kernel(sc, b0, b1, b2, b3, w, nt, cos_ref, sin_ref, tokens, dn_ref, gq_ref, st):
+    z = sc[1]
+    h = HEAD_DIM
+    for d, b in enumerate((b0, b1, b2, b3)):
+        st[d] = b[...]
+    cos = jnp.concatenate([cos_ref[...]] * 3, axis=1)
+    sin = jnp.concatenate([sin_ref[...]] * 3, axis=1)
+    grads = [None] * 3
+    gain_grad = jnp.zeros((1, 768), F32)
+    for s in range(2):
+        blocks = [[st[jnp.bitwise_xor(z, 2 * s + half), j] for j in range(3)] for half in range(2)]
+        dn = None
+        for c in range(3):
+            rows = []
+            for r in range(2):
+                at = r * 192 + c * h
+                rows.append(
+                    jnp.concatenate(
+                        [blocks[half][j][:, at : at + h] for half in range(2) for j in range(3)], axis=1
+                    )
+                )
+            g = jnp.concatenate(rows, axis=0)
+            if c < 2:
+                g = g.astype(F32)
+                g = (g * cos - swap_halves(g) * sin).astype(BF)
+            term = mm_nt(g, w[c])
+            dn = term if dn is None else dn + term
+            gr = mm(nt[:, s * 512 : (s + 1) * 512], g)
+            grads[c] = gr if grads[c] is None else grads[c] + gr
+        dn_ref[s] = dn.astype(BF)
+        v = tokens[s].astype(F32)
+        inverse = lax.rsqrt(jnp.mean(v * v, axis=-1, keepdims=True) + epsilon)
+        gain_grad = gain_grad + jnp.sum(dn * v * inverse, axis=0, keepdims=True)
+    for f in range(4):
+        for c in range(3):
+            gq_ref[f, c * 192 : (c + 1) * 192, :] = grads[c][f * 192 : (f + 1) * 192].astype(BF)
+        piece = jnp.broadcast_to(gain_grad[:, f * 192 : (f + 1) * 192], (16, 192))
+        gq_ref[f, 576:592, :] = jnp.concatenate([piece, piece], axis=1).astype(BF)
+
+
+def tokens_kernel(sc, tokens, gain, dh, own, recv, o_ref):
+    for s in range(2):
+        v = tokens[s].astype(F32)
+        inverse = lax.rsqrt(jnp.mean(v * v, axis=-1, keepdims=True) + epsilon)
+        u = (own[s].astype(F32) + recv[s].astype(F32)) * gain[...]
+        mean = jnp.mean(u * v, axis=-1, keepdims=True)
+        o_ref[s] = dh[s].astype(F32) + inverse * u - v * (inverse * inverse * inverse * mean)
+
+
+def fast(
+    tokens, prev_logits, routes, prefix, norm_gains, query_key_value_weight,
+    output_projection_weight, router_gate_weight, const_vec, gate_up, down_weight, cotangent,
+):
+    f, z, x = lax.axis_index("fsdp"), lax.axis_index("ctx"), lax.axis_index("tp")
+    me = 2 * f + x
+    rows, width = tokens.shape[1], tokens.shape[2]
+    head_cols = query_key_value_weight.shape[2]
+    scalars = jnp.stack([me, z, x, f, prefix[z // 2]]).astype(jnp.int32)
+
+    def flip_fsdp(v, k):
+        return lax.ppermute(v, "fsdp", [(i, i ^ k) for i in range(4)])
+
+    def flip_tp(v):
+        return lax.ppermute(v, "tp", [(0, 1), (1, 0)])
+
+    def flip_ctx(v, k):
+        return lax.ppermute(v, "ctx", [(i, i ^ k) for i in range(4)])
+
+    def flip_plane(v, k):
+        return lax.ppermute(v, ("fsdp", "tp"), [(i, i ^ k) for i in range(8)])
+
+    pack = jnp.concatenate(
+        [query_key_value_weight.reshape(3 * 192, head_cols), output_projection_weight], axis=0
+    )
+    pack2 = flip_fsdp(pack, 2)
+    pack1 = flip_fsdp(pack, 1)
+    pack3 = flip_fsdp(pack2, 1)
+    small = lax.all_gather(
+        jnp.concatenate([router_gate_weight, norm_gains.T, const_vec.T], axis=1), "fsdp", axis=0, tiled=True
+    )
+    gate = small[:, 0:16]
+    gate_t = gate.T
+    gain_one_row = small[:, 16:17].T.astype(F32)
+    gain_two = small[:, 17:18].astype(F32)
+    const = small[:, 18:20]
+
+    down4 = down_weight[:, None]
+    weight_blocks = []
+    for k in range(8):
+        e = jnp.bitwise_xor(me, k)
+        block = jnp.concatenate(
+            [lax.dynamic_index_in_dim(gate_up, e, 0, False), lax.dynamic_index_in_dim(down4, e, 0, False)], axis=0
+        )
+        weight_blocks.append(block)
+
+    own_routes = lax.dynamic_index_in_dim(routes, x, 0, False).T
+    own_prev = jnp.pad(lax.dynamic_index_in_dim(prev_logits, x, 0, False).T, ((0, 4), (0, 0)))
+    own_gy = lax.dynamic_index_in_dim(cotangent, x, 0, False)
+
+    positions = z * rows + jnp.arange(rows, dtype=jnp.int32)
+    half_dim = HEAD_DIM // 2
+    frequency = 10000.0 ** (-(jnp.arange(half_dim, dtype=F32) * 2.0 / HEAD_DIM))
+    angles = positions.astype(F32)[:, None] * frequency[None, :]
+    cosine, sine = jnp.cos(angles), jnp.sin(angles)
+    cos = jnp.concatenate([cosine] * 4, axis=1)
+    sin = jnp.concatenate([-sine, sine] * 2, axis=1)
+
+    packed = run(
+        pack_kernel, "pack_cotangent", scalars, [own_routes, own_gy],
+        [out((8 * CAPACITY, rows)), out((width, rows))] + [out((width, CAPACITY))] * 8,
+    )
+    hot, gyt, g_blocks = packed[0], packed[1], packed[2:]
+    normed_one, normed_one_t, xt = run(
+        norm_kernel, "norm_one", scalars, [tokens, gain_one_row],
+        [out((2, rows, width)), out((width, 2 * rows)), out((width, rows))],
+    )
+
+    qkv_out = run(
+        qkv_kernel, "qkv", scalars, [normed_one, pack, pack1, pack2, pack3, cos, sin],
+        [out((3, rows // 2, head_cols))] * 4 + [out((3, width, head_cols)), out((width, head_cols))],
+        scratch=[pltpu.VMEM((4, 3, rows // 2, head_cols), BF)], flops=2 * 1024 * 768 * 1152,
+    )
+    blocks, w_full, wo_full = qkv_out[:4], qkv_out[4], qkv_out[5]
+    blocks = [blocks[0]] + [flip_ctx(blocks[d], d) for d in (1, 2, 3)]
+
+    weights_in = [weight_blocks[0]] + [flip_plane(weight_blocks[k], k) for k in range(1, 8)]
+    g_in = [g_blocks[0]] + [flip_plane(g_blocks[k], k) for k in range(1, 8)]
+
+    length = 4 * rows
+    unit_scratch = [pltpu.VMEM((3, length, HEAD_DIM), BF)] * 3
+    attn = run(
+        attn_kernel, "attention", scalars, list(blocks),
+        [out((192, rows))] * 4 + [out((3, HEAD_DIM + 8, length), F32)],
+        scratch=unit_scratch + [pltpu.VMEM((4, 192, rows), BF)], flops=3 * 11 * 512 * 512 * 64 * 4,
+    )
+    mixed_blocks, mixed_lse = attn[:4], attn[4]
+    mixed_in = [mixed_blocks[0]] + [flip_ctx(mixed_blocks[d], d) for d in (1, 2, 3)]
+
+    w_exp, wt_exp = run(
+        wprep_kernel, "expert_weights", scalars, weights_in,
+        [out((3, width, 2048)), out((3, 2048, width))],
+    )
+    gs = jnp.stack(g_in)
+    g_more = [flip_ctx(gs, d) for d in (1, 2, 3)]
+
+    mixed, attn_own, attn_send = run(
+        outproj_kernel, "out_projection", scalars, [*mixed_in, wo_full],
+        [out((2, head_cols, rows)), out((width, rows)), out((width, rows))],
+        scratch=[pltpu.VMEM((4, 192, rows), BF)], flops=2 * 1024 * 768 * 384,
+    )
+    attn_recv = flip_tp(attn_send)
+
+    routed = run(
+        router_kernel, "router", scalars,
+        [xt, attn_own, attn_recv, gain_two, gate_t, own_prev, own_routes, hot],
+        [out((width, rows), F32)] + [out((width + 16, CAPACITY))] * 8, flops=2 * 512 * 1024 * 784,
+    )
+    hidden, x_blocks = routed[0], routed[1:]
+    xs = jnp.stack([x_blocks[0]] + [flip_plane(x_blocks[k], k) for k in range(1, 8)])
+    x_more = [flip_ctx(xs, d) for d in (1, 2, 3)]
+
+    def plane(d):
+        return jnp.stack([jnp.bitwise_xor(z, d), me]).astype(jnp.int32)
+
+    done = expert_call(True, plane(0), xs, gs, w_exp, wt_exp, None)
+    y_blocks, r_blocks, held = done[:8], done[8:16], done[16:]
+    y_in = [y_blocks[0]] + [flip_plane(y_blocks[k], k) for k in range(1, 8)]
+    r_in = [r_blocks[0]] + [flip_plane(r_blocks[k], k) for k in range(1, 8)]
+
+    d_t, grad_prev_t, small_grads = run(
+        combine_kernel, "combine", scalars,
+        [hidden, gain_two, gate_t, gate, own_prev, own_routes, const, gyt, hot, *y_in],
+        [out((width, rows)), out((16, rows), F32), out((width, 128), F32)], flops=2 * 512 * 1024 * 784,
+    )
+    d_other = flip_tp(d_t)
+    dm_blocks = run(
+        dmixed_kernel, "d_mixed", scalars, [d_t, d_other, wo_full], [out((192, rows))] * 4,
+        scratch=[pltpu.VMEM((4, 192, rows), BF)], flops=2 * 1024 * 768 * 384,
+    )
+    dm_in = [dm_blocks[0]] + [flip_ctx(dm_blocks[d], d) for d in (1, 2, 3)]
+
+    for d in (1, 2, 3):
+        held = expert_call(False, plane(d), x_more[d - 1], g_more[d - 1], w_exp, wt_exp, held)
+
+    back = run(
+        attn_back_kernel, "attention_backward", scalars, [*blocks, mixed_lse, *dm_in],
+        [out((3, rows // 2, head_cols))] * 4,
+        scratch=unit_scratch
+        + [pltpu.VMEM((3, HEAD_DIM, length), BF)]
+        + [pltpu.VMEM((length, HEAD_DIM), F32)] * 3
+        + [pltpu.VMEM((4, 3, rows // 2, head_cols), BF)],
+        flops=3 * 11 * 512 * 512 * 64 * 10,
+    )
+    back_in = [back[0]] + [flip_ctx(back[d], d) for d in (1, 2, 3)]
+
+    og, d_hidden = run(
+        outgrad_kernel, "out_grads", scalars, [d_t, d_other, mixed, small_grads],
+        [out((4, 192, 512)), out((2, rows, width))], flops=2 * 1024 * 768 * 384,
+    )
+
+    layer_own = run(
+        layer_kernel, "layer_out", scalars,
+        [hidden, gain_two, gate_t, own_prev, own_routes, const, hot, *r_in],
+        [out((rows, width))], flops=2 * 512 * 1024 * 768,
+    )[0]
+
+    def both(own):
+        other = flip_tp(own)
+        return jnp.where(x == 0, jnp.stack([own, other]), jnp.stack([other, own]))
+
+    layer_out = both(layer_own)
+    grad_prev = both(grad_prev_t[0:NEXP].T)
+
+    parts = 4
+    me_scalar = jnp.stack([me]).astype(jnp.int32)
+    placed = None
+    for part in range(parts):
+        g = grads_call(me_scalar, part, parts, held)
+        g = [g[0]] + [flip_plane(g[k], k) for k in range(1, 8)]
+        placed = place_call(me_scalar, part, parts, g, placed)
+    grad_gu, grad_down = placed
+
+    def rounded(v):
+        return lax.reduce_precision(v, 8, 7).astype(BF)
+
+    def to_owner(v):
+        core, y = f % 2, f // 2
+        pairs = v.reshape((2, 2) + v.shape[1:])
+        send = lax.dynamic_index_in_dim(pairs, 1 - core, 1, False)
+        mine = lax.dynamic_index_in_dim(pairs, core, 1, False).astype(F32)
+        mine = rounded(mine + flip_fsdp(send, 1).astype(F32))
+        send = lax.dynamic_index_in_dim(mine, 1 - y, 0, False)
+        keep = lax.dynamic_index_in_dim(mine, y, 0, False).astype(F32)
+        keep = rounded(keep + flip_fsdp(send, 2).astype(F32))
+        keep = rounded(keep.astype(F32) + flip_ctx(keep, 1).astype(F32))
+        return keep.astype(F32) + flip_ctx(keep, 2).astype(F32)
+
+    owned = to_owner(og)
+    grad_out = owned[:, 0:384]
+    tail = owned[:, 384:512]
+    tail = tail + flip_tp(tail)
+    grad_gate = tail[:, 0:16]
+    grad_const = tail[:, 16:18].T
+    gain_two_grad = tail[:, 18]
+
+    dn, gq = run(
+        dproj_kernel, "d_projection", scalars, [*back_in, w_full, normed_one_t, cos, sin, tokens],
+        [out((2, rows, width)), out((4, 592, head_cols))],
+        scratch=[pltpu.VMEM((4, 3, rows // 2, head_cols), BF)], flops=4 * 1024 * 768 * 1152,
+    )
+    dn_other = flip_tp(dn)
+    grad_tokens = run(
+        tokens_kernel, "grad_tokens", scalars, [tokens, gain_one_row, d_hidden, dn, dn_other],
+        [out((2, rows, width), F32)],
+    )[0]
+    owned = to_owner(gq)
+    grad_qkv = owned[0:576].reshape(3, 192, head_cols)
+    line = owned[576:577, 0:192]
+    line = line + flip_tp(line)
+    grad_gains = jnp.stack([line[0], gain_two_grad])
+    return (
+        layer_out, grad_tokens, grad_prev, grad_gains, grad_qkv, grad_out, grad_gate, grad_const,
+        grad_gu, grad_down,
+    )
+
+
 def solution(mesh):
     in_specs = (
         P("fsdp", "ctx", None),
@@ -440,6 +1291,7 @@
         P(None, None, "fsdp", "tp"),
         P(None, "fsdp", "tp"),
     )
+    small = dict(mesh.shape) == {"fsdp": 4, "ctx": 4, "tp": 2}
     return jax.shard_map(
-        on_device, mesh=mesh, in_specs=in_specs, out_specs=out_specs, check_vma=False
-    )
+        fast if small else on_device, mesh=mesh, in_specs=in_specs, out_specs=out_specs, check_vma=False
+    )

time: 1840 us -> 981 us (0.53)
  waiting for transfers between devices: 1160 us -> 414 us
  Pallas kernels: 0 us -> 298 us
  matrix products: 288 us -> 0 us
  starting transfers between devices: 1.41 us -> 181 us
  local copies, waits for them, and re-layouts: 176 us -> 52.4 us
  other arithmetic: 139 us -> 24.9 us
  blocking collectives: 49 us -> 5.52 us
    ppermute x0 -> x99, waiting for transfers between devices: none -> 414 us  [the longest x22 252 us: flip_ctx(): return lax.ppermute(v, 'ctx', [(i, i ^ k) for i in range(4)])]
    reduce_scatter x5 -> x0, waiting for transfers between devices: 402 us -> none  [the longest x1 183 us: on_device(): lax.psum_scatter(grad_gu_local.astype(jnp.bfloat16), 'fsdp', scatter_dime...]
    psum x4 -> x0, waiting for transfers between devices: 374 us -> none  [the longest x1 333 us: on_device(): lax.psum(attention_owned[1].astype(jnp.bfloat16), 'ctx').astype(jnp.float32)]
    pallas_call x0 -> x26, Pallas kernels: none -> 298 us  [the longest x14 123 us: run(): pl.pallas_call(body, out_shape=tuple(outs), in_specs=[SCALARS] + [WHOLE]...]
    all_gather x5 -> x0, waiting for transfers between devices: 295 us -> none  [the longest x1 110 us: on_device(): lax.all_gather(gate_up, 'fsdp', axis=2, tiled=True)]
    dot_general x29 -> x0, matrix products: 288 us -> none  [the longest x2 33 us: back_step(): jnp.einsum('sqhd,skhd->shqk', d_mixed, value_part, preferred_element_type...]
    ppermute x0 -> x99, starting transfers between devices: none -> 181 us  [the longest x22 110 us: flip_ctx(): return lax.ppermute(v, 'ctx', [(i, i ^ k) for i in range(4)])]
    unnamed x22 -> x0, waiting for transfers between devices: 90.6 us -> none
  transfers between devices with their start and end apart: 18 -> 99, of which waited for: 18 -> 28; matrix products, arithmetic and copies ran while one was open for 14% -> 6% of each run, Pallas kernels for 0% -> 26%
where the time goes in v1:
time: 981 us; the launch traced here: 978 us
  waiting for transfers between devices  414 us (42%)
  Pallas kernels  298 us (30%)
  starting transfers between devices  181 us (18%)
  local copies, waits for them, and re-layouts  52.4 us (5%)
  other arithmetic  24.9 us (3%)
    ppermute x22, waiting for transfers between devices, flip_ctx(): return lax.ppermute(v, 'ctx', [(i, i ^ k) for i in range(4)])  252 us
    ppermute x63, waiting for transfers between devices, flip_plane(): return lax.ppermute(v, ('fsdp', 'tp'), [(i, i ^ k) for i in range(8)])  133 us
    pallas_call x14, Pallas kernels, run(): pl.pallas_call(body, out_shape=tuple(outs), in_specs=[SCALARS] + [WHOLE]...  123 us
    ppermute x22, starting transfers between devices, flip_ctx(): return lax.ppermute(v, 'ctx', [(i, i ^ k) for i in range(4)])  110 us
    pallas_call x4, Pallas kernels, expert_call(): pl.pallas_call(functools.partial(expert_body, first), out_shape=tuple(out...  94.7 us
    pallas_call x4, Pallas kernels, grads_call(): pl.pallas_call(functools.partial(grads_body, cols), out_shape=tuple([out(...  62.7 us
    ppermute x63, starting transfers between devices, flip_plane(): return lax.ppermute(v, ('fsdp', 'tp'), [(i, i ^ k) for i in range(8)])  57.1 us
    unnamed x200, local copies, waits for them, and re-layouts  31.1 us
  transfers between devices with their start and end apart: 99, of which 28 were waited for; matrix products, arithmetic and copies ran while one was open for 6% of the time, Pallas kernels for 26%

profile of v1, /device:TPU:0, one launch (start us, length us, event | category | flops | bytes accessed | tf_op | source)
XLA Modules:
  0.0 978.2 jit_solution(5844338382436571115)
XLA Ops:
  9.8 3.9 pack_cotangent.1
  15.9 5.5 all-gather
  27.5 4.1 norm_one.1
  44.1 7.6 qkv.1
  66.4 6.1 collective-permute-done.3.b1
  74.9 27.3 %collective-permute-done.4.b2 = bf16[3,256,384]{2,1,0:T(8,128)(2,1)} collective-permute-done((bf16[3,256,384]{2,1,0:T(8,128)(2,1)}, bf16[3,256,384]{2,1,0:T(8,128)(2,1)}, u32[]{:S(2)}, u32[]{:S(2)}) %collective-permute-start.4) | collective-permute-done | bytes 589856 | tf_op jit(solution)/shard_map/ppermute | solution.py:1067
  104.8 19.3 %attention.1 = (bf16[192,512]{1,0:T(8,128)(2,1)}, bf16[192,512]{1,0:T(8,128)(2,1)}, bf16[192,512]{1,0:T(8,128)(2,1)}, bf16[192,512]{1,0:T(8,128)(2,1)}, f32[3,72,2048]{2,1,0:T(8,128)}) custom-call(s32[5]{0:T(128)} %stack.131.sc, bf16[3,256,384]{2,1,0:T(8,128)(2,1)} %get-tuple-element.141.b0, bf16[3,256,384]{2,1,0:T(8,128)(2,1)} %collective-permute-done.3.b1, ...), custom_call_target="tpu_custom_call" | custom-call | flops 2214592512 | bytes 4915200 | tf_op jit(solution)/shard_map/attention/pallas_call | solution.py:448
  124.1 12.1 %collective-permute-start.6 = (bf16[192,512]{1,0:T(8,128)(2,1)}, bf16[192,512]{1,0:T(8,128)(2,1)S(1)}, u32[]{:S(2)}, u32[]{:S(2)}) collective-permute-start(bf16[192,512]{1,0:T(8,128)(2,1)} %get-tuple-element.146), channel_id=1, source_target_pairs={{0,2},{2,0},{4,6},{6,4},{1,3},{3,1},{5,7},{7,5},{8,10},{10,8},{12,... | collective-permute-start | bytes 589832 | tf_op jit(solution)/shard_map/ppermute | solution.py:1067
  140.5 5.3 collective-permute-done.6.b1
  146.5 7.1 collective-permute-done.7.b2
  168.8 55.5 %collective-permute-done.27.refs_4_ = bf16[3,192,1024]{2,1,0:T(8,128)(2,1)S(1)} collective-permute-done((bf16[3,192,1024]{2,1,0:T(8,128)(2,1)}, bf16[3,192,1024]{2,1,0:T(8,128)(2,1)S(1)}, u32[]{:S(2)}, u32[]{:S(2)}) %collective-permute-start.27) | collective-permute-done | bytes 1179680 | tf_op jit(solution)/shard_map/ppermute | solution.py:1070
  225.7 13.7 %expert_weights.1 = (bf16[3,768,2048]{2,1,0:T(8,128)(2,1)}, bf16[3,2048,768]{2,1,0:T(8,128)(2,1)}) custom-call(s32[5]{0:T(128)} %stack.131.sc, bf16[3,192,1024]{2,1,0:T(8,128)(2,1)} %pad_maximum_fusion.refs_0_, bf16[3,192,1024]{2,1,0:T(8,128)(2,1)} %copy-done.31, bf16[3,192,1024]{2,1,0:T(8,128)(2,1)} %copy-done.32, bf16[3,192,1024]{2,1,0:T(8,128)(2,1)} %copy-done.33, ...), custom_call_target="tpu_custom_call" | custom-call | bytes 28311552 | tf_op jit(solution)/shard_map/expert_weights/pallas_call | solution.py:448
  240.3 5.5 router.1
  257.8 5.2 collective-permute-done.14
  263.7 5.2 collective-permute-done.15
  270.3 34.1 %experts_own.1 = (bf16[784,128]{1,0:T(8,128)(2,1)}, bf16[784,128]{1,0:T(8,128)(2,1)}, bf16[784,128]{1,0:T(8,128)(2,1)}, bf16[784,128]{1,0:T(8,128)(2,1)}, bf16[7...) custom-call(s32[2]{0:T(128)} %pad_add_fusion.sc, ...), custom_call_target="tpu_custom_call" | custom-call | flops 19327352832 | bytes 41943040 | tf_op jit(solution)/shard_map/experts_own/pallas_call | solution.py:766
  308.5 4.1 collective-permute-done.39.refs_1_
  314.9 6.5 collective-permute-done.43.refs_5_
  321.4 6.4 collective-permute-done.44.refs_6_
  328.6 6.5 combine.1
  339.6 16.2 %collective-permute-done.46.other = bf16[768,512]{1,0:T(8,128)(2,1)S(1)} collective-permute-done((bf16[768,512]{1,0:T(8,128)(2,1)}, bf16[768,512]{1,0:T(8,128)(2,1)S(1)}, u32[]{:S(2)}, u32[]{:S(2)}) %collective-permute-start.46) | collective-permute-done | bytes 786464 | tf_op jit(solution)/shard_map/ppermute | solution.py:1064
  357.5 4.1 out_grads.1
  369.9 6.3 collective-permute-done.36.refs_6_
  376.8 4.9 layer_out.1
  390.4 56.0 %collective-permute-done.47.g1 = bf16[192,512]{1,0:T(8,128)(2,1)S(1)} collective-permute-done((bf16[192,512]{1,0:T(8,128)(2,1)}, bf16[192,512]{1,0:T(8,128)(2,1)S(1)}, u32[]{:S(2)}, u32[]{:S(2)}) %collective-permute-start.47) | collective-permute-done | bytes 196640 | tf_op jit(solution)/shard_map/ppermute | solution.py:1067
  452.6 30.7 %attention_backward.1 = (bf16[3,256,384]{2,1,0:T(8,128)(2,1)}, bf16[3,256,384]{2,1,0:T(8,128)(2,1)}, bf16[3,256,384]{2,1,0:T(8,128)(2,1)}, bf16[3,256,384]{2,1,0:T(8,128)(2,1)}) custom-call(s32[5]{0:T(128)} %stack.131.sc, bf16[3,256,384]{2,1,0:T(8,128)(2,1)} %get-tuple-element.141.b0, bf16[3,256,384]{2,1,0:T(8,128)(2,1)} %collective-permute-done.3.b1, ...), custom_call_target="tpu_custom_call" | custom-call | flops 5536481280 | bytes 7274496 | tf_op jit(solution)/shard_map/attention_backward/pallas_call | solution.py:448
  489.5 20.1 %experts_more.3 = (bf16[4,768,1024]{2,1,0:T(8,128)(2,1)}, bf16[4,768,1024]{2,1,0:T(8,128)(2,1)}, bf16[4,2048,1024]{2,1,0:T(8,128)(2,1)}, bf16[4,2048,1024]{2,1,0:T(8,128)(2,1)}, bf16[4,2048,1024]{2,1,0:T(8,128)(2,1)}) custom-call(s32[2]{0:T(128)} %pad_add_fusion.3.sc, ...), custom_call_target="tpu_custom_call", output_to_operand_aliasing={{0}: (5, {}), {1}: (6, {}), {2}: (7, {}), {3}: (8, {}), {4}... | custom-call | flops 9663676416 | bytes 41943040 | tf_op jit(solution)/shard_map/experts_more/pallas_call | solution.py:766
  509.6 109.9 %collective-permute-done.68.gs = bf16[8,768,128]{2,1,0:T(8,128)(2,1)} collective-permute-done((bf16[8,768,128]{2,1,0:T(8,128)(2,1)}, bf16[8,768,128]{2,1,0:T(8,128)(2,1)}, u32[]{:S(2)}, u32[]{:S(2)}) %collective-permute-start.68) | collective-permute-done | bytes 1572896 | tf_op jit(solution)/shard_map/ppermute | solution.py:1067
  620.6 33.2 %collective-permute-done.67.xs = bf16[8,784,128]{2,1,0:T(8,128)(2,1)S(1)} collective-permute-done((bf16[8,784,128]{2,1,0:T(8,128)(2,1)}, bf16[8,784,128]{2,1,0:T(8,128)(2,1)S(1)}, u32[]{:S(2)}, u32[]{:S(2)}) %collective-permute-start.67) | collective-permute-done | bytes 1605664 | tf_op jit(solution)/shard_map/ppermute | solution.py:1067
  655.0 20.4 %experts_more.4 = (bf16[4,768,1024]{2,1,0:T(8,128)(2,1)}, bf16[4,768,1024]{2,1,0:T(8,128)(2,1)}, bf16[4,2048,1024]{2,1,0:T(8,128)(2,1)}, bf16[4,2048,1024]{2,1,0:T(8,128)(2,1)}, bf16[4,2048,1024]{2,1,0:T(8,128)(2,1)}) custom-call(s32[2]{0:T(128)} %pad_add_fusion.2.sc, ...), custom_call_target="tpu_custom_call", output_to_operand_aliasing={{0}: (5, {}), {1}: (6, {}), {2}: (7, {}), {3}: (8, {}), {4}... | custom-call | flops 9663676416 | bytes 41943040 | tf_op jit(solution)/shard_map/experts_more/pallas_call | solution.py:766
  675.4 13.5 %collective-permute-start.51 = (bf16[3,256,384]{2,1,0:T(8,128)(2,1)}, bf16[3,256,384]{2,1,0:T(8,128)(2,1)S(1)}, u32[]{:S(2)}, u32[]{:S(2)}) collective-permute-start(bf16[3,256,384]{2,1,0:T(8,128)(2,1)} %get-tuple-element.200), channel_id=1, source_target_pairs={{0,4},{2,6},{4,0},{6,2},{1,5},{3,7},{5,1},{7,3},{8,12},{10,14},{12... | collective-permute-start | bytes 1769480 | tf_op jit(solution)/shard_map/ppermute | solution.py:1067
  690.5 20.0 %experts_more.5 = (bf16[4,768,1024]{2,1,0:T(8,128)(2,1)}, bf16[4,768,1024]{2,1,0:T(8,128)(2,1)}, bf16[4,2048,1024]{2,1,0:T(8,128)(2,1)}, bf16[4,2048,1024]{2,1,0:T(8,128)(2,1)}, bf16[4,2048,1024]{2,1,0:T(8,128)(2,1)}) custom-call(s32[2]{0:T(128)} %pad_add_fusion.1.sc, ...), custom_call_target="tpu_custom_call", output_to_operand_aliasing={{0}: (5, {}), {1}: (6, {}), {2}: (7, {}), {3}: (8, {}), {4}... | custom-call | flops 9663676416 | bytes 41943040 | tf_op jit(solution)/shard_map/experts_more/pallas_call | solution.py:766
  710.6 15.6 %expert_grads.7 = (bf16[3,192,256]{2,1,0:T(8,128)(2,1)}, bf16[3,192,256]{2,1,0:T(8,128)(2,1)}, bf16[3,192,256]{2,1,0:T(8,128)(2,1)}, bf16[3,192,256]{2,1,0:T(8,1...) custom-call(s32[1]{0:T(128)} %bitcast.sc, ...), custom_call_target="tpu_custom_call" | custom-call | flops 9663676416 | bytes 31457280 | tf_op jit(solution)/shard_map/expert_grads/pallas_call | solution.py:811
  726.1 58.7 %collective-permute-start.62 = (bf16[192,512]{0,1:T(8,128)(2,1)S(1)}, bf16[192,512]{0,1:T(8,128)(2,1)S(1)}, u32[]{:S(2)}, u32[]{:S(2)}) collective-permute-start(bf16[192,512]{0,1:T(8,128)(2,1)S(1)} %fusion.7), channel_id=1, source_target_pairs={{0,2},{2,0},{4,6},{6,4},{1,3},{3,1},{5,7},{7,5},{8,10},{10,8},{12,... | collective-permute-start | bytes 589832 | tf_op jit(solution)/shard_map/ppermute | solution.py:1067
  787.9 15.8 %expert_grads.6 = (bf16[3,192,256]{2,1,0:T(8,128)(2,1)}, bf16[3,192,256]{2,1,0:T(8,128)(2,1)}, bf16[3,192,256]{2,1,0:T(8,128)(2,1)}, bf16[3,192,256]{2,1,0:T(8,1...) custom-call(s32[1]{0:T(128)} %bitcast.sc, ...), custom_call_target="tpu_custom_call" | custom-call | flops 9663676416 | bytes 31457280 | tf_op jit(solution)/shard_map/expert_grads/pallas_call | solution.py:811
  810.3 10.3 %d_projection.1 = (bf16[2,512,768]{2,1,0:T(8,128)(2,1)}, bf16[4,592,384]{2,1,0:T(8,128)(2,1)}) custom-call(s32[5]{0:T(128)} %stack.131.sc, bf16[3,256,384]{2,1,0:T(8,128)(2,1)} %get-tuple-element.198.b0, bf16[3,256,384]{2,1,0:T(8,128)(2,1)} %copy-done.65, bf16[3,256,384]{2,1,0:T(8,128)(2,1)} %copy-done.66, bf16[3,256,384]{2,1,0:T(8,128)(2,1)} %copy-done.67, ...), custom_call_target="tpu_custom_call" | custom-call | flops 3623878656 | bytes 11190272 | tf_op jit(solution)/shard_map/d_projection/pallas_call | solution.py:448
  822.0 4.3 collective-permute-done.95.refs_4_
  826.8 3.9 collective-permute-done.97.refs_6_
  834.7 15.9 %expert_grads.5 = (bf16[3,192,256]{2,1,0:T(8,128)(2,1)}, bf16[3,192,256]{2,1,0:T(8,128)(2,1)}, bf16[3,192,256]{2,1,0:T(8,128)(2,1)}, bf16[3,192,256]{2,1,0:T(8,1...) custom-call(s32[1]{0:T(128)} %bitcast.sc, ...), custom_call_target="tpu_custom_call" | custom-call | flops 9663676416 | bytes 31457280 | tf_op jit(solution)/shard_map/expert_grads/pallas_call | solution.py:811
  856.3 9.7 collective-permute-done.90.refs_6_
  875.1 15.5 %expert_grads.4 = (bf16[3,192,256]{2,1,0:T(8,128)(2,1)}, bf16[3,192,256]{2,1,0:T(8,128)(2,1)}, bf16[3,192,256]{2,1,0:T(8,128)(2,1)}, bf16[3,192,256]{2,1,0:T(8,1...) custom-call(s32[1]{0:T(128)} %bitcast.sc, ...), custom_call_target="tpu_custom_call" | custom-call | flops 9663676416 | bytes 31457280 | tf_op jit(solution)/shard_map/expert_grads/pallas_call | solution.py:811
  908.0 16.3 %collective-permute-done.74.refs_4_ = bf16[3,192,256]{2,1,0:T(8,128)(2,1)S(1)} collective-permute-done((bf16[3,192,256]{2,1,0:T(8,128)(2,1)}, bf16[3,192,256]{2,1,0:T(8,128)(2,1)S(1)}, u32[]{:S(2)}, u32[]{:S(2)}) %collective-permute-start.74) | collective-permute-done | bytes 294944 | tf_op jit(solution)/shard_map/ppermute | solution.py:1070
  931.4 3.7 place_grads.5
  935.2 4.8 place_grads.6
  940.0 4.8 place_grads.7
  950.0 12.3 %collective-permute-done.64 = f32[192,128]{0,1:T(8,128)S(1)} collective-permute-done((f32[192,128]{0,1:T(8,128)S(1)}, f32[192,128]{0,1:T(8,128)S(1)}, u32[]{:S(2)}, u32[]{:S(2)}) %collective-permute-start.64) | collective-permute-done | bytes 98336 | tf_op jit(solution)/shard_map/ppermute | solution.py:1064
  962.9 5.4 collective-permute-done.58
  970.3 6.1 grad_tokens.1
  (438 shorter events, 197.0 us)
Async XLA Ops:
  2.8 36.6 %collective-permute-start.1 = (bf16[768,384]{1,0:T(8,128)(2,1)}, bf16[768,384]{1,0:T(8,128)(2,1)}, u32[]{:S(2)}, u32[]{:S(2)}) collective-permute-start(bf16[768,384]{1,0:T(8,128)(2,1)} %pad_maximum_fusion.8.p0), channel_id=1, source_target_pairs={{0,16},{8,24},{16,0},{24,8},{1,17},{9,25},{17,1},{25,9},{2,18},{10... | collective-permute-start | bytes 1769480 | tf_op jit(solution)/shard_map/ppermute | solution.py:1061
  5.7 36.9 %collective-permute-start = (bf16[768,384]{1,0:T(8,128)(2,1)}, bf16[768,384]{1,0:T(8,128)(2,1)}, u32[]{:S(2)}, u32[]{:S(2)}) collective-permute-start(bf16[768,384]{1,0:T(8,128)(2,1)} %pad_maximum_fusion.8.p0), channel_id=1, source_target_pairs={{0,8},{8,0},{16,24},{24,16},{1,9},{9,1},{17,25},{25,17},{2,10},{10... | collective-permute-start | bytes 1769480 | tf_op jit(solution)/shard_map/ppermute | solution.py:1061
  13.7 40.7 %collective-permute-start.17 = (bf16[768,128]{1,0:T(8,128)(2,1)}, bf16[768,128]{1,0:T(8,128)(2,1)}, u32[]{:S(2)}, u32[]{:S(2)}) collective-permute-start(bf16[768,128]{1,0:T(8,128)(2,1)} %get-tuple-element.163), channel_id=1, source_target_pairs={{0,1},{1,0},{8,9},{9,8},{16,17},{17,16},{24,25},{25,24},{2,3},{3,2... | collective-permute-start | bytes 589832 | tf_op jit(solution)/shard_map/ppermute | solution.py:1070
  15.2 41.5 %collective-permute-start.18 = (bf16[768,128]{1,0:T(8,128)(2,1)}, bf16[768,128]{1,0:T(8,128)(2,1)}, u32[]{:S(2)}, u32[]{:S(2)}) collective-permute-start(bf16[768,128]{1,0:T(8,128)(2,1)} %get-tuple-element.164), channel_id=1, source_target_pairs={{0,8},{1,9},{8,0},{9,1},{16,24},{17,25},{24,16},{25,17},{2,10},{3,... | collective-permute-start | bytes 589832 | tf_op jit(solution)/shard_map/ppermute | solution.py:1070
  15.5 42.4 %collective-permute-start.19 = (bf16[768,128]{1,0:T(8,128)(2,1)}, bf16[768,128]{1,0:T(8,128)(2,1)S(1)}, u32[]{:S(2)}, u32[]{:S(2)}) collective-permute-start(bf16[768,128]{1,0:T(8,128)(2,1)} %get-tuple-element.165), channel_id=1, source_target_pairs={{0,9},{1,8},{8,1},{9,0},{16,25},{17,24},{24,17},{25,16},{2,11},{3,... | collective-permute-start | bytes 589832 | tf_op jit(solution)/shard_map/ppermute | solution.py:1070
  56.7 80.6 %collective-permute-start.29 = (bf16[3,192,1024]{2,1,0:T(8,128)(2,1)}, bf16[3,192,1024]{2,1,0:T(8,128)(2,1)S(1)}, u32[]{:S(2)}, u32[]{:S(2)}) collective-permute-start(bf16[3,192,1024]{2,1,0:T(8,128)(2,1)} %pad_maximum_fusion.6), channel_id=1, source_target_pairs={{0,24},{1,25},{8,16},{9,17},{16,8},{17,9},{24,0},{25,1},{2,26},{3,... | collective-permute-start | bytes 3538952 | tf_op jit(solution)/shard_map/ppermute | solution.py:1070
  57.8 82.6 %collective-permute-start.24 = (bf16[3,192,1024]{2,1,0:T(8,128)(2,1)}, bf16[3,192,1024]{2,1,0:T(8,128)(2,1)S(1)}, u32[]{:S(2)}, u32[]{:S(2)}) collective-permute-start(bf16[3,192,1024]{2,1,0:T(8,128)(2,1)} %pad_maximum_fusion.1), channel_id=1, source_target_pairs={{0,1},{1,0},{8,9},{9,8},{16,17},{17,16},{24,25},{25,24},{2,3},{3,2... | collective-permute-start | bytes 3538952 | tf_op jit(solution)/shard_map/ppermute | solution.py:1070
  59.5 42.7 %collective-permute-start.4 = (bf16[3,256,384]{2,1,0:T(8,128)(2,1)}, bf16[3,256,384]{2,1,0:T(8,128)(2,1)}, u32[]{:S(2)}, u32[]{:S(2)}) collective-permute-start(bf16[3,256,384]{2,1,0:T(8,128)(2,1)} %get-tuple-element.143), channel_id=1, source_target_pairs={{0,4},{2,6},{4,0},{6,2},{1,5},{3,7},{5,1},{7,3},{8,12},{10,14},{12... | collective-permute-start | bytes 1769480 | tf_op jit(solution)/shard_map/ppermute | solution.py:1067
  62.1 40.7 %collective-permute-start.5 = (bf16[3,256,384]{2,1,0:T(8,128)(2,1)}, bf16[3,256,384]{2,1,0:T(8,128)(2,1)}, u32[]{:S(2)}, u32[]{:S(2)}) collective-permute-start(bf16[3,256,384]{2,1,0:T(8,128)(2,1)} %get-tuple-element.144), channel_id=1, source_target_pairs={{0,6},{2,4},{4,2},{6,0},{1,7},{3,5},{5,3},{7,1},{8,14},{10,12},{12... | collective-permute-start | bytes 1769480 | tf_op jit(solution)/shard_map/ppermute | solution.py:1067
  72.6 85.5 %collective-permute-start.25 = (bf16[3,192,1024]{2,1,0:T(8,128)(2,1)}, bf16[3,192,1024]{2,1,0:T(8,128)(2,1)S(1)}, u32[]{:S(2)}, u32[]{:S(2)}) collective-permute-start(bf16[3,192,1024]{2,1,0:T(8,128)(2,1)} %pad_maximum_fusion.2), channel_id=1, source_target_pairs={{0,8},{1,9},{8,0},{9,1},{16,24},{17,25},{24,16},{25,17},{2,10},{3,... | collective-permute-start | bytes 3538952 | tf_op jit(solution)/shard_map/ppermute | solution.py:1070
  102.8 33.5 %collective-permute-start.23 = (bf16[768,128]{1,0:T(8,128)(2,1)}, bf16[768,128]{1,0:T(8,128)(2,1)S(1)}, u32[]{:S(2)}, u32[]{:S(2)}) collective-permute-start(bf16[768,128]{1,0:T(8,128)(2,1)} %get-tuple-element.169), channel_id=1, source_target_pairs={{0,25},{1,24},{8,17},{9,16},{16,9},{17,8},{24,1},{25,0},{2,27},{3,... | collective-permute-start | bytes 589832 | tf_op jit(solution)/shard_map/ppermute | solution.py:1070
  140.4 28.4 %collective-permute-start.26 = (bf16[3,192,1024]{2,1,0:T(8,128)(2,1)}, bf16[3,192,1024]{2,1,0:T(8,128)(2,1)S(1)}, u32[]{:S(2)}, u32[]{:S(2)}) collective-permute-start(bf16[3,192,1024]{2,1,0:T(8,128)(2,1)} %pad_maximum_fusion.3), channel_id=1, source_target_pairs={{0,9},{1,8},{8,1},{9,0},{16,25},{17,24},{24,17},{25,16},{2,11},{3,... | collective-permute-start | bytes 3538952 | tf_op jit(solution)/shard_map/ppermute | solution.py:1070
  145.8 78.5 %collective-permute-start.27 = (bf16[3,192,1024]{2,1,0:T(8,128)(2,1)}, bf16[3,192,1024]{2,1,0:T(8,128)(2,1)S(1)}, u32[]{:S(2)}, u32[]{:S(2)}) collective-permute-start(bf16[3,192,1024]{2,1,0:T(8,128)(2,1)} %pad_maximum_fusion.4), channel_id=1, source_target_pairs={{0,16},{1,17},{8,24},{9,25},{16,0},{17,1},{24,8},{25,9},{2,18},{3,... | collective-permute-start | bytes 3538952 | tf_op jit(solution)/shard_map/ppermute | solution.py:1070
  153.6 70.7 %collective-permute-start.28 = (bf16[3,192,1024]{2,1,0:T(8,128)(2,1)}, bf16[3,192,1024]{2,1,0:T(8,128)(2,1)S(1)}, u32[]{:S(2)}, u32[]{:S(2)}) collective-permute-start(bf16[3,192,1024]{2,1,0:T(8,128)(2,1)} %pad_maximum_fusion.5), channel_id=1, source_target_pairs={{0,17},{1,16},{8,25},{9,24},{16,1},{17,0},{24,9},{25,8},{2,19},{3,... | collective-permute-start | bytes 3538952 | tf_op jit(solution)/shard_map/ppermute | solution.py:1070
  153.9 70.4 %collective-permute-start.30 = (bf16[3,192,1024]{2,1,0:T(8,128)(2,1)}, bf16[3,192,1024]{2,1,0:T(8,128)(2,1)}, u32[]{:S(2)}, u32[]{:S(2)}) collective-permute-start(bf16[3,192,1024]{2,1,0:T(8,128)(2,1)} %pad_maximum_fusion.7), channel_id=1, source_target_pairs={{0,25},{1,24},{8,17},{9,16},{16,9},{17,8},{24,1},{25,0},{2,27},{3,... | collective-permute-start | bytes 3538952 | tf_op jit(solution)/shard_map/ppermute | solution.py:1070
  158.1 81.3 %collective-permute-start.9 = (bf16[768,512]{1,0:T(8,128)(2,1)}, bf16[768,512]{1,0:T(8,128)(2,1)S(1)}, u32[]{:S(2)}, u32[]{:S(2)}) collective-permute-start(bf16[768,512]{1,0:T(8,128)(2,1)} %get-tuple-element.151), channel_id=1, source_target_pairs={{0,1},{1,0},{2,3},{3,2},{4,5},{5,4},{6,7},{7,6},{8,9},{9,8},{10,11... | collective-permute-start | bytes 2359304 | tf_op jit(solution)/shard_map/ppermute | solution.py:1064
  335.4 26.2 %collective-permute-start.31 = (bf16[768,128]{1,0:T(8,128)(2,1)S(1)}, bf16[768,128]{1,0:T(8,128)(2,1)S(1)}, u32[]{:S(2)}, u32[]{:S(2)}) collective-permute-start(bf16[768,128]{1,0:T(8,128)(2,1)S(1)} %copy-done.83), channel_id=1, source_target_pairs={{0,1},{1,0},{8,9},{9,8},{16,17},{17,16},{24,25},{25,24},{2,3},{3,2... | collective-permute-start | bytes 589832 | tf_op jit(solution)/shard_map/ppermute | solution.py:1070
  337.1 24.6 %collective-permute-start.32 = (bf16[768,128]{1,0:T(8,128)(2,1)S(1)}, bf16[768,128]{1,0:T(8,128)(2,1)S(1)}, u32[]{:S(2)}, u32[]{:S(2)}) collective-permute-start(bf16[768,128]{1,0:T(8,128)(2,1)S(1)} %copy-done.82), channel_id=1, source_target_pairs={{0,8},{1,9},{8,0},{9,1},{16,24},{17,25},{24,16},{25,17},{2,10},{3,... | collective-permute-start | bytes 589832 | tf_op jit(solution)/shard_map/ppermute | solution.py:1070
  337.7 28.9 %collective-permute-start.33 = (bf16[768,128]{1,0:T(8,128)(2,1)S(1)}, bf16[768,128]{1,0:T(8,128)(2,1)S(1)}, u32[]{:S(2)}, u32[]{:S(2)}) collective-permute-start(bf16[768,128]{1,0:T(8,128)(2,1)S(1)} %copy-done.81), channel_id=1, source_target_pairs={{0,9},{1,8},{8,1},{9,0},{16,25},{17,24},{24,17},{25,16},{2,11},{3,... | collective-permute-start | bytes 589832 | tf_op jit(solution)/shard_map/ppermute | solution.py:1070
  338.1 29.1 %collective-permute-start.34 = (bf16[768,128]{1,0:T(8,128)(2,1)S(1)}, bf16[768,128]{1,0:T(8,128)(2,1)}, u32[]{:S(2)}, u32[]{:S(2)}) collective-permute-start(bf16[768,128]{1,0:T(8,128)(2,1)S(1)} %copy-done.80), channel_id=1, source_target_pairs={{0,16},{1,17},{8,24},{9,25},{16,0},{17,1},{24,8},{25,9},{2,18},{3,... | collective-permute-start | bytes 589832 | tf_op jit(solution)/shard_map/ppermute | solution.py:1070
  366.6 118.0 %collective-permute-start.70 = (bf16[8,768,128]{2,1,0:T(8,128)(2,1)}, bf16[8,768,128]{2,1,0:T(8,128)(2,1)}, u32[]{:S(2)}, u32[]{:S(2)}) collective-permute-start(bf16[8,768,128]{2,1,0:T(8,128)(2,1)} %bitcast_dynamic-update-slice_fusion.8.gs), channel_id=1, source_target_pairs={{0,2},{2,0},{4,6},{6,4},{1,3},{3,1},{5,7},{7,5},{8,10},{10,8},{12,... | collective-permute-start | bytes 4718600 | tf_op jit(solution)/shard_map/ppermute | solution.py:1067
  367.3 120.1 %collective-permute-start.69 = (bf16[8,784,128]{2,1,0:T(8,128)(2,1)}, bf16[8,784,128]{2,1,0:T(8,128)(2,1)S(1)}, u32[]{:S(2)}, u32[]{:S(2)}) collective-permute-start(bf16[8,784,128]{2,1,0:T(8,128)(2,1)} %bitcast_dynamic-update-slice_fusion.xs), channel_id=1, source_target_pairs={{0,2},{2,0},{4,6},{6,4},{1,3},{3,1},{5,7},{7,5},{8,10},{10,8},{12,... | collective-permute-start | bytes 4816904 | tf_op jit(solution)/shard_map/ppermute | solution.py:1067
  385.8 60.5 %collective-permute-start.47 = (bf16[192,512]{1,0:T(8,128)(2,1)}, bf16[192,512]{1,0:T(8,128)(2,1)S(1)}, u32[]{:S(2)}, u32[]{:S(2)}) collective-permute-start(bf16[192,512]{1,0:T(8,128)(2,1)} %get-tuple-element.195), channel_id=1, source_target_pairs={{0,2},{2,0},{4,6},{6,4},{1,3},{3,1},{5,7},{7,5},{8,10},{10,8},{12,... | collective-permute-start | bytes 589832 | tf_op jit(solution)/shard_map/ppermute | solution.py:1067
  385.8 60.5 %collective-permute-start.48 = (bf16[192,512]{1,0:T(8,128)(2,1)}, bf16[192,512]{1,0:T(8,128)(2,1)S(1)}, u32[]{:S(2)}, u32[]{:S(2)}) collective-permute-start(bf16[192,512]{1,0:T(8,128)(2,1)} %get-tuple-element.196), channel_id=1, source_target_pairs={{0,4},{2,6},{4,0},{6,2},{1,5},{3,7},{5,1},{7,3},{8,12},{10,14},{12... | collective-permute-start | bytes 589832 | tf_op jit(solution)/shard_map/ppermute | solution.py:1067
  387.8 62.8 %collective-permute-start.49 = (bf16[192,512]{1,0:T(8,128)(2,1)}, bf16[192,512]{1,0:T(8,128)(2,1)S(1)}, u32[]{:S(2)}, u32[]{:S(2)}) collective-permute-start(bf16[192,512]{1,0:T(8,128)(2,1)} %get-tuple-element.197), channel_id=1, source_target_pairs={{0,6},{2,4},{4,2},{6,0},{1,7},{3,5},{5,3},{7,1},{8,14},{10,12},{12... | collective-permute-start | bytes 589832 | tf_op jit(solution)/shard_map/ppermute | solution.py:1067
  446.4 173.1 %collective-permute-start.68 = (bf16[8,768,128]{2,1,0:T(8,128)(2,1)}, bf16[8,768,128]{2,1,0:T(8,128)(2,1)}, u32[]{:S(2)}, u32[]{:S(2)}) collective-permute-start(bf16[8,768,128]{2,1,0:T(8,128)(2,1)} %bitcast_dynamic-update-slice_fusion.8.gs), channel_id=1, source_target_pairs={{0,4},{2,6},{4,0},{6,2},{1,5},{3,7},{5,1},{7,3},{8,12},{10,14},{12... | collective-permute-start | bytes 4718600 | tf_op jit(solution)/shard_map/ppermute | solution.py:1067
  446.4 207.4 %collective-permute-start.67 = (bf16[8,784,128]{2,1,0:T(8,128)(2,1)}, bf16[8,784,128]{2,1,0:T(8,128)(2,1)S(1)}, u32[]{:S(2)}, u32[]{:S(2)}) collective-permute-start(bf16[8,784,128]{2,1,0:T(8,128)(2,1)} %bitcast_dynamic-update-slice_fusion.xs), channel_id=1, source_target_pairs={{0,4},{2,6},{4,0},{6,2},{1,5},{3,7},{5,1},{7,3},{8,12},{10,14},{12... | collective-permute-start | bytes 4816904 | tf_op jit(solution)/shard_map/ppermute | solution.py:1067
  450.6 32.7 %collective-permute-start.61 = (bf16[192,512]{0,1:T(8,128)(2,1)S(1)}, bf16[192,512]{0,1:T(8,128)(2,1)S(1)}, u32[]{:S(2)}, u32[]{:S(2)}) collective-permute-start(bf16[192,512]{0,1:T(8,128)(2,1)S(1)} %dynamic-slice_bitcast_fusion.11), channel_id=1, source_target_pairs={{0,16},{8,24},{16,0},{24,8},{1,17},{9,25},{17,1},{25,9},{2,18},{10... | collective-permute-start | bytes 589832 | tf_op jit(solution)/shard_map/ppermute | solution.py:1061
  483.3 192.0 %collective-permute-start.66 = (bf16[8,768,128]{2,1,0:T(8,128)(2,1)}, bf16[8,768,128]{2,1,0:T(8,128)(2,1)}, u32[]{:S(2)}, u32[]{:S(2)}) collective-permute-start(bf16[8,768,128]{2,1,0:T(8,128)(2,1)} %bitcast_dynamic-update-slice_fusion.8.gs), channel_id=1, source_target_pairs={{0,6},{2,4},{4,2},{6,0},{1,7},{3,5},{5,3},{7,1},{8,14},{10,12},{12... | collective-permute-start | bytes 4718600 | tf_op jit(solution)/shard_map/ppermute | solution.py:1067
  484.6 204.2 %collective-permute-start.65 = (bf16[8,784,128]{2,1,0:T(8,128)(2,1)}, bf16[8,784,128]{2,1,0:T(8,128)(2,1)}, u32[]{:S(2)}, u32[]{:S(2)}) collective-permute-start(bf16[8,784,128]{2,1,0:T(8,128)(2,1)} %bitcast_dynamic-update-slice_fusion.xs), channel_id=1, source_target_pairs={{0,6},{2,4},{4,2},{6,0},{1,7},{3,5},{5,3},{7,1},{8,14},{10,12},{12... | collective-permute-start | bytes 4816904 | tf_op jit(solution)/shard_map/ppermute | solution.py:1067
  487.3 297.5 %collective-permute-start.38 = (bf16[512,768]{1,0:T(8,128)(2,1)S(1)}, bf16[512,768]{1,0:T(8,128)(2,1)S(1)}, u32[]{:S(2)}, u32[]{:S(2)}) collective-permute-start(bf16[512,768]{1,0:T(8,128)(2,1)S(1)} %copy-done.22), channel_id=1, source_target_pairs={{0,1},{1,0},{2,3},{3,2},{4,5},{5,4},{6,7},{7,6},{8,9},{9,8},{10,11... | collective-permute-start | bytes 2359304 | tf_op jit(solution)/shard_map/ppermute | solution.py:1064
  619.5 106.6 %collective-permute-start.54 = (f32[512,12]{0,1:T(8,128)S(1)}, f32[512,12]{0,1:T(8,128)S(1)}, u32[]{:S(2)}, u32[]{:S(2)}) collective-permute-start(f32[512,12]{0,1:T(8,128)S(1)} %get-tuple-element.329), channel_id=1, source_target_pairs={{0,1},{1,0},{2,3},{3,2},{4,5},{5,4},{6,7},{7,6},{8,9},{9,8},{10,11... | collective-permute-start | bytes 73736 | tf_op jit(solution)/shard_map/ppermute | solution.py:1064
  653.8 132.2 %collective-permute-start.50 = (bf16[3,256,384]{2,1,0:T(8,128)(2,1)}, bf16[3,256,384]{2,1,0:T(8,128)(2,1)S(1)}, u32[]{:S(2)}, u32[]{:S(2)}) collective-permute-start(bf16[3,256,384]{2,1,0:T(8,128)(2,1)} %get-tuple-element.199), channel_id=1, source_target_pairs={{0,2},{2,0},{4,6},{6,4},{1,3},{3,1},{5,7},{7,5},{8,10},{10,8},{12,... | collective-permute-start | bytes 1769480 | tf_op jit(solution)/shard_map/ppermute | solution.py:1067
  675.4 111.5 %collective-permute-start.51 = (bf16[3,256,384]{2,1,0:T(8,128)(2,1)}, bf16[3,256,384]{2,1,0:T(8,128)(2,1)S(1)}, u32[]{:S(2)}, u32[]{:S(2)}) collective-permute-start(bf16[3,256,384]{2,1,0:T(8,128)(2,1)} %get-tuple-element.200), channel_id=1, source_target_pairs={{0,4},{2,6},{4,0},{6,2},{1,5},{3,7},{5,1},{7,3},{8,12},{10,14},{12... | collective-permute-start | bytes 1769480 | tf_op jit(solution)/shard_map/ppermute | solution.py:1067
  688.8 114.8 %collective-permute-start.52 = (bf16[3,256,384]{2,1,0:T(8,128)(2,1)S(1)}, bf16[3,256,384]{2,1,0:T(8,128)(2,1)S(1)}, u32[]{:S(2)}, u32[]{:S(2)}) collective-permute-start(bf16[3,256,384]{2,1,0:T(8,128)(2,1)S(1)} %copy-done.64), channel_id=1, source_target_pairs={{0,6},{2,4},{4,2},{6,0},{1,7},{3,5},{5,3},{7,1},{8,14},{10,12},{12... | collective-permute-start | bytes 1769480 | tf_op jit(solution)/shard_map/ppermute | solution.py:1067
  726.1 78.9 %collective-permute-start.62 = (bf16[192,512]{0,1:T(8,128)(2,1)S(1)}, bf16[192,512]{0,1:T(8,128)(2,1)S(1)}, u32[]{:S(2)}, u32[]{:S(2)}) collective-permute-start(bf16[192,512]{0,1:T(8,128)(2,1)S(1)} %fusion.7), channel_id=1, source_target_pairs={{0,2},{2,0},{4,6},{6,4},{1,3},{3,1},{5,7},{7,5},{8,10},{10,8},{12,... | collective-permute-start | bytes 589832 | tf_op jit(solution)/shard_map/ppermute | solution.py:1067
  807.4 24.8 %collective-permute-start.98 = (bf16[3,192,256]{2,1,0:T(8,128)(2,1)S(1)}, bf16[3,192,256]{2,1,0:T(8,128)(2,1)S(1)}, u32[]{:S(2)}, u32[]{:S(2)}) collective-permute-start(bf16[3,192,256]{2,1,0:T(8,128)(2,1)S(1)} %copy-done.72), channel_id=1, source_target_pairs={{0,25},{1,24},{8,17},{9,16},{16,9},{17,8},{24,1},{25,0},{2,27},{3,... | collective-permute-start | bytes 884744 | tf_op jit(solution)/shard_map/ppermute | solution.py:1070
  809.2 24.3 %collective-permute-start.85 = (bf16[3,192,256]{2,1,0:T(8,128)(2,1)}, bf16[3,192,256]{2,1,0:T(8,128)(2,1)S(1)}, u32[]{:S(2)}, u32[]{:S(2)}) collective-permute-start(bf16[3,192,256]{2,1,0:T(8,128)(2,1)} %get-tuple-element.245), channel_id=1, source_target_pairs={{0,1},{1,0},{8,9},{9,8},{16,17},{17,16},{24,25},{25,24},{2,3},{3,2... | collective-permute-start | bytes 884744 | tf_op jit(solution)/shard_map/ppermute | solution.py:1070
  826.3 27.6 %collective-permute-start.55 = (bf16[2,592,384]{2,1,0:T(8,128)(2,1)S(1)}, bf16[2,592,384]{2,1,0:T(8,128)(2,1)S(1)}, u32[]{:S(2)}, u32[]{:S(2)}) collective-permute-start(bf16[2,592,384]{2,1,0:T(8,128)(2,1)S(1)} %dynamic-slice_bitcast_fusion), channel_id=1, source_target_pairs={{0,8},{8,0},{16,24},{24,16},{1,9},{9,1},{17,25},{25,17},{2,10},{10... | collective-permute-start | bytes 2727944 | tf_op jit(solution)/shard_map/ppermute | solution.py:1061
  826.3 24.3 %collective-permute-start.86 = (bf16[3,192,256]{2,1,0:T(8,128)(2,1)}, bf16[3,192,256]{2,1,0:T(8,128)(2,1)S(1)}, u32[]{:S(2)}, u32[]{:S(2)}) collective-permute-start(bf16[3,192,256]{2,1,0:T(8,128)(2,1)} %get-tuple-element.246), channel_id=1, source_target_pairs={{0,8},{1,9},{8,0},{9,1},{16,24},{17,25},{24,16},{25,17},{2,10},{3,... | collective-permute-start | bytes 884744 | tf_op jit(solution)/shard_map/ppermute | solution.py:1070
  868.3 24.3 %collective-permute-start.82 = (bf16[3,192,256]{2,1,0:T(8,128)(2,1)S(1)}, bf16[3,192,256]{2,1,0:T(8,128)(2,1)S(1)}, u32[]{:S(2)}, u32[]{:S(2)}) collective-permute-start(bf16[3,192,256]{2,1,0:T(8,128)(2,1)S(1)} %copy-done.74), channel_id=1, source_target_pairs={{0,17},{1,16},{8,25},{9,24},{16,1},{17,0},{24,9},{25,8},{2,19},{3,... | collective-permute-start | bytes 884744 | tf_op jit(solution)/shard_map/ppermute | solution.py:1070
  871.5 25.1 %collective-permute-start.84 = (bf16[3,192,256]{2,1,0:T(8,128)(2,1)}, bf16[3,192,256]{2,1,0:T(8,128)(2,1)}, u32[]{:S(2)}, u32[]{:S(2)}) collective-permute-start(bf16[3,192,256]{2,1,0:T(8,128)(2,1)} %get-tuple-element.243), channel_id=1, source_target_pairs={{0,25},{1,24},{8,17},{9,16},{16,9},{17,8},{24,1},{25,0},{2,27},{3,... | collective-permute-start | bytes 884744 | tf_op jit(solution)/shard_map/ppermute | solution.py:1070
  874.3 31.1 %collective-permute-start.56 = (bf16[592,384]{1,0:T(8,128)(2,1)}, bf16[592,384]{1,0:T(8,128)(2,1)}, u32[]{:S(2)}, u32[]{:S(2)}) collective-permute-start(bf16[592,384]{1,0:T(8,128)(2,1)} %dynamic-slice_bitcast_fusion.10), channel_id=1, source_target_pairs={{0,16},{8,24},{16,0},{24,8},{1,17},{9,25},{17,1},{25,9},{2,18},{10... | collective-permute-start | bytes 1363976 | tf_op jit(solution)/shard_map/ppermute | solution.py:1061
  896.6 27.7 %collective-permute-start.74 = (bf16[3,192,256]{2,1,0:T(8,128)(2,1)}, bf16[3,192,256]{2,1,0:T(8,128)(2,1)S(1)}, u32[]{:S(2)}, u32[]{:S(2)}) collective-permute-start(bf16[3,192,256]{2,1,0:T(8,128)(2,1)} %get-tuple-element.232), channel_id=1, source_target_pairs={{0,16},{1,17},{8,24},{9,25},{16,0},{17,1},{24,8},{25,9},{2,18},{3,... | collective-permute-start | bytes 884744 | tf_op jit(solution)/shard_map/ppermute | solution.py:1070
  903.3 36.7 %collective-permute-start.76 = (bf16[3,192,256]{2,1,0:T(8,128)(2,1)}, bf16[3,192,256]{2,1,0:T(8,128)(2,1)S(1)}, u32[]{:S(2)}, u32[]{:S(2)}) collective-permute-start(bf16[3,192,256]{2,1,0:T(8,128)(2,1)} %get-tuple-element.234), channel_id=1, source_target_pairs={{0,24},{1,25},{8,16},{9,17},{16,8},{17,9},{24,0},{25,1},{2,26},{3,... | collective-permute-start | bytes 884744 | tf_op jit(solution)/shard_map/ppermute | solution.py:1070
  905.5 34.5 %collective-permute-start.77 = (bf16[3,192,256]{2,1,0:T(8,128)(2,1)}, bf16[3,192,256]{2,1,0:T(8,128)(2,1)S(1)}, u32[]{:S(2)}, u32[]{:S(2)}) collective-permute-start(bf16[3,192,256]{2,1,0:T(8,128)(2,1)} %get-tuple-element.235), channel_id=1, source_target_pairs={{0,25},{1,24},{8,17},{9,16},{16,9},{17,8},{24,1},{25,0},{2,27},{3,... | collective-permute-start | bytes 884744 | tf_op jit(solution)/shard_map/ppermute | solution.py:1070
  908.0 36.7 %collective-permute-start.63 = (bf16[192,512]{0,1:T(8,128)(2,1)S(1)}, bf16[192,512]{0,1:T(8,128)(2,1)S(1)}, u32[]{:S(2)}, u32[]{:S(2)}) collective-permute-start(bf16[192,512]{0,1:T(8,128)(2,1)S(1)} %reduce-precision_convert_fusion.1), channel_id=1, source_target_pairs={{0,4},{2,6},{4,0},{6,2},{1,5},{3,7},{5,1},{7,3},{8,12},{10,14},{12... | collective-permute-start | bytes 589832 | tf_op jit(solution)/shard_map/ppermute | solution.py:1067
  925.1 45.2 %collective-permute-start.53 = (bf16[2,512,768]{2,1,0:T(8,128)(2,1)}, bf16[2,512,768]{2,1,0:T(8,128)(2,1)}, u32[]{:S(2)}, u32[]{:S(2)}) collective-permute-start(bf16[2,512,768]{2,1,0:T(8,128)(2,1)} %get-tuple-element.204.own), channel_id=1, source_target_pairs={{0,1},{1,0},{2,3},{3,2},{4,5},{5,4},{6,7},{7,6},{8,9},{9,8},{10,11... | collective-permute-start | bytes 4718600 | tf_op jit(solution)/shard_map/ppermute | solution.py:1064
  (142 other events, 2097.1 us)

commit v2 on v1

--- a/solution.py
+++ b/solution.py
@@ -422,8 +422,11 @@
 MIB = 1 << 20
 F32 = jnp.float32
 BF = jnp.bfloat16
+MESH = pl.DeviceIdType.MESH
+HBM = pl.BlockSpec(memory_space=pl.ANY)
 WHOLE = pl.BlockSpec(memory_space=pltpu.VMEM)
 SCALARS = pl.BlockSpec(memory_space=pltpu.SMEM)
+COST = pl.CostEstimate(flops=1024, bytes_accessed=1024, transcendentals=0)
 LOG2E = 1.4426950408889634
 
 
@@ -444,7 +447,6 @@
 
 
 def run(body, name, scalars, ins, outs, scratch=(), flops=0, vmem=56):
-    moved = sum(math.prod(a.shape) * a.dtype.itemsize for a in (*ins, *outs))
     return pl.pallas_call(
         body,
         out_shape=tuple(outs),
@@ -452,41 +454,9 @@
         out_specs=tuple([WHOLE] * len(outs)),
         scratch_shapes=list(scratch),
         compiler_params=pltpu.CompilerParams(vmem_limit_bytes=vmem * MIB),
-        cost_estimate=pl.CostEstimate(flops=flops, bytes_accessed=moved, transcendentals=0),
+        cost_estimate=COST,
         name=name,
     )(scalars, *ins)
-
-
-def pack_kernel(sc, routes_ref, gy_ref, hot_ref, gyt_ref, *g_refs):
-    me = sc[0]
-    rows = gy_ref.shape[0]
-    named = routes_ref[...]
-    named = jnp.where(named < NFFN, jnp.bitwise_xor(named, me), named)
-    first, second = named[0:1], named[1:2]
-    gyt = gy_ref[...].T
-    gyt_ref[...] = gyt
-    ids = lax.broadcasted_iota(jnp.int32, (16, rows), 0)
-    hits = ((ids == first) | (ids == second)).astype(F32)
-    before = lax.broadcasted_iota(jnp.int32, (rows, rows), 0)
-    after = lax.broadcasted_iota(jnp.int32, (rows, rows), 1)
-    upper = (before <= after).astype(F32).astype(BF)
-    places = mm(hits.astype(BF), upper) - 1.0
-    slots = lax.broadcasted_iota(jnp.int32, (CAPACITY, rows), 0).astype(F32)
-    for k in range(NFFN):
-        hot = jnp.where((slots == places[k : k + 1]) & (hits[k : k + 1] > 0.5), 1.0, 0.0)
-        hot = hot.astype(BF)
-        hot_ref[k * CAPACITY : (k + 1) * CAPACITY, :] = hot
-        g_refs[k][...] = mm_nt(gyt, hot).astype(BF)
-
-
-def norm_kernel(sc, tokens_ref, gain_ref, n_ref, nt_ref, xt_ref):
-    for s in range(2):
-        x = tokens_ref[s].astype(F32)
-        inverse = lax.rsqrt(jnp.mean(x * x, axis=-1, keepdims=True) + epsilon)
-        n = (x * inverse * gain_ref[...]).astype(BF)
-        n_ref[s] = n
-        nt_ref[:, s * x.shape[0] : (s + 1) * x.shape[0]] = n.T
-    xt_ref[...] = tokens_ref[sc[2]].T
 
 
 def swap_halves(v):
@@ -497,42 +467,11 @@
     return jnp.where(low, pltpu.roll(v, width - half, 1), pltpu.roll(v, half, 1))
 
 
-def qkv_kernel(sc, n_ref, p0, p1, p2, p3, cos_ref, sin_ref, o0, o1, o2, o3, w_out, wo_out, st):
-    z, f = sc[1], sc[3]
-    for j, p in enumerate((p0, p1, p2, p3)):
-        src = jnp.bitwise_xor(f, j)
-        rows = pl.multiple_of(src * 192, 192)
-        for c in range(3):
-            w_out[c, pl.ds(rows, 192), :] = p[c * 192 : (c + 1) * 192, :]
-        wo_out[pl.ds(rows, 192), :] = p[576:768, :]
-    cos = jnp.concatenate([cos_ref[...]] * 3, axis=1)
-    sin = jnp.concatenate([sin_ref[...]] * 3, axis=1)
-    half_rows = cos.shape[0] // 2
-    for s in range(2):
-        n = n_ref[s]
-        q = mm(n, w_out[0])
-        k = mm(n, w_out[1])
-        q = (q * cos + swap_halves(q) * sin).astype(BF)
-        k = (k * cos + swap_halves(k) * sin).astype(BF)
-        v = mm(n, w_out[2]).astype(BF)
-        for half in range(2):
-            d = jnp.bitwise_xor(z, 2 * s + half)
-            for j in range(3):
-                col = (half * 3 + j) * HEAD_DIM
-                parts = [
-                    a[r * half_rows : (r + 1) * half_rows, col : col + HEAD_DIM]
-                    for r in range(2)
-                    for a in (q, k, v)
-                ]
-                st[d, j] = jnp.concatenate(parts, axis=1)
-    for d, o in enumerate((o0, o1, o2, o3)):
-        o[...] = st[d]
-
-
 def unpack_qkv(z, blocks, q_s, k_s, v_s):
     h = HEAD_DIM
-    for d, b in enumerate(blocks):
-        base = pl.multiple_of(jnp.bitwise_xor(z, d) * 512, 512)
+    for d in range(4):
+        b = blocks.at[d]
+        base = pl.multiple_of(flip4(z, d) * 512, 512)
         for j in range(3):
             blk = b[j]
             for r in range(2):
@@ -552,9 +491,17 @@
     return (key <= query) | (key < prefix)
 
 
-def attn_kernel(sc, b0, b1, b2, b3, o0, o1, o2, o3, m_ref, q_s, k_s, v_s, st):
-    z, prefix = sc[1], sc[4]
-    unpack_qkv(z, (b0, b1, b2, b3), q_s, k_s, v_s)
+def attn_kernel(prefix_ref, blocks, m3, mixed_in, m_ref, l3, q_s, k_s, v_s, st, z_sems, w_sems):
+    f, z, x = here()
+    barrier = pltpu.get_barrier_semaphore()
+    for d in range(1, 4):
+        pl.semaphore_signal(barrier, inc=1, device_id=(f, flip4(z, d), x), device_id_type=MESH)
+    pl.semaphore_signal(barrier, inc=1, device_id=(flip4(f, 2), z, flip2(x, 1)), device_id_type=MESH)
+    pl.semaphore_wait(barrier, 4)
+    weights = to_plane(5, m3, l3, w_sems)
+    weights.start()
+    prefix = prefix_ref[0]
+    unpack_qkv(z, blocks, q_s, k_s, v_s)
     scale = HEAD_DIM ** (-0.5) * LOG2E
 
     def unit(j, carry):
@@ -586,22 +533,16 @@
         return carry
 
     lax.fori_loop(0, 3, unit, 0)
-    for d, o in enumerate((o0, o1, o2, o3)):
-        o[...] = st[jnp.bitwise_xor(z, d)]
-
-
-def outproj_kernel(sc, b0, b1, b2, b3, wo_ref, mixed_ref, own_ref, send_ref, st):
-    z, x = sc[1], sc[2]
-    for d, b in enumerate((b0, b1, b2, b3)):
-        st[d] = b[...]
-    for s in range(2):
-        for half in range(2):
-            mixed_ref[s, half * 192 : (half + 1) * 192, :] = st[jnp.bitwise_xor(z, 2 * s + half)]
-    own_ref[...] = mm(wo_ref[...], mixed_ref[x]).astype(BF)
-    send_ref[...] = mm(wo_ref[...], mixed_ref[1 - x]).astype(BF)
-
-
-def row_state(me, hidden, gain, gate_t, prev, routes):
+    copies = [to_column(d, st.at[flip4(z, d)], mixed_in.at[d], z_sems) for d in (3, 2, 1)]
+    for c in copies:
+        c.start()
+    mixed_in[0] = st[z]
+    for c in copies:
+        c.wait()
+    weights.wait()
+
+
+def row_state(hidden, gain, gate_t, prev, routes, f, x):
     rows = hidden.shape[1]
     inverse = lax.rsqrt(jnp.mean(hidden * hidden, axis=0, keepdims=True) + epsilon)
     normed = hidden * inverse * gain
@@ -614,7 +555,7 @@
     top = jnp.maximum(picks[0], picks[1])
     e = [jnp.exp(p - top) for p in picks]
     gates = [v / (e[0] + e[1]) for v in e]
-    ks = [jnp.where(r < NFFN, jnp.bitwise_xor(r, me), r) for r in named]
+    ks = [expert_flip(r, f, x) for r in named]
     copy_w = sum(jnp.where(r == NFFN + 1, g, 0.0) for r, g in zip(named, gates))
     const_w = [
         sum(jnp.where(r == NFFN + 2 + c, g, 0.0) for r, g in zip(named, gates))
@@ -632,29 +573,14 @@
     )
 
 
-def router_kernel(sc, xt, own, recv, gain, gate_t, prev, routes, hot, hidden_ref, *x_refs):
-    me = sc[0]
-    hidden = xt[...].astype(F32) + (own[...].astype(F32) + recv[...].astype(F32))
-    hidden_ref[...] = hidden
-    s = row_state(me, hidden, gain[...], gate_t[...], prev[...], routes[...])
-    ids = s["ids"][0:8]
-    gate_rows = sum(jnp.where(ids == k, g, 0.0) for k, g in zip(s["ks"], s["gates"]))
-    high = gate_rows.astype(BF).astype(F32)
-    extra = jnp.concatenate([high, gate_rows - high], axis=0).astype(BF)
-    ext = jnp.concatenate([s["normed_b"], extra], axis=0)
-    for k in range(NFFN):
-        x_refs[k][...] = mm_nt(ext, hot[k * CAPACITY : (k + 1) * CAPACITY, :]).astype(BF)
-
-
-def wprep_kernel(sc, *refs):
-    blocks, w_ref, wt_ref = refs[:8], refs[8], refs[9]
-    me = sc[0]
-    for k, b in enumerate(blocks):
-        s = jnp.bitwise_xor(me, k)
-        rows = pl.multiple_of((s // 2) * 192, 192)
-        cols = pl.multiple_of((s % 2) * 1024, 1024)
-        for m in range(3):
-            w_ref[m, pl.ds(rows, 192), pl.ds(cols, 1024)] = b[m]
+def wprep_kernel(sc, b0, b1, b2, b3, w_ref, wt_ref):
+    f, x = sc[3], sc[2]
+    for j, b in enumerate((b0, b1, b2, b3)):
+        for cc in range(2):
+            rows = pl.multiple_of(jnp.bitwise_xor(f, 2 * (j // 2) + cc) * 192, 192)
+            cols = pl.multiple_of(jnp.bitwise_xor(x, j % 2) * 1024, 1024)
+            for m in range(3):
+                w_ref[m, pl.ds(rows, 192), pl.ds(cols, 1024)] = b[cc, m]
     tile = 256
 
     def step(t, carry):
@@ -668,8 +594,8 @@
 
 def expert_body(first, sc, xs, gs, w, wt, *refs):
     if first:
-        y_refs, r_refs = refs[0:8], refs[8:16]
-        refs = refs[16:]
+        y_ref, r_ref = refs[0:2]
+        refs = refs[2:]
     else:
         refs = refs[5:]
     bx, bg, ba, bp, bu = refs[:5]
@@ -677,17 +603,17 @@
     xt, gt, grow = refs[:3]
     if first:
         din, res, graw = refs[3:]
-    j = pl.program_id(0)
+    j = pl.program_id(1)
 
     @pl.when(j == 0)
     def _():
         for k in range(8):
             cols = slice(k * CAPACITY, (k + 1) * CAPACITY)
-            xt[:, cols] = xs[k, 0:768]
-            pair = xs[k, 768:784].astype(F32)
-            gate = pair[k : k + 1] + pair[8 + k : 9 + k]
+            both = xs[0, k].astype(F32)
+            xt[:, cols] = both[0:768].astype(BF)
+            gate = both[768 + k : 769 + k] + both[776 + k : 777 + k]
             grow[:, cols] = jnp.broadcast_to(gate, (8, CAPACITY))
-            g = gs[k]
+            g = gs[0, k]
             if first:
                 graw[:, cols] = g
             gt[:, cols] = (g.astype(F32) * gate).astype(BF)
@@ -713,7 +639,7 @@
         din[...] += mm(w[0], dp) + mm(w[1], du)
         res[...] += mm(w[2], act)
 
-        @pl.when(j == pl.num_programs(0) - 1)
+        @pl.when(j == pl.num_programs(1) - 1)
         def _():
             row = lax.broadcasted_iota(jnp.int32, (8, CAPACITY), 0)
             for k in range(8):
@@ -724,13 +650,13 @@
                 tail = jnp.concatenate(
                     [jnp.where(row == k, high, 0.0), jnp.where(row == k, dg - high, 0.0)], axis=0
                 )
-                y_refs[k][0:768, :] = din[:, cols].astype(BF)
-                y_refs[k][768:784, :] = tail.astype(BF)
-                r_refs[k][...] = (r * grow[0:1, cols]).astype(BF)
-
-
-def expert_call(first, plane, xs, gs, w, wt, held):
-    tile = 512 if first else 512
+                y_ref[k, 0:768, :] = din[:, cols].astype(BF)
+                y_ref[k, 768:784, :] = tail.astype(BF)
+                r_ref[k] = (r * grow[0:1, cols]).astype(BF)
+
+
+def expert_call(first, planes, xs, gs, w, wt, held):
+    tile = 512
     steps = w.shape[2] // tile
     slots = 8 * CAPACITY
     width = w.shape[1]
@@ -739,46 +665,44 @@
         out((n_ctx, width, slots)), out((n_ctx, width, slots)),
         out((n_ctx, w.shape[2], slots)), out((n_ctx, w.shape[2], slots)), out((n_ctx, w.shape[2], slots)),
     ]
-    fixed3 = lambda j, s: (0, 0, 0)
-    specs_in = [
-        pl.BlockSpec(xs.shape, fixed3), pl.BlockSpec(gs.shape, fixed3),
-        pl.BlockSpec((3, width, tile), lambda j, s: (0, 0, j)),
-        pl.BlockSpec((3, tile, width), lambda j, s: (0, j, 0)),
+    at = (lambda i, j, s: (0, 0, 0, 0)) if first else (lambda i, j, s: (s[i], 0, 0, 0))
+    specs_in = [pl.BlockSpec((1,) + a.shape[1:], at) for a in (xs, gs)] + [
+        pl.BlockSpec((3, width, tile), lambda i, j, s: (0, 0, j)),
+        pl.BlockSpec((3, tile, width), lambda i, j, s: (0, j, 0)),
     ]
     buffer_specs = [
-        pl.BlockSpec((1, width, slots), lambda j, s: (s[0], 0, 0)),
-        pl.BlockSpec((1, width, slots), lambda j, s: (s[0], 0, 0)),
-    ] + [pl.BlockSpec((1, tile, slots), lambda j, s: (s[0], j, 0))] * 3
+        pl.BlockSpec((1, width, slots), lambda i, j, s: (s[i], 0, 0)),
+        pl.BlockSpec((1, width, slots), lambda i, j, s: (s[i], 0, 0)),
+    ] + [pl.BlockSpec((1, tile, slots), lambda i, j, s: (s[i], j, 0))] * 3
     scratch = [
         pltpu.VMEM((width, slots), BF), pltpu.VMEM((width, slots), BF), pltpu.VMEM((8, slots), F32),
     ]
     outs, specs_out, aliases, extra_in = list(buffers), list(buffer_specs), {}, []
     if first:
-        packet = [out((width + 16, CAPACITY))] * 8 + [out((width, CAPACITY))] * 8
+        packet = [out((8, width + 16, CAPACITY)), out((8, width, CAPACITY))]
         outs = packet + outs
-        specs_out = [pl.BlockSpec(p.shape, lambda j, s: (0, 0)) for p in packet] + specs_out
+        specs_out = [pl.BlockSpec(p.shape, lambda i, j, s: (0, 0, 0)) for p in packet] + specs_out
         scratch += [pltpu.VMEM((width, slots), F32)] * 2 + [pltpu.VMEM((width, slots), BF)]
     else:
         extra_in = list(held)
         specs_in += [pl.BlockSpec(memory_space=pl.ANY)] * 5
         aliases = {5 + i: i for i in range(5)}
-    macs = width * w.shape[2] * slots * (6 if first else 3)
     return pl.pallas_call(
         functools.partial(expert_body, first),
         out_shape=tuple(outs),
         grid_spec=pltpu.PrefetchScalarGridSpec(
-            num_scalar_prefetch=1, grid=(steps,), in_specs=specs_in, out_specs=tuple(specs_out),
-            scratch_shapes=scratch,
+            num_scalar_prefetch=1, grid=(planes.shape[0], steps), in_specs=specs_in,
+            out_specs=tuple(specs_out), scratch_shapes=scratch,
         ),
         input_output_aliases=aliases,
         compiler_params=pltpu.CompilerParams(vmem_limit_bytes=58 * MIB),
-        cost_estimate=pl.CostEstimate(flops=2 * macs, bytes_accessed=40 * MIB, transcendentals=0),
+        cost_estimate=COST,
         name="experts_own" if first else "experts_more",
-    )(plane, xs, gs, w, wt, *extra_in)
+    )(planes, xs, gs, w, wt, *extra_in)
 
 
 def grads_body(w_cols, sc, bx, bg, ba, bp, bu, *refs):
-    outs, acc = refs[:8], refs[8]
+    outs, acc = refs[:4], refs[4]
     p = pl.program_id(0)
 
     @pl.when(p == 0)
@@ -792,12 +716,13 @@
 
     @pl.when(p == pl.num_programs(0) - 1)
     def _():
-        me = sc[0]
-        for k in range(8):
-            s = jnp.bitwise_xor(me, k)
-            rows = pl.multiple_of((s // 2) * 192, 192)
-            for m in range(3):
-                outs[k][m] = acc[s % 2, m, pl.ds(rows, 192), :].astype(BF)
+        f, x = sc[1], sc[2]
+        for j in range(4):
+            for cc in range(2):
+                rows = pl.multiple_of(jnp.bitwise_xor(f, 2 * (j // 2) + cc) * 192, 192)
+                xh = jnp.bitwise_xor(x, j % 2)
+                for m in range(3):
+                    outs[j][cc, m] = acc[xh, m, pl.ds(rows, 192), :].astype(BF)
 
 
 def grads_call(scalars, part, parts, held):
@@ -810,34 +735,36 @@
     macs = 3 * width * slots * n_ctx * 2 * cols
     return pl.pallas_call(
         functools.partial(grads_body, cols),
-        out_shape=tuple([out((3, 192, cols))] * 8),
+        out_shape=tuple([out((2, 3, 192, cols))] * 4),
         grid_spec=pltpu.PrefetchScalarGridSpec(
             num_scalar_prefetch=1, grid=(n_ctx,),
             in_specs=[pl.BlockSpec((1, width, slots), lambda p, s: (p, 0, 0))] * 2 + [tall] * 3,
-            out_specs=tuple([pl.BlockSpec((3, 192, cols), lambda p, s: (0, 0, 0))] * 8),
+            out_specs=tuple([pl.BlockSpec((2, 3, 192, cols), lambda p, s: (0, 0, 0, 0))] * 4),
             scratch_shapes=[pltpu.VMEM((2, 3, width, cols), F32)],
         ),
         compiler_params=pltpu.CompilerParams(vmem_limit_bytes=56 * MIB),
-        cost_estimate=pl.CostEstimate(flops=2 * macs, bytes_accessed=30 * MIB, transcendentals=0),
+        cost_estimate=COST,
         name="expert_grads",
     )(scalars, bx, bg, split(ba), split(bp), split(bu))
 
 
 def place_body(first, sc, *refs):
-    blocks = refs[:8]
-    gu, dn = refs[8:] if first else refs[10:]
+    near, far = refs[:4], refs[4]
+    gu, dn = refs[5:] if first else refs[7:]
     at = pl.program_id(0)
     for k in range(8):
 
         @pl.when(at == k)
         def _(k=k):
-            gu[0, 0] = blocks[k][0].astype(F32)
-            gu[0, 1] = blocks[k][1].astype(F32)
-            dn[0] = blocks[k][2].astype(F32)
+            j = 2 * (k // 4) + k % 2
+            block = far.at[j] if (k // 2) % 2 else near[j].at[0]
+            gu[0, 0] = block[0].astype(F32)
+            gu[0, 1] = block[1].astype(F32)
+            dn[0] = block[2].astype(F32)
 
 
 def place_call(scalars, part, parts, blocks, held):
-    cols = blocks[0].shape[2]
+    cols = blocks[0].shape[3]
     first = held is None
     xor = lambda k, s: jnp.bitwise_xor(k, s[0])
     extra = [] if first else list(held)
@@ -846,97 +773,34 @@
         out_shape=(out((NFFN, 2, 192, cols * parts), F32), out((NFFN, 192, cols * parts), F32)),
         grid_spec=pltpu.PrefetchScalarGridSpec(
             num_scalar_prefetch=1, grid=(NFFN,),
-            in_specs=[pl.BlockSpec((3, 192, cols), lambda k, s: (0, 0, 0))] * 8
+            in_specs=[pl.BlockSpec(b.shape, lambda k, s: (0, 0, 0, 0)) for b in blocks]
             + [pl.BlockSpec(memory_space=pl.ANY)] * len(extra),
             out_specs=(
                 pl.BlockSpec((1, 2, 192, cols), lambda k, s: (xor(k, s), 0, 0, part)),
                 pl.BlockSpec((1, 192, cols), lambda k, s: (xor(k, s), 0, part)),
             ),
         ),
-        input_output_aliases={} if first else {9: 0, 10: 1},
+        input_output_aliases={} if first else {6: 0, 7: 1},
         compiler_params=pltpu.CompilerParams(vmem_limit_bytes=40 * MIB),
-        cost_estimate=pl.CostEstimate(flops=0, bytes_accessed=28 * MIB // parts, transcendentals=0),
+        cost_estimate=COST,
         name="place_grads",
     )(scalars, *blocks, *extra)
 
 
-def combine_kernel(sc, hidden_ref, gain, gate_t, gate, prev, routes, const, gyt, hot, *refs):
-    ys, (dt_ref, gprev_ref, small_ref) = refs[:8], refs[8:]
+def layer_kernel(sc, hidden_ref, small, small_t, prev, routes, hot, rin, out_ref):
     hidden = hidden_ref[...]
-    width, rows = hidden.shape
-    s = row_state(sc[0], hidden, gain[...], gate_t[...], prev[...], routes[...])
-    y = jnp.concatenate([r[...] for r in ys], axis=1)
-    back = mm(y, hot[...])
-    ids, named, gates, mixing = s["ids"], s["named"], s["gates"], s["mixing"]
-    normed, inverse = s["normed"], s["inverse"]
-    d_expert = back[768:776] + back[776:784]
-    gy = gyt[...].astype(F32)
-    dy_normed = jnp.sum(gy * normed, axis=0, keepdims=True)
-    vecs = const[...].astype(F32)
-    dy_vec = [jnp.sum(gy * vecs[:, c : c + 1], axis=0, keepdims=True) for c in range(NCONST)]
-    d_gates = []
-    for j in range(TOP):
-        g = jnp.sum(jnp.where(ids[0:8] == s["ks"][j], d_expert, 0.0), axis=0, keepdims=True)
-        g = g + jnp.where(named[j] == NFFN + 1, dy_normed, 0.0)
-        for c in range(NCONST):
-            dy_const = mixing[c][0] * dy_normed + mixing[c][1] * dy_vec[c]
-            g = g + jnp.where(named[j] == NFFN + 2 + c, dy_const, 0.0)
-        d_gates.append(g)
-    inner = gates[0] * d_gates[0] + gates[1] * d_gates[1]
-    d_chosen = [gates[j] * (d_gates[j] - inner) for j in range(TOP)]
-    d_logits = sum(jnp.where(ids == named[j], d_chosen[j], 0.0) for j in range(TOP))
-    gprev_ref[...] = d_logits
-    coefs = []
-    direct = s["copy_w"]
-    for c in range(NCONST):
-        w, (m0, m1) = s["const_w"][c], mixing[c]
-        d0, d1 = w * dy_normed, w * dy_vec[c]
-        mid = m0 * d0 + m1 * d1
-        d_logits = d_logits + jnp.where(ids == NEXP + 2 * c, m0 * (d0 - mid), 0.0)
-        d_logits = d_logits + jnp.where(ids == NEXP + 2 * c + 1, m1 * (d1 - mid), 0.0)
-        direct = direct + w * m0
-        coefs.append(w * m1)
-    d_logits_b = d_logits.astype(BF)
-    d_normed = back[0:768] + direct * gy + mm(gate[...], d_logits_b)
-    u = gain[...] * d_normed
-    mean = jnp.mean(u * hidden, axis=0, keepdims=True)
-    d_hidden = gy + inverse * u - hidden * (inverse * inverse * inverse * mean)
-    dt_ref[...] = d_hidden.astype(BF)
-    lane = lax.broadcasted_iota(jnp.int32, (width, 128), 1)
-    g_gate = mm_nt(s["normed_b"], jnp.concatenate([d_logits_b] + [jnp.zeros_like(d_logits_b)] * 7, axis=0))
-    g_gain = jnp.sum(d_normed * hidden * inverse, axis=1, keepdims=True)
-    small = jnp.where(lane < 16, g_gate, 0.0)
-    for c in range(NCONST):
-        g_const = jnp.sum(gy * coefs[c], axis=1, keepdims=True)
-        small = jnp.where(lane == 16 + c, g_const, small)
-    small = jnp.where(lane == 18, g_gain, small)
-    small_ref[...] = small
-
-
-def layer_kernel(sc, hidden_ref, gain, gate_t, prev, routes, const, hot, *refs):
-    rs, out_ref = refs[:8], refs[8]
-    hidden = hidden_ref[...]
-    s = row_state(sc[0], hidden, gain[...], gate_t[...], prev[...], routes[...])
-    r = jnp.concatenate([v[...] for v in rs], axis=1)
-    total = hidden + mm(r, hot[...])
+    gain, gate_t = small[:, 17:18].astype(F32), small_t[0:16].astype(BF)
+    s = row_state(hidden, gain, gate_t, prev[...], routes[...], sc[3], sc[2])
+    total = hidden
+    for k in range(8):
+        total = total + mm(rin[k], hot[k * CAPACITY : (k + 1) * CAPACITY, :])
     weight = s["copy_w"]
-    vecs = const[...].astype(F32)
+    vecs = small[:, 18:20].astype(F32)
     for c in range(NCONST):
         weight = weight + s["const_w"][c] * s["mixing"][c][0]
         total = total + (s["const_w"][c] * s["mixing"][c][1]) * vecs[:, c : c + 1]
     total = total + weight * s["normed"]
     out_ref[...] = total.astype(BF).T
-
-
-def dmixed_kernel(sc, own, other, wo, o0, o1, o2, o3, st):
-    z, x = sc[1], sc[2]
-    for r, d_ref in enumerate((own, other)):
-        s = jnp.bitwise_xor(x, r)
-        dm = mm_tn(wo[...], d_ref[...]).astype(BF)
-        for half in range(2):
-            st[jnp.bitwise_xor(z, 2 * s + half)] = dm[half * 192 : (half + 1) * 192]
-    for d, o in enumerate((o0, o1, o2, o3)):
-        o[...] = st[d]
 
 
 def outgrad_kernel(sc, own, other, mixed, small, o_ref, dh_ref):
@@ -950,12 +814,13 @@
     dh_ref[1 - x] = other[...].T
 
 
-def attn_back_kernel(sc, b0, b1, b2, b3, m_ref, g0, g1, g2, g3, o0, o1, o2, o3,
+def attn_back_kernel(sc, blocks, m_ref, dm, o0, o1, o2, o3,
                      q_s, k_s, v_s, g_s, dq_s, dk_s, dv_s, st):
     z, prefix = sc[1], sc[4]
-    unpack_qkv(z, (b0, b1, b2, b3), q_s, k_s, v_s)
+    unpack_qkv(z, blocks, q_s, k_s, v_s)
     h = HEAD_DIM
-    for d, g in enumerate((g0, g1, g2, g3)):
+    for d in range(4):
+        g = dm.at[d]
         base = pl.multiple_of(jnp.bitwise_xor(z, d) * 512, 512)
         for j in range(3):
             g_s[j, :, pl.ds(base, 512)] = g[j * h : (j + 1) * h, :]
@@ -1047,6 +912,346 @@
         o_ref[s] = dh[s].astype(F32) + inverse * u - v * (inverse * inverse * inverse * mean)
 
 
+def flip4(v, k):
+    return (v, v + 1 - 2 * (v % 2), (v + 2) % 4, 3 - v)[k]
+
+
+def flip2(v, k):
+    return 1 - v if k else v
+
+
+def bit_flip(v, b):
+    return v + b - 2 * v * b
+
+
+def here():
+    return lax.axis_index("fsdp"), lax.axis_index("ctx"), lax.axis_index("tp")
+
+
+def place_of(z, s, half):
+    return 2 * bit_flip(z // 2, s) + bit_flip(z % 2, half)
+
+
+def greet():
+    f, z, x = here()
+    barrier = pltpu.get_barrier_semaphore()
+    for k in range(1, 8):
+        pl.semaphore_signal(
+            barrier, inc=1, device_id=(flip4(f, k // 2), z, flip2(x, k % 2)), device_id_type=MESH
+        )
+    for d in range(1, 4):
+        pl.semaphore_signal(barrier, inc=1, device_id=(f, flip4(z, d), x), device_id_type=MESH)
+    pl.semaphore_wait(barrier, 10)
+
+
+def greet_plane():
+    f, z, x = here()
+    barrier = pltpu.get_barrier_semaphore()
+    for k in range(1, 8):
+        pl.semaphore_signal(
+            barrier, inc=1, device_id=(flip4(f, k // 2), z, flip2(x, k % 2)), device_id_type=MESH
+        )
+    pl.semaphore_wait(barrier, 7)
+
+
+def to_plane(k, src, dst, sems, at=None):
+    f, z, x = here()
+    at = k if at is None else at
+    return pltpu.make_async_remote_copy(
+        src_ref=src, dst_ref=dst, send_sem=sems.at[0, at], recv_sem=sems.at[1, at],
+        device_id=(flip4(f, k // 2), z, flip2(x, k % 2)), device_id_type=MESH,
+    )
+
+
+def to_column(d, src, dst, sems):
+    f, z, x = here()
+    return pltpu.make_async_remote_copy(
+        src_ref=src, dst_ref=dst, send_sem=sems.at[0, d], recv_sem=sems.at[1, d],
+        device_id=(f, flip4(z, d), x), device_id_type=MESH,
+    )
+
+
+def expert_flip(named, f, x):
+    me = 2 * f + x
+    return jnp.where(named < NFFN, jnp.bitwise_xor(named, me), named)
+
+
+def gather_kernel(pack, smallp, routes, gy, gu, dw,
+                  hot, gyt, gin, w_out, wo_out, small_out, small_t, m0, m1, m2, m3,
+                  packs, smalls, gsend, pack_sems, small_sems, g_sems, w_sems, own_sems):
+    f, z, x = here()
+    barrier = pltpu.get_barrier_semaphore()
+    for k in range(1, 8):
+        pl.semaphore_signal(
+            barrier, inc=1, device_id=(flip4(f, k // 2), z, flip2(x, k % 2)), device_id_type=MESH
+        )
+    pl.semaphore_wait(barrier, 7)
+    pack_copies = [None] + [to_plane(2 * j, pack, packs.at[j], pack_sems) for j in (1, 2)]
+    small_copies = [None] + [to_plane(2 * j, smallp, smalls.at[j], small_sems) for j in (1, 2)]
+    for j in (2, 1):
+        small_copies[j].start()
+        pack_copies[j].start()
+    moves = []
+    for j, m in enumerate((m0, m1, m2, m3)):
+        for cc in range(2):
+            owner = flip4(flip4(f, 2 * (j // 2)), cc)
+            e = 2 * owner + flip2(x, j % 2)
+            for part in range(2):
+                src = gu.at[e] if part == 0 else dw.at[e]
+                dst = m.at[cc, pl.ds(0, 2)] if part == 0 else m.at[cc, pl.ds(2, 1)]
+                at = 2 * j + part
+                if cc:
+                    moves.append(to_plane(2, src, dst, w_sems, at))
+                else:
+                    moves.append(pltpu.make_async_copy(src, dst, own_sems.at[at]))
+    for c in moves:
+        c.start()
+
+    rows = gy.shape[0]
+    named = expert_flip(routes[...], f, x)
+    first, second = named[0:1], named[1:2]
+    g_t = gy[...].T
+    gyt[...] = g_t
+    ids = lax.broadcasted_iota(jnp.int32, (16, rows), 0)
+    hits = ((ids == first) | (ids == second)).astype(F32)
+    before = lax.broadcasted_iota(jnp.int32, (rows, rows), 0)
+    after = lax.broadcasted_iota(jnp.int32, (rows, rows), 1)
+    upper = (before <= after).astype(F32).astype(BF)
+    places = mm(hits.astype(BF), upper) - 1.0
+    slots = lax.broadcasted_iota(jnp.int32, (CAPACITY, rows), 0).astype(F32)
+    for k in range(NFFN):
+        one = jnp.where((slots == places[k : k + 1]) & (hits[k : k + 1] > 0.5), 1.0, 0.0)
+        one = one.astype(BF)
+        hot[k * CAPACITY : (k + 1) * CAPACITY, :] = one
+        block = mm_nt(g_t, one).astype(BF)
+        if k == 0:
+            gin[0] = block
+        else:
+            gsend[k] = block
+    g_copies = [to_plane(k, gsend.at[k], gin.at[k], g_sems) for k in (5, 7, 4, 6, 1, 3, 2)]
+
+    def assemble(j, pack_ref, small_ref):
+        at = pl.ds(pl.multiple_of(flip4(f, j) * 192, 64), 192)
+        for c in range(3):
+            w_out[c, at, :] = pack_ref[c * 192 : (c + 1) * 192, :]
+        wo_out[at, :] = pack_ref[576:768, :]
+        small_out[at, :] = small_ref[...]
+
+    assemble(0, pack, smallp)
+    small_copies[2].wait_recv()
+    pack_copies[2].wait_recv()
+    small_copies.append(to_plane(2, smalls.at[2], smalls.at[3], small_sems, 3))
+    pack_copies.append(to_plane(2, packs.at[2], packs.at[3], pack_sems, 3))
+    small_copies[3].start()
+    pack_copies[3].start()
+    for c in g_copies:
+        c.start()
+    assemble(2, packs.at[2], smalls.at[2])
+    small_copies[1].wait_recv()
+    pack_copies[1].wait_recv()
+    assemble(1, packs.at[1], smalls.at[1])
+    small_copies[3].wait_recv()
+    pack_copies[3].wait_recv()
+    assemble(3, packs.at[3], smalls.at[3])
+    small_t[...] = small_out[...].astype(F32).T
+    for c in pack_copies[1:] + small_copies[1:]:
+        c.wait_send()
+    for c in moves + g_copies:
+        c.wait()
+
+
+def project_kernel(tokens, w, small_t, cos_ref, sin_ref, m1, m2, nt, xt, blocks, l1, l2,
+                   n_s, st, z_sems, w_sems):
+    f, z, x = here()
+    barrier = pltpu.get_barrier_semaphore()
+    for d in range(1, 4):
+        pl.semaphore_signal(barrier, inc=1, device_id=(f, flip4(z, d), x), device_id_type=MESH)
+    for k in (1, 4):
+        pl.semaphore_signal(
+            barrier, inc=1, device_id=(flip4(f, k // 2), z, flip2(x, k % 2)), device_id_type=MESH
+        )
+    pl.semaphore_wait(barrier, 5)
+    weights = [to_plane(1, m1, l1, w_sems), to_plane(4, m2, l2, w_sems)]
+    for c in weights:
+        c.start()
+    gain = small_t[16:17]
+    cos = jnp.concatenate([cos_ref[...]] * 3, axis=1)
+    sin = jnp.concatenate([sin_ref[...]] * 3, axis=1)
+    rows = tokens.shape[1]
+    half_rows = rows // 2
+    for s in range(2):
+        v = tokens[s].astype(F32)
+        inverse = lax.rsqrt(jnp.mean(v * v, axis=-1, keepdims=True) + epsilon)
+        n = (v * inverse * gain).astype(BF)
+        n_s[s] = n
+        q = mm(n, w[0])
+        k = mm(n, w[1])
+        q = (q * cos + swap_halves(q) * sin).astype(BF)
+        k = (k * cos + swap_halves(k) * sin).astype(BF)
+        v = mm(n, w[2]).astype(BF)
+        for half in range(2):
+            d = place_of(z, s, half)
+            for j in range(3):
+                col = (half * 3 + j) * HEAD_DIM
+                parts = [
+                    a[r * half_rows : (r + 1) * half_rows, col : col + HEAD_DIM]
+                    for r in range(2)
+                    for a in (q, k, v)
+                ]
+                st[d, j] = jnp.concatenate(parts, axis=1)
+    z_copies = [to_column(d, st.at[d], blocks.at[d], z_sems) for d in (3, 2, 1)]
+    for c in z_copies:
+        c.start()
+    blocks[0] = st[0]
+    for s in range(2):
+        nt[:, s * rows : (s + 1) * rows] = n_s[s].T
+    xt[...] = tokens[x].T
+    for c in z_copies + weights:
+        c.wait()
+
+
+def route_kernel(land, wo, xt, small, small_t, prev, routes, hot,
+                 mixed, hidden_ref, xin, attn_send, attn_land, xsend, a_sems, x_sems):
+    f, z, x = here()
+    greet_plane()
+    for s in range(2):
+        for half in range(2):
+            mixed[s, half * 192 : (half + 1) * 192, :] = land[place_of(z, s, half)]
+    attn_send[...] = mm(wo[...], mixed[1 - x]).astype(BF)
+    swap = to_plane(1, attn_send, attn_land, a_sems)
+    swap.start()
+    own = mm(wo[...], mixed[x]).astype(BF).astype(F32)
+    own = own + xt[...].astype(F32)
+    swap.wait()
+    hidden = own + attn_land[...].astype(F32)
+    hidden_ref[...] = hidden
+    gain = small[:, 17:18].astype(F32)
+    gate_t = small_t[0:16].astype(BF)
+    s = row_state(hidden, gain, gate_t, prev[...], routes[...], f, x)
+    ids = s["ids"][0:8]
+    gate_rows = sum(jnp.where(ids == k, g, 0.0) for k, g in zip(s["ks"], s["gates"]))
+    high = gate_rows.astype(BF).astype(F32)
+    extra = jnp.concatenate([high, gate_rows - high], axis=0).astype(BF)
+    ext = jnp.concatenate([s["normed_b"], extra], axis=0)
+    sent = []
+    for k in (5, 7, 4, 6, 1, 3, 2, 0):
+        block = mm_nt(ext, hot[k * CAPACITY : (k + 1) * CAPACITY, :]).astype(BF)
+        if k == 0:
+            xin[0] = block
+        else:
+            xsend[k] = block
+            sent.append(to_plane(k, xsend.at[k], xin.at[k], x_sems))
+            sent[-1].start()
+    for c in sent:
+        c.wait()
+
+
+def return_kernel(ysend, rsend, hidden_ref, small, small_t, prev, routes, gyt, hot, wo,
+                  rin, dt, d_other, gprev_ref, small_ref, dm_in, yin, dm_send,
+                  y_sems, r_sems, t_sems, z_sems):
+    f, z, x = here()
+    greet()
+    ys = [to_plane(k, ysend.at[k], yin.at[k], y_sems) for k in (5, 7, 4, 6, 1, 3, 2)]
+    for c in ys:
+        c.start()
+    yin[0] = ysend[0]
+    rin[0] = rsend[0]
+    hidden = hidden_ref[...]
+    width, rows = hidden.shape
+    gain = small[:, 17:18].astype(F32)
+    gate = small[:, 0:16]
+    gate_t = small_t[0:16].astype(BF)
+    s = row_state(hidden, gain, gate_t, prev[...], routes[...], f, x)
+    ids, named, gates, mixing = s["ids"], s["named"], s["gates"], s["mixing"]
+    normed, inverse = s["normed"], s["inverse"]
+    gy = gyt[...].astype(F32)
+    dy_normed = jnp.sum(gy * normed, axis=0, keepdims=True)
+    vecs = [small[:, 18 + c : 19 + c].astype(F32) for c in range(NCONST)]
+    dy_vec = [jnp.sum(gy * vecs[c], axis=0, keepdims=True) for c in range(NCONST)]
+    for c in ys:
+        c.wait()
+    back = mm(yin[0], hot[0:CAPACITY, :])
+    for k in range(1, 8):
+        back = back + mm(yin[k], hot[k * CAPACITY : (k + 1) * CAPACITY, :])
+    d_expert = back[768:776] + back[776:784]
+    d_gates = []
+    for j in range(TOP):
+        g = jnp.sum(jnp.where(ids[0:8] == s["ks"][j], d_expert, 0.0), axis=0, keepdims=True)
+        g = g + jnp.where(named[j] == NFFN + 1, dy_normed, 0.0)
+        for c in range(NCONST):
+            dy_const = mixing[c][0] * dy_normed + mixing[c][1] * dy_vec[c]
+            g = g + jnp.where(named[j] == NFFN + 2 + c, dy_const, 0.0)
+        d_gates.append(g)
+    inner = gates[0] * d_gates[0] + gates[1] * d_gates[1]
+    d_chosen = [gates[j] * (d_gates[j] - inner) for j in range(TOP)]
+    d_logits = sum(jnp.where(ids == named[j], d_chosen[j], 0.0) for j in range(TOP))
+    gprev_ref[...] = d_logits
+    coefs = []
+    direct = s["copy_w"]
+    for c in range(NCONST):
+        w, (m0, m1) = s["const_w"][c], mixing[c]
+        d0, d1 = w * dy_normed, w * dy_vec[c]
+        mid = m0 * d0 + m1 * d1
+        d_logits = d_logits + jnp.where(ids == NEXP + 2 * c, m0 * (d0 - mid), 0.0)
+        d_logits = d_logits + jnp.where(ids == NEXP + 2 * c + 1, m1 * (d1 - mid), 0.0)
+        direct = direct + w * m0
+        coefs.append(w * m1)
+    d_logits_b = d_logits.astype(BF)
+    d_normed = back[0:768] + direct * gy + mm(gate, d_logits_b)
+    u = gain * d_normed
+    mean = jnp.mean(u * hidden, axis=0, keepdims=True)
+    d_hidden = gy + inverse * u - hidden * (inverse * inverse * inverse * mean)
+    dt[...] = d_hidden.astype(BF)
+    swap = to_plane(1, dt, d_other, t_sems)
+    swap.start()
+    for half in range(2):
+        dm = mm_tn(wo[:, half * 192 : (half + 1) * 192], dt[...])
+        dm_send[place_of(z, x, half)] = dm.astype(BF)
+    lane = lax.broadcasted_iota(jnp.int32, (width, 128), 1)
+    padded = jnp.concatenate([d_logits, jnp.zeros((112, rows), F32)], axis=0).astype(BF)
+    g_gate = mm_nt(s["normed_b"], padded)
+    g_gain = jnp.sum(d_normed * hidden * inverse, axis=1, keepdims=True)
+    total = jnp.where(lane < 16, g_gate, 0.0)
+    for c in range(NCONST):
+        g_const = jnp.sum(gy * coefs[c], axis=1, keepdims=True)
+        total = jnp.where(lane == 16 + c, g_const, total)
+    small_ref[...] = jnp.where(lane == 18, g_gain, total)
+    swap.wait()
+    rs = [to_plane(k, rsend.at[k], rin.at[k], r_sems) for k in range(1, 8)]
+    for c in rs:
+        c.start()
+    for half in range(2):
+        dm = mm_tn(wo[:, half * 192 : (half + 1) * 192], d_other[...])
+        dm_send[place_of(z, 1 - x, half)] = dm.astype(BF)
+    zs = [to_column(d, dm_send.at[d], dm_in.at[d], z_sems) for d in (1, 2, 3)]
+    for c in zs:
+        c.start()
+    dm_in[0] = dm_send[0]
+    for c in zs + rs:
+        c.wait()
+
+
+def run_remote(body, name, number, ins, outs, scratch, vmem=56, hbm_ins=(), hbm_outs=(), smem_ins=()):
+    return pl.pallas_call(
+        body,
+        out_shape=tuple(outs),
+        in_specs=[
+            HBM if i in hbm_ins else SCALARS if i in smem_ins else WHOLE for i in range(len(ins))
+        ],
+        out_specs=tuple(HBM if i in hbm_outs else WHOLE for i in range(len(outs))),
+        scratch_shapes=list(scratch),
+        compiler_params=pltpu.CompilerParams(
+            vmem_limit_bytes=vmem * MIB, collective_id=number, has_side_effects=True
+        ),
+        cost_estimate=COST,
+        name=name,
+    )(*ins)
+
+
+def sems(n):
+    return pltpu.SemaphoreType.DMA((2, n))
+
+
 def fast(
     tokens, prev_logits, routes, prefix, norm_gains, query_key_value_weight,
     output_projection_weight, router_gate_weight, const_vec, gate_up, down_weight, cotangent,
@@ -1072,27 +1277,9 @@
     pack = jnp.concatenate(
         [query_key_value_weight.reshape(3 * 192, head_cols), output_projection_weight], axis=0
     )
-    pack2 = flip_fsdp(pack, 2)
-    pack1 = flip_fsdp(pack, 1)
-    pack3 = flip_fsdp(pack2, 1)
-    small = lax.all_gather(
-        jnp.concatenate([router_gate_weight, norm_gains.T, const_vec.T], axis=1), "fsdp", axis=0, tiled=True
-    )
-    gate = small[:, 0:16]
-    gate_t = gate.T
-    gain_one_row = small[:, 16:17].T.astype(F32)
-    gain_two = small[:, 17:18].astype(F32)
-    const = small[:, 18:20]
-
-    down4 = down_weight[:, None]
-    weight_blocks = []
-    for k in range(8):
-        e = jnp.bitwise_xor(me, k)
-        block = jnp.concatenate(
-            [lax.dynamic_index_in_dim(gate_up, e, 0, False), lax.dynamic_index_in_dim(down4, e, 0, False)], axis=0
-        )
-        weight_blocks.append(block)
-
+    small_own = jnp.pad(
+        jnp.concatenate([router_gate_weight, norm_gains.T, const_vec.T], axis=1), ((0, 0), (0, 108))
+    )
     own_routes = lax.dynamic_index_in_dim(routes, x, 0, False).T
     own_prev = jnp.pad(lax.dynamic_index_in_dim(prev_logits, x, 0, False).T, ((0, 4), (0, 0)))
     own_gy = lax.dynamic_index_in_dim(cotangent, x, 0, False)
@@ -1105,85 +1292,72 @@
     cos = jnp.concatenate([cosine] * 4, axis=1)
     sin = jnp.concatenate([-sine, sine] * 2, axis=1)
 
-    packed = run(
-        pack_kernel, "pack_cotangent", scalars, [own_routes, own_gy],
-        [out((8 * CAPACITY, rows)), out((width, rows))] + [out((width, CAPACITY))] * 8,
-    )
-    hot, gyt, g_blocks = packed[0], packed[1], packed[2:]
-    normed_one, normed_one_t, xt = run(
-        norm_kernel, "norm_one", scalars, [tokens, gain_one_row],
-        [out((2, rows, width)), out((width, 2 * rows)), out((width, rows))],
-    )
-
-    qkv_out = run(
-        qkv_kernel, "qkv", scalars, [normed_one, pack, pack1, pack2, pack3, cos, sin],
-        [out((3, rows // 2, head_cols))] * 4 + [out((3, width, head_cols)), out((width, head_cols))],
-        scratch=[pltpu.VMEM((4, 3, rows // 2, head_cols), BF)], flops=2 * 1024 * 768 * 1152,
-    )
-    blocks, w_full, wo_full = qkv_out[:4], qkv_out[4], qkv_out[5]
-    blocks = [blocks[0]] + [flip_ctx(blocks[d], d) for d in (1, 2, 3)]
-
-    weights_in = [weight_blocks[0]] + [flip_plane(weight_blocks[k], k) for k in range(1, 8)]
-    g_in = [g_blocks[0]] + [flip_plane(g_blocks[k], k) for k in range(1, 8)]
-
+    vm = pltpu.VMEM
+    messages = [out((2, 3, 192, 1024))] * 4
+    hot, gyt, gs, w_full, wo_full, small, small_t, *messages = run_remote(
+        gather_kernel, "gather", 0,
+        [pack, small_own, own_routes, own_gy, gate_up, down_weight[:, None]],
+        [
+            out((8 * CAPACITY, rows)), out((width, rows)), out((8, width, CAPACITY)),
+            out((3, width, head_cols)), out((width, head_cols)), out((width, 128)), out((128, width), F32),
+            *messages,
+        ],
+        [
+            vm((4, 768, head_cols), BF), vm((4, 192, 128), BF), vm((8, width, CAPACITY), BF),
+            sems(8), sems(8), sems(8), sems(8),
+            pltpu.SemaphoreType.DMA((8,)),
+        ],
+        hbm_ins=(4, 5),
+    )
+    normed_one_t, xt, blocks, w1, w2 = run_remote(
+        project_kernel, "project", 3, [tokens, w_full, small_t, cos, sin, messages[1], messages[2]],
+        [
+            out((width, 2 * rows)), out((width, rows)), out((4, 3, rows // 2, head_cols)),
+            out((2, 3, 192, 1024)), out((2, 3, 192, 1024)),
+        ],
+        [vm((2, rows, width), BF), vm((4, 3, rows // 2, head_cols), BF), sems(4), sems(8)],
+        hbm_ins=(5, 6), hbm_outs=(3, 4),
+    )
+    gain_one_row = small_t[16:17]
+
+    gs, blocks = lax.optimization_barrier((gs, blocks))
     length = 4 * rows
     unit_scratch = [pltpu.VMEM((3, length, HEAD_DIM), BF)] * 3
-    attn = run(
-        attn_kernel, "attention", scalars, list(blocks),
-        [out((192, rows))] * 4 + [out((3, HEAD_DIM + 8, length), F32)],
-        scratch=unit_scratch + [pltpu.VMEM((4, 192, rows), BF)], flops=3 * 11 * 512 * 512 * 64 * 4,
-    )
-    mixed_blocks, mixed_lse = attn[:4], attn[4]
-    mixed_in = [mixed_blocks[0]] + [flip_ctx(mixed_blocks[d], d) for d in (1, 2, 3)]
-
+    mixed_in, mixed_lse, w3 = run_remote(
+        attn_kernel, "attention", 4, [scalars[4:5], blocks, messages[3]],
+        [out((4, 192, rows)), out((3, HEAD_DIM + 8, length), F32), out((2, 3, 192, 1024))],
+        unit_scratch + [vm((4, 192, rows), BF), sems(4), sems(8)],
+        hbm_ins=(2,), hbm_outs=(2,), smem_ins=(0,),
+    )
     w_exp, wt_exp = run(
-        wprep_kernel, "expert_weights", scalars, weights_in,
+        wprep_kernel, "expert_weights", scalars, [messages[0], w1, w2, w3],
         [out((3, width, 2048)), out((3, 2048, width))],
     )
-    gs = jnp.stack(g_in)
-    g_more = [flip_ctx(gs, d) for d in (1, 2, 3)]
-
-    mixed, attn_own, attn_send = run(
-        outproj_kernel, "out_projection", scalars, [*mixed_in, wo_full],
-        [out((2, head_cols, rows)), out((width, rows)), out((width, rows))],
-        scratch=[pltpu.VMEM((4, 192, rows), BF)], flops=2 * 1024 * 768 * 384,
-    )
-    attn_recv = flip_tp(attn_send)
-
-    routed = run(
-        router_kernel, "router", scalars,
-        [xt, attn_own, attn_recv, gain_two, gate_t, own_prev, own_routes, hot],
-        [out((width, rows), F32)] + [out((width + 16, CAPACITY))] * 8, flops=2 * 512 * 1024 * 784,
-    )
-    hidden, x_blocks = routed[0], routed[1:]
-    xs = jnp.stack([x_blocks[0]] + [flip_plane(x_blocks[k], k) for k in range(1, 8)])
-    x_more = [flip_ctx(xs, d) for d in (1, 2, 3)]
-
-    def plane(d):
-        return jnp.stack([jnp.bitwise_xor(z, d), me]).astype(jnp.int32)
-
-    done = expert_call(True, plane(0), xs, gs, w_exp, wt_exp, None)
-    y_blocks, r_blocks, held = done[:8], done[8:16], done[16:]
-    y_in = [y_blocks[0]] + [flip_plane(y_blocks[k], k) for k in range(1, 8)]
-    r_in = [r_blocks[0]] + [flip_plane(r_blocks[k], k) for k in range(1, 8)]
-
-    d_t, grad_prev_t, small_grads = run(
-        combine_kernel, "combine", scalars,
-        [hidden, gain_two, gate_t, gate, own_prev, own_routes, const, gyt, hot, *y_in],
-        [out((width, rows)), out((16, rows), F32), out((width, 128), F32)], flops=2 * 512 * 1024 * 784,
-    )
-    d_other = flip_tp(d_t)
-    dm_blocks = run(
-        dmixed_kernel, "d_mixed", scalars, [d_t, d_other, wo_full], [out((192, rows))] * 4,
-        scratch=[pltpu.VMEM((4, 192, rows), BF)], flops=2 * 1024 * 768 * 384,
-    )
-    dm_in = [dm_blocks[0]] + [flip_ctx(dm_blocks[d], d) for d in (1, 2, 3)]
-
-    for d in (1, 2, 3):
-        held = expert_call(False, plane(d), x_more[d - 1], g_more[d - 1], w_exp, wt_exp, held)
+    g_all = lax.all_gather(gs, "ctx")
+
+    mixed, hidden, xs = run_remote(
+        route_kernel, "route", 1, [mixed_in, wo_full, xt, small, small_t, own_prev, own_routes, hot],
+        [out((2, head_cols, rows)), out((width, rows), F32), out((8, width + 16, CAPACITY))],
+        [vm((width, rows), BF), vm((width, rows), BF), vm((8, width + 16, CAPACITY), BF), sems(8), sems(8)],
+    )
+    x_all = lax.all_gather(xs, "ctx")
+
+    done = expert_call(True, jnp.stack([z]).astype(jnp.int32), xs[None], gs[None], w_exp, wt_exp, None)
+    ysend, rsend, held = done[0], done[1], done[2:]
+    r_in, d_t, d_other, grad_prev_t, small_grads, dm_in = run_remote(
+        return_kernel, "give_back", 2,
+        [ysend, rsend, hidden, small, small_t, own_prev, own_routes, gyt, hot, wo_full],
+        [
+            out((8, width, CAPACITY)), out((width, rows)), out((width, rows)), out((16, rows), F32),
+            out((width, 128), F32), out((4, 192, rows)),
+        ],
+        [vm((8, width + 16, CAPACITY), BF), vm((4, 192, rows), BF), sems(8), sems(8), sems(8), sems(4)],
+    )
+
+    others = jnp.stack([jnp.bitwise_xor(z, d) for d in (1, 2, 3)]).astype(jnp.int32)
 
     back = run(
-        attn_back_kernel, "attention_backward", scalars, [*blocks, mixed_lse, *dm_in],
+        attn_back_kernel, "attention_backward", scalars, [blocks, mixed_lse, dm_in],
         [out((3, rows // 2, head_cols))] * 4,
         scratch=unit_scratch
         + [pltpu.VMEM((3, HEAD_DIM, length), BF)]
@@ -1192,6 +1366,9 @@
         flops=3 * 11 * 512 * 512 * 64 * 10,
     )
     back_in = [back[0]] + [flip_ctx(back[d], d) for d in (1, 2, 3)]
+    held = expert_call(False, others, x_all, g_all, w_exp, wt_exp, held)
+    *back_in, first = lax.optimization_barrier((*back_in, held[0]))
+    held = [first, *held[1:]]
 
     og, d_hidden = run(
         outgrad_kernel, "out_grads", scalars, [d_t, d_other, mixed, small_grads],
@@ -1200,7 +1377,7 @@
 
     layer_own = run(
         layer_kernel, "layer_out", scalars,
-        [hidden, gain_two, gate_t, own_prev, own_routes, const, hot, *r_in],
+        [hidden, small, small_t, own_prev, own_routes, hot, r_in],
         [out((rows, width))], flops=2 * 512 * 1024 * 768,
     )[0]
 
@@ -1212,12 +1389,13 @@
     grad_prev = both(grad_prev_t[0:NEXP].T)
 
     parts = 4
-    me_scalar = jnp.stack([me]).astype(jnp.int32)
+    spot = jnp.stack([me, f, x]).astype(jnp.int32)
     placed = None
     for part in range(parts):
-        g = grads_call(me_scalar, part, parts, held)
-        g = [g[0]] + [flip_plane(g[k], k) for k in range(1, 8)]
-        placed = place_call(me_scalar, part, parts, g, placed)
+        g = grads_call(spot, part, parts, held)
+        g = [g[0]] + [flip_plane(g[j], 4 * (j // 2) + j % 2) for j in (1, 2, 3)]
+        far = flip_fsdp(jnp.stack([v[1] for v in g]), 1)
+        placed = place_call(spot, part, parts, [*g, far], placed)
     grad_gu, grad_down = placed
 
     def rounded(v):

time: 981 us -> 707 us (0.72)
  waiting for transfers between devices: 414 us -> 63.3 us
  Pallas kernels: 298 us -> 534 us
  starting transfers between devices: 181 us -> 41.2 us
  local copies, waits for them, and re-layouts: 52.4 us -> 27.6 us
  between operations: 1.74 us -> 15 us
    pallas_call x0 -> x5, Pallas kernels: none -> 294 us  [run_remote(): pl.pallas_call(body, out_shape=tuple(outs), in_specs=[HBM if i in hbm_ins...]
    ppermute x22 -> x7, waiting for transfers between devices: 252 us -> 13.1 us  [flip_ctx(): return lax.ppermute(v, 'ctx', [(i, i ^ k) for i in range(4)])]
    ppermute x22 -> x7, starting transfers between devices: 110 us -> 18.5 us  [flip_ctx(): return lax.ppermute(v, 'ctx', [(i, i ^ k) for i in range(4)])]
    ppermute x63 -> x12, waiting for transfers between devices: 133 us -> 50.1 us  [flip_plane(): return lax.ppermute(v, ('fsdp', 'tp'), [(i, i ^ k) for i in range(8)])]
    pallas_call x14 -> x6, Pallas kernels: 123 us -> 70.4 us  [run(): pl.pallas_call(body, out_shape=tuple(outs), in_specs=[SCALARS] + [WHOLE]...]
    ppermute x63 -> x12, starting transfers between devices: 57.1 us -> 14.2 us  [flip_plane(): return lax.ppermute(v, ('fsdp', 'tp'), [(i, i ^ k) for i in range(8)])]
    ppermute x7 -> x5, waiting for transfers between devices: 28.5 us -> 0.01 us  [flip_tp(): return lax.ppermute(v, 'tp', [(0, 1), (1, 0)])]
    unnamed x200 -> x82, local copies, waits for them, and re-layouts: 31.1 us -> 7.45 us
  transfers between devices with their start and end apart: 99 -> 34, of which waited for: 28 -> 5; matrix products, arithmetic and copies ran while one was open for 6% -> 5% of each run, Pallas kernels for 26% -> 61%
where the time goes in v2:
time: 707 us; the launch traced here: 699 us
  Pallas kernels  534 us (76%)
  waiting for transfers between devices  63.3 us (9%)
  starting transfers between devices  41.2 us (6%)
  local copies, waits for them, and re-layouts  27.6 us (4%)
  other arithmetic  18 us (3%)
  between operations  15 us (2%)
    pallas_call x5, Pallas kernels, run_remote(): pl.pallas_call(body, out_shape=tuple(outs), in_specs=[HBM if i in hbm_ins...  294 us
    pallas_call x2, Pallas kernels, expert_call(): pl.pallas_call(functools.partial(expert_body, first), out_shape=tuple(out...  84.6 us
    pallas_call x6, Pallas kernels, run(): pl.pallas_call(body, out_shape=tuple(outs), in_specs=[SCALARS] + [WHOLE]...  70.4 us
    pallas_call x4, Pallas kernels, grads_call(): pl.pallas_call(functools.partial(grads_body, cols), out_shape=tuple([out(...  65.8 us
    ppermute x12, waiting for transfers between devices, flip_plane(): return lax.ppermute(v, ('fsdp', 'tp'), [(i, i ^ k) for i in range(8)])  50.1 us
    pallas_call x4, Pallas kernels, place_call(): pl.pallas_call(functools.partial(place_body, first), out_shape=(out((NFFN...  19.5 us
    ppermute x7, starting transfers between devices, flip_ctx(): return lax.ppermute(v, 'ctx', [(i, i ^ k) for i in range(4)])  18.5 us
    ppermute x12, starting transfers between devices, flip_plane(): return lax.ppermute(v, ('fsdp', 'tp'), [(i, i ^ k) for i in range(8)])  14.2 us
  transfers between devices with their start and end apart: 34, of which 5 were waited for; matrix products, arithmetic and copies ran while one was open for 5% of the time, Pallas kernels for 61%

profile of v2, /device:TPU:0, one launch (start us, length us, event | category | flops | bytes accessed | tf_op | source)
XLA Modules:
  0.0 699.4 jit_solution(7528740018311728330)
XLA Ops:
  8.3 1.3 dynamic-slice_bitcast_fusion.4.routes
  13.0 1.3 pad_maximum_fusion.5
  14.3 45.3 %gather.1 = (bf16[1024,512]{1,0:T(8,128)(2,1)}, bf16[768,512]{1,0:T(8,128)(2,1)}, bf16[8,768,128]{2,1,0:T(8,128)(2,1)}, bf16[3,768,384]{2,1,0:T(8,128)(2,1)}, bf...) custom-call(bf16[768,384]{1,0:T(8,128)(2,1)} %pad_maximum_fusion.4.p, ...), custom_call_target="tpu_custom_call" | custom-call | flops 1024 | bytes 1024 | tf_op jit(solution)/shard_map/gather/pallas_call | solution.py:1235
  59.6 64.0 %project.1 = (bf16[768,1024]{1,0:T(8,128)(2,1)}, bf16[768,512]{1,0:T(8,128)(2,1)}, bf16[4,3,256,384]{3,2,1,0:T(8,128)(2,1)}, bf16[2,3,192,1024]{3,2,1,0:T(8,128)(2,1)}, bf16[2,3,192,1024]{3,2,1,0:T(8,128)(2,1)}) custom-call(bf16[2,512,768]{2,1,0:T(8,128)(2,1)} %tokens.5, bf16[3,768,384]{2,1,0:T(8,128)(2,1)} %get-tuple-element.92.w, ...), custom_call_target="tpu_custom_call" | custom-call | flops 1024 | bytes 1024 | tf_op jit(solution)/shard_map/project/pallas_call | solution.py:1235
  124.9 59.7 %attention.1 = (bf16[4,192,512]{2,1,0:T(8,128)(2,1)}, f32[3,72,2048]{2,1,0:T(8,128)}, bf16[2,3,192,1024]{3,2,1,0:T(8,128)(2,1)}) custom-call(s32[1]{0:T(128)} %dynamic_slice.43.prefix_ref, bf16[4,3,256,384]{3,2,1,0:T(8,128)(2,1)} %get-tuple-element.97.blocks, bf16[2,3,192,1024]{3,2,1,0:T(8,128)(2,1)} %get-tuple-element.98.m3), custom_call_target="tpu_custom_call" | custom-call | flops 1024 | bytes 1024 | tf_op jit(solution)/shard_map/attention/pallas_call | solution.py:1235
  185.3 46.0 %route.1 = (bf16[2,384,512]{2,1,0:T(8,128)(2,1)}, f32[768,512]{1,0:T(8,128)}, bf16[8,784,128]{2,1,0:T(8,128)(2,1)}) custom-call(bf16[4,192,512]{2,1,0:T(8,128)(2,1)} %get-tuple-element.99.land, bf16[768,384]{1,0:T(8,128)(2,1)} %get-tuple-element.100.wo, bf16[768,512]{1,0:T(8,128)(2,1)} %get-tuple-element.101.xt, bf16[768,128]{1,0:T(8,128)(2,1)} %get-tuple-element.102.small, ...), custom_call_target="tpu_custom_call" | custom-call | flops 1024 | bytes 1024 | tf_op jit(solution)/shard_map/route/pallas_call | solution.py:1235
  231.4 1.3 stack.81.sc
  232.7 13.6 %expert_weights.1 = (bf16[3,768,2048]{2,1,0:T(8,128)(2,1)}, bf16[3,2048,768]{2,1,0:T(8,128)(2,1)}) custom-call(s32[5]{0:T(128)} %stack.81.sc, bf16[2,3,192,1024]{3,2,1,0:T(8,128)(2,1)} %get-tuple-element.107.b0, bf16[2,3,192,1024]{3,2,1,0:T(8,128)(2,1)} %get-tuple-element.108.b1, bf16[2,3,192,1024]{3,2,1,0:T(8,128)(2,1)} %get-tuple-element.109.b2, ...), custom_call_target="tpu_custom_call" | custom-call | flops 1024 | bytes 1024 | tf_op jit(solution)/shard_map/expert_weights/pallas_call | solution.py:450
  246.3 33.4 %experts_own.1 = (bf16[8,784,128]{2,1,0:T(8,128)(2,1)}, bf16[8,768,128]{2,1,0:T(8,128)(2,1)}, bf16[4,768,1024]{2,1,0:T(8,128)(2,1)}, bf16[4,768,1024]{2,1,0:T(8,...) custom-call(s32[1]{0:T(128)} %bitcast.1.sc, ...), custom_call_target="tpu_custom_call" | custom-call | flops 1024 | bytes 1024 | tf_op jit(solution)/shard_map/experts_own/pallas_call | solution.py:690
  279.8 79.0 %give_back.1 = (bf16[8,768,128]{2,1,0:T(8,128)(2,1)}, bf16[768,512]{1,0:T(8,128)(2,1)}, bf16[768,512]{1,0:T(8,128)(2,1)}, f32[16,512]{1,0:T(8,128)}, f32[768,128]{1,0:T(8,128)}, /*index=5*/bf16[4,192,512]{2,1,0:T(8,128)(2,1)}) custom-call(bf16[8,784,128]{2,1,0:T(8,128)(2,1)} %get-tuple-element.113.ysend, bf16[8,768,128]{2,1,0:T(8,128)(2,1)} %get-tuple-element.114.rsend, ...), custom_call_target="tpu_custom_call" | custom-call | flops 1024 | bytes 1024 | tf_op jit(solution)/shard_map/give_back/pallas_call | solution.py:1235
  358.8 4.1 out_grads.1
  364.4 30.4 %attention_backward.1 = (bf16[3,256,384]{2,1,0:T(8,128)(2,1)}, bf16[3,256,384]{2,1,0:T(8,128)(2,1)}, bf16[3,256,384]{2,1,0:T(8,128)(2,1)}, bf16[3,256,384]{2,1,0:T(8,128)(2,1)}) custom-call(s32[5]{0:T(128)} %stack.81.sc, bf16[4,3,256,384]{3,2,1,0:T(8,128)(2,1)} %get-tuple-element.97.blocks, f32[3,72,2048]{2,1,0:T(8,128)} %get-tuple-element.122.m_ref, ...), custom_call_target="tpu_custom_call" | custom-call | flops 1024 | bytes 1024 | tf_op jit(solution)/shard_map/attention_backward/pallas_call | solution.py:450
  394.8 11.3 %collective-permute-start.1 = (bf16[3,256,384]{2,1,0:T(8,128)(2,1)}, bf16[3,256,384]{2,1,0:T(8,128)(2,1)S(1)}, u32[]{:S(2)}, u32[]{:S(2)}) collective-permute-start(bf16[3,256,384]{2,1,0:T(8,128)(2,1)} %get-tuple-element.125), channel_id=1, source_target_pairs={{0,2},{2,0},{4,6},{6,4},{1,3},{3,1},{5,7},{7,5},{8,10},{10,8},{12,... | collective-permute-start | bytes 1769480 | tf_op jit(solution)/shard_map/ppermute | solution.py:1272
  406.1 2.4 collective-permute-start.3
  408.9 1.5 collective-permute-start.12
  410.4 5.9 layer_out.1
  416.3 1.3 collective-permute-start
  419.5 51.2 %experts_more.1 = (bf16[4,768,1024]{2,1,0:T(8,128)(2,1)}, bf16[4,768,1024]{2,1,0:T(8,128)(2,1)}, bf16[4,2048,1024]{2,1,0:T(8,128)(2,1)}, bf16[4,2048,1024]{2,1,0:T(8,128)(2,1)}, bf16[4,2048,1024]{2,1,0:T(8,128)(2,1)}) custom-call(s32[3]{0:T(128)} %pad_add_fusion.sc, ...), custom_call_target="tpu_custom_call", output_to_operand_aliasing={{0}: (5, {}), {1}: (6, {}), {2}: (7, {}), {3}: (8, {}), {4}... | custom-call | flops 1024 | bytes 1024 | tf_op jit(solution)/shard_map/experts_more/pallas_call | solution.py:690
  471.7 10.3 %d_projection.1 = (bf16[2,512,768]{2,1,0:T(8,128)(2,1)}, bf16[4,592,384]{2,1,0:T(8,128)(2,1)}) custom-call(s32[5]{0:T(128)} %stack.81.sc, bf16[3,256,384]{2,1,0:T(8,128)(2,1)} %get-tuple-element.134.b0, bf16[3,256,384]{2,1,0:T(8,128)(2,1)} %copy-done.29, bf16[3,256,384]{2,1,0:T(8,128)(2,1)} %copy-done.30, bf16[3,256,384]{2,1,0:T(8,128)(2,1)} %collective-permute-done.3.b3, ...), custom_call_target="tpu_custom_call" | custom-call | flops 1024 | bytes 1024 | tf_op jit(solution)/shard_map/d_projection/pallas_call | solution.py:450
  482.1 2.2 dynamic-slice_bitcast_fusion
  485.7 16.2 %expert_grads.7 = (bf16[2,3,192,256]{3,2,1,0:T(8,128)(2,1)}, bf16[2,3,192,256]{3,2,1,0:T(8,128)(2,1)}, bf16[2,3,192,256]{3,2,1,0:T(8,128)(2,1)}, bf16[2,3,192,256]{3,2,1,0:T(8,128)(2,1)}) custom-call(s32[3]{0:T(128)} %pad_add_fusion.1.sc, bf16[4,768,1024]{2,1,0:T(8,128)(2,1)} %get-tuple-element.143.bx, bf16[4,768,1024]{2,1,0:T(8,128)(2,1)} %get-tuple-element.144.bg, ...), custom_call_target="tpu_custom_call" | custom-call | flops 1024 | bytes 1024 | tf_op jit(solution)/shard_map/expert_grads/pallas_call | solution.py:736
  501.9 1.3 collective-permute-start.28
  503.9 1.5 collective-permute-start.30
  506.5 16.7 %expert_grads.6 = (bf16[2,3,192,256]{3,2,1,0:T(8,128)(2,1)}, bf16[2,3,192,256]{3,2,1,0:T(8,128)(2,1)}, bf16[2,3,192,256]{3,2,1,0:T(8,128)(2,1)}, bf16[2,3,192,256]{3,2,1,0:T(8,128)(2,1)}) custom-call(s32[3]{0:T(128)} %pad_add_fusion.1.sc, bf16[4,768,1024]{2,1,0:T(8,128)(2,1)} %get-tuple-element.143.bx, bf16[4,768,1024]{2,1,0:T(8,128)(2,1)} %get-tuple-element.144.bg, ...), custom_call_target="tpu_custom_call" | custom-call | flops 1024 | bytes 1024 | tf_op jit(solution)/shard_map/expert_grads/pallas_call | solution.py:736
  523.2 1.3 collective-permute-start.24
  525.3 16.3 %expert_grads.5 = (bf16[2,3,192,256]{3,2,1,0:T(8,128)(2,1)}, bf16[2,3,192,256]{3,2,1,0:T(8,128)(2,1)}, bf16[2,3,192,256]{3,2,1,0:T(8,128)(2,1)}, bf16[2,3,192,256]{3,2,1,0:T(8,128)(2,1)}) custom-call(s32[3]{0:T(128)} %pad_add_fusion.1.sc, bf16[4,768,1024]{2,1,0:T(8,128)(2,1)} %get-tuple-element.143.bx, bf16[4,768,1024]{2,1,0:T(8,128)(2,1)} %get-tuple-element.144.bg, ...), custom_call_target="tpu_custom_call" | custom-call | flops 1024 | bytes 1024 | tf_op jit(solution)/shard_map/expert_grads/pallas_call | solution.py:736
  541.6 1.6 collective-permute-start.26
  544.0 1.3 collective-permute-start.20
  546.9 1.4 fusion.1
  549.4 1.3 collective-permute-start.7
  550.7 1.3 slice.75.gain
  553.5 5.6 collective-permute-done.26.refs_3_
  559.1 1.5 collective-permute-start.22
  560.6 3.3 maximum_select_fusion
  563.9 16.6 %expert_grads.4 = (bf16[2,3,192,256]{3,2,1,0:T(8,128)(2,1)}, bf16[2,3,192,256]{3,2,1,0:T(8,128)(2,1)}, bf16[2,3,192,256]{3,2,1,0:T(8,128)(2,1)}, bf16[2,3,192,256]{3,2,1,0:T(8,128)(2,1)}) custom-call(s32[3]{0:T(128)} %pad_add_fusion.1.sc, bf16[4,768,1024]{2,1,0:T(8,128)(2,1)} %get-tuple-element.143.bx, bf16[4,768,1024]{2,1,0:T(8,128)(2,1)} %get-tuple-element.144.bg, ...), custom_call_target="tpu_custom_call" | custom-call | flops 1024 | bytes 1024 | tf_op jit(solution)/shard_map/expert_grads/pallas_call | solution.py:736
  580.5 1.3 collective-permute-start.16
  582.6 1.5 collective-permute-start.18
  585.8 1.9 copy.64
  591.1 27.1 %collective-permute-done.22.refs_3_ = bf16[2,3,192,256]{3,2,1,0:T(8,128)(2,1)} collective-permute-done((bf16[2,3,192,256]{3,2,1,0:T(8,128)(2,1)}, bf16[2,3,192,256]{3,2,1,0:T(8,128)(2,1)}, u32[]{:S(2)}, u32[]{:S(2)}) %collective-permute-start.22) | collective-permute-done | bytes 589856 | tf_op jit(solution)/shard_map/ppermute | solution.py:1275
  621.0 9.7 %collective-permute-done.16.refs_1_ = bf16[2,3,192,256]{3,2,1,0:T(8,128)(2,1)} collective-permute-done((bf16[2,3,192,256]{3,2,1,0:T(8,128)(2,1)}, bf16[2,3,192,256]{3,2,1,0:T(8,128)(2,1)}, u32[]{:S(2)}, u32[]{:S(2)}) %collective-permute-start.16) | collective-permute-done | bytes 589856 | tf_op jit(solution)/shard_map/ppermute | solution.py:1275
  634.8 7.7 %collective-permute-done.18.refs_3_ = bf16[2,3,192,256]{3,2,1,0:T(8,128)(2,1)} collective-permute-done((bf16[2,3,192,256]{3,2,1,0:T(8,128)(2,1)}, bf16[2,3,192,256]{3,2,1,0:T(8,128)(2,1)}, u32[]{:S(2)}, u32[]{:S(2)}) %collective-permute-start.18) | collective-permute-done | bytes 589856 | tf_op jit(solution)/shard_map/ppermute | solution.py:1275
  646.7 2.2 collective-permute-start.9
  650.9 6.1 grad_tokens.1
  657.0 13.1 %collective-permute-done.9 = bf16[592,384]{1,0:T(8,128)(2,1)S(1)} collective-permute-done((bf16[592,384]{1,0:T(8,128)(2,1)S(1)}, bf16[592,384]{1,0:T(8,128)(2,1)S(1)}, u32[]{:S(2)}, u32[]{:S(2)}) %collective-permute-start.9) | collective-permute-done | bytes 454688 | tf_op jit(solution)/shard_map/ppermute | solution.py:1272
  671.3 4.2 place_grads.4
  675.6 4.3 place_grads.5
  679.9 5.3 place_grads.6
  685.2 5.7 place_grads.7
  (196 shorter events, 41.7 us)
Async XLA Ops:
  7.2 412.3 %all-gather.7.cloned.1.call-start = ((), (), s32[]{:S(2)}) async-start(), calls=%async_computation.1 | async-start | bytes 7864320 | tf_op jit(solution)/shard_map/all_gather | solution.py:1336
  123.7 295.8 %all-gather.5.cloned.1.call-start = ((), (), s32[]{:S(2)}) async-start(), calls=%async_computation | async-start | bytes 8028160 | tf_op jit(solution)/shard_map/all_gather | solution.py:1343
  124.9 59.7 %copy-start.37 = (f32[2,512,12]{1,0,2:T(2,128)S(1)}, f32[2,512,12]{1,0,2:T(2,128)}, u32[]{:S(2)}) copy-start(f32[2,512,12]{1,0,2:T(2,128)} %param.13) | copy-start | bytes 147460
  364.3 44.4 %collective-permute-start.11 = (bf16[2,192,512]{1,2,0:T(8,128)(2,1)S(1)}, bf16[2,192,512]{1,2,0:T(8,128)(2,1)S(1)}, u32[]{:S(2)}, u32[]{:S(2)}) collective-permute-start(bf16[2,192,512]{1,2,0:T(8,128)(2,1)S(1)} %bitcast.88), channel_id=1, source_target_pairs={{0,8},{8,0},{16,24},{24,16},{1,9},{9,1},{17,25},{25,17},{2,10},{10... | collective-permute-start | bytes 1179656 | tf_op jit(solution)/shard_map/ppermute | solution.py:1266
  394.8 75.8 %collective-permute-start.1 = (bf16[3,256,384]{2,1,0:T(8,128)(2,1)}, bf16[3,256,384]{2,1,0:T(8,128)(2,1)S(1)}, u32[]{:S(2)}, u32[]{:S(2)}) collective-permute-start(bf16[3,256,384]{2,1,0:T(8,128)(2,1)} %get-tuple-element.125), channel_id=1, source_target_pairs={{0,2},{2,0},{4,6},{6,4},{1,3},{3,1},{5,7},{7,5},{8,10},{10,8},{12,... | collective-permute-start | bytes 1769480 | tf_op jit(solution)/shard_map/ppermute | solution.py:1272
  406.1 64.6 %collective-permute-start.2 = (bf16[3,256,384]{2,1,0:T(8,128)(2,1)}, bf16[3,256,384]{2,1,0:T(8,128)(2,1)S(1)}, u32[]{:S(2)}, u32[]{:S(2)}) collective-permute-start(bf16[3,256,384]{2,1,0:T(8,128)(2,1)} %get-tuple-element.126), channel_id=1, source_target_pairs={{0,4},{2,6},{4,0},{6,2},{1,5},{3,7},{5,1},{7,3},{8,12},{10,14},{12... | collective-permute-start | bytes 1769480 | tf_op jit(solution)/shard_map/ppermute | solution.py:1272
  406.1 64.6 %collective-permute-start.3 = (bf16[3,256,384]{2,1,0:T(8,128)(2,1)}, bf16[3,256,384]{2,1,0:T(8,128)(2,1)}, u32[]{:S(2)}, u32[]{:S(2)}) collective-permute-start(bf16[3,256,384]{2,1,0:T(8,128)(2,1)} %get-tuple-element.127), channel_id=1, source_target_pairs={{0,6},{2,4},{4,2},{6,0},{1,7},{3,5},{5,3},{7,1},{8,14},{10,12},{12... | collective-permute-start | bytes 1769480 | tf_op jit(solution)/shard_map/ppermute | solution.py:1272
  408.9 9.4 %collective-permute-start.12 = (bf16[192,512]{0,1:T(8,128)(2,1)S(1)}, bf16[192,512]{0,1:T(8,128)(2,1)S(1)}, u32[]{:S(2)}, u32[]{:S(2)}) collective-permute-start(bf16[192,512]{0,1:T(8,128)(2,1)S(1)} %dynamic-slice_bitcast_fusion.3), channel_id=1, source_target_pairs={{0,16},{8,24},{16,0},{24,8},{1,17},{9,25},{17,1},{25,9},{2,18},{10... | collective-permute-start | bytes 589832 | tf_op jit(solution)/shard_map/ppermute | solution.py:1266
  416.3 89.3 %collective-permute-start = (bf16[512,768]{1,0:T(8,128)(2,1)}, bf16[512,768]{1,0:T(8,128)(2,1)S(1)}, u32[]{:S(2)}, u32[]{:S(2)}) collective-permute-start(bf16[512,768]{1,0:T(8,128)(2,1)} %layer_out.1), channel_id=1, source_target_pairs={{0,1},{1,0},{2,3},{3,2},{4,5},{5,4},{6,7},{7,6},{8,9},{9,8},{10,11... | collective-permute-start | bytes 2359304 | tf_op jit(solution)/shard_map/ppermute | solution.py:1269
  418.3 85.6 %collective-permute-start.13 = (bf16[192,512]{0,1:T(8,128)(2,1)S(1)}, bf16[192,512]{0,1:T(8,128)(2,1)S(1)}, u32[]{:S(2)}, u32[]{:S(2)}) collective-permute-start(bf16[192,512]{0,1:T(8,128)(2,1)S(1)} %fusion.7), channel_id=1, source_target_pairs={{0,2},{2,0},{4,6},{6,4},{1,3},{3,1},{5,7},{7,5},{8,10},{10,8},{12,... | collective-permute-start | bytes 589832 | tf_op jit(solution)/shard_map/ppermute | solution.py:1272
  484.2 61.0 %collective-permute-start.6 = (bf16[2,592,384]{2,1,0:T(8,128)(2,1)}, bf16[2,592,384]{2,1,0:T(8,128)(2,1)S(1)}, u32[]{:S(2)}, u32[]{:S(2)}) collective-permute-start(bf16[2,592,384]{2,1,0:T(8,128)(2,1)} %dynamic-slice_bitcast_fusion), channel_id=1, source_target_pairs={{0,8},{8,0},{16,24},{24,16},{1,9},{9,1},{17,25},{25,17},{2,10},{10... | collective-permute-start | bytes 2727944 | tf_op jit(solution)/shard_map/ppermute | solution.py:1266
  484.3 19.0 %collective-permute-start.5 = (f32[512,12]{0,1:T(8,128)S(1)}, f32[512,12]{0,1:T(8,128)S(1)}, u32[]{:S(2)}, u32[]{:S(2)}) collective-permute-start(f32[512,12]{0,1:T(8,128)S(1)} %get-tuple-element.215), channel_id=1, source_target_pairs={{0,1},{1,0},{2,3},{3,2},{4,5},{5,4},{6,7},{7,6},{8,9},{9,8},{10,11... | collective-permute-start | bytes 73736 | tf_op jit(solution)/shard_map/ppermute | solution.py:1269
  501.9 22.6 %collective-permute-start.28 = (bf16[2,3,192,256]{3,2,1,0:T(8,128)(2,1)}, bf16[2,3,192,256]{3,2,1,0:T(8,128)(2,1)S(1)}, u32[]{:S(2)}, u32[]{:S(2)}) collective-permute-start(bf16[2,3,192,256]{3,2,1,0:T(8,128)(2,1)} %get-tuple-element.161), channel_id=1, source_target_pairs={{0,1},{1,0},{8,9},{9,8},{16,17},{17,16},{24,25},{25,24},{2,3},{3,2... | collective-permute-start | bytes 1769480 | tf_op jit(solution)/shard_map/ppermute | solution.py:1275
  503.2 38.3 %collective-permute-start.29 = (bf16[2,3,192,256]{3,2,1,0:T(8,128)(2,1)}, bf16[2,3,192,256]{3,2,1,0:T(8,128)(2,1)S(1)}, u32[]{:S(2)}, u32[]{:S(2)}) collective-permute-start(bf16[2,3,192,256]{3,2,1,0:T(8,128)(2,1)} %get-tuple-element.162), channel_id=1, source_target_pairs={{0,16},{1,17},{8,24},{9,25},{16,0},{17,1},{24,8},{25,9},{2,18},{3,... | collective-permute-start | bytes 1769480 | tf_op jit(solution)/shard_map/ppermute | solution.py:1275
  503.9 39.3 %collective-permute-start.30 = (bf16[2,3,192,256]{3,2,1,0:T(8,128)(2,1)}, bf16[2,3,192,256]{3,2,1,0:T(8,128)(2,1)S(1)}, u32[]{:S(2)}, u32[]{:S(2)}) collective-permute-start(bf16[2,3,192,256]{3,2,1,0:T(8,128)(2,1)} %get-tuple-element.163), channel_id=1, source_target_pairs={{0,17},{1,16},{8,25},{9,24},{16,1},{17,0},{24,9},{25,8},{2,19},{3,... | collective-permute-start | bytes 1769480 | tf_op jit(solution)/shard_map/ppermute | solution.py:1275
  505.5 17.7 %copy-start.28 = (bf16[512,768]{1,0:T(8,128)(2,1)}, bf16[512,768]{1,0:T(8,128)(2,1)S(1)}, u32[]{:S(2)}) copy-start(bf16[512,768]{1,0:T(8,128)(2,1)S(1)} %collective-permute-done) | copy-start | bytes 2359300
  505.5 17.7 %collective-permute-start.14 = (bf16[192,512]{0,1:T(8,128)(2,1)S(1)}, bf16[192,512]{0,1:T(8,128)(2,1)S(1)}, u32[]{:S(2)}, u32[]{:S(2)}) collective-permute-start(bf16[192,512]{0,1:T(8,128)(2,1)S(1)} %reduce-precision_convert_fusion.1), channel_id=1, source_target_pairs={{0,4},{2,6},{4,0},{6,2},{1,5},{3,7},{5,1},{7,3},{8,12},{10,14},{12... | collective-permute-start | bytes 589832 | tf_op jit(solution)/shard_map/ppermute | solution.py:1272
  523.2 26.0 %collective-permute-start.24 = (bf16[2,3,192,256]{3,2,1,0:T(8,128)(2,1)}, bf16[2,3,192,256]{3,2,1,0:T(8,128)(2,1)S(1)}, u32[]{:S(2)}, u32[]{:S(2)}) collective-permute-start(bf16[2,3,192,256]{3,2,1,0:T(8,128)(2,1)} %get-tuple-element.157), channel_id=1, source_target_pairs={{0,1},{1,0},{8,9},{9,8},{16,17},{17,16},{24,25},{25,24},{2,3},{3,2... | collective-permute-start | bytes 1769480 | tf_op jit(solution)/shard_map/ppermute | solution.py:1275
  524.5 17.0 %copy-start.16 = (bf16[2,3,192,256]{3,2,1,0:T(8,128)(2,1)}, bf16[2,3,192,256]{3,2,1,0:T(8,128)(2,1)S(1)}, u32[]{:S(2)}) copy-start(bf16[2,3,192,256]{3,2,1,0:T(8,128)(2,1)S(1)} %collective-permute-done.28.refs_1_) | copy-start | bytes 1769476
  524.5 22.4 %copy-start.26 = (bf16[4,592,384]{2,1,0:T(8,128)(2,1)S(1)}, bf16[4,592,384]{2,1,0:T(8,128)(2,1)}, u32[]{:S(2)}) copy-start(bf16[4,592,384]{2,1,0:T(8,128)(2,1)} %get-tuple-element.141) | copy-start | bytes 5455876
  524.5 27.5 %collective-permute-start.25 = (bf16[2,3,192,256]{3,2,1,0:T(8,128)(2,1)}, bf16[2,3,192,256]{3,2,1,0:T(8,128)(2,1)S(1)}, u32[]{:S(2)}, u32[]{:S(2)}) collective-permute-start(bf16[2,3,192,256]{3,2,1,0:T(8,128)(2,1)} %get-tuple-element.158), channel_id=1, source_target_pairs={{0,16},{1,17},{8,24},{9,25},{16,0},{17,1},{24,8},{25,9},{2,18},{3,... | collective-permute-start | bytes 1769480 | tf_op jit(solution)/shard_map/ppermute | solution.py:1275
  541.6 17.5 %collective-permute-start.26 = (bf16[2,3,192,256]{3,2,1,0:T(8,128)(2,1)}, bf16[2,3,192,256]{3,2,1,0:T(8,128)(2,1)S(1)}, u32[]{:S(2)}, u32[]{:S(2)}) collective-permute-start(bf16[2,3,192,256]{3,2,1,0:T(8,128)(2,1)} %get-tuple-element.159), channel_id=1, source_target_pairs={{0,17},{1,16},{8,25},{9,24},{16,1},{17,0},{24,9},{25,8},{2,19},{3,... | collective-permute-start | bytes 1769480 | tf_op jit(solution)/shard_map/ppermute | solution.py:1275
  544.0 36.4 %collective-permute-start.20 = (bf16[2,3,192,256]{3,2,1,0:T(8,128)(2,1)}, bf16[2,3,192,256]{3,2,1,0:T(8,128)(2,1)S(1)}, u32[]{:S(2)}, u32[]{:S(2)}) collective-permute-start(bf16[2,3,192,256]{3,2,1,0:T(8,128)(2,1)} %get-tuple-element.153), channel_id=1, source_target_pairs={{0,1},{1,0},{8,9},{9,8},{16,17},{17,16},{24,25},{25,24},{2,3},{3,2... | collective-permute-start | bytes 1769480 | tf_op jit(solution)/shard_map/ppermute | solution.py:1275
  546.2 35.6 %collective-permute-start.21 = (bf16[2,3,192,256]{3,2,1,0:T(8,128)(2,1)}, bf16[2,3,192,256]{3,2,1,0:T(8,128)(2,1)S(1)}, u32[]{:S(2)}, u32[]{:S(2)}) collective-permute-start(bf16[2,3,192,256]{3,2,1,0:T(8,128)(2,1)} %get-tuple-element.154), channel_id=1, source_target_pairs={{0,16},{1,17},{8,24},{9,25},{16,0},{17,1},{24,8},{25,9},{2,18},{3,... | collective-permute-start | bytes 1769480 | tf_op jit(solution)/shard_map/ppermute | solution.py:1275
  549.4 70.5 %copy-start.4 = (bf16[2,3,192,256]{3,2,1,0:T(8,128)(2,1)}, bf16[2,3,192,256]{3,2,1,0:T(8,128)(2,1)S(1)}, u32[]{:S(2)}) copy-start(bf16[2,3,192,256]{3,2,1,0:T(8,128)(2,1)S(1)} %collective-permute-done.24.refs_1_) | copy-start | bytes 1769476
  549.4 33.1 %collective-permute-start.7 = (bf16[592,384]{1,0:T(8,128)(2,1)}, bf16[592,384]{1,0:T(8,128)(2,1)}, u32[]{:S(2)}, u32[]{:S(2)}) collective-permute-start(bf16[592,384]{1,0:T(8,128)(2,1)} %dynamic-slice_bitcast_fusion.2), channel_id=1, source_target_pairs={{0,16},{8,24},{16,0},{24,8},{1,17},{9,25},{17,1},{25,9},{2,18},{10... | collective-permute-start | bytes 1363976 | tf_op jit(solution)/shard_map/ppermute | solution.py:1266
  552.0 67.9 %copy-start.6 = (bf16[2,3,192,256]{3,2,1,0:T(8,128)(2,1)}, bf16[2,3,192,256]{3,2,1,0:T(8,128)(2,1)S(1)}, u32[]{:S(2)}) copy-start(bf16[2,3,192,256]{3,2,1,0:T(8,128)(2,1)S(1)} %collective-permute-done.25.refs_2_) | copy-start | bytes 1769476
  552.1 94.6 %collective-permute-start.4 = (bf16[2,512,768]{2,1,0:T(8,128)(2,1)}, bf16[2,512,768]{2,1,0:T(8,128)(2,1)}, u32[]{:S(2)}, u32[]{:S(2)}) collective-permute-start(bf16[2,512,768]{2,1,0:T(8,128)(2,1)} %get-tuple-element.139.own), channel_id=1, source_target_pairs={{0,1},{1,0},{2,3},{3,2},{4,5},{5,4},{6,7},{7,6},{8,9},{9,8},{10,11... | collective-permute-start | bytes 4718600 | tf_op jit(solution)/shard_map/ppermute | solution.py:1269
  559.1 60.8 %copy-start.10 = (bf16[2,3,192,256]{3,2,1,0:T(8,128)(2,1)}, bf16[2,3,192,256]{3,2,1,0:T(8,128)(2,1)S(1)}, u32[]{:S(2)}) copy-start(bf16[2,3,192,256]{3,2,1,0:T(8,128)(2,1)S(1)} %collective-permute-done.26.refs_3_) | copy-start | bytes 1769476
  559.1 59.1 %collective-permute-start.22 = (bf16[2,3,192,256]{3,2,1,0:T(8,128)(2,1)}, bf16[2,3,192,256]{3,2,1,0:T(8,128)(2,1)}, u32[]{:S(2)}, u32[]{:S(2)}) collective-permute-start(bf16[2,3,192,256]{3,2,1,0:T(8,128)(2,1)} %get-tuple-element.155), channel_id=1, source_target_pairs={{0,17},{1,16},{8,25},{9,24},{16,1},{17,0},{24,9},{25,8},{2,19},{3,... | collective-permute-start | bytes 1769480 | tf_op jit(solution)/shard_map/ppermute | solution.py:1275
  563.9 20.2 %copy-start.33 = (bf16[192,512]{0,1:T(8,128)(2,1)S(1)}, bf16[192,512]{0,1:T(8,128)(2,1)}, u32[]{:S(2)}) copy-start(bf16[192,512]{0,1:T(8,128)(2,1)} %copy-done.32) | copy-start | bytes 589828
  580.5 39.4 %copy-start.8 = (bf16[2,3,192,256]{3,2,1,0:T(8,128)(2,1)}, bf16[2,3,192,256]{3,2,1,0:T(8,128)(2,1)S(1)}, u32[]{:S(2)}) copy-start(bf16[2,3,192,256]{3,2,1,0:T(8,128)(2,1)S(1)} %collective-permute-done.20.refs_1_) | copy-start | bytes 1769476
  580.5 50.2 %collective-permute-start.16 = (bf16[2,3,192,256]{3,2,1,0:T(8,128)(2,1)}, bf16[2,3,192,256]{3,2,1,0:T(8,128)(2,1)}, u32[]{:S(2)}, u32[]{:S(2)}) collective-permute-start(bf16[2,3,192,256]{3,2,1,0:T(8,128)(2,1)} %get-tuple-element.149), channel_id=1, source_target_pairs={{0,1},{1,0},{8,9},{9,8},{16,17},{17,16},{24,25},{25,24},{2,3},{3,2... | collective-permute-start | bytes 1769480 | tf_op jit(solution)/shard_map/ppermute | solution.py:1275
  581.8 50.6 %collective-permute-start.17 = (bf16[2,3,192,256]{3,2,1,0:T(8,128)(2,1)}, bf16[2,3,192,256]{3,2,1,0:T(8,128)(2,1)}, u32[]{:S(2)}, u32[]{:S(2)}) collective-permute-start(bf16[2,3,192,256]{3,2,1,0:T(8,128)(2,1)} %get-tuple-element.150), channel_id=1, source_target_pairs={{0,16},{1,17},{8,24},{9,25},{16,0},{17,1},{24,8},{25,9},{2,18},{3,... | collective-permute-start | bytes 1769480 | tf_op jit(solution)/shard_map/ppermute | solution.py:1275
  582.6 59.9 %collective-permute-start.18 = (bf16[2,3,192,256]{3,2,1,0:T(8,128)(2,1)}, bf16[2,3,192,256]{3,2,1,0:T(8,128)(2,1)}, u32[]{:S(2)}, u32[]{:S(2)}) collective-permute-start(bf16[2,3,192,256]{3,2,1,0:T(8,128)(2,1)} %get-tuple-element.151), channel_id=1, source_target_pairs={{0,17},{1,16},{8,25},{9,24},{16,1},{17,0},{24,9},{25,8},{2,19},{3,... | collective-permute-start | bytes 1769480 | tf_op jit(solution)/shard_map/ppermute | solution.py:1275
  588.8 29.9 %slice-start.5 = ((bf16[2,3,192,256]{3,2,1,0:T(8,128)(2,1)}), bf16[1,3,192,256]{3,2,1,0:T(8,128)(2,1)S(1)}, s32[]{:S(2)}) async-start(bf16[2,3,192,256]{3,2,1,0:T(8,128)(2,1)} %copy-done.16), calls=%async_computation.7 | async-start | bytes 589824 | tf_op jit(solution)/shard_map/slice | solution.py:1397
  588.8 29.9 %slice-start.6 = ((bf16[2,3,192,256]{3,2,1,0:T(8,128)(2,1)}), bf16[1,3,192,256]{3,2,1,0:T(8,128)(2,1)S(1)}, s32[]{:S(2)}) async-start(bf16[2,3,192,256]{3,2,1,0:T(8,128)(2,1)} %copy-done.18), calls=%async_computation.8 | async-start | bytes 589824 | tf_op jit(solution)/shard_map/slice | solution.py:1397
  588.8 29.9 %slice-start.7 = ((bf16[2,3,192,256]{3,2,1,0:T(8,128)(2,1)}), bf16[1,3,192,256]{3,2,1,0:T(8,128)(2,1)S(1)}, s32[]{:S(2)}) async-start(bf16[2,3,192,256]{3,2,1,0:T(8,128)(2,1)} %copy-done.20), calls=%async_computation.9 | async-start | bytes 589824 | tf_op jit(solution)/shard_map/slice | solution.py:1397
  618.2 28.3 %collective-permute-start.8 = (bf16[592,384]{1,0:T(8,128)(2,1)S(1)}, bf16[592,384]{1,0:T(8,128)(2,1)S(1)}, u32[]{:S(2)}, u32[]{:S(2)}) collective-permute-start(bf16[592,384]{1,0:T(8,128)(2,1)S(1)} %fusion.5), channel_id=1, source_target_pairs={{0,2},{2,0},{4,6},{6,4},{1,3},{3,1},{5,7},{7,5},{8,10},{10,8},{12,... | collective-permute-start | bytes 1363976 | tf_op jit(solution)/shard_map/ppermute | solution.py:1272
  630.7 15.3 %collective-permute-start.15 = (f32[192,128]{0,1:T(8,128)S(1)}, f32[192,128]{0,1:T(8,128)S(1)}, u32[]{:S(2)}, u32[]{:S(2)}) collective-permute-start(f32[192,128]{0,1:T(8,128)S(1)} %copy-done.35), channel_id=1, source_target_pairs={{0,1},{1,0},{2,3},{3,2},{4,5},{5,4},{6,7},{7,6},{8,9},{9,8},{10,11... | collective-permute-start | bytes 294920 | tf_op jit(solution)/shard_map/ppermute | solution.py:1269
  632.4 38.8 %collective-permute-start.31 = (bf16[4,3,192,256]{3,2,1,0:T(8,128)(2,1)}, bf16[4,3,192,256]{3,2,1,0:T(8,128)(2,1)S(1)}, u32[]{:S(2)}, u32[]{:S(2)}) collective-permute-start(bf16[4,3,192,256]{3,2,1,0:T(8,128)(2,1)} %pad_maximum_fusion.3), channel_id=1, source_target_pairs={{0,8},{8,0},{16,24},{24,16},{1,9},{9,1},{17,25},{25,17},{2,10},{10... | collective-permute-start | bytes 3538952 | tf_op jit(solution)/shard_map/ppermute | solution.py:1266
  642.5 33.1 %collective-permute-start.27 = (bf16[4,3,192,256]{3,2,1,0:T(8,128)(2,1)}, bf16[4,3,192,256]{3,2,1,0:T(8,128)(2,1)S(1)}, u32[]{:S(2)}, u32[]{:S(2)}) collective-permute-start(bf16[4,3,192,256]{3,2,1,0:T(8,128)(2,1)} %pad_maximum_fusion.2), channel_id=1, source_target_pairs={{0,8},{8,0},{16,24},{24,16},{1,9},{9,1},{17,25},{25,17},{2,10},{10... | collective-permute-start | bytes 3538952 | tf_op jit(solution)/shard_map/ppermute | solution.py:1266
  645.9 39.3 %collective-permute-start.19 = (bf16[4,3,192,256]{3,2,1,0:T(8,128)(2,1)}, bf16[4,3,192,256]{3,2,1,0:T(8,128)(2,1)S(1)}, u32[]{:S(2)}, u32[]{:S(2)}) collective-permute-start(bf16[4,3,192,256]{3,2,1,0:T(8,128)(2,1)} %pad_maximum_fusion), channel_id=1, source_target_pairs={{0,8},{8,0},{16,24},{24,16},{1,9},{9,1},{17,25},{25,17},{2,10},{10... | collective-permute-start | bytes 3538952 | tf_op jit(solution)/shard_map/ppermute | solution.py:1266
  646.4 33.4 %collective-permute-start.23 = (bf16[4,3,192,256]{3,2,1,0:T(8,128)(2,1)}, bf16[4,3,192,256]{3,2,1,0:T(8,128)(2,1)S(1)}, u32[]{:S(2)}, u32[]{:S(2)}) collective-permute-start(bf16[4,3,192,256]{3,2,1,0:T(8,128)(2,1)} %pad_maximum_fusion.1), channel_id=1, source_target_pairs={{0,8},{8,0},{16,24},{24,16},{1,9},{9,1},{17,25},{25,17},{2,10},{10... | collective-permute-start | bytes 3538952 | tf_op jit(solution)/shard_map/ppermute | solution.py:1266
  646.7 23.5 %collective-permute-start.9 = (bf16[592,384]{1,0:T(8,128)(2,1)S(1)}, bf16[592,384]{1,0:T(8,128)(2,1)S(1)}, u32[]{:S(2)}, u32[]{:S(2)}) collective-permute-start(bf16[592,384]{1,0:T(8,128)(2,1)S(1)} %reduce-precision_convert_fusion), channel_id=1, source_target_pairs={{0,4},{2,6},{4,0},{6,2},{1,5},{3,7},{5,1},{7,3},{8,12},{10,14},{12... | collective-permute-start | bytes 1363976 | tf_op jit(solution)/shard_map/ppermute | solution.py:1272
  650.9 20.3 %copy-start.21 = (bf16[2,3,192,256]{3,2,1,0:T(8,128)(2,1)S(1)}, bf16[2,3,192,256]{3,2,1,0:T(8,128)(2,1)}, u32[]{:S(2)}) copy-start(bf16[2,3,192,256]{3,2,1,0:T(8,128)(2,1)} %copy-done.20) | copy-start | bytes 1769476
  657.0 14.3 %copy-start.22 = (s32[3]{0:T(128)S(1)}, s32[3]{0:T(128)}, u32[]{:S(2)}) copy-start(s32[3]{0:T(128)} %pad_add_fusion.1.sc) | copy-start | bytes 40
  670.3 21.5 %collective-permute-start.10 = (f32[1,192]{1,0:T(1,128)S(1)}, f32[1,192]{1,0:T(1,128)S(1)}, u32[]{:S(2)}, u32[]{:S(2)}) collective-permute-start(f32[1,192]{1,0:T(1,128)S(1)} %slice.100), channel_id=1, source_target_pairs={{0,1},{1,0},{2,3},{3,2},{4,5},{5,4},{6,7},{7,6},{8,9},{9,8},{10,11... | collective-permute-start | bytes 2312 | tf_op jit(solution)/shard_map/ppermute | solution.py:1269
  (33 other events, 187.4 us)
Sparse Core Ops, SparseCore 0:
  123.8 130.9 all-gather.6
  256.4 132.3 all-gather.4

commit v3 on v2

--- a/solution.py
+++ b/solution.py
@@ -491,15 +491,19 @@
     return (key <= query) | (key < prefix)
 
 
-def attn_kernel(prefix_ref, blocks, m3, mixed_in, m_ref, l3, q_s, k_s, v_s, st, z_sems, w_sems):
+def attn_kernel(prefix_ref, blocks, m0, l1, l2, l3, m3, mixed_in, m_ref, w_ref, wt_ref,
+                q_s, k_s, v_s, st, z_sems, w_sems):
     f, z, x = here()
     barrier = pltpu.get_barrier_semaphore()
     for d in range(1, 4):
         pl.semaphore_signal(barrier, inc=1, device_id=(f, flip4(z, d), x), device_id_type=MESH)
     pl.semaphore_signal(barrier, inc=1, device_id=(flip4(f, 2), z, flip2(x, 1)), device_id_type=MESH)
     pl.semaphore_wait(barrier, 4)
-    weights = to_plane(5, m3, l3, w_sems)
-    weights.start()
+    far = [
+        to_plane(5, m3.at[0, m], w_ref.at[m, 384:576, 1024:2048], w_sems, m) for m in (1, 2)
+    ] + [to_plane(5, m3.at[1, m], w_ref.at[m, 576:768, 1024:2048], w_sems, 3 + m) for m in range(3)]
+    for c in far:
+        c.start()
     prefix = prefix_ref[0]
     unpack_qkv(z, blocks, q_s, k_s, v_s)
     scale = HEAD_DIM ** (-0.5) * LOG2E
@@ -537,9 +541,26 @@
     for c in copies:
         c.start()
     mixed_in[0] = st[z]
+    w_ref[0, 384:576, 1024:2048] = l3[...]
+
+    def turn(m, r, jx):
+        wt_ref[m, jx * 1024 : (jx + 1) * 1024, r * 192 : (r + 1) * 192] = w_ref[
+            m, r * 192 : (r + 1) * 192, jx * 1024 : (jx + 1) * 1024
+        ].T
+
+    for j, b in enumerate((m0, l1, l2)):
+        for cc in range(2):
+            for m in range(3):
+                r, jx = 2 * (j // 2) + cc, j % 2
+                w_ref[m, r * 192 : (r + 1) * 192, jx * 1024 : (jx + 1) * 1024] = b[cc, m]
+                turn(m, r, jx)
+    for c in far:
+        c.wait()
+    for r in (2, 3):
+        for m in range(3):
+            turn(m, r, 1)
     for c in copies:
         c.wait()
-    weights.wait()
 
 
 def row_state(hidden, gain, gate_t, prev, routes, f, x):
@@ -573,25 +594,6 @@
     )
 
 
-def wprep_kernel(sc, b0, b1, b2, b3, w_ref, wt_ref):
-    f, x = sc[3], sc[2]
-    for j, b in enumerate((b0, b1, b2, b3)):
-        for cc in range(2):
-            rows = pl.multiple_of(jnp.bitwise_xor(f, 2 * (j // 2) + cc) * 192, 192)
-            cols = pl.multiple_of(jnp.bitwise_xor(x, j % 2) * 1024, 1024)
-            for m in range(3):
-                w_ref[m, pl.ds(rows, 192), pl.ds(cols, 1024)] = b[cc, m]
-    tile = 256
-
-    def step(t, carry):
-        at = pl.ds(pl.multiple_of(t * tile, tile), tile)
-        for m in range(3):
-            wt_ref[m, at, :] = w_ref[m, :, at].T
-        return carry
-
-    lax.fori_loop(0, w_ref.shape[2] // tile, step, 0)
-
-
 def expert_body(first, sc, xs, gs, w, wt, *refs):
     if first:
         y_ref, r_ref = refs[0:2]
@@ -604,19 +606,25 @@
     if first:
         din, res, graw = refs[3:]
     j = pl.program_id(1)
+    f = sc[pl.num_programs(0)]
+
+    def shard(r):
+        return pl.ds(pl.multiple_of(jnp.bitwise_xor(f, r) * 192, 64), 192)
 
     @pl.when(j == 0)
     def _():
         for k in range(8):
             cols = slice(k * CAPACITY, (k + 1) * CAPACITY)
-            both = xs[0, k].astype(F32)
-            xt[:, cols] = both[0:768].astype(BF)
-            gate = both[768 + k : 769 + k] + both[776 + k : 777 + k]
+            pair = xs[0, k, 768:784].astype(F32)
+            gate = pair[k : k + 1] + pair[8 + k : 9 + k]
             grow[:, cols] = jnp.broadcast_to(gate, (8, CAPACITY))
-            g = gs[0, k]
-            if first:
-                graw[:, cols] = g
-            gt[:, cols] = (g.astype(F32) * gate).astype(BF)
+            for r in range(4):
+                to, at = slice(r * 192, (r + 1) * 192), shard(r)
+                xt[to, cols] = xs[0, k, at]
+                g = gs[0, k, at]
+                if first:
+                    graw[to, cols] = g
+                gt[to, cols] = (g.astype(F32) * gate).astype(BF)
         if first:
             din[...] = jnp.zeros_like(din)
             res[...] = jnp.zeros_like(res)
@@ -650,9 +658,11 @@
                 tail = jnp.concatenate(
                     [jnp.where(row == k, high, 0.0), jnp.where(row == k, dg - high, 0.0)], axis=0
                 )
-                y_ref[k, 0:768, :] = din[:, cols].astype(BF)
                 y_ref[k, 768:784, :] = tail.astype(BF)
-                r_ref[k] = (r * grow[0:1, cols]).astype(BF)
+                r = (r * grow[0:1, cols]).astype(BF)
+                for q in range(4):
+                    y_ref[k, shard(q), :] = din[q * 192 : (q + 1) * 192, cols].astype(BF)
+                    r_ref[k, shard(q), :] = r[q * 192 : (q + 1) * 192]
 
 
 def expert_call(first, planes, xs, gs, w, wt, held):
@@ -691,7 +701,7 @@
         functools.partial(expert_body, first),
         out_shape=tuple(outs),
         grid_spec=pltpu.PrefetchScalarGridSpec(
-            num_scalar_prefetch=1, grid=(planes.shape[0], steps), in_specs=specs_in,
+            num_scalar_prefetch=1, grid=(planes.shape[0] - 1, steps), in_specs=specs_in,
             out_specs=tuple(specs_out), scratch_shapes=scratch,
         ),
         input_output_aliases=aliases,
@@ -701,117 +711,147 @@
     )(planes, xs, gs, w, wt, *extra_in)
 
 
-def grads_body(w_cols, sc, bx, bg, ba, bp, bu, *refs):
-    outs, acc = refs[:4], refs[4]
-    p = pl.program_id(0)
-
-    @pl.when(p == 0)
-    def _():
-        acc[...] = jnp.zeros_like(acc)
-
-    for xh in range(2):
-        acc[xh, 0] += mm_nt(bx[0], bp[0, xh])
-        acc[xh, 1] += mm_nt(bx[0], bu[0, xh])
-        acc[xh, 2] += mm_nt(bg[0], ba[0, xh])
-
-    @pl.when(p == pl.num_programs(0) - 1)
-    def _():
-        f, x = sc[1], sc[2]
-        for j in range(4):
-            for cc in range(2):
-                rows = pl.multiple_of(jnp.bitwise_xor(f, 2 * (j // 2) + cc) * 192, 192)
-                xh = jnp.bitwise_xor(x, j % 2)
-                for m in range(3):
-                    outs[j][cc, m] = acc[xh, m, pl.ds(rows, 192), :].astype(BF)
-
-
-def grads_call(scalars, part, parts, held):
-    bx, bg, ba, bp, bu = held
-    n_ctx, width, slots = bx.shape
-    half = ba.shape[1] // 2
-    cols = half // parts
-    split = lambda a: a.reshape(n_ctx, 2, half, slots)
-    tall = pl.BlockSpec((1, 2, cols, slots), lambda p, s: (p, 0, part, 0))
-    macs = 3 * width * slots * n_ctx * 2 * cols
+def finish_kernel(bx, bg, bp, bu, ba, dn, gq, og, gin, dn_other, att, outg, small_f, line_f,
+                  x_s, g_s, tiles, acc, send, q1, o1, qm, om, q2, o2, qk, ok, q3, o3, q4, o4, s_x, l_x,
+                  xg_sems, tile_sems, send_sems, own_sems, step_sems, dn_sems):
+    f, z, x = here()
+    core, y = f % 2, f // 2
+    cols = tiles.shape[2]
+    parts, planes = gin.shape[0], bx.shape[0]
+    greet()
+    loads = []
+    for p in range(planes):
+        loads.append(pltpu.make_async_copy(bx.at[p], x_s.at[p], xg_sems.at[0, p]))
+    for p in range(planes):
+        loads.append(pltpu.make_async_copy(bg.at[p], g_s.at[p], xg_sems.at[1, p]))
+
+    def tile_copy(part, m, p):
+        src = (bp, bu, ba)[m]
+        return pltpu.make_async_copy(
+            src.at[p, :, pl.ds(part * cols, cols), :], tiles.at[p % 2], tile_sems.at[p % 2]
+        )
+
+    for c in [tile_copy(0, 0, 0)] + loads:
+        c.start()
+    swap = to_plane(1, dn, dn_other, dn_sems)
+    swap.start()
+    first = []
+    for yy in range(2):
+        at = 2 * yy + 1 - core
+        first.append(to_plane(2, gq.at[at], q1.at[yy], step_sems, 2 * yy))
+        first.append(to_plane(2, og.at[at], o1.at[yy], step_sems, 2 * yy + 1))
+    for c in first:
+        c.start()
+
+    def plus(a, b):
+        return a.astype(F32) + b.astype(F32)
+
+    def after(part):
+        if part == 0:
+            for c in first:
+                c.wait()
+            for yy in range(2):
+                qm[yy] = plus(gq[2 * yy + core], q1[yy]).astype(BF)
+                om[yy] = plus(og[2 * yy + core], o1[yy]).astype(BF)
+            copies = [to_plane(4, qm.at[1 - y], q2, step_sems, 4), to_plane(4, om.at[1 - y], o2, step_sems, 5)]
+        elif part == 1:
+            qk[...] = plus(qm[y], q2[...]).astype(BF)
+            ok[...] = plus(om[y], o2[...]).astype(BF)
+            copies = [step_z(1, qk, q3, 6), step_z(1, ok, o3, 7)]
+        elif part == 2:
+            qm[0] = plus(qk[...], q3[...]).astype(BF)
+            om[0] = plus(ok[...], o3[...]).astype(BF)
+            copies = [step_z(2, qm.at[0], q4, 8), step_z(2, om.at[0], o4, 9)]
+        else:
+            att[...] = plus(qm[0], q4[...])
+            outg[...] = plus(om[0], o4[...])
+            s_x[0] = outg[:, 384:512]
+            l_x[0] = att[576:584, :]
+            copies = [to_plane(1, s_x.at[0], s_x.at[1], step_sems, 10), to_plane(1, l_x.at[0], l_x.at[1], step_sems, 11)]
+        return copies
+
+    def step_z(d, src, dst, at):
+        return pltpu.make_async_remote_copy(
+            src_ref=src, dst_ref=dst, send_sem=step_sems.at[0, at], recv_sem=step_sems.at[1, at],
+            device_id=(f, flip4(z, d), x), device_id_type=MESH,
+        )
+
+    flying, sent, steps = [], [], []
+    for part in range(parts):
+        for m in range(3):
+            rows_s, at = (g_s, 1) if m == 2 else (x_s, 0)
+            acc[...] = jnp.zeros_like(acc)
+
+            def plane_step(p, carry, part=part, m=m, rows_s=rows_s, at=at):
+                tile_copy(part, m, p).wait()
+
+                @pl.when(p < planes - 1)
+                def _():
+                    tile_copy(part, m, p + 1).start()
+
+                if part < parts - 1 or m < 2:
+
+                    @pl.when(p == planes - 1)
+                    def _():
+                        tile_copy(part + (m + 1) // 3, (m + 1) % 3, 0).start()
+
+                if part == 0 and m != 1:
+                    pltpu.make_async_copy((bx, bg)[at].at[p], rows_s.at[p], xg_sems.at[at, p]).wait()
+                for xh in range(2):
+                    acc[xh] += mm_nt(rows_s[p], tiles[p % 2, xh])
+                return carry
+
+            lax.fori_loop(0, planes, plane_step, 0)
+            for k in (5, 7, 4, 6, 1, 3, 2, 0):
+                r, jx = k // 2, k % 2
+                send[part, k, m] = acc[jx, r * 192 : (r + 1) * 192, :].astype(BF)
+                src, dst, number = send.at[part, k, m], gin.at[part, k, m], 3 * part + m
+                if k:
+                    sent.append(to_plane(k, src, dst, send_sems, number * 8 + k))
+                else:
+                    sent.append(pltpu.make_async_copy(src, dst, own_sems.at[number]))
+                sent[-1].start()
+        for c in steps:
+            c.wait()
+        steps = after(part)
+        for c in steps:
+            c.start()
+    for c in steps:
+        c.wait()
+    small_f[...] = s_x[0] + s_x[1]
+    line_f[...] = l_x[0] + l_x[1]
+    swap.wait()
+    for c in sent:
+        c.wait()
+
+
+def place_body(sc, block, gu, dn):
+    parts, cols = block.shape[0], block.shape[4]
+    for part in range(parts):
+        at = slice(part * cols, (part + 1) * cols)
+        gu[0, 0, :, at] = block[part, 0, 0].astype(F32)
+        gu[0, 1, :, at] = block[part, 0, 1].astype(F32)
+        dn[0, :, at] = block[part, 0, 2].astype(F32)
+
+
+def place_call(scalars, gin):
+    parts, cols = gin.shape[0], gin.shape[4]
+    xor = lambda k, s: jnp.bitwise_xor(k, s[0])
     return pl.pallas_call(
-        functools.partial(grads_body, cols),
-        out_shape=tuple([out((2, 3, 192, cols))] * 4),
-        grid_spec=pltpu.PrefetchScalarGridSpec(
-            num_scalar_prefetch=1, grid=(n_ctx,),
-            in_specs=[pl.BlockSpec((1, width, slots), lambda p, s: (p, 0, 0))] * 2 + [tall] * 3,
-            out_specs=tuple([pl.BlockSpec((2, 3, 192, cols), lambda p, s: (0, 0, 0, 0))] * 4),
-            scratch_shapes=[pltpu.VMEM((2, 3, width, cols), F32)],
-        ),
-        compiler_params=pltpu.CompilerParams(vmem_limit_bytes=56 * MIB),
-        cost_estimate=COST,
-        name="expert_grads",
-    )(scalars, bx, bg, split(ba), split(bp), split(bu))
-
-
-def place_body(first, sc, *refs):
-    near, far = refs[:4], refs[4]
-    gu, dn = refs[5:] if first else refs[7:]
-    at = pl.program_id(0)
-    for k in range(8):
-
-        @pl.when(at == k)
-        def _(k=k):
-            j = 2 * (k // 4) + k % 2
-            block = far.at[j] if (k // 2) % 2 else near[j].at[0]
-            gu[0, 0] = block[0].astype(F32)
-            gu[0, 1] = block[1].astype(F32)
-            dn[0] = block[2].astype(F32)
-
-
-def place_call(scalars, part, parts, blocks, held):
-    cols = blocks[0].shape[3]
-    first = held is None
-    xor = lambda k, s: jnp.bitwise_xor(k, s[0])
-    extra = [] if first else list(held)
-    return pl.pallas_call(
-        functools.partial(place_body, first),
+        place_body,
         out_shape=(out((NFFN, 2, 192, cols * parts), F32), out((NFFN, 192, cols * parts), F32)),
         grid_spec=pltpu.PrefetchScalarGridSpec(
             num_scalar_prefetch=1, grid=(NFFN,),
-            in_specs=[pl.BlockSpec(b.shape, lambda k, s: (0, 0, 0, 0)) for b in blocks]
-            + [pl.BlockSpec(memory_space=pl.ANY)] * len(extra),
+            in_specs=[pl.BlockSpec((parts, 1, 3, 192, cols), lambda k, s: (0, k, 0, 0, 0))],
             out_specs=(
-                pl.BlockSpec((1, 2, 192, cols), lambda k, s: (xor(k, s), 0, 0, part)),
-                pl.BlockSpec((1, 192, cols), lambda k, s: (xor(k, s), 0, part)),
+                pl.BlockSpec((1, 2, 192, cols * parts), lambda k, s: (xor(k, s), 0, 0, 0)),
+                pl.BlockSpec((1, 192, cols * parts), lambda k, s: (xor(k, s), 0, 0)),
             ),
         ),
-        input_output_aliases={} if first else {6: 0, 7: 1},
         compiler_params=pltpu.CompilerParams(vmem_limit_bytes=40 * MIB),
         cost_estimate=COST,
         name="place_grads",
-    )(scalars, *blocks, *extra)
-
-
-def layer_kernel(sc, hidden_ref, small, small_t, prev, routes, hot, rin, out_ref):
-    hidden = hidden_ref[...]
-    gain, gate_t = small[:, 17:18].astype(F32), small_t[0:16].astype(BF)
-    s = row_state(hidden, gain, gate_t, prev[...], routes[...], sc[3], sc[2])
-    total = hidden
-    for k in range(8):
-        total = total + mm(rin[k], hot[k * CAPACITY : (k + 1) * CAPACITY, :])
-    weight = s["copy_w"]
-    vecs = small[:, 18:20].astype(F32)
-    for c in range(NCONST):
-        weight = weight + s["const_w"][c] * s["mixing"][c][0]
-        total = total + (s["const_w"][c] * s["mixing"][c][1]) * vecs[:, c : c + 1]
-    total = total + weight * s["normed"]
-    out_ref[...] = total.astype(BF).T
-
-
-def outgrad_kernel(sc, own, other, mixed, small, o_ref, dh_ref):
-    x = sc[2]
-    g = mm_nt(own[...], mixed[x]) + mm_nt(other[...], mixed[1 - x])
-    for f in range(4):
-        rows = slice(f * 192, (f + 1) * 192)
-        o_ref[f, :, 0:384] = g[rows].astype(BF)
-        o_ref[f, :, 384:512] = small[rows, :].astype(BF)
-    dh_ref[x] = own[...].T
-    dh_ref[1 - x] = other[...].T
+    )(scalars, gin)
 
 
 def attn_back_kernel(sc, blocks, m_ref, dm, o0, o1, o2, o3,
@@ -976,9 +1016,9 @@
     return jnp.where(named < NFFN, jnp.bitwise_xor(named, me), named)
 
 
-def gather_kernel(pack, smallp, routes, gy, gu, dw,
+def gather_kernel(qkv, wo, smallp, routes, gy_both, gu, dw,
                   hot, gyt, gin, w_out, wo_out, small_out, small_t, m0, m1, m2, m3,
-                  packs, smalls, gsend, pack_sems, small_sems, g_sems, w_sems, own_sems):
+                  packs, outs_in, smalls, gsend, pack_sems, small_sems, g_sems, w_sems, own_sems):
     f, z, x = here()
     barrier = pltpu.get_barrier_semaphore()
     for k in range(1, 8):
@@ -986,11 +1026,17 @@
             barrier, inc=1, device_id=(flip4(f, k // 2), z, flip2(x, k % 2)), device_id_type=MESH
         )
     pl.semaphore_wait(barrier, 7)
-    pack_copies = [None] + [to_plane(2 * j, pack, packs.at[j], pack_sems) for j in (1, 2)]
-    small_copies = [None] + [to_plane(2 * j, smallp, smalls.at[j], small_sems) for j in (1, 2)]
-    for j in (2, 1):
-        small_copies[j].start()
-        pack_copies[j].start()
+    def shares(k, at, q, o, small):
+        return [
+            to_plane(k, small, smalls.at[at], small_sems, at),
+            to_plane(k, q, packs.at[at], pack_sems, at),
+            to_plane(k, o, outs_in.at[at], pack_sems, 4 + at),
+        ]
+
+    over = shares(4, 2, qkv, wo, smallp)
+    beside = shares(2, 1, qkv, wo, smallp)
+    for c in over + beside:
+        c.start()
     moves = []
     for j, m in enumerate((m0, m1, m2, m3)):
         for cc in range(2):
@@ -1007,10 +1053,10 @@
     for c in moves:
         c.start()
 
-    rows = gy.shape[0]
+    rows = gy_both.shape[1]
     named = expert_flip(routes[...], f, x)
     first, second = named[0:1], named[1:2]
-    g_t = gy[...].T
+    g_t = gy_both[x].T
     gyt[...] = g_t
     ids = lax.broadcasted_iota(jnp.int32, (16, rows), 0)
     hits = ((ids == first) | (ids == second)).astype(F32)
@@ -1029,49 +1075,50 @@
         else:
             gsend[k] = block
     g_copies = [to_plane(k, gsend.at[k], gin.at[k], g_sems) for k in (5, 7, 4, 6, 1, 3, 2)]
-
-    def assemble(j, pack_ref, small_ref):
+    for c in g_copies:
+        c.start()
+
+    def assemble(j, q, o, small):
         at = pl.ds(pl.multiple_of(flip4(f, j) * 192, 64), 192)
         for c in range(3):
-            w_out[c, at, :] = pack_ref[c * 192 : (c + 1) * 192, :]
-        wo_out[at, :] = pack_ref[576:768, :]
-        small_out[at, :] = small_ref[...]
-
-    assemble(0, pack, smallp)
-    small_copies[2].wait_recv()
-    pack_copies[2].wait_recv()
-    small_copies.append(to_plane(2, smalls.at[2], smalls.at[3], small_sems, 3))
-    pack_copies.append(to_plane(2, packs.at[2], packs.at[3], pack_sems, 3))
-    small_copies[3].start()
-    pack_copies[3].start()
-    for c in g_copies:
+            w_out[c, at, :] = q[c]
+        wo_out[at, :] = o[...]
+        small_out[at, :] = small[...]
+
+    assemble(0, qkv, wo, smallp)
+    for c in over:
+        c.wait_recv()
+    onward = shares(2, 3, packs.at[2], outs_in.at[2], smalls.at[2])
+    for c in onward:
         c.start()
-    assemble(2, packs.at[2], smalls.at[2])
-    small_copies[1].wait_recv()
-    pack_copies[1].wait_recv()
-    assemble(1, packs.at[1], smalls.at[1])
-    small_copies[3].wait_recv()
-    pack_copies[3].wait_recv()
-    assemble(3, packs.at[3], smalls.at[3])
+    assemble(2, packs.at[2], outs_in.at[2], smalls.at[2])
+    for c in beside:
+        c.wait_recv()
+    assemble(1, packs.at[1], outs_in.at[1], smalls.at[1])
+    for c in onward:
+        c.wait_recv()
+    assemble(3, packs.at[3], outs_in.at[3], smalls.at[3])
     small_t[...] = small_out[...].astype(F32).T
-    for c in pack_copies[1:] + small_copies[1:]:
+    for c in over + beside + onward:
         c.wait_send()
     for c in moves + g_copies:
         c.wait()
 
 
-def project_kernel(tokens, w, small_t, cos_ref, sin_ref, m1, m2, nt, xt, blocks, l1, l2,
+def project_kernel(tokens, w, small_t, cos_ref, sin_ref, m1, m2, m3, nt, xt, blocks, l1, l2, l3,
                    n_s, st, z_sems, w_sems):
     f, z, x = here()
     barrier = pltpu.get_barrier_semaphore()
     for d in range(1, 4):
         pl.semaphore_signal(barrier, inc=1, device_id=(f, flip4(z, d), x), device_id_type=MESH)
-    for k in (1, 4):
+    for k in (1, 4, 5):
         pl.semaphore_signal(
             barrier, inc=1, device_id=(flip4(f, k // 2), z, flip2(x, k % 2)), device_id_type=MESH
         )
-    pl.semaphore_wait(barrier, 5)
-    weights = [to_plane(1, m1, l1, w_sems), to_plane(4, m2, l2, w_sems)]
+    pl.semaphore_wait(barrier, 6)
+    weights = [
+        to_plane(1, m1, l1, w_sems), to_plane(4, m2, l2, w_sems), to_plane(5, m3.at[0, 0], l3, w_sems),
+    ]
     for c in weights:
         c.start()
     gain = small_t[16:17]
@@ -1099,9 +1146,15 @@
                     for a in (q, k, v)
                 ]
                 st[d, j] = jnp.concatenate(parts, axis=1)
-    z_copies = [to_column(d, st.at[d], blocks.at[d], z_sems) for d in (3, 2, 1)]
-    for c in z_copies:
-        c.start()
+
+            @pl.when(d > 0)
+            def _(d=d, b=2 * s + half):
+                pltpu.make_async_remote_copy(
+                    src_ref=st.at[d], dst_ref=blocks.at[d], send_sem=z_sems.at[0, d],
+                    recv_sem=z_sems.at[1, d], device_id=(f, b, x), device_id_type=MESH,
+                ).start()
+
+    z_copies = [to_column(d, st.at[d], blocks.at[d], z_sems) for d in (1, 2, 3)]
     blocks[0] = st[0]
     for s in range(2):
         nt[:, s * rows : (s + 1) * rows] = n_s[s].T
@@ -1146,9 +1199,9 @@
         c.wait()
 
 
-def return_kernel(ysend, rsend, hidden_ref, small, small_t, prev, routes, gyt, hot, wo,
-                  rin, dt, d_other, gprev_ref, small_ref, dm_in, yin, dm_send,
-                  y_sems, r_sems, t_sems, z_sems):
+def return_kernel(ysend, rsend, hidden_ref, small, small_t, prev, routes, gyt, hot, wo, mixed,
+                  layer, gprev, dm_in, og, dh, yin, rin, dm_send, dt, d_other,
+                  y_sems, r_sems, t_sems, z_sems, o_sems):
     f, z, x = here()
     greet()
     ys = [to_plane(k, ysend.at[k], yin.at[k], y_sems) for k in (5, 7, 4, 6, 1, 3, 2)]
@@ -1185,7 +1238,7 @@
     inner = gates[0] * d_gates[0] + gates[1] * d_gates[1]
     d_chosen = [gates[j] * (d_gates[j] - inner) for j in range(TOP)]
     d_logits = sum(jnp.where(ids == named[j], d_chosen[j], 0.0) for j in range(TOP))
-    gprev_ref[...] = d_logits
+    gprev[x] = d_logits
     coefs = []
     direct = s["copy_w"]
     for c in range(NCONST):
@@ -1215,7 +1268,7 @@
     for c in range(NCONST):
         g_const = jnp.sum(gy * coefs[c], axis=1, keepdims=True)
         total = jnp.where(lane == 16 + c, g_const, total)
-    small_ref[...] = jnp.where(lane == 18, g_gain, total)
+    total = jnp.where(lane == 18, g_gain, total).astype(BF)
     swap.wait()
     rs = [to_plane(k, rsend.at[k], rin.at[k], r_sems) for k in range(1, 8)]
     for c in rs:
@@ -1227,8 +1280,28 @@
     for c in zs:
         c.start()
     dm_in[0] = dm_send[0]
-    for c in zs + rs:
+    lines = to_plane(1, gprev.at[x], gprev.at[x], o_sems, 0)
+    lines.start()
+    weight = direct
+    total_out = hidden
+    for c in range(NCONST):
+        total_out = total_out + coefs[c] * vecs[c]
+    total_out = total_out + weight * normed
+    g = mm_nt(dt[...], mixed[x]) + mm_nt(d_other[...], mixed[1 - x])
+    for q in range(4):
+        at = slice(q * 192, (q + 1) * 192)
+        og[q, :, 0:384] = g[at].astype(BF)
+        og[q, :, 384:512] = total[at]
+    dh[x] = dt[...].T
+    dh[1 - x] = d_other[...].T
+    for c in rs:
         c.wait()
+    for k in range(8):
+        total_out = total_out + mm(rin[k], hot[k * CAPACITY : (k + 1) * CAPACITY, :])
+    layer[...] = total_out.astype(BF).T
+    for c in zs:
+        c.wait()
+    lines.wait()
 
 
 def run_remote(body, name, number, ins, outs, scratch, vmem=56, hbm_ins=(), hbm_outs=(), smem_ins=()):
@@ -1274,15 +1347,11 @@
     def flip_plane(v, k):
         return lax.ppermute(v, ("fsdp", "tp"), [(i, i ^ k) for i in range(8)])
 
-    pack = jnp.concatenate(
-        [query_key_value_weight.reshape(3 * 192, head_cols), output_projection_weight], axis=0
-    )
     small_own = jnp.pad(
         jnp.concatenate([router_gate_weight, norm_gains.T, const_vec.T], axis=1), ((0, 0), (0, 108))
     )
     own_routes = lax.dynamic_index_in_dim(routes, x, 0, False).T
     own_prev = jnp.pad(lax.dynamic_index_in_dim(prev_logits, x, 0, False).T, ((0, 4), (0, 0)))
-    own_gy = lax.dynamic_index_in_dim(cotangent, x, 0, False)
 
     positions = z * rows + jnp.arange(rows, dtype=jnp.int32)
     half_dim = HEAD_DIM // 2
@@ -1296,42 +1365,45 @@
     messages = [out((2, 3, 192, 1024))] * 4
     hot, gyt, gs, w_full, wo_full, small, small_t, *messages = run_remote(
         gather_kernel, "gather", 0,
-        [pack, small_own, own_routes, own_gy, gate_up, down_weight[:, None]],
+        [
+            query_key_value_weight, output_projection_weight, small_own, own_routes, cotangent, gate_up,
+            down_weight[:, None],
+        ],
         [
             out((8 * CAPACITY, rows)), out((width, rows)), out((8, width, CAPACITY)),
             out((3, width, head_cols)), out((width, head_cols)), out((width, 128)), out((128, width), F32),
             *messages,
         ],
         [
-            vm((4, 768, head_cols), BF), vm((4, 192, 128), BF), vm((8, width, CAPACITY), BF),
+            vm((4, 3, 192, head_cols), BF), vm((4, 192, head_cols), BF), vm((4, 192, 128), BF),
+            vm((8, width, CAPACITY), BF),
             sems(8), sems(8), sems(8), sems(8),
             pltpu.SemaphoreType.DMA((8,)),
         ],
-        hbm_ins=(4, 5),
-    )
-    normed_one_t, xt, blocks, w1, w2 = run_remote(
-        project_kernel, "project", 3, [tokens, w_full, small_t, cos, sin, messages[1], messages[2]],
+        hbm_ins=(5, 6),
+    )
+    normed_one_t, xt, blocks, w1, w2, w3 = run_remote(
+        project_kernel, "project", 3, [tokens, w_full, small_t, cos, sin, *messages[1:]],
         [
             out((width, 2 * rows)), out((width, rows)), out((4, 3, rows // 2, head_cols)),
-            out((2, 3, 192, 1024)), out((2, 3, 192, 1024)),
+            out((2, 3, 192, 1024)), out((2, 3, 192, 1024)), out((192, 1024)),
         ],
         [vm((2, rows, width), BF), vm((4, 3, rows // 2, head_cols), BF), sems(4), sems(8)],
-        hbm_ins=(5, 6), hbm_outs=(3, 4),
+        hbm_ins=(5, 6, 7), hbm_outs=(3, 4, 5),
     )
     gain_one_row = small_t[16:17]
 
     gs, blocks = lax.optimization_barrier((gs, blocks))
     length = 4 * rows
     unit_scratch = [pltpu.VMEM((3, length, HEAD_DIM), BF)] * 3
-    mixed_in, mixed_lse, w3 = run_remote(
-        attn_kernel, "attention", 4, [scalars[4:5], blocks, messages[3]],
-        [out((4, 192, rows)), out((3, HEAD_DIM + 8, length), F32), out((2, 3, 192, 1024))],
+    mixed_in, mixed_lse, w_exp, wt_exp = run_remote(
+        attn_kernel, "attention", 4, [scalars[4:5], blocks, messages[0], w1, w2, w3, messages[3]],
+        [
+            out((4, 192, rows)), out((3, HEAD_DIM + 8, length), F32), out((3, width, 2048)),
+            out((3, 2048, width)),
+        ],
         unit_scratch + [vm((4, 192, rows), BF), sems(4), sems(8)],
-        hbm_ins=(2,), hbm_outs=(2,), smem_ins=(0,),
-    )
-    w_exp, wt_exp = run(
-        wprep_kernel, "expert_weights", scalars, [messages[0], w1, w2, w3],
-        [out((3, width, 2048)), out((3, 2048, width))],
+        hbm_ins=(6,), smem_ins=(0,), vmem=60,
     )
     g_all = lax.all_gather(gs, "ctx")
 
@@ -1342,19 +1414,22 @@
     )
     x_all = lax.all_gather(xs, "ctx")
 
-    done = expert_call(True, jnp.stack([z]).astype(jnp.int32), xs[None], gs[None], w_exp, wt_exp, None)
+    done = expert_call(True, jnp.stack([z, f]).astype(jnp.int32), xs[None], gs[None], w_exp, wt_exp, None)
     ysend, rsend, held = done[0], done[1], done[2:]
-    r_in, d_t, d_other, grad_prev_t, small_grads, dm_in = run_remote(
+    layer_own, grad_prev_t, dm_in, og, d_hidden = run_remote(
         return_kernel, "give_back", 2,
-        [ysend, rsend, hidden, small, small_t, own_prev, own_routes, gyt, hot, wo_full],
+        [ysend, rsend, hidden, small, small_t, own_prev, own_routes, gyt, hot, wo_full, mixed],
         [
-            out((8, width, CAPACITY)), out((width, rows)), out((width, rows)), out((16, rows), F32),
-            out((width, 128), F32), out((4, 192, rows)),
+            out((rows, width)), out((2, 16, rows), F32), out((4, 192, rows)), out((4, 192, 512)),
+            out((2, rows, width)),
         ],
-        [vm((8, width + 16, CAPACITY), BF), vm((4, 192, rows), BF), sems(8), sems(8), sems(8), sems(4)],
-    )
-
-    others = jnp.stack([jnp.bitwise_xor(z, d) for d in (1, 2, 3)]).astype(jnp.int32)
+        [
+            vm((8, width + 16, CAPACITY), BF), vm((8, width, CAPACITY), BF), vm((4, 192, rows), BF),
+            vm((width, rows), BF), vm((width, rows), BF), sems(8), sems(8), sems(8), sems(4), sems(2),
+        ],
+    )
+    grad_prev = jnp.swapaxes(grad_prev_t[:, 0:NEXP], 1, 2)
+    others = jnp.stack([jnp.bitwise_xor(z, d) for d in (1, 2, 3)] + [f]).astype(jnp.int32)
 
     back = run(
         attn_back_kernel, "attention_backward", scalars, [blocks, mixed_lse, dm_in],
@@ -1370,72 +1445,43 @@
     *back_in, first = lax.optimization_barrier((*back_in, held[0]))
     held = [first, *held[1:]]
 
-    og, d_hidden = run(
-        outgrad_kernel, "out_grads", scalars, [d_t, d_other, mixed, small_grads],
-        [out((4, 192, 512)), out((2, rows, width))], flops=2 * 1024 * 768 * 384,
-    )
-
-    layer_own = run(
-        layer_kernel, "layer_out", scalars,
-        [hidden, small, small_t, own_prev, own_routes, hot, r_in],
-        [out((rows, width))], flops=2 * 512 * 1024 * 768,
-    )[0]
-
-    def both(own):
-        other = flip_tp(own)
-        return jnp.where(x == 0, jnp.stack([own, other]), jnp.stack([other, own]))
-
-    layer_out = both(layer_own)
-    grad_prev = both(grad_prev_t[0:NEXP].T)
-
-    parts = 4
-    spot = jnp.stack([me, f, x]).astype(jnp.int32)
-    placed = None
-    for part in range(parts):
-        g = grads_call(spot, part, parts, held)
-        g = [g[0]] + [flip_plane(g[j], 4 * (j // 2) + j % 2) for j in (1, 2, 3)]
-        far = flip_fsdp(jnp.stack([v[1] for v in g]), 1)
-        placed = place_call(spot, part, parts, [*g, far], placed)
-    grad_gu, grad_down = placed
-
-    def rounded(v):
-        return lax.reduce_precision(v, 8, 7).astype(BF)
-
-    def to_owner(v):
-        core, y = f % 2, f // 2
-        pairs = v.reshape((2, 2) + v.shape[1:])
-        send = lax.dynamic_index_in_dim(pairs, 1 - core, 1, False)
-        mine = lax.dynamic_index_in_dim(pairs, core, 1, False).astype(F32)
-        mine = rounded(mine + flip_fsdp(send, 1).astype(F32))
-        send = lax.dynamic_index_in_dim(mine, 1 - y, 0, False)
-        keep = lax.dynamic_index_in_dim(mine, y, 0, False).astype(F32)
-        keep = rounded(keep + flip_fsdp(send, 2).astype(F32))
-        keep = rounded(keep.astype(F32) + flip_ctx(keep, 1).astype(F32))
-        return keep.astype(F32) + flip_ctx(keep, 2).astype(F32)
-
-    owned = to_owner(og)
-    grad_out = owned[:, 0:384]
-    tail = owned[:, 384:512]
-    tail = tail + flip_tp(tail)
-    grad_gate = tail[:, 0:16]
-    grad_const = tail[:, 16:18].T
-    gain_two_grad = tail[:, 18]
-
+    other = flip_tp(layer_own)
+    layer_out = jnp.where(x == 0, jnp.stack([layer_own, other]), jnp.stack([other, layer_own]))
     dn, gq = run(
         dproj_kernel, "d_projection", scalars, [*back_in, w_full, normed_one_t, cos, sin, tokens],
         [out((2, rows, width)), out((4, 592, head_cols))],
-        scratch=[pltpu.VMEM((4, 3, rows // 2, head_cols), BF)], flops=4 * 1024 * 768 * 1152,
-    )
-    dn_other = flip_tp(dn)
+        scratch=[pltpu.VMEM((4, 3, rows // 2, head_cols), BF)],
+    )
+    parts, cols = 4, 256
+    tall = lambda v: v.reshape(4, 2, 1024, 1024)
+    bx, bg, ba, bp, bu = held
+    gin, dn_other, att, outg, small_f, line_f = run_remote(
+        finish_kernel, "finish", 5, [bx, bg, tall(bp), tall(bu), tall(ba), dn, gq, og],
+        [
+            out((parts, 8, 3, 192, cols)), out((2, rows, width)), out((592, head_cols), F32), out((192, 512), F32),
+            out((192, 128), F32), out((8, head_cols), F32),
+        ],
+        [
+            vm((4, width, 1024), BF), vm((4, width, 1024), BF), vm((2, 2, cols, 1024), BF),
+            vm((2, width, cols), F32), vm((parts, 8, 3, 192, cols), BF),
+            vm((2, 592, head_cols), BF), vm((2, 192, 512), BF), vm((2, 592, head_cols), BF), vm((2, 192, 512), BF),
+            vm((592, head_cols), BF), vm((192, 512), BF), vm((592, head_cols), BF), vm((192, 512), BF),
+            vm((592, head_cols), BF), vm((192, 512), BF), vm((592, head_cols), BF), vm((192, 512), BF),
+            vm((2, 192, 128), F32), vm((2, 8, head_cols), F32),
+            sems(4), pltpu.SemaphoreType.DMA((2,)), sems(96), pltpu.SemaphoreType.DMA((12,)), sems(12), sems(8),
+        ],
+        vmem=60, hbm_ins=(0, 1, 2, 3, 4, 5), hbm_outs=(0, 1),
+    )
+    grad_gu, grad_down = place_call(me[None].astype(jnp.int32), gin)
+    grad_out = outg[:, 0:384]
+    grad_gate = small_f[:, 0:16]
+    grad_const = small_f[:, 16:18].T
     grad_tokens = run(
         tokens_kernel, "grad_tokens", scalars, [tokens, gain_one_row, d_hidden, dn, dn_other],
         [out((2, rows, width), F32)],
     )[0]
-    owned = to_owner(gq)
-    grad_qkv = owned[0:576].reshape(3, 192, head_cols)
-    line = owned[576:577, 0:192]
-    line = line + flip_tp(line)
-    grad_gains = jnp.stack([line[0], gain_two_grad])
+    grad_qkv = att[0:576].reshape(3, 192, head_cols)
+    grad_gains = jnp.stack([line_f[0, 0:192], small_f[:, 18]])
     return (
         layer_out, grad_tokens, grad_prev, grad_gains, grad_qkv, grad_out, grad_gate, grad_const,
         grad_gu, grad_down,

time: 707 us -> 659 us (0.932)
  waiting for transfers between devices: 63.3 us -> 0.05 us
  Pallas kernels: 534 us -> 593 us
  starting transfers between devices: 41.2 us -> 16.3 us
  other arithmetic: 18 us -> 6.22 us
  local copies, waits for them, and re-layouts: 27.6 us -> 20.3 us
    pallas_call x5 -> x6, Pallas kernels: 294 us -> 454 us  [run_remote(): pl.pallas_call(body, out_shape=tuple(outs), in_specs=[HBM if i in hbm_ins...]
    pallas_call x8 -> x1, Pallas kernels: 85.3 us -> 7.16 us  [place_call(): pl.pallas_call(place_body, out_shape=(out((NFFN, 2, 192, cols * parts), F...]
    ppermute x20 -> x0, waiting for transfers between devices: 50.1 us -> none  [the longest x12 50.1 us: flip_plane(): return lax.ppermute(v, ('fsdp', 'tp'), [(i, i ^ k) for i in range(8)])]
    pallas_call x6 -> x3, Pallas kernels: 70.4 us -> 47.1 us  [run(): pl.pallas_call(body, out_shape=tuple(outs), in_specs=[SCALARS] + [WHOLE]...]
    ppermute x20 -> x0, starting transfers between devices: 17.8 us -> none  [the longest x12 14.2 us: flip_plane(): return lax.ppermute(v, ('fsdp', 'tp'), [(i, i ^ k) for i in range(8)])]
    ppermute x7 -> x3, waiting for transfers between devices: 13.1 us -> 0.01 us  [flip_ctx(): return lax.ppermute(v, 'ctx', [(i, i ^ k) for i in range(4)])]
    ppermute x7 -> x3, starting transfers between devices: 18.5 us -> 14.9 us  [flip_ctx(): return lax.ppermute(v, 'ctx', [(i, i ^ k) for i in range(4)])]
  transfers between devices with their start and end apart: 34 -> 6, of which waited for: 5 -> 0; matrix products, arithmetic and copies ran while one was open for 5% -> 1% of each run, Pallas kernels for 61% -> 48%
where the time goes in v3:
time: 659 us; the launch traced here: 651 us
  Pallas kernels  593 us (90%)
  local copies, waits for them, and re-layouts  20.3 us (3%)
  starting transfers between devices  16.3 us (2%)
  between operations  14.5 us (2%)
    pallas_call x6, Pallas kernels, run_remote(): pl.pallas_call(body, out_shape=tuple(outs), in_specs=[HBM if i in hbm_ins...  454 us
    pallas_call x2, Pallas kernels, expert_call(): pl.pallas_call(functools.partial(expert_body, first), out_shape=tuple(out...  85.1 us
    pallas_call x3, Pallas kernels, run(): pl.pallas_call(body, out_shape=tuple(outs), in_specs=[SCALARS] + [WHOLE]...  47.1 us
    ppermute x3, starting transfers between devices, flip_ctx(): return lax.ppermute(v, 'ctx', [(i, i ^ k) for i in range(4)])  14.9 us
  transfers between devices with their start and end apart: 6, of which 0 were waited for; matrix products, arithmetic and copies ran while one was open for 1% of the time, Pallas kernels for 48%

profile of v3, /device:TPU:0, one launch (start us, length us, event | category | flops | bytes accessed | tf_op | source)
XLA Modules:
  0.0 650.5 jit_solution(13314514456122381238)
XLA Ops:
  7.2 0.0 copy-start
  7.2 0.0 all-gather.7.cloned.1.call-start
  7.3 0.7 pad_maximum_fusion.2
  8.0 0.1 copy.45
  8.1 1.3 dynamic-slice_bitcast_fusion.routes
  9.4 0.6 pad.8.smallp
  10.1 1.0 fusion
  11.1 1.3 pad_maximum_fusion
  12.3 43.4 %gather.1 = (bf16[1024,512]{1,0:T(8,128)(2,1)}, bf16[768,512]{1,0:T(8,128)(2,1)}, bf16[8,768,128]{2,1,0:T(8,128)(2,1)}, bf16[3,768,384]{2,1,0:T(8,128)(2,1)}, bf...) custom-call(bf16[3,192,384]{2,1,0:T(8,128)(2,1)} %qkv.1, ...), custom_call_target="tpu_custom_call" | custom-call | flops 1024 | bytes 1024 | tf_op jit(solution)/shard_map/gather/pallas_call | solution.py:1308
  55.7 0.0 copy-start.8
  55.7 69.7 %project.1 = (bf16[768,1024]{1,0:T(8,128)(2,1)}, bf16[768,512]{1,0:T(8,128)(2,1)}, bf16[4,3,256,384]{3,2,1,0:T(8,128)(2,1)}, bf16[2,3,192,1024]{3,2,1,0:T(8,128)...) custom-call(bf16[2,512,768]{2,1,0:T(8,128)(2,1)} %tokens.5, ...), custom_call_target="tpu_custom_call" | custom-call | flops 1024 | bytes 1024 | tf_op jit(solution)/shard_map/project/pallas_call | solution.py:1308
  125.5 0.0 all-gather.7.cloned.1.call-update
  125.5 0.6 all-gather.5.cloned.1.call-start
  126.1 0.7 dynamic_slice.11.prefix_ref
  126.8 69.9 %attention.1 = (bf16[4,192,512]{2,1,0:T(8,128)(2,1)}, f32[3,72,2048]{2,1,0:T(8,128)}, bf16[3,768,2048]{2,1,0:T(8,128)(2,1)}, bf16[3,2048,768]{2,1,0:T(8,128)(2,1)}) custom-call(s32[1]{0:T(128)} %dynamic_slice.11.prefix_ref, bf16[4,3,256,384]{3,2,1,0:T(8,128)(2,1)} %get-tuple-element.79.blocks, bf16[2,3,192,1024]{3,2,1,0:T(8,128)(2,1)} %get-tuple-element.80.m0, ...), custom_call_target="tpu_custom_call" | custom-call | flops 1024 | bytes 1024 | tf_op jit(solution)/shard_map/attention/pallas_call | solution.py:1308
  196.7 0.6 pad.9.prev
  197.4 45.8 %route.1 = (bf16[2,384,512]{2,1,0:T(8,128)(2,1)}, f32[768,512]{1,0:T(8,128)}, bf16[8,784,128]{2,1,0:T(8,128)(2,1)}) custom-call(bf16[4,192,512]{2,1,0:T(8,128)(2,1)} %get-tuple-element.84.land, bf16[768,384]{1,0:T(8,128)(2,1)} %get-tuple-element.85.wo, bf16[768,512]{1,0:T(8,128)(2,1)} %get-tuple-element.86.xt, bf16[768,128]{1,0:T(8,128)(2,1)} %get-tuple-element.87.small, ...), custom_call_target="tpu_custom_call" | custom-call | flops 1024 | bytes 1024 | tf_op jit(solution)/shard_map/route/pallas_call | solution.py:1308
  243.2 0.0 all-gather.5.cloned.1.call-update
  243.3 0.6 pad_add_fusion.sc
  243.8 34.2 %experts_own.1 = (bf16[8,784,128]{2,1,0:T(8,128)(2,1)}, bf16[8,768,128]{2,1,0:T(8,128)(2,1)}, bf16[4,768,1024]{2,1,0:T(8,128)(2,1)}, bf16[4,768,1024]{2,1,0:T(8,...) custom-call(s32[2]{0:T(128)} %pad_add_fusion.sc, ...), custom_call_target="tpu_custom_call" | custom-call | flops 1024 | bytes 1024 | tf_op jit(solution)/shard_map/experts_own/pallas_call | solution.py:700
  278.1 77.7 %give_back.1 = (bf16[512,768]{1,0:T(8,128)(2,1)}, f32[2,16,512]{2,1,0:T(8,128)}, bf16[4,192,512]{2,1,0:T(8,128)(2,1)}, bf16[4,192,512]{2,1,0:T(8,128)(2,1)}, bf16[2,512,768]{2,1,0:T(8,128)(2,1)}) custom-call(bf16[8,784,128]{2,1,0:T(8,128)(2,1)} %get-tuple-element.93.ysend, bf16[8,768,128]{2,1,0:T(8,128)(2,1)} %get-tuple-element.94.rsend, ...), custom_call_target="tpu_custom_call" | custom-call | flops 1024 | bytes 1024 | tf_op jit(solution)/shard_map/give_back/pallas_call | solution.py:1308
  355.8 0.8 collective-permute-start
  356.6 1.3 stack.59.sc
  357.9 30.8 %attention_backward.1 = (bf16[3,256,384]{2,1,0:T(8,128)(2,1)}, bf16[3,256,384]{2,1,0:T(8,128)(2,1)}, bf16[3,256,384]{2,1,0:T(8,128)(2,1)}, bf16[3,256,384]{2,1,0:T(8,128)(2,1)}) custom-call(s32[5]{0:T(128)} %stack.59.sc, bf16[4,3,256,384]{3,2,1,0:T(8,128)(2,1)} %get-tuple-element.79.blocks, f32[3,72,2048]{2,1,0:T(8,128)} %get-tuple-element.100.m_ref, ...), custom_call_target="tpu_custom_call" | custom-call | flops 1024 | bytes 1024 | tf_op jit(solution)/shard_map/attention_backward/pallas_call | solution.py:450
  388.7 12.5 %collective-permute-start.1 = (bf16[3,256,384]{2,1,0:T(8,128)(2,1)}, bf16[3,256,384]{2,1,0:T(8,128)(2,1)S(1)}, u32[]{:S(2)}, u32[]{:S(2)}) collective-permute-start(bf16[3,256,384]{2,1,0:T(8,128)(2,1)} %get-tuple-element.103), channel_id=1, source_target_pairs={{0,2},{2,0},{4,6},{6,4},{1,3},{3,1},{5,7},{7,5},{8,10},{10,8},{12,... | collective-permute-start | bytes 1769480 | tf_op jit(solution)/shard_map/ppermute | solution.py:1345
  401.3 0.0 collective-permute-start.2
  401.3 2.4 collective-permute-start.3
  403.6 1.3 slice.24.gain
  405.0 0.7 copy.48
  405.6 0.7 pad_add_fusion.1.sc
  406.3 1.4 maximum_select_fusion
  407.7 50.8 %experts_more.1 = (bf16[4,768,1024]{2,1,0:T(8,128)(2,1)}, bf16[4,768,1024]{2,1,0:T(8,128)(2,1)}, bf16[4,2048,1024]{2,1,0:T(8,128)(2,1)}, bf16[4,2048,1024]{2,1,0:T(8,128)(2,1)}, bf16[4,2048,1024]{2,1,0:T(8,128)(2,1)}) custom-call(s32[4]{0:T(128)} %pad_add_fusion.1.sc, ...), custom_call_target="tpu_custom_call", output_to_operand_aliasing={{0}: (5, {}), {1}: (6, {}), {2}: (7, {}), {3}: (8, {}), {4}... | custom-call | flops 1024 | bytes 1024 | tf_op jit(solution)/shard_map/experts_more/pallas_call | solution.py:700
  458.6 0.8 copy-done.4
  459.4 0.2 copy-done.5
  459.6 0.2 copy-done.6
  459.8 10.3 %d_projection.1 = (bf16[2,512,768]{2,1,0:T(8,128)(2,1)}, bf16[4,592,384]{2,1,0:T(8,128)(2,1)}) custom-call(s32[5]{0:T(128)} %stack.59.sc, bf16[3,256,384]{2,1,0:T(8,128)(2,1)} %get-tuple-element.112.b0, bf16[3,256,384]{2,1,0:T(8,128)(2,1)} %copy-done.4, bf16[3,256,384]{2,1,0:T(8,128)(2,1)} %copy-done.5, bf16[3,256,384]{2,1,0:T(8,128)(2,1)} %copy-done.6, ...), custom_call_target="tpu_custom_call" | custom-call | flops 1024 | bytes 1024 | tf_op jit(solution)/shard_map/d_projection/pallas_call | solution.py:450
  470.1 147.1 %finish.1 = (bf16[4,8,3,192,256]{4,3,2,1,0:T(8,128)(2,1)}, bf16[2,512,768]{2,1,0:T(8,128)(2,1)}, f32[592,384]{1,0:T(8,128)}, f32[192,512]{1,0:T(8,128)}, f32[192,128]{1,0:T(8,128)}, /*index=5*/f32[8,384]{1,0:T(8,128)}) custom-call(bf16[4,768,1024]{2,1,0:T(8,128)(2,1)} %get-tuple-element.118.bx, bf16[4,768,1024]{2,1,0:T(8,128)(2,1)} %get-tuple-element.119.bg, ...), custom_call_target="tpu_custom_call" | custom-call | flops 1024 | bytes 1024 | tf_op jit(solution)/shard_map/finish/pallas_call | solution.py:1308
  617.2 1.1 slice_reduce_fusion
  618.3 1.0 slice_bitcast_fusion
  619.3 0.7 slice.26
  620.0 1.6 copy.49
  621.5 0.7 copy.50
  622.2 1.7 slice.29
  623.9 2.1 slice.28
  626.0 3.7 copy-done.2
  629.7 7.2 %place_grads.1 = (f32[8,2,192,1024]{3,2,1,0:T(8,128)}, f32[8,192,1024]{2,1,0:T(8,128)}) custom-call(s32[1]{0:T(128)} %bitcast.13.sc, bf16[4,8,3,192,256]{4,3,2,1,0:T(8,128)(2,1)S(1)} %copy-done.2), custom_call_target="tpu_custom_call" | custom-call | flops 1024 | bytes 1024 | tf_op jit(solution)/shard_map/place_grads/pallas_call | solution.py:840
  636.9 0.6 pad_maximum_fusion.3
  637.5 6.0 grad_tokens.1
  (23 shorter events, 0.1 us)
Async XLA Ops:
  7.2 189.5 %copy-start = (f32[2,512,12]{1,0,2:T(2,128)S(1)}, f32[2,512,12]{1,0,2:T(2,128)}, u32[]{:S(2)}) copy-start(f32[2,512,12]{1,0,2:T(2,128)} %param.13) | copy-start | bytes 147460
  7.2 400.5 %all-gather.7.cloned.1.call-start = ((), (), s32[]{:S(2)}) async-start(), calls=%async_computation.1 | async-start | bytes 7864320 | tf_op jit(solution)/shard_map/all_gather | solution.py:1408
  55.7 70.4 %copy-start.8 = (s32[2]{0:T(128)S(1)}, s32[2]{0:T(128)}, u32[]{:S(2)}) copy-start(s32[2]{0:T(128)} %param.15) | copy-start | bytes 28
  125.5 282.2 %all-gather.5.cloned.1.call-start = ((), (), s32[]{:S(2)}) async-start(), calls=%async_computation | async-start | bytes 8028160 | tf_op jit(solution)/shard_map/all_gather | solution.py:1415
  355.8 50.4 %collective-permute-start = (bf16[512,768]{1,0:T(8,128)(2,1)}, bf16[512,768]{1,0:T(8,128)(2,1)S(1)}, u32[]{:S(2)}, u32[]{:S(2)}) collective-permute-start(bf16[512,768]{1,0:T(8,128)(2,1)} %get-tuple-element.98), channel_id=1, source_target_pairs={{0,1},{1,0},{2,3},{3,2},{4,5},{5,4},{6,7},{7,6},{8,9},{9,8},{10,11... | collective-permute-start | bytes 2359304 | tf_op jit(solution)/shard_map/ppermute | solution.py:1342
  357.9 47.0 %copy-start.7 = (f32[2,16,512]{2,1,0:T(8,128)S(1)}, f32[2,16,512]{2,1,0:T(8,128)}, u32[]{:S(2)}) copy-start(f32[2,16,512]{2,1,0:T(8,128)} %get-tuple-element.126) | copy-start | bytes 196612
  357.9 48.3 %copy-start.3 = (bf16[512,768]{1,0:T(8,128)(2,1)S(1)}, bf16[512,768]{1,0:T(8,128)(2,1)}, u32[]{:S(2)}) copy-start(bf16[512,768]{1,0:T(8,128)(2,1)} %get-tuple-element.98) | copy-start | bytes 2359300
  388.7 69.8 %collective-permute-start.1 = (bf16[3,256,384]{2,1,0:T(8,128)(2,1)}, bf16[3,256,384]{2,1,0:T(8,128)(2,1)S(1)}, u32[]{:S(2)}, u32[]{:S(2)}) collective-permute-start(bf16[3,256,384]{2,1,0:T(8,128)(2,1)} %get-tuple-element.103), channel_id=1, source_target_pairs={{0,2},{2,0},{4,6},{6,4},{1,3},{3,1},{5,7},{7,5},{8,10},{10,8},{12,... | collective-permute-start | bytes 1769480 | tf_op jit(solution)/shard_map/ppermute | solution.py:1345
  401.3 57.3 %collective-permute-start.2 = (bf16[3,256,384]{2,1,0:T(8,128)(2,1)}, bf16[3,256,384]{2,1,0:T(8,128)(2,1)S(1)}, u32[]{:S(2)}, u32[]{:S(2)}) collective-permute-start(bf16[3,256,384]{2,1,0:T(8,128)(2,1)} %get-tuple-element.104), channel_id=1, source_target_pairs={{0,4},{2,6},{4,0},{6,2},{1,5},{3,7},{5,1},{7,3},{8,12},{10,14},{12... | collective-permute-start | bytes 1769480 | tf_op jit(solution)/shard_map/ppermute | solution.py:1345
  401.3 57.3 %collective-permute-start.3 = (bf16[3,256,384]{2,1,0:T(8,128)(2,1)}, bf16[3,256,384]{2,1,0:T(8,128)(2,1)S(1)}, u32[]{:S(2)}, u32[]{:S(2)}) collective-permute-start(bf16[3,256,384]{2,1,0:T(8,128)(2,1)} %get-tuple-element.105), channel_id=1, source_target_pairs={{0,6},{2,4},{4,2},{6,0},{1,7},{3,5},{5,3},{7,1},{8,14},{10,12},{12... | collective-permute-start | bytes 1769480 | tf_op jit(solution)/shard_map/ppermute | solution.py:1345
  458.5 0.8 copy-start.4
  458.5 1.0 copy-start.5
  458.6 1.2 copy-start.6
  626.0 3.7 copy-start.2
  637.5 6.0 copy-start.1
Sparse Core Ops, SparseCore 0:
  125.6 130.1 all-gather.6
  257.4 132.2 all-gather.4

commit v4 on v3

--- a/solution.py
+++ b/solution.py
@@ -491,78 +491,6 @@
     return (key <= query) | (key < prefix)
 
 
-def attn_kernel(prefix_ref, blocks, m0, l1, l2, l3, m3, mixed_in, m_ref, w_ref, wt_ref,
-                q_s, k_s, v_s, st, z_sems, w_sems):
-    f, z, x = here()
-    barrier = pltpu.get_barrier_semaphore()
-    for d in range(1, 4):
-        pl.semaphore_signal(barrier, inc=1, device_id=(f, flip4(z, d), x), device_id_type=MESH)
-    pl.semaphore_signal(barrier, inc=1, device_id=(flip4(f, 2), z, flip2(x, 1)), device_id_type=MESH)
-    pl.semaphore_wait(barrier, 4)
-    far = [
-        to_plane(5, m3.at[0, m], w_ref.at[m, 384:576, 1024:2048], w_sems, m) for m in (1, 2)
-    ] + [to_plane(5, m3.at[1, m], w_ref.at[m, 576:768, 1024:2048], w_sems, 3 + m) for m in range(3)]
-    for c in far:
-        c.start()
-    prefix = prefix_ref[0]
-    unpack_qkv(z, blocks, q_s, k_s, v_s)
-    scale = HEAD_DIM ** (-0.5) * LOG2E
-
-    def unit(j, carry):
-        vt = v_s[j].T
-        for i, tiles in attn_masks(prefix):
-            q = q_s[j, i * 512 : (i + 1) * 512, :]
-            scores = []
-            for t, masked in tiles:
-                s = mm_nt(k_s[j, t * 512 : (t + 1) * 512, :], q)
-                if masked:
-                    s = jnp.where(allowed_tile(t, i, prefix), s, -1e30)
-                scores.append(s)
-            top = scores[0].max(axis=0, keepdims=True)
-            for s in scores[1:]:
-                top = jnp.maximum(top, s.max(axis=0, keepdims=True))
-            total = jnp.zeros_like(top)
-            acc = jnp.zeros((HEAD_DIM, 512), F32)
-            for (t, masked), s in zip(tiles, scores):
-                p = jnp.exp2((s - top) * scale)
-                total = total + p.sum(axis=0, keepdims=True)
-                acc = acc + mm(vt[:, t * 512 : (t + 1) * 512], p.astype(BF))
-            mixed = acc / total
-            cols = slice(i * 512, (i + 1) * 512)
-            m_ref[j, 0:HEAD_DIM, cols] = mixed
-            m_ref[j, HEAD_DIM : HEAD_DIM + 8, cols] = jnp.broadcast_to(
-                top * scale + jnp.log2(total), (8, 512)
-            )
-            st[i, pl.ds(pl.multiple_of(j * HEAD_DIM, HEAD_DIM), HEAD_DIM), :] = mixed.astype(BF)
-        return carry
-
-    lax.fori_loop(0, 3, unit, 0)
-    copies = [to_column(d, st.at[flip4(z, d)], mixed_in.at[d], z_sems) for d in (3, 2, 1)]
-    for c in copies:
-        c.start()
-    mixed_in[0] = st[z]
-    w_ref[0, 384:576, 1024:2048] = l3[...]
-
-    def turn(m, r, jx):
-        wt_ref[m, jx * 1024 : (jx + 1) * 1024, r * 192 : (r + 1) * 192] = w_ref[
-            m, r * 192 : (r + 1) * 192, jx * 1024 : (jx + 1) * 1024
-        ].T
-
-    for j, b in enumerate((m0, l1, l2)):
-        for cc in range(2):
-            for m in range(3):
-                r, jx = 2 * (j // 2) + cc, j % 2
-                w_ref[m, r * 192 : (r + 1) * 192, jx * 1024 : (jx + 1) * 1024] = b[cc, m]
-                turn(m, r, jx)
-    for c in far:
-        c.wait()
-    for r in (2, 3):
-        for m in range(3):
-            turn(m, r, 1)
-    for c in copies:
-        c.wait()
-
-
 def row_state(hidden, gain, gate_t, prev, routes, f, x):
     rows = hidden.shape[1]
     inverse = lax.rsqrt(jnp.mean(hidden * hidden, axis=0, keepdims=True) + epsilon)
@@ -594,17 +522,7 @@
     )
 
 
-def expert_body(first, sc, xs, gs, w, wt, *refs):
-    if first:
-        y_ref, r_ref = refs[0:2]
-        refs = refs[2:]
-    else:
-        refs = refs[5:]
-    bx, bg, ba, bp, bu = refs[:5]
-    refs = refs[5:]
-    xt, gt, grow = refs[:3]
-    if first:
-        din, res, graw = refs[3:]
+def expert_body(sc, xs, gs, w, wt, y_ref, r_ref, bx, bg, ba, bp, bu, xt, gt, grow, din, res, graw):
     j = pl.program_id(1)
     f = sc[pl.num_programs(0)]
 
@@ -622,12 +540,10 @@
                 to, at = slice(r * 192, (r + 1) * 192), shard(r)
                 xt[to, cols] = xs[0, k, at]
                 g = gs[0, k, at]
-                if first:
-                    graw[to, cols] = g
+                graw[to, cols] = g
                 gt[to, cols] = (g.astype(F32) * gate).astype(BF)
-        if first:
-            din[...] = jnp.zeros_like(din)
-            res[...] = jnp.zeros_like(res)
+        din[...] = jnp.zeros_like(din)
+        res[...] = jnp.zeros_like(res)
         bx[0] = xt[...]
         bg[0] = gt[...]
 
@@ -643,81 +559,118 @@
     du = (da * silu).astype(BF)
     bp[0] = dp
     bu[0] = du
-    if first:
-        din[...] += mm(w[0], dp) + mm(w[1], du)
-        res[...] += mm(w[2], act)
-
-        @pl.when(j == pl.num_programs(1) - 1)
-        def _():
-            row = lax.broadcasted_iota(jnp.int32, (8, CAPACITY), 0)
-            for k in range(8):
-                cols = slice(k * CAPACITY, (k + 1) * CAPACITY)
-                r = res[:, cols]
-                dg = jnp.sum(graw[:, cols].astype(F32) * r, axis=0, keepdims=True)
-                high = dg.astype(BF).astype(F32)
-                tail = jnp.concatenate(
-                    [jnp.where(row == k, high, 0.0), jnp.where(row == k, dg - high, 0.0)], axis=0
-                )
-                y_ref[k, 768:784, :] = tail.astype(BF)
-                r = (r * grow[0:1, cols]).astype(BF)
-                for q in range(4):
-                    y_ref[k, shard(q), :] = din[q * 192 : (q + 1) * 192, cols].astype(BF)
-                    r_ref[k, shard(q), :] = r[q * 192 : (q + 1) * 192]
-
-
-def expert_call(first, planes, xs, gs, w, wt, held):
-    tile = 512
-    steps = w.shape[2] // tile
-    slots = 8 * CAPACITY
-    width = w.shape[1]
-    n_ctx = 4
-    buffers = [
-        out((n_ctx, width, slots)), out((n_ctx, width, slots)),
-        out((n_ctx, w.shape[2], slots)), out((n_ctx, w.shape[2], slots)), out((n_ctx, w.shape[2], slots)),
-    ]
-    at = (lambda i, j, s: (0, 0, 0, 0)) if first else (lambda i, j, s: (s[i], 0, 0, 0))
-    specs_in = [pl.BlockSpec((1,) + a.shape[1:], at) for a in (xs, gs)] + [
-        pl.BlockSpec((3, width, tile), lambda i, j, s: (0, 0, j)),
-        pl.BlockSpec((3, tile, width), lambda i, j, s: (0, j, 0)),
-    ]
-    buffer_specs = [
-        pl.BlockSpec((1, width, slots), lambda i, j, s: (s[i], 0, 0)),
-        pl.BlockSpec((1, width, slots), lambda i, j, s: (s[i], 0, 0)),
-    ] + [pl.BlockSpec((1, tile, slots), lambda i, j, s: (s[i], j, 0))] * 3
-    scratch = [
-        pltpu.VMEM((width, slots), BF), pltpu.VMEM((width, slots), BF), pltpu.VMEM((8, slots), F32),
-    ]
-    outs, specs_out, aliases, extra_in = list(buffers), list(buffer_specs), {}, []
-    if first:
-        packet = [out((8, width + 16, CAPACITY)), out((8, width, CAPACITY))]
-        outs = packet + outs
-        specs_out = [pl.BlockSpec(p.shape, lambda i, j, s: (0, 0, 0)) for p in packet] + specs_out
-        scratch += [pltpu.VMEM((width, slots), F32)] * 2 + [pltpu.VMEM((width, slots), BF)]
-    else:
-        extra_in = list(held)
-        specs_in += [pl.BlockSpec(memory_space=pl.ANY)] * 5
-        aliases = {5 + i: i for i in range(5)}
+    din[...] += mm(w[0], dp) + mm(w[1], du)
+    res[...] += mm(w[2], act)
+
+    @pl.when(j == pl.num_programs(1) - 1)
+    def _():
+        row = lax.broadcasted_iota(jnp.int32, (8, CAPACITY), 0)
+        for k in range(8):
+            cols = slice(k * CAPACITY, (k + 1) * CAPACITY)
+            r = res[:, cols]
+            dg = jnp.sum(graw[:, cols].astype(F32) * r, axis=0, keepdims=True)
+            high = dg.astype(BF).astype(F32)
+            tail = jnp.concatenate(
+                [jnp.where(row == k, high, 0.0), jnp.where(row == k, dg - high, 0.0)], axis=0
+            )
+            y_ref[k, 768:784, :] = tail.astype(BF)
+            r = (r * grow[0:1, cols]).astype(BF)
+            for q in range(4):
+                y_ref[k, shard(q), :] = din[q * 192 : (q + 1) * 192, cols].astype(BF)
+                r_ref[k, shard(q), :] = r[q * 192 : (q + 1) * 192]
+
+
+def more_body(sc, xs, g0, g1, g2, g3, wt, h0, h1, h2, h3, h4, bx, bg, ba, bp, bu, xt, gt):
+    f = sc[3]
+
+    @pl.when(pl.program_id(1) == 0)
+    def _():
+        for k in range(8):
+            cols = slice(k * CAPACITY, (k + 1) * CAPACITY)
+            g = (g0, g1, g2, g3)[2 * (k // 4) + k % 2]
+            pair = xs[0, k, 768:784].astype(F32)
+            gate = pair[k : k + 1] + pair[8 + k : 9 + k]
+            for r in range(4):
+                to = slice(r * 192, (r + 1) * 192)
+                at = pl.ds(pl.multiple_of(jnp.bitwise_xor(f, r) * 192, 64), 192)
+                xt[to, cols] = xs[0, k, at]
+                gt[to, cols] = (g[(k // 2) % 2, 0, at].astype(F32) * gate).astype(BF)
+        bx[0] = xt[...]
+        bg[0] = gt[...]
+
+    x = xt[...]
+    pre = mm(wt[0], x)
+    up = mm(wt[1], x)
+    sig = 1.0 / (1.0 + jnp.exp(-pre))
+    silu = pre * sig
+    ba[0] = (silu * up).astype(BF)
+    da = mm(wt[2], gt[...])
+    bp[0] = (da * up * (sig * (1.0 + pre * (1.0 - sig)))).astype(BF)
+    bu[0] = (da * silu).astype(BF)
+
+
+def more_call(planes, x_more, g_more, wt, held):
+    tile, slots, width = 512, 8 * CAPACITY, x_more.shape[2] - 16
+    row = lambda i, j, s: (s[i], 0, 0)
+    tall = lambda i, j, s: (s[i], j, 0)
     return pl.pallas_call(
-        functools.partial(expert_body, first),
-        out_shape=tuple(outs),
+        more_body,
+        out_shape=tuple(out(h.shape) for h in held),
         grid_spec=pltpu.PrefetchScalarGridSpec(
-            num_scalar_prefetch=1, grid=(planes.shape[0] - 1, steps), in_specs=specs_in,
-            out_specs=tuple(specs_out), scratch_shapes=scratch,
+            num_scalar_prefetch=1, grid=(planes.shape[0] - 1, wt.shape[1] // tile),
+            in_specs=[pl.BlockSpec((1, 8, width + 16, CAPACITY), lambda i, j, s: (s[i], 0, 0, 0))]
+            + [pl.BlockSpec((2, 1, width, CAPACITY), lambda i, j, s: (0, i, 0, 0))] * 4
+            + [pl.BlockSpec((3, tile, width), lambda i, j, s: (0, j, 0))]
+            + [HBM] * 5,
+            out_specs=tuple([pl.BlockSpec((1, width, slots), row)] * 2 + [pl.BlockSpec((1, tile, slots), tall)] * 3),
+            scratch_shapes=[pltpu.VMEM((width, slots), BF), pltpu.VMEM((width, slots), BF)],
         ),
-        input_output_aliases=aliases,
+        input_output_aliases={7 + i: i for i in range(5)},
+        compiler_params=pltpu.CompilerParams(vmem_limit_bytes=56 * MIB),
+        cost_estimate=COST,
+        name="experts_more",
+    )(planes, x_more, *g_more, wt, *held)
+
+
+def expert_call(plane, xs, gs, w, wt):
+    tile, n_ctx = 512, 4
+    slots, width = 8 * CAPACITY, w.shape[1]
+    packet = [out((8, width + 16, CAPACITY)), out((8, width, CAPACITY))]
+    wide, high = out((n_ctx, width, slots)), out((n_ctx, w.shape[2], slots))
+    return pl.pallas_call(
+        expert_body,
+        out_shape=tuple(packet + [wide] * 2 + [high] * 3),
+        grid_spec=pltpu.PrefetchScalarGridSpec(
+            num_scalar_prefetch=1, grid=(1, w.shape[2] // tile),
+            in_specs=[pl.BlockSpec((1,) + a.shape[1:], lambda i, j, s: (0, 0, 0, 0)) for a in (xs, gs)]
+            + [
+                pl.BlockSpec((3, width, tile), lambda i, j, s: (0, 0, j)),
+                pl.BlockSpec((3, tile, width), lambda i, j, s: (0, j, 0)),
+            ],
+            out_specs=tuple(
+                [pl.BlockSpec(p.shape, lambda i, j, s: (0, 0, 0)) for p in packet]
+                + [pl.BlockSpec((1, width, slots), lambda i, j, s: (s[0], 0, 0))] * 2
+                + [pl.BlockSpec((1, tile, slots), lambda i, j, s: (s[0], j, 0))] * 3
+            ),
+            scratch_shapes=[pltpu.VMEM((width, slots), BF)] * 2
+            + [pltpu.VMEM((8, slots), F32)]
+            + [pltpu.VMEM((width, slots), F32)] * 2
+            + [pltpu.VMEM((width, slots), BF)],
+        ),
         compiler_params=pltpu.CompilerParams(vmem_limit_bytes=58 * MIB),
         cost_estimate=COST,
-        name="experts_own" if first else "experts_more",
-    )(planes, xs, gs, w, wt, *extra_in)
+        name="experts_own",
+    )(plane, xs, gs, w, wt)
 
 
 def finish_kernel(bx, bg, bp, bu, ba, dn, gq, og, gin, dn_other, att, outg, small_f, line_f,
                   x_s, g_s, tiles, acc, send, q1, o1, qm, om, q2, o2, qk, ok, q3, o3, q4, o4, s_x, l_x,
-                  xg_sems, tile_sems, send_sems, own_sems, step_sems, dn_sems):
+                  xg_sems, tile_sems, send_sems, own_sems, step_sems, dn_sems, over_sems):
     f, z, x = here()
     core, y = f % 2, f // 2
     cols = tiles.shape[2]
-    parts, planes = gin.shape[0], bx.shape[0]
+    planes = bx.shape[0]
+    parity = z % 2
     greet()
     loads = []
     for p in range(planes):
@@ -728,10 +681,11 @@
     def tile_copy(part, m, p):
         src = (bp, bu, ba)[m]
         return pltpu.make_async_copy(
-            src.at[p, :, pl.ds(part * cols, cols), :], tiles.at[p % 2], tile_sems.at[p % 2]
+            src.at[p, :, pl.ds(pl.multiple_of(part * cols, cols), cols), :], tiles.at[p % 2], tile_sems.at[p % 2]
         )
 
-    for c in [tile_copy(0, 0, 0)] + loads:
+    plan = [(parity, m) for m in range(3)] + [(part, m) for part in (2, 3) for m in range(3)]
+    for c in [tile_copy(*plan[0], 0)] + loads:
         c.start()
     swap = to_plane(1, dn, dn_other, dn_sems)
     swap.start()
@@ -776,52 +730,68 @@
             device_id=(f, flip4(z, d), x), device_id_type=MESH,
         )
 
-    flying, sent, steps = [], [], []
-    for part in range(parts):
-        for m in range(3):
-            rows_s, at = (g_s, 1) if m == 2 else (x_s, 0)
-            acc[...] = jnp.zeros_like(acc)
-
-            def plane_step(p, carry, part=part, m=m, rows_s=rows_s, at=at):
-                tile_copy(part, m, p).wait()
-
-                @pl.when(p < planes - 1)
+    def hand_over(m):
+        for c in sent[m]:
+            c.wait()
+        over = pltpu.make_async_remote_copy(
+            src_ref=gin.at[parity, :, m], dst_ref=gin.at[parity, :, m], send_sem=over_sems.at[0, m],
+            recv_sem=over_sems.at[1, m], device_id=(f, flip4(z, 1), x), device_id_type=MESH,
+        )
+        over.start()
+        return over
+
+    sent, steps, overs = [], [], []
+    for number, (part, m) in enumerate(plan):
+        rows_s, at = (g_s, 1) if m == 2 else (x_s, 0)
+        acc[...] = jnp.zeros_like(acc)
+
+        def plane_step(p, carry, number=number, part=part, m=m, rows_s=rows_s, at=at):
+            tile_copy(part, m, p).wait()
+
+            @pl.when(p < planes - 1)
+            def _():
+                tile_copy(part, m, p + 1).start()
+
+            if number + 1 < len(plan):
+
+                @pl.when(p == planes - 1)
                 def _():
-                    tile_copy(part, m, p + 1).start()
-
-                if part < parts - 1 or m < 2:
-
-                    @pl.when(p == planes - 1)
-                    def _():
-                        tile_copy(part + (m + 1) // 3, (m + 1) % 3, 0).start()
-
-                if part == 0 and m != 1:
-                    pltpu.make_async_copy((bx, bg)[at].at[p], rows_s.at[p], xg_sems.at[at, p]).wait()
-                for xh in range(2):
-                    acc[xh] += mm_nt(rows_s[p], tiles[p % 2, xh])
-                return carry
-
-            lax.fori_loop(0, planes, plane_step, 0)
-            for k in (5, 7, 4, 6, 1, 3, 2, 0):
-                r, jx = k // 2, k % 2
-                send[part, k, m] = acc[jx, r * 192 : (r + 1) * 192, :].astype(BF)
-                src, dst, number = send.at[part, k, m], gin.at[part, k, m], 3 * part + m
-                if k:
-                    sent.append(to_plane(k, src, dst, send_sems, number * 8 + k))
-                else:
-                    sent.append(pltpu.make_async_copy(src, dst, own_sems.at[number]))
-                sent[-1].start()
-        for c in steps:
-            c.wait()
-        steps = after(part)
-        for c in steps:
-            c.start()
+                    tile_copy(*plan[number + 1], 0).start()
+
+            if number in (0, 2):
+                pltpu.make_async_copy((bx, bg)[at].at[p], rows_s.at[p], xg_sems.at[at, p]).wait()
+            for xh in range(2):
+                acc[xh] += mm_nt(rows_s[p], tiles[p % 2, xh])
+            return carry
+
+        lax.fori_loop(0, planes, plane_step, 0)
+        sent.append([])
+        for k in (5, 7, 4, 6, 1, 3, 2, 0):
+            r, jx = k // 2, k % 2
+            send[number, k] = acc[jx, r * 192 : (r + 1) * 192, :].astype(BF)
+            src, dst = send.at[number, k], gin.at[part, k, m]
+            if k:
+                sent[-1].append(to_plane(k, src, dst, send_sems, number * 8 + k))
+            else:
+                sent[-1].append(pltpu.make_async_copy(src, dst, own_sems.at[number]))
+            sent[-1][-1].start()
+        if number in (1, 3, 5, 8):
+            for c in steps:
+                c.wait()
+            steps = after((1, 3, 5, 8).index(number))
+            for c in steps:
+                c.start()
+        if number > 5:
+            overs.append(hand_over(number - 6))
     for c in steps:
         c.wait()
     small_f[...] = s_x[0] + s_x[1]
     line_f[...] = l_x[0] + l_x[1]
     swap.wait()
-    for c in sent:
+    for copies in sent[3:]:
+        for c in copies:
+            c.wait()
+    for c in overs:
         c.wait()
 
 
@@ -943,13 +913,25 @@
         gq_ref[f, 576:592, :] = jnp.concatenate([piece, piece], axis=1).astype(BF)
 
 
-def tokens_kernel(sc, tokens, gain, dh, own, recv, o_ref):
+def last_kernel(sc, tokens, gain, dh, own, recv, att, outg, small_f, line_f, layer_own, layer_other, gprev_t,
+                layer, o_ref, gprev, gains, gq, go, ggate, gconst):
+    x = sc[2]
     for s in range(2):
         v = tokens[s].astype(F32)
         inverse = lax.rsqrt(jnp.mean(v * v, axis=-1, keepdims=True) + epsilon)
         u = (own[s].astype(F32) + recv[s].astype(F32)) * gain[...]
         mean = jnp.mean(u * v, axis=-1, keepdims=True)
         o_ref[s] = dh[s].astype(F32) + inverse * u - v * (inverse * inverse * inverse * mean)
+        gprev[s] = gprev_t[s].T[:, 0:NEXP]
+    layer[x] = layer_own[...]
+    layer[1 - x] = layer_other[...]
+    for c in range(3):
+        gq[c] = att[c * 192 : (c + 1) * 192, :]
+    go[...] = outg[:, 0:384]
+    ggate[...] = small_f[:, 0:16]
+    turned = small_f[...].T
+    gconst[...] = turned[16:18]
+    gains[...] = jnp.concatenate([line_f[0:1, 0:192], turned[18:19]], axis=0)
 
 
 def flip4(v, k):
@@ -984,6 +966,23 @@
     pl.semaphore_wait(barrier, 10)
 
 
+def slot_hot(named, f, x):
+    rows = named.shape[1]
+    named = expert_flip(named, f, x)
+    first, second = named[0:1], named[1:2]
+    ids = lax.broadcasted_iota(jnp.int32, (16, rows), 0)
+    hits = ((ids == first) | (ids == second)).astype(F32)
+    before = lax.broadcasted_iota(jnp.int32, (rows, rows), 0)
+    after = lax.broadcasted_iota(jnp.int32, (rows, rows), 1)
+    upper = (before <= after).astype(F32).astype(BF)
+    places = mm(hits.astype(BF), upper) - 1.0
+    slots = lax.broadcasted_iota(jnp.int32, (CAPACITY, rows), 0).astype(F32)
+    return [
+        jnp.where((slots == places[k : k + 1]) & (hits[k : k + 1] > 0.5), 1.0, 0.0).astype(BF)
+        for k in range(NFFN)
+    ]
+
+
 def greet_plane():
     f, z, x = here()
     barrier = pltpu.get_barrier_semaphore()
@@ -1003,10 +1002,11 @@
     )
 
 
-def to_column(d, src, dst, sems):
+def to_column(d, src, dst, sems, at=None):
     f, z, x = here()
+    at = d if at is None else at
     return pltpu.make_async_remote_copy(
-        src_ref=src, dst_ref=dst, send_sem=sems.at[0, d], recv_sem=sems.at[1, d],
+        src_ref=src, dst_ref=dst, send_sem=sems.at[0, at], recv_sem=sems.at[1, at],
         device_id=(f, flip4(z, d), x), device_id_type=MESH,
     )
 
@@ -1018,7 +1018,7 @@
 
 def gather_kernel(qkv, wo, smallp, routes, gy_both, gu, dw,
                   hot, gyt, gin, w_out, wo_out, small_out, small_t, m0, m1, m2, m3,
-                  packs, outs_in, smalls, gsend, pack_sems, small_sems, g_sems, w_sems, own_sems):
+                  packs, outs_in, smalls, gsend, own_w, pack_sems, small_sems, g_sems, w_sems, own_sems):
     f, z, x = here()
     barrier = pltpu.get_barrier_semaphore()
     for k in range(1, 8):
@@ -1037,37 +1037,24 @@
     beside = shares(2, 1, qkv, wo, smallp)
     for c in over + beside:
         c.start()
-    moves = []
+    moves, inward, outward = [], [], []
     for j, m in enumerate((m0, m1, m2, m3)):
         for cc in range(2):
             owner = flip4(flip4(f, 2 * (j // 2)), cc)
             e = 2 * owner + flip2(x, j % 2)
             for part in range(2):
-                src = gu.at[e] if part == 0 else dw.at[e]
-                dst = m.at[cc, pl.ds(0, 2)] if part == 0 else m.at[cc, pl.ds(2, 1)]
-                at = 2 * j + part
+                src, at = (gu, dw)[part].at[e], pl.ds(2 * part, 2 - part)
                 if cc:
-                    moves.append(to_plane(2, src, dst, w_sems, at))
+                    moves.append(to_plane(2, src, m.at[1, at], w_sems, 2 * j + part))
                 else:
-                    moves.append(pltpu.make_async_copy(src, dst, own_sems.at[at]))
-    for c in moves:
+                    inward.append(pltpu.make_async_copy(src, own_w.at[j, at], own_sems.at[2 * j + part]))
+        outward.append(pltpu.make_async_copy(own_w.at[j], m.at[0], own_sems.at[8 + j]))
+    for c in moves + inward:
         c.start()
 
-    rows = gy_both.shape[1]
-    named = expert_flip(routes[...], f, x)
-    first, second = named[0:1], named[1:2]
     g_t = gy_both[x].T
     gyt[...] = g_t
-    ids = lax.broadcasted_iota(jnp.int32, (16, rows), 0)
-    hits = ((ids == first) | (ids == second)).astype(F32)
-    before = lax.broadcasted_iota(jnp.int32, (rows, rows), 0)
-    after = lax.broadcasted_iota(jnp.int32, (rows, rows), 1)
-    upper = (before <= after).astype(F32).astype(BF)
-    places = mm(hits.astype(BF), upper) - 1.0
-    slots = lax.broadcasted_iota(jnp.int32, (CAPACITY, rows), 0).astype(F32)
-    for k in range(NFFN):
-        one = jnp.where((slots == places[k : k + 1]) & (hits[k : k + 1] > 0.5), 1.0, 0.0)
-        one = one.astype(BF)
+    for k, one in enumerate(slot_hot(routes[...], f, x)):
         hot[k * CAPACITY : (k + 1) * CAPACITY, :] = one
         block = mm_nt(g_t, one).astype(BF)
         if k == 0:
@@ -1085,6 +1072,10 @@
         wo_out[at, :] = o[...]
         small_out[at, :] = small[...]
 
+    for c in inward:
+        c.wait()
+    for c in outward:
+        c.start()
     assemble(0, qkv, wo, smallp)
     for c in over:
         c.wait_recv()
@@ -1101,26 +1092,36 @@
     small_t[...] = small_out[...].astype(F32).T
     for c in over + beside + onward:
         c.wait_send()
-    for c in moves + g_copies:
+    for c in moves + g_copies + outward:
         c.wait()
 
 
-def project_kernel(tokens, w, small_t, cos_ref, sin_ref, m1, m2, m3, nt, xt, blocks, l1, l2, l3,
-                   n_s, st, z_sems, w_sems):
+def attend_kernel(prefix_ref, tokens, w, small_t, cos_ref, sin_ref, m0, m1, m2, m3,
+                  nt, xt, blocks, mixed_in, m_ref, w_hbm, wt_hbm,
+                  n_s, st, q_s, k_s, v_s, mix, w_s, wt_s,
+                  z_sems, x_sems, w_sems, own_sems, out_sems):
     f, z, x = here()
-    barrier = pltpu.get_barrier_semaphore()
-    for d in range(1, 4):
-        pl.semaphore_signal(barrier, inc=1, device_id=(f, flip4(z, d), x), device_id_type=MESH)
-    for k in (1, 4, 5):
-        pl.semaphore_signal(
-            barrier, inc=1, device_id=(flip4(f, k // 2), z, flip2(x, k % 2)), device_id_type=MESH
+    greet()
+
+    def home(ref, m, j, cc):
+        r, jx = 2 * (j // 2) + cc, j % 2
+        return ref.at[m, r * 192 : (r + 1) * 192, jx * 1024 : (jx + 1) * 1024]
+
+    pieces = [(cc, m) for cc in range(2) for m in range(3)]
+    arrivals = [[
+        pltpu.make_async_copy(m0.at[cc, m], home(w_s, m, 0, cc), own_sems.at[3 * cc + m]) for cc, m in pieces
+    ]]
+    for j, message in ((1, m1), (2, m2), (3, m3)):
+        k = 4 * (j // 2) + j % 2
+        arrivals.append(
+            [
+                to_plane(k, message.at[cc, m], home(w_s, m, j, cc), w_sems, 8 * j + 3 * cc + m)
+                for cc, m in pieces
+            ]
         )
-    pl.semaphore_wait(barrier, 6)
-    weights = [
-        to_plane(1, m1, l1, w_sems), to_plane(4, m2, l2, w_sems), to_plane(5, m3.at[0, 0], l3, w_sems),
-    ]
-    for c in weights:
-        c.start()
+    for j in (1, 2, 0, 3):
+        for c in arrivals[j]:
+            c.start()
     gain = small_t[16:17]
     cos = jnp.concatenate([cos_ref[...]] * 3, axis=1)
     sin = jnp.concatenate([sin_ref[...]] * 3, axis=1)
@@ -1146,25 +1147,92 @@
                     for a in (q, k, v)
                 ]
                 st[d, j] = jnp.concatenate(parts, axis=1)
-
-            @pl.when(d > 0)
-            def _(d=d, b=2 * s + half):
-                pltpu.make_async_remote_copy(
-                    src_ref=st.at[d], dst_ref=blocks.at[d], send_sem=z_sems.at[0, d],
-                    recv_sem=z_sems.at[1, d], device_id=(f, b, x), device_id_type=MESH,
-                ).start()
-
-    z_copies = [to_column(d, st.at[d], blocks.at[d], z_sems) for d in (1, 2, 3)]
+    unit_copies = [
+        [to_column(d, st.at[d, j], blocks.at[d, j], z_sems, 4 * j + d) for d in (3, 2, 1)] for j in range(3)
+    ]
+    for copies in unit_copies:
+        for c in copies:
+            c.start()
     blocks[0] = st[0]
     for s in range(2):
         nt[:, s * rows : (s + 1) * rows] = n_s[s].T
     xt[...] = tokens[x].T
-    for c in z_copies + weights:
+    flushes = []
+
+    def settle(j):
+        for c, (cc, m) in zip(arrivals[j], pieces):
+            c.wait()
+            r, jx = 2 * (j // 2) + cc, j % 2
+            part = home(w_s, m, j, cc)
+            wt_s[m, jx * 1024 : (jx + 1) * 1024, r * 192 : (r + 1) * 192] = part[...].T
+            flushes.append(
+                pltpu.make_async_copy(part, home(w_hbm, m, j, cc), out_sems.at[6 * j + 3 * cc + m])
+            )
+            flushes[-1].start()
+
+    settle(0)
+    prefix = prefix_ref[0]
+    scale = HEAD_DIM ** (-0.5) * LOG2E
+    sent = []
+    for j in range(3):
+        for c in unit_copies[j]:
+            c.wait_recv()
+        for d in range(4):
+            base = pl.multiple_of(flip4(z, d) * 512, 512)
+            blk = blocks[d, j]
+            for r in range(2):
+                at = pl.ds(base + r * 256, 256)
+                for number, to in enumerate((q_s, k_s, v_s)):
+                    col = r * 192 + number * HEAD_DIM
+                    to[at, :] = blk[:, col : col + HEAD_DIM]
+        vt = v_s[...].T
+        for i, tiles in attn_masks(prefix):
+            q = q_s[i * 512 : (i + 1) * 512, :]
+            scores = []
+            for t, masked in tiles:
+                s = mm_nt(k_s[t * 512 : (t + 1) * 512, :], q)
+                if masked:
+                    s = jnp.where(allowed_tile(t, i, prefix), s, -1e30)
+                scores.append(s)
+            top = scores[0].max(axis=0, keepdims=True)
+            for s in scores[1:]:
+                top = jnp.maximum(top, s.max(axis=0, keepdims=True))
+            total = jnp.zeros_like(top)
+            acc = jnp.zeros((HEAD_DIM, 512), F32)
+            for (t, masked), s in zip(tiles, scores):
+                p = jnp.exp2((s - top) * scale)
+                total = total + p.sum(axis=0, keepdims=True)
+                acc = acc + mm(vt[:, t * 512 : (t + 1) * 512], p.astype(BF))
+            got = acc / total
+            cols = slice(i * 512, (i + 1) * 512)
+            m_ref[j, 0:HEAD_DIM, cols] = got
+            m_ref[j, HEAD_DIM : HEAD_DIM + 8, cols] = jnp.broadcast_to(top * scale + jnp.log2(total), (8, 512))
+            mix[i, j] = got.astype(BF)
+        for d in (3, 2, 1):
+            sent.append(
+                to_column(d, mix.at[flip4(z, d), j], mixed_in.at[d, j * 64 : (j + 1) * 64], x_sems, 4 * j + d)
+            )
+            sent[-1].start()
+        mixed_in[0, j * 64 : (j + 1) * 64] = mix[z, j]
+    settle(1)
+    settle(2)
+    half = pltpu.make_async_copy(wt_s.at[:, 0:1024], wt_hbm.at[:, 0:1024], out_sems.at[24])
+    half.start()
+    settle(3)
+    rest = pltpu.make_async_copy(wt_s.at[:, 1024:2048], wt_hbm.at[:, 1024:2048], out_sems.at[25])
+    rest.start()
+    for copies in unit_copies:
+        for c in copies:
+            c.wait_send()
+    for c in sent:
         c.wait()
-
-
-def route_kernel(land, wo, xt, small, small_t, prev, routes, hot,
-                 mixed, hidden_ref, xin, attn_send, attn_land, xsend, a_sems, x_sems):
+    for c in flushes + [half, rest]:
+        c.wait()
+
+
+def route_kernel(land, wo, xt, small, small_t, prev, routes, hot, g_rows,
+                 mixed, hidden_ref, xin, m0, m1, m2, m3,
+                 attn_send, attn_land, xsend, beside, a_sems, x_sems, b_sems):
     f, z, x = here()
     greet_plane()
     for s in range(2):
@@ -1175,6 +1243,22 @@
     swap.start()
     own = mm(wo[...], mixed[x]).astype(BF).astype(F32)
     own = own + xt[...].astype(F32)
+    messages = (m0, m1, m2, m3)
+    rows = hidden_ref.shape[1]
+    for i in range(1, 4):
+        block = g_rows[flip4(z, i)]
+        named = block[rows : rows + 16].astype(F32)[0:2, 0:rows].astype(jnp.int32)
+        g_t = block[0:rows].T
+        for k, one in enumerate(slot_hot(named, f, x)):
+            piece = mm_nt(g_t, one).astype(BF)
+            j = 2 * (k // 4) + k % 2
+            if (k // 2) % 2:
+                beside[j, i - 1] = piece
+            else:
+                messages[j][0, i - 1] = piece
+    near = [to_plane(2, beside.at[j], messages[j].at[1], b_sems, j) for j in range(4)]
+    for c in near:
+        c.start()
     swap.wait()
     hidden = own + attn_land[...].astype(F32)
     hidden_ref[...] = hidden
@@ -1195,7 +1279,7 @@
             xsend[k] = block
             sent.append(to_plane(k, xsend.at[k], xin.at[k], x_sems))
             sent[-1].start()
-    for c in sent:
+    for c in sent + near:
         c.wait()
 
 
@@ -1353,6 +1437,10 @@
     own_routes = lax.dynamic_index_in_dim(routes, x, 0, False).T
     own_prev = jnp.pad(lax.dynamic_index_in_dim(prev_logits, x, 0, False).T, ((0, 4), (0, 0)))
 
+    own_gy = lax.dynamic_index_in_dim(cotangent, x, 0, False)
+    marks = jnp.pad(own_routes.astype(BF), ((0, 14), (0, width - rows)))
+    g_rows = lax.all_gather(jnp.concatenate([own_gy, marks], axis=0), "ctx")
+
     positions = z * rows + jnp.arange(rows, dtype=jnp.int32)
     half_dim = HEAD_DIM // 2
     frequency = 10000.0 ** (-(jnp.arange(half_dim, dtype=F32) * 2.0 / HEAD_DIM))
@@ -1376,45 +1464,47 @@
         ],
         [
             vm((4, 3, 192, head_cols), BF), vm((4, 192, head_cols), BF), vm((4, 192, 128), BF),
-            vm((8, width, CAPACITY), BF),
+            vm((8, width, CAPACITY), BF), vm((4, 3, 192, 1024), BF),
             sems(8), sems(8), sems(8), sems(8),
-            pltpu.SemaphoreType.DMA((8,)),
+            pltpu.SemaphoreType.DMA((12,)),
         ],
-        hbm_ins=(5, 6),
-    )
-    normed_one_t, xt, blocks, w1, w2, w3 = run_remote(
-        project_kernel, "project", 3, [tokens, w_full, small_t, cos, sin, *messages[1:]],
+        hbm_ins=(5, 6), hbm_outs=(7, 8, 9, 10),
+    )
+    length = 4 * rows
+    normed_one_t, xt, blocks, mixed_in, mixed_lse, w_exp, wt_exp = run_remote(
+        attend_kernel, "attend", 3, [scalars[4:5], tokens, w_full, small_t, cos, sin, *messages],
         [
-            out((width, 2 * rows)), out((width, rows)), out((4, 3, rows // 2, head_cols)),
-            out((2, 3, 192, 1024)), out((2, 3, 192, 1024)), out((192, 1024)),
+            out((width, 2 * rows)), out((width, rows)), out((4, 3, rows // 2, head_cols)), out((4, 192, rows)),
+            out((3, HEAD_DIM + 8, length), F32), out((3, width, 2048)), out((3, 2048, width)),
         ],
-        [vm((2, rows, width), BF), vm((4, 3, rows // 2, head_cols), BF), sems(4), sems(8)],
-        hbm_ins=(5, 6, 7), hbm_outs=(3, 4, 5),
+        [
+            vm((2, rows, width), BF), vm((4, 3, rows // 2, head_cols), BF), vm((length, HEAD_DIM), BF),
+            vm((length, HEAD_DIM), BF), vm((length, HEAD_DIM), BF), vm((4, 3, HEAD_DIM, rows), BF),
+            vm((3, width, 2048), BF), vm((3, 2048, width), BF),
+            sems(12), sems(12), sems(32), pltpu.SemaphoreType.DMA((6,)), pltpu.SemaphoreType.DMA((26,)),
+        ],
+        smem_ins=(0,), hbm_ins=(6, 7, 8, 9), hbm_outs=(5, 6), vmem=61,
     )
     gain_one_row = small_t[16:17]
 
-    gs, blocks = lax.optimization_barrier((gs, blocks))
     length = 4 * rows
     unit_scratch = [pltpu.VMEM((3, length, HEAD_DIM), BF)] * 3
-    mixed_in, mixed_lse, w_exp, wt_exp = run_remote(
-        attn_kernel, "attention", 4, [scalars[4:5], blocks, messages[0], w1, w2, w3, messages[3]],
+    mixed, hidden, xs, *g_messages = run_remote(
+        route_kernel, "route", 1,
+        [mixed_in, wo_full, xt, small, small_t, own_prev, own_routes, hot, g_rows],
         [
-            out((4, 192, rows)), out((3, HEAD_DIM + 8, length), F32), out((3, width, 2048)),
-            out((3, 2048, width)),
+            out((2, head_cols, rows)), out((width, rows), F32), out((8, width + 16, CAPACITY)),
+            *[out((2, 3, width, CAPACITY))] * 4,
         ],
-        unit_scratch + [vm((4, 192, rows), BF), sems(4), sems(8)],
-        hbm_ins=(6,), smem_ins=(0,), vmem=60,
-    )
-    g_all = lax.all_gather(gs, "ctx")
-
-    mixed, hidden, xs = run_remote(
-        route_kernel, "route", 1, [mixed_in, wo_full, xt, small, small_t, own_prev, own_routes, hot],
-        [out((2, head_cols, rows)), out((width, rows), F32), out((8, width + 16, CAPACITY))],
-        [vm((width, rows), BF), vm((width, rows), BF), vm((8, width + 16, CAPACITY), BF), sems(8), sems(8)],
+        [
+            vm((width, rows), BF), vm((width, rows), BF), vm((8, width + 16, CAPACITY), BF),
+            vm((4, 3, width, CAPACITY), BF), sems(8), sems(8), sems(4),
+        ],
     )
     x_all = lax.all_gather(xs, "ctx")
-
-    done = expert_call(True, jnp.stack([z, f]).astype(jnp.int32), xs[None], gs[None], w_exp, wt_exp, None)
+    g_more = [g_messages[0]] + [flip_plane(g_messages[j], 4 * (j // 2) + j % 2) for j in (1, 2, 3)]
+
+    done = expert_call(jnp.stack([z, f]).astype(jnp.int32), xs[None], gs[None], w_exp, wt_exp)
     ysend, rsend, held = done[0], done[1], done[2:]
     layer_own, grad_prev_t, dm_in, og, d_hidden = run_remote(
         return_kernel, "give_back", 2,
@@ -1428,7 +1518,6 @@
             vm((width, rows), BF), vm((width, rows), BF), sems(8), sems(8), sems(8), sems(4), sems(2),
         ],
     )
-    grad_prev = jnp.swapaxes(grad_prev_t[:, 0:NEXP], 1, 2)
     others = jnp.stack([jnp.bitwise_xor(z, d) for d in (1, 2, 3)] + [f]).astype(jnp.int32)
 
     back = run(
@@ -1441,12 +1530,10 @@
         flops=3 * 11 * 512 * 512 * 64 * 10,
     )
     back_in = [back[0]] + [flip_ctx(back[d], d) for d in (1, 2, 3)]
-    held = expert_call(False, others, x_all, g_all, w_exp, wt_exp, held)
+    held = more_call(others, x_all, g_more, wt_exp, held)
     *back_in, first = lax.optimization_barrier((*back_in, held[0]))
     held = [first, *held[1:]]
-
     other = flip_tp(layer_own)
-    layer_out = jnp.where(x == 0, jnp.stack([layer_own, other]), jnp.stack([other, layer_own]))
     dn, gq = run(
         dproj_kernel, "d_projection", scalars, [*back_in, w_full, normed_one_t, cos, sin, tokens],
         [out((2, rows, width)), out((4, 592, head_cols))],
@@ -1463,25 +1550,27 @@
         ],
         [
             vm((4, width, 1024), BF), vm((4, width, 1024), BF), vm((2, 2, cols, 1024), BF),
-            vm((2, width, cols), F32), vm((parts, 8, 3, 192, cols), BF),
+            vm((2, width, cols), F32), vm((9, 8, 192, cols), BF),
             vm((2, 592, head_cols), BF), vm((2, 192, 512), BF), vm((2, 592, head_cols), BF), vm((2, 192, 512), BF),
             vm((592, head_cols), BF), vm((192, 512), BF), vm((592, head_cols), BF), vm((192, 512), BF),
             vm((592, head_cols), BF), vm((192, 512), BF), vm((592, head_cols), BF), vm((192, 512), BF),
             vm((2, 192, 128), F32), vm((2, 8, head_cols), F32),
-            sems(4), pltpu.SemaphoreType.DMA((2,)), sems(96), pltpu.SemaphoreType.DMA((12,)), sems(12), sems(8),
+            sems(4), pltpu.SemaphoreType.DMA((2,)), sems(72), pltpu.SemaphoreType.DMA((9,)), sems(12), sems(8), sems(3),
         ],
         vmem=60, hbm_ins=(0, 1, 2, 3, 4, 5), hbm_outs=(0, 1),
     )
     grad_gu, grad_down = place_call(me[None].astype(jnp.int32), gin)
-    grad_out = outg[:, 0:384]
-    grad_gate = small_f[:, 0:16]
-    grad_const = small_f[:, 16:18].T
-    grad_tokens = run(
-        tokens_kernel, "grad_tokens", scalars, [tokens, gain_one_row, d_hidden, dn, dn_other],
-        [out((2, rows, width), F32)],
-    )[0]
-    grad_qkv = att[0:576].reshape(3, 192, head_cols)
-    grad_gains = jnp.stack([line_f[0, 0:192], small_f[:, 18]])
+    layer_out, grad_tokens, grad_prev, grad_gains, grad_qkv, grad_out, grad_gate, grad_const = run(
+        last_kernel, "last", scalars,
+        [
+            tokens, gain_one_row, d_hidden, dn, dn_other, att, outg, small_f, line_f, layer_own, other,
+            grad_prev_t,
+        ],
+        [
+            out((2, rows, width)), out((2, rows, width), F32), out((2, rows, NEXP), F32), out((2, 192), F32),
+            out((3, 192, head_cols), F32), out((192, head_cols), F32), out((192, 16), F32), out((NCONST, 192), F32),
+        ],
+    )
     return (
         layer_out, grad_tokens, grad_prev, grad_gains, grad_qkv, grad_out, grad_gate, grad_const,
         grad_gu, grad_down,

time: 659 us -> 613 us (0.930)
  Pallas kernels: 593 us -> 553 us
    pallas_call x6 -> x5, Pallas kernels: 454 us -> 416 us  [run_remote(): pl.pallas_call(body, out_shape=tuple(outs), in_specs=[HBM if i in hbm_ins...]
  transfers between devices with their start and end apart: 6 -> 9, of which waited for: 0 -> 0; matrix products, arithmetic and copies ran while one was open for 1% -> 1% of each run, Pallas kernels for 48% -> 81%
where the time goes in v4:
time: 613 us; the launch traced here: 602 us
  Pallas kernels  553 us (90%)
  starting transfers between devices  15.3 us (2%)
  between operations  14.7 us (2%)
  local copies, waits for them, and re-layouts  14 us (2%)
    pallas_call x5, Pallas kernels, run_remote(): pl.pallas_call(body, out_shape=tuple(outs), in_specs=[HBM if i in hbm_ins...  416 us
    pallas_call x3, Pallas kernels, run(): pl.pallas_call(body, out_shape=tuple(outs), in_specs=[SCALARS] + [WHOLE]...  48.7 us
    pallas_call x1, Pallas kernels, more_call(): pl.pallas_call(more_body, out_shape=tuple((out(h.shape) for h in held)),...  46.4 us
    pallas_call x1, Pallas kernels, expert_call(): pl.pallas_call(expert_body, out_shape=tuple(packet + [wide] * 2 + [high]...  34.9 us
  transfers between devices with their start and end apart: 9, of which 0 were waited for; matrix products, arithmetic and copies ran while one was open for 1% of the time, Pallas kernels for 81%

profile of v4, /device:TPU:0, one launch (start us, length us, event | category | flops | bytes accessed | tf_op | source)
XLA Modules:
  0.0 602.5 jit_solution(280533752413926325)
XLA Ops:
  7.2 0.0 copy-start
  7.2 0.0 all-gather.5.cloned.1.call-start
  7.2 1.3 fusion.3
  8.5 1.2 dynamic-slice_bitcast_fusion
  9.8 0.9 fusion.1
  10.7 0.0 all-gather.5.cloned.1.call-update
  10.7 0.0 all-gather.7.cloned.1.call-start
  10.8 0.1 copy.42
  11.0 0.6 pad.12.smallp
  11.6 40.7 %gather.1 = (bf16[1024,512]{1,0:T(8,128)(2,1)}, bf16[768,512]{1,0:T(8,128)(2,1)}, bf16[8,768,128]{2,1,0:T(8,128)(2,1)}, bf16[3,768,384]{2,1,0:T(8,128)(2,1)}, bf...) custom-call(bf16[3,192,384]{2,1,0:T(8,128)(2,1)} %qkv.1, ...), custom_call_target="tpu_custom_call" | custom-call | flops 1024 | bytes 1024 | tf_op jit(solution)/shard_map/gather/pallas_call | solution.py:1392
  52.3 0.0 copy-done.9
  52.3 0.7 dynamic_slice.15.prefix_ref
  53.0 1.0 fusion.2
  54.0 1.3 pad_maximum_fusion
  55.2 117.2 %attend.1 = (bf16[768,1024]{1,0:T(8,128)(2,1)}, bf16[768,512]{1,0:T(8,128)(2,1)}, bf16[4,3,256,384]{3,2,1,0:T(8,128)(2,1)}, bf16[4,192,512]{2,1,0:T(8,128)(2,1)}...) custom-call(s32[1]{0:T(128)} %dynamic_slice.15.prefix_ref, ...), custom_call_target="tpu_custom_call" | custom-call | flops 1024 | bytes 1024 | tf_op jit(solution)/shard_map/attend/pallas_call | solution.py:1392
  172.5 0.6 pad.13.prev
  173.1 48.4 %route.1 = (bf16[2,384,512]{2,1,0:T(8,128)(2,1)}, f32[768,512]{1,0:T(8,128)}, bf16[8,784,128]{2,1,0:T(8,128)(2,1)}, bf16[2,3,768,128]{3,2,1,0:T(8,128)(2,1)}, bf...) custom-call(bf16[4,192,512]{2,1,0:T(8,128)(2,1)} %get-tuple-element.85.land, ...), custom_call_target="tpu_custom_call" | custom-call | flops 1024 | bytes 1024 | tf_op jit(solution)/shard_map/route/pallas_call | solution.py:1392
  221.6 0.0 all-gather.7.cloned.1.call-update
  221.6 0.6 collective-permute-start.3
  222.2 0.6 collective-permute-start.4
  222.8 2.4 collective-permute-start.5
  225.1 0.6 pad_add_fusion.sc
  225.7 34.9 %experts_own.1 = (bf16[8,784,128]{2,1,0:T(8,128)(2,1)}, bf16[8,768,128]{2,1,0:T(8,128)(2,1)}, bf16[4,768,1024]{2,1,0:T(8,128)(2,1)}, bf16[4,768,1024]{2,1,0:T(8,...) custom-call(s32[2]{0:T(128)} %pad_add_fusion.sc, ...), custom_call_target="tpu_custom_call" | custom-call | flops 1024 | bytes 1024 | tf_op jit(solution)/shard_map/experts_own/pallas_call | solution.py:640
  260.7 84.9 %give_back.1 = (bf16[512,768]{1,0:T(8,128)(2,1)}, f32[2,16,512]{2,1,0:T(8,128)}, bf16[4,192,512]{2,1,0:T(8,128)(2,1)}, bf16[4,192,512]{2,1,0:T(8,128)(2,1)}, bf16[2,512,768]{2,1,0:T(8,128)(2,1)}) custom-call(bf16[8,784,128]{2,1,0:T(8,128)(2,1)} %get-tuple-element.94.ysend, bf16[8,768,128]{2,1,0:T(8,128)(2,1)} %get-tuple-element.95.rsend, ...), custom_call_target="tpu_custom_call" | custom-call | flops 1024 | bytes 1024 | tf_op jit(solution)/shard_map/give_back/pallas_call | solution.py:1392
  345.5 0.9 collective-permute-start.6
  346.5 1.2 stack.37.sc
  347.7 30.4 %attention_backward.1 = (bf16[3,256,384]{2,1,0:T(8,128)(2,1)}, bf16[3,256,384]{2,1,0:T(8,128)(2,1)}, bf16[3,256,384]{2,1,0:T(8,128)(2,1)}, bf16[3,256,384]{2,1,0:T(8,128)(2,1)}) custom-call(s32[5]{0:T(128)} %stack.37.sc, bf16[4,3,256,384]{3,2,1,0:T(8,128)(2,1)} %get-tuple-element.100.blocks, f32[3,72,2048]{2,1,0:T(8,128)} %get-tuple-element.101.m_ref, ...), custom_call_target="tpu_custom_call" | custom-call | flops 1024 | bytes 1024 | tf_op jit(solution)/shard_map/attention_backward/pallas_call | solution.py:450
  378.1 8.3 %collective-permute-start = (bf16[3,256,384]{2,1,0:T(8,128)(2,1)}, bf16[3,256,384]{2,1,0:T(8,128)(2,1)}, u32[]{:S(2)}, u32[]{:S(2)}) collective-permute-start(bf16[3,256,384]{2,1,0:T(8,128)(2,1)} %get-tuple-element.104), channel_id=1, source_target_pairs={{0,2},{2,0},{4,6},{6,4},{1,3},{3,1},{5,7},{7,5},{8,10},{10,8},{12,... | collective-permute-start | bytes 1769480 | tf_op jit(solution)/shard_map/ppermute | solution.py:1429
  386.4 0.0 collective-permute-done.3.g1
  386.4 0.6 collective-permute-start.1
  387.0 0.0 collective-permute-done.4.g2
  387.1 1.8 collective-permute-start.2
  388.9 1.3 slice.3.gain
  390.2 0.6 pad_add_fusion.1.sc
  390.7 0.0 collective-permute-done.5.g3
  390.8 1.0 copy-done.5
  391.8 46.4 %experts_more.1 = (bf16[4,768,1024]{2,1,0:T(8,128)(2,1)}, bf16[4,768,1024]{2,1,0:T(8,128)(2,1)}, bf16[4,2048,1024]{2,1,0:T(8,128)(2,1)}, bf16[4,2048,1024]{2,1,0:T(8,128)(2,1)}, bf16[4,2048,1024]{2,1,0:T(8,128)(2,1)}) custom-call(s32[4]{0:T(128)} %pad_add_fusion.1.sc, ...), custom_call_target="tpu_custom_call", output_to_operand_aliasing={{0}: (7, {}), {1}: (8, {}), {2}: (9, {}), {3}: (10, {}), {4... | custom-call | flops 1024 | bytes 1024 | tf_op jit(solution)/shard_map/experts_more/pallas_call | solution.py:616
  438.2 0.0 collective-permute-done.b1
  438.2 0.0 collective-permute-done.1.b2
  438.2 0.0 collective-permute-done.2.b3
  438.2 10.4 %d_projection.1 = (bf16[2,512,768]{2,1,0:T(8,128)(2,1)}, bf16[4,592,384]{2,1,0:T(8,128)(2,1)}) custom-call(s32[5]{0:T(128)} %stack.37.sc, bf16[3,256,384]{2,1,0:T(8,128)(2,1)} %get-tuple-element.117.b0, bf16[3,256,384]{2,1,0:T(8,128)(2,1)} %collective-permute-done.b1, bf16[3,256,384]{2,1,0:T(8,128)(2,1)} %collective-permute-done.1.b2, ...), custom_call_target="tpu_custom_call" | custom-call | flops 1024 | bytes 1024 | tf_op jit(solution)/shard_map/d_projection/pallas_call | solution.py:450
  448.6 124.4 %finish.1 = (bf16[4,8,3,192,256]{4,3,2,1,0:T(8,128)(2,1)}, bf16[2,512,768]{2,1,0:T(8,128)(2,1)}, f32[592,384]{1,0:T(8,128)}, f32[192,512]{1,0:T(8,128)}, f32[192,128]{1,0:T(8,128)}, /*index=5*/f32[8,384]{1,0:T(8,128)}) custom-call(bf16[4,768,1024]{2,1,0:T(8,128)(2,1)} %get-tuple-element.123.bx, bf16[4,768,1024]{2,1,0:T(8,128)(2,1)} %get-tuple-element.124.bg, ...), custom_call_target="tpu_custom_call" | custom-call | flops 1024 | bytes 1024 | tf_op jit(solution)/shard_map/finish/pallas_call | solution.py:1392
  573.0 0.0 collective-permute-done.6.layer_other
  573.0 7.9 %last.1 = (bf16[2,512,768]{2,1,0:T(8,128)(2,1)}, f32[2,512,768]{2,1,0:T(8,128)}, f32[2,512,12]{2,1,0:T(8,128)}, f32[2,192]{1,0:T(2,128)}, f32[3,192,384]{2,1,0:T...) custom-call(s32[5]{0:T(128)} %stack.37.sc, bf16[2,512,768]{2,1,0:T(8,128)(2,1)} %tokens.5, ...), custom_call_target="tpu_custom_call" | custom-call | flops 1024 | bytes 1024 | tf_op jit(solution)/shard_map/last/pallas_call | solution.py:450
  580.9 1.9 copy.45
  582.8 1.6 copy.46
  584.4 3.7 copy-done.2
  588.0 7.2 %place_grads.1 = (f32[8,2,192,1024]{3,2,1,0:T(8,128)}, f32[8,192,1024]{2,1,0:T(8,128)}) custom-call(s32[1]{0:T(128)} %bitcast.sc, bf16[4,8,3,192,256]{4,3,2,1,0:T(8,128)(2,1)S(1)} %copy-done.2), custom_call_target="tpu_custom_call" | custom-call | flops 1024 | bytes 1024 | tf_op jit(solution)/shard_map/place_grads/pallas_call | solution.py:810
  (23 shorter events, 0.1 us)
Async XLA Ops:
  7.2 165.3 %copy-start = (f32[2,512,12]{1,0,2:T(2,128)S(1)}, f32[2,512,12]{1,0,2:T(2,128)}, u32[]{:S(2)}) copy-start(f32[2,512,12]{1,0,2:T(2,128)} %param.13) | copy-start | bytes 147460
  7.2 165.9 %all-gather.5.cloned.1.call-start = ((), (), s32[]{:S(2)}) async-start(), calls=%async_computation | async-start | bytes 4055040 | tf_op jit(solution)/shard_map/all_gather | solution.py:1442
  8.5 2.3 copy-start.6
  8.5 2.3 copy-start.7
  8.5 2.3 copy-start.8
  10.7 380.0 %all-gather.7.cloned.1.call-start = ((), (), s32[]{:S(2)}) async-start(), calls=%async_computation.1 | async-start | bytes 8028160 | tf_op jit(solution)/shard_map/all_gather | solution.py:1504
  11.6 40.7 %copy-start.9 = (s32[2]{0:T(128)S(1)}, s32[2]{0:T(128)}, u32[]{:S(2)}) copy-start(s32[2]{0:T(128)} %param.15) | copy-start | bytes 28
  221.6 164.8 %collective-permute-start.3 = (bf16[2,3,768,128]{3,2,1,0:T(8,128)(2,1)}, bf16[2,3,768,128]{3,2,1,0:T(8,128)(2,1)S(1)}, u32[]{:S(2)}, u32[]{:S(2)}) collective-permute-start(bf16[2,3,768,128]{3,2,1,0:T(8,128)(2,1)} %get-tuple-element.108), channel_id=1, source_target_pairs={{0,1},{1,0},{8,9},{9,8},{16,17},{17,16},{24,25},{25,24},{2,3},{3,2... | collective-permute-start | bytes 3538952 | tf_op jit(solution)/shard_map/ppermute | solution.py:1432
  222.2 164.8 %collective-permute-start.4 = (bf16[2,3,768,128]{3,2,1,0:T(8,128)(2,1)}, bf16[2,3,768,128]{3,2,1,0:T(8,128)(2,1)S(1)}, u32[]{:S(2)}, u32[]{:S(2)}) collective-permute-start(bf16[2,3,768,128]{3,2,1,0:T(8,128)(2,1)} %get-tuple-element.109), channel_id=1, source_target_pairs={{0,16},{1,17},{8,24},{9,25},{16,0},{17,1},{24,8},{25,9},{2,18},{3,... | collective-permute-start | bytes 3538952 | tf_op jit(solution)/shard_map/ppermute | solution.py:1432
  222.8 168.0 %collective-permute-start.5 = (bf16[2,3,768,128]{3,2,1,0:T(8,128)(2,1)}, bf16[2,3,768,128]{3,2,1,0:T(8,128)(2,1)S(1)}, u32[]{:S(2)}, u32[]{:S(2)}) collective-permute-start(bf16[2,3,768,128]{3,2,1,0:T(8,128)(2,1)} %get-tuple-element.110), channel_id=1, source_target_pairs={{0,17},{1,16},{8,25},{9,24},{16,1},{17,0},{24,9},{25,8},{2,19},{3,... | collective-permute-start | bytes 3538952 | tf_op jit(solution)/shard_map/ppermute | solution.py:1432
  345.5 227.4 %collective-permute-start.6 = (bf16[512,768]{1,0:T(8,128)(2,1)}, bf16[512,768]{1,0:T(8,128)(2,1)}, u32[]{:S(2)}, u32[]{:S(2)}) collective-permute-start(bf16[512,768]{1,0:T(8,128)(2,1)} %get-tuple-element.135.layer_own), channel_id=1, source_target_pairs={{0,1},{1,0},{2,3},{3,2},{4,5},{5,4},{6,7},{7,6},{8,9},{9,8},{10,11... | collective-permute-start | bytes 2359304 | tf_op jit(solution)/shard_map/ppermute | solution.py:1426
  378.1 60.1 %collective-permute-start = (bf16[3,256,384]{2,1,0:T(8,128)(2,1)}, bf16[3,256,384]{2,1,0:T(8,128)(2,1)}, u32[]{:S(2)}, u32[]{:S(2)}) collective-permute-start(bf16[3,256,384]{2,1,0:T(8,128)(2,1)} %get-tuple-element.104), channel_id=1, source_target_pairs={{0,2},{2,0},{4,6},{6,4},{1,3},{3,1},{5,7},{7,5},{8,10},{10,8},{12,... | collective-permute-start | bytes 1769480 | tf_op jit(solution)/shard_map/ppermute | solution.py:1429
  386.4 4.3 copy-start.3
  386.4 51.8 %collective-permute-start.1 = (bf16[3,256,384]{2,1,0:T(8,128)(2,1)}, bf16[3,256,384]{2,1,0:T(8,128)(2,1)}, u32[]{:S(2)}, u32[]{:S(2)}) collective-permute-start(bf16[3,256,384]{2,1,0:T(8,128)(2,1)} %get-tuple-element.105), channel_id=1, source_target_pairs={{0,4},{2,6},{4,0},{6,2},{1,5},{3,7},{5,1},{7,3},{8,12},{10,14},{12... | collective-permute-start | bytes 1769480 | tf_op jit(solution)/shard_map/ppermute | solution.py:1429
  387.1 3.7 copy-start.4
  387.1 51.2 %collective-permute-start.2 = (bf16[3,256,384]{2,1,0:T(8,128)(2,1)}, bf16[3,256,384]{2,1,0:T(8,128)(2,1)}, u32[]{:S(2)}, u32[]{:S(2)}) collective-permute-start(bf16[3,256,384]{2,1,0:T(8,128)(2,1)} %get-tuple-element.106), channel_id=1, source_target_pairs={{0,6},{2,4},{4,2},{6,0},{1,7},{3,5},{5,3},{7,1},{8,14},{10,12},{12... | collective-permute-start | bytes 1769480 | tf_op jit(solution)/shard_map/ppermute | solution.py:1429
  390.7 1.0 copy-start.5
  584.4 3.7 copy-start.2
  588.0 7.2 %copy-start.1 = (f32[2,512,12]{1,0,2:T(2,128)S(1)}, f32[2,512,12]{1,0,2:T(2,128)}, u32[]{:S(2)}) copy-start(f32[2,512,12]{1,0,2:T(2,128)} %param.13) | copy-start | bytes 147460
Sparse Core Ops, SparseCore 0:
  10.8 90.6 all-gather.4
  221.7 132.4 all-gather.6

commit v5 on v4

--- a/solution.py
+++ b/solution.py
@@ -426,6 +426,7 @@
 HBM = pl.BlockSpec(memory_space=pl.ANY)
 WHOLE = pl.BlockSpec(memory_space=pltpu.VMEM)
 SCALARS = pl.BlockSpec(memory_space=pltpu.SMEM)
+EARLY = 6
 COST = pl.CostEstimate(flops=1024, bytes_accessed=1024, transcendentals=0)
 LOG2E = 1.4426950408889634
 
@@ -522,7 +523,7 @@
     )
 
 
-def expert_body(sc, xs, gs, w, wt, y_ref, r_ref, bx, bg, ba, bp, bu, xt, gt, grow, din, res, graw):
+def expert_body(sc, xa, xb, gs, w, wt, y_ref, r_ref, bx, bg, ba, bp, bu, xt, gt, grow, din, res, graw):
     j = pl.program_id(1)
     f = sc[pl.num_programs(0)]
 
@@ -533,12 +534,13 @@
     def _():
         for k in range(8):
             cols = slice(k * CAPACITY, (k + 1) * CAPACITY)
-            pair = xs[0, k, 768:784].astype(F32)
+            xs = xa.at[0, k] if k < EARLY else xb.at[0, k - EARLY]
+            pair = xs[768:784].astype(F32)
             gate = pair[k : k + 1] + pair[8 + k : 9 + k]
             grow[:, cols] = jnp.broadcast_to(gate, (8, CAPACITY))
             for r in range(4):
                 to, at = slice(r * 192, (r + 1) * 192), shard(r)
-                xt[to, cols] = xs[0, k, at]
+                xt[to, cols] = xs[at]
                 g = gs[0, k, at]
                 graw[to, cols] = g
                 gt[to, cols] = (g.astype(F32) * gate).astype(BF)
@@ -580,7 +582,7 @@
                 r_ref[k, shard(q), :] = r[q * 192 : (q + 1) * 192]
 
 
-def more_body(sc, xs, g0, g1, g2, g3, wt, h0, h1, h2, h3, h4, bx, bg, ba, bp, bu, xt, gt):
+def more_body(sc, xa, xb, g0, g1, g2, g3, wt, h0, h1, h2, h3, h4, bx, bg, ba, bp, bu, xt, gt):
     f = sc[3]
 
     @pl.when(pl.program_id(1) == 0)
@@ -588,12 +590,13 @@
         for k in range(8):
             cols = slice(k * CAPACITY, (k + 1) * CAPACITY)
             g = (g0, g1, g2, g3)[2 * (k // 4) + k % 2]
-            pair = xs[0, k, 768:784].astype(F32)
+            xs = xa.at[0, k] if k < EARLY else xb.at[0, k - EARLY]
+            pair = xs[768:784].astype(F32)
             gate = pair[k : k + 1] + pair[8 + k : 9 + k]
             for r in range(4):
                 to = slice(r * 192, (r + 1) * 192)
                 at = pl.ds(pl.multiple_of(jnp.bitwise_xor(f, r) * 192, 64), 192)
-                xt[to, cols] = xs[0, k, at]
+                xt[to, cols] = xs[at]
                 gt[to, cols] = (g[(k // 2) % 2, 0, at].astype(F32) * gate).astype(BF)
         bx[0] = xt[...]
         bg[0] = gt[...]
@@ -609,30 +612,31 @@
     bu[0] = (da * silu).astype(BF)
 
 
-def more_call(planes, x_more, g_more, wt, held):
-    tile, slots, width = 512, 8 * CAPACITY, x_more.shape[2] - 16
+def more_call(planes, xa, xb, g_more, wt, held):
+    tile, slots, width = 256, 8 * CAPACITY, wt.shape[2]
     row = lambda i, j, s: (s[i], 0, 0)
-    tall = lambda i, j, s: (s[i], j, 0)
+    part = lambda j, s: 4 * (j // 3) + jnp.where(j % 3 == 0, s[4], j % 3 + 1)
+    tall = lambda i, j, s: (s[i], part(j, s), 0)
     return pl.pallas_call(
         more_body,
         out_shape=tuple(out(h.shape) for h in held),
         grid_spec=pltpu.PrefetchScalarGridSpec(
-            num_scalar_prefetch=1, grid=(planes.shape[0] - 1, wt.shape[1] // tile),
-            in_specs=[pl.BlockSpec((1, 8, width + 16, CAPACITY), lambda i, j, s: (s[i], 0, 0, 0))]
+            num_scalar_prefetch=1, grid=(3, 6),
+            in_specs=[pl.BlockSpec((1,) + a.shape[1:], lambda i, j, s: (s[i], 0, 0, 0)) for a in (xa, xb)]
             + [pl.BlockSpec((2, 1, width, CAPACITY), lambda i, j, s: (0, i, 0, 0))] * 4
-            + [pl.BlockSpec((3, tile, width), lambda i, j, s: (0, j, 0))]
+            + [pl.BlockSpec((3, tile, width), lambda i, j, s: (0, part(j, s), 0))]
             + [HBM] * 5,
             out_specs=tuple([pl.BlockSpec((1, width, slots), row)] * 2 + [pl.BlockSpec((1, tile, slots), tall)] * 3),
             scratch_shapes=[pltpu.VMEM((width, slots), BF), pltpu.VMEM((width, slots), BF)],
         ),
-        input_output_aliases={7 + i: i for i in range(5)},
+        input_output_aliases={8 + i: i for i in range(5)},
         compiler_params=pltpu.CompilerParams(vmem_limit_bytes=56 * MIB),
         cost_estimate=COST,
         name="experts_more",
-    )(planes, x_more, *g_more, wt, *held)
-
-
-def expert_call(plane, xs, gs, w, wt):
+    )(planes, xa, xb, *g_more, wt, *held)
+
+
+def expert_call(plane, xa, xb, gs, w, wt):
     tile, n_ctx = 512, 4
     slots, width = 8 * CAPACITY, w.shape[1]
     packet = [out((8, width + 16, CAPACITY)), out((8, width, CAPACITY))]
@@ -642,7 +646,7 @@
         out_shape=tuple(packet + [wide] * 2 + [high] * 3),
         grid_spec=pltpu.PrefetchScalarGridSpec(
             num_scalar_prefetch=1, grid=(1, w.shape[2] // tile),
-            in_specs=[pl.BlockSpec((1,) + a.shape[1:], lambda i, j, s: (0, 0, 0, 0)) for a in (xs, gs)]
+            in_specs=[pl.BlockSpec((1,) + a.shape[1:], lambda i, j, s: (0, 0, 0, 0)) for a in (xa, xb, gs)]
             + [
                 pl.BlockSpec((3, width, tile), lambda i, j, s: (0, 0, j)),
                 pl.BlockSpec((3, tile, width), lambda i, j, s: (0, j, 0)),
@@ -660,11 +664,12 @@
         compiler_params=pltpu.CompilerParams(vmem_limit_bytes=58 * MIB),
         cost_estimate=COST,
         name="experts_own",
-    )(plane, xs, gs, w, wt)
-
-
-def finish_kernel(bx, bg, bp, bu, ba, dn, gq, og, gin, dn_other, att, outg, small_f, line_f,
-                  x_s, g_s, tiles, acc, send, q1, o1, qm, om, q2, o2, qk, ok, q3, o3, q4, o4, s_x, l_x,
+    )(plane, xa, xb, gs, w, wt)
+
+
+def finish_kernel(bx, bg, bp, bu, ba, b0, b1, b2, b3, w, nt, cos_ref, sin_ref, tokens, og,
+                  gin, dn, dn_other, att, outg, small_f, line_f,
+                  gq, back, x_s, g_s, tiles, acc, send, q1, o1, qm, om, q2, o2, qk, ok, q3, o3, q4, o4, s_x, l_x,
                   xg_sems, tile_sems, send_sems, own_sems, step_sems, dn_sems, over_sems):
     f, z, x = here()
     core, y = f % 2, f // 2
@@ -687,16 +692,6 @@
     plan = [(parity, m) for m in range(3)] + [(part, m) for part in (2, 3) for m in range(3)]
     for c in [tile_copy(*plan[0], 0)] + loads:
         c.start()
-    swap = to_plane(1, dn, dn_other, dn_sems)
-    swap.start()
-    first = []
-    for yy in range(2):
-        at = 2 * yy + 1 - core
-        first.append(to_plane(2, gq.at[at], q1.at[yy], step_sems, 2 * yy))
-        first.append(to_plane(2, og.at[at], o1.at[yy], step_sems, 2 * yy + 1))
-    for c in first:
-        c.start()
-
     def plus(a, b):
         return a.astype(F32) + b.astype(F32)
 
@@ -730,6 +725,55 @@
             device_id=(f, flip4(z, d), x), device_id_type=MESH,
         )
 
+    first, swaps = [], []
+
+    def project_back():
+        for d, b in enumerate((b0, b1, b2, b3)):
+            back[d] = b[...]
+        cos = jnp.concatenate([cos_ref[...]] * 3, axis=1)
+        sin = jnp.concatenate([sin_ref[...]] * 3, axis=1)
+        grads = [None] * 3
+        gain_grad = jnp.zeros((1, 768), F32)
+        swaps.extend(to_plane(1, dn.at[s], dn_other.at[s], dn_sems, s) for s in range(2))
+        for s in range(2):
+            blocks = [[back[place_of(z, s, half), j] for j in range(3)] for half in range(2)]
+            total, parts_g = None, []
+            for c in range(3):
+                lines = []
+                for r in range(2):
+                    at = r * 192 + c * HEAD_DIM
+                    lines.append(
+                        jnp.concatenate(
+                            [blocks[half][j][:, at : at + HEAD_DIM] for half in range(2) for j in range(3)], axis=1
+                        )
+                    )
+                g = jnp.concatenate(lines, axis=0)
+                if c < 2:
+                    g = g.astype(F32)
+                    g = (g * cos - swap_halves(g) * sin).astype(BF)
+                term = mm_nt(g, w[c])
+                total = term if total is None else total + term
+                parts_g.append(g)
+            dn[s] = total.astype(BF)
+            swaps[s].start()
+            for c in range(3):
+                gr = mm(nt[:, s * 512 : (s + 1) * 512], parts_g[c])
+                grads[c] = gr if grads[c] is None else grads[c] + gr
+            v = tokens[s].astype(F32)
+            inverse = lax.rsqrt(jnp.mean(v * v, axis=-1, keepdims=True) + epsilon)
+            gain_grad = gain_grad + jnp.sum(total * v * inverse, axis=0, keepdims=True)
+        for q in range(4):
+            for c in range(3):
+                gq[q, c * 192 : (c + 1) * 192, :] = grads[c][q * 192 : (q + 1) * 192].astype(BF)
+            piece = jnp.broadcast_to(gain_grad[:, q * 192 : (q + 1) * 192], (16, 192))
+            gq[q, 576:592, :] = jnp.concatenate([piece, piece], axis=1).astype(BF)
+        for yy in range(2):
+            at = 2 * yy + 1 - core
+            first.append(to_plane(2, gq.at[at], q1.at[yy], step_sems, 2 * yy))
+            first.append(to_plane(2, og.at[at], o1.at[yy], step_sems, 2 * yy + 1))
+        for c in first:
+            c.start()
+
     def hand_over(m):
         for c in sent[m]:
             c.wait()
@@ -775,53 +819,29 @@
             else:
                 sent[-1].append(pltpu.make_async_copy(src, dst, own_sems.at[number]))
             sent[-1][-1].start()
-        if number in (1, 3, 5, 8):
+        if number == 2:
+            overs.append(hand_over(0))
+            project_back()
+            overs.append(hand_over(1))
+        if number == 3:
+            overs.append(hand_over(2))
+        if number > 4:
             for c in steps:
                 c.wait()
-            steps = after((1, 3, 5, 8).index(number))
+            steps = after(number - 5)
             for c in steps:
                 c.start()
-        if number > 5:
-            overs.append(hand_over(number - 6))
     for c in steps:
         c.wait()
     small_f[...] = s_x[0] + s_x[1]
     line_f[...] = l_x[0] + l_x[1]
-    swap.wait()
+    for c in swaps:
+        c.wait()
     for copies in sent[3:]:
         for c in copies:
             c.wait()
     for c in overs:
         c.wait()
-
-
-def place_body(sc, block, gu, dn):
-    parts, cols = block.shape[0], block.shape[4]
-    for part in range(parts):
-        at = slice(part * cols, (part + 1) * cols)
-        gu[0, 0, :, at] = block[part, 0, 0].astype(F32)
-        gu[0, 1, :, at] = block[part, 0, 1].astype(F32)
-        dn[0, :, at] = block[part, 0, 2].astype(F32)
-
-
-def place_call(scalars, gin):
-    parts, cols = gin.shape[0], gin.shape[4]
-    xor = lambda k, s: jnp.bitwise_xor(k, s[0])
-    return pl.pallas_call(
-        place_body,
-        out_shape=(out((NFFN, 2, 192, cols * parts), F32), out((NFFN, 192, cols * parts), F32)),
-        grid_spec=pltpu.PrefetchScalarGridSpec(
-            num_scalar_prefetch=1, grid=(NFFN,),
-            in_specs=[pl.BlockSpec((parts, 1, 3, 192, cols), lambda k, s: (0, k, 0, 0, 0))],
-            out_specs=(
-                pl.BlockSpec((1, 2, 192, cols * parts), lambda k, s: (xor(k, s), 0, 0, 0)),
-                pl.BlockSpec((1, 192, cols * parts), lambda k, s: (xor(k, s), 0, 0)),
-            ),
-        ),
-        compiler_params=pltpu.CompilerParams(vmem_limit_bytes=40 * MIB),
-        cost_estimate=COST,
-        name="place_grads",
-    )(scalars, gin)
 
 
 def attn_back_kernel(sc, blocks, m_ref, dm, o0, o1, o2, o3,
@@ -873,65 +893,71 @@
         o[...] = st[jnp.bitwise_xor(z, d)]
 
 
-def dproj_kernel(sc, b0, b1, b2, b3, w, nt, cos_ref, sin_ref, tokens, dn_ref, gq_ref, st):
-    z = sc[1]
-    h = HEAD_DIM
-    for d, b in enumerate((b0, b1, b2, b3)):
-        st[d] = b[...]
-    cos = jnp.concatenate([cos_ref[...]] * 3, axis=1)
-    sin = jnp.concatenate([sin_ref[...]] * 3, axis=1)
-    grads = [None] * 3
-    gain_grad = jnp.zeros((1, 768), F32)
-    for s in range(2):
-        blocks = [[st[jnp.bitwise_xor(z, 2 * s + half), j] for j in range(3)] for half in range(2)]
-        dn = None
+def last_body(sc, block, tokens, gain, dh, own, recv, att, outg, small_f, line_f, layer_own, layer_other, gprev_t,
+              gu, dn, layer, o_ref, gprev, gains, gq, go, ggate, gconst):
+    step = pl.program_id(0)
+    parts, cols = block.shape[0], block.shape[4]
+    for part in range(parts):
+        at = slice(part * cols, (part + 1) * cols)
+        gu[0, 0, :, at] = block[part, 0, 0].astype(F32)
+        gu[0, 1, :, at] = block[part, 0, 1].astype(F32)
+        dn[0, :, at] = block[part, 0, 2].astype(F32)
+    v = tokens[0].astype(F32)
+    inverse = lax.rsqrt(jnp.mean(v * v, axis=-1, keepdims=True) + epsilon)
+    u = (own[0].astype(F32) + recv[0].astype(F32)) * gain[...]
+    mean = jnp.mean(u * v, axis=-1, keepdims=True)
+    o_ref[0] = dh[0].astype(F32) + inverse * u - v * (inverse * inverse * inverse * mean)
+    layer[0] = jnp.where(step // 4 == sc[1], layer_own[...].astype(F32), layer_other[...].astype(F32)).astype(BF)
+
+    @pl.when(step == 0)
+    def _():
+        for s in range(2):
+            gprev[s] = gprev_t[s].T[:, 0:NEXP]
         for c in range(3):
-            rows = []
-            for r in range(2):
-                at = r * 192 + c * h
-                rows.append(
-                    jnp.concatenate(
-                        [blocks[half][j][:, at : at + h] for half in range(2) for j in range(3)], axis=1
-                    )
-                )
-            g = jnp.concatenate(rows, axis=0)
-            if c < 2:
-                g = g.astype(F32)
-                g = (g * cos - swap_halves(g) * sin).astype(BF)
-            term = mm_nt(g, w[c])
-            dn = term if dn is None else dn + term
-            gr = mm(nt[:, s * 512 : (s + 1) * 512], g)
-            grads[c] = gr if grads[c] is None else grads[c] + gr
-        dn_ref[s] = dn.astype(BF)
-        v = tokens[s].astype(F32)
-        inverse = lax.rsqrt(jnp.mean(v * v, axis=-1, keepdims=True) + epsilon)
-        gain_grad = gain_grad + jnp.sum(dn * v * inverse, axis=0, keepdims=True)
-    for f in range(4):
-        for c in range(3):
-            gq_ref[f, c * 192 : (c + 1) * 192, :] = grads[c][f * 192 : (f + 1) * 192].astype(BF)
-        piece = jnp.broadcast_to(gain_grad[:, f * 192 : (f + 1) * 192], (16, 192))
-        gq_ref[f, 576:592, :] = jnp.concatenate([piece, piece], axis=1).astype(BF)
-
-
-def last_kernel(sc, tokens, gain, dh, own, recv, att, outg, small_f, line_f, layer_own, layer_other, gprev_t,
-                layer, o_ref, gprev, gains, gq, go, ggate, gconst):
-    x = sc[2]
-    for s in range(2):
-        v = tokens[s].astype(F32)
-        inverse = lax.rsqrt(jnp.mean(v * v, axis=-1, keepdims=True) + epsilon)
-        u = (own[s].astype(F32) + recv[s].astype(F32)) * gain[...]
-        mean = jnp.mean(u * v, axis=-1, keepdims=True)
-        o_ref[s] = dh[s].astype(F32) + inverse * u - v * (inverse * inverse * inverse * mean)
-        gprev[s] = gprev_t[s].T[:, 0:NEXP]
-    layer[x] = layer_own[...]
-    layer[1 - x] = layer_other[...]
-    for c in range(3):
-        gq[c] = att[c * 192 : (c + 1) * 192, :]
-    go[...] = outg[:, 0:384]
-    ggate[...] = small_f[:, 0:16]
-    turned = small_f[...].T
-    gconst[...] = turned[16:18]
-    gains[...] = jnp.concatenate([line_f[0:1, 0:192], turned[18:19]], axis=0)
+            gq[c] = att[c * 192 : (c + 1) * 192, :]
+        go[...] = outg[:, 0:384]
+        ggate[...] = small_f[:, 0:16]
+        turned = small_f[...].T
+        gconst[...] = turned[16:18]
+        gains[...] = jnp.concatenate([line_f[0:1, 0:192], turned[18:19]], axis=0)
+
+
+def last_call(spot, gin, tokens, gain, dh, own, recv, att, outg, small_f, line_f, layer_own, layer_other, gprev_t):
+    parts, cols = gin.shape[0], gin.shape[4]
+    seqs, rows, width = tokens.shape
+    head_cols = att.shape[1]
+    some = rows // 4
+    xor = lambda k, s: jnp.bitwise_xor(k, s[0])
+    row = pl.BlockSpec((1, some, width), lambda k, s: (k // 4, k % 4, 0))
+    flat = pl.BlockSpec((some, width), lambda k, s: (k % 4, 0))
+    whole = lambda shape: pl.BlockSpec(shape, lambda k, s: (0,) * len(shape))
+    small = [
+        out((seqs, rows, NEXP), F32), out((2, 192), F32), out((3, 192, head_cols), F32), out((192, head_cols), F32),
+        out((192, 16), F32), out((NCONST, 192), F32),
+    ]
+    return pl.pallas_call(
+        last_body,
+        out_shape=(
+            out((NFFN, 2, 192, cols * parts), F32), out((NFFN, 192, cols * parts), F32), out(tokens.shape),
+            out(tokens.shape, F32), *small,
+        ),
+        grid_spec=pltpu.PrefetchScalarGridSpec(
+            num_scalar_prefetch=1, grid=(NFFN,),
+            in_specs=[pl.BlockSpec((parts, 1, 3, 192, cols), lambda k, s: (0, k, 0, 0, 0)), row, whole(gain.shape)]
+            + [row] * 3
+            + [whole(a.shape) for a in (att, outg, small_f, line_f)]
+            + [flat] * 2
+            + [whole(gprev_t.shape)],
+            out_specs=(
+                pl.BlockSpec((1, 2, 192, cols * parts), lambda k, s: (xor(k, s), 0, 0, 0)),
+                pl.BlockSpec((1, 192, cols * parts), lambda k, s: (xor(k, s), 0, 0)),
+                row, row, *[whole(a.shape) for a in small],
+            ),
+        ),
+        compiler_params=pltpu.CompilerParams(vmem_limit_bytes=56 * MIB),
+        cost_estimate=COST,
+        name="last",
+    )(spot, gin, tokens, gain, dh, own, recv, att, outg, small_f, line_f, layer_own, layer_other, gprev_t)
 
 
 def flip4(v, k):
@@ -1231,7 +1257,7 @@
 
 
 def route_kernel(land, wo, xt, small, small_t, prev, routes, hot, g_rows,
-                 mixed, hidden_ref, xin, m0, m1, m2, m3,
+                 mixed, hidden_ref, xa, xb, m0, m1, m2, m3,
                  attn_send, attn_land, xsend, beside, a_sems, x_sems, b_sems):
     f, z, x = here()
     greet_plane()
@@ -1274,10 +1300,10 @@
     for k in (5, 7, 4, 6, 1, 3, 2, 0):
         block = mm_nt(ext, hot[k * CAPACITY : (k + 1) * CAPACITY, :]).astype(BF)
         if k == 0:
-            xin[0] = block
+            xa[0] = block
         else:
             xsend[k] = block
-            sent.append(to_plane(k, xsend.at[k], xin.at[k], x_sems))
+            sent.append(to_plane(k, xsend.at[k], xa.at[k] if k < EARLY else xb.at[k - EARLY], x_sems))
             sent[-1].start()
     for c in sent + near:
         c.wait()
@@ -1341,9 +1367,19 @@
     dt[...] = d_hidden.astype(BF)
     swap = to_plane(1, dt, d_other, t_sems)
     swap.start()
-    for half in range(2):
-        dm = mm_tn(wo[:, half * 192 : (half + 1) * 192], dt[...])
-        dm_send[place_of(z, x, half)] = dm.astype(BF)
+    def d_mixed(s, rows_ref):
+        for half in range(2):
+            d = place_of(z, s, half)
+            dm_send[d] = mm_tn(wo[:, half * 192 : (half + 1) * 192], rows_ref[...]).astype(BF)
+
+            @pl.when(d > 0)
+            def _(d=d, b=2 * s + half):
+                pltpu.make_async_remote_copy(
+                    src_ref=dm_send.at[d], dst_ref=dm_in.at[d], send_sem=z_sems.at[0, d],
+                    recv_sem=z_sems.at[1, d], device_id=(f, b, x), device_id_type=MESH,
+                ).start()
+
+    d_mixed(x, dt)
     lane = lax.broadcasted_iota(jnp.int32, (width, 128), 1)
     padded = jnp.concatenate([d_logits, jnp.zeros((112, rows), F32)], axis=0).astype(BF)
     g_gate = mm_nt(s["normed_b"], padded)
@@ -1357,12 +1393,8 @@
     rs = [to_plane(k, rsend.at[k], rin.at[k], r_sems) for k in range(1, 8)]
     for c in rs:
         c.start()
-    for half in range(2):
-        dm = mm_tn(wo[:, half * 192 : (half + 1) * 192], d_other[...])
-        dm_send[place_of(z, 1 - x, half)] = dm.astype(BF)
+    d_mixed(1 - x, d_other)
     zs = [to_column(d, dm_send.at[d], dm_in.at[d], z_sems) for d in (1, 2, 3)]
-    for c in zs:
-        c.start()
     dm_in[0] = dm_send[0]
     lines = to_plane(1, gprev.at[x], gprev.at[x], o_sems, 0)
     lines.start()
@@ -1489,11 +1521,12 @@
 
     length = 4 * rows
     unit_scratch = [pltpu.VMEM((3, length, HEAD_DIM), BF)] * 3
-    mixed, hidden, xs, *g_messages = run_remote(
+    mixed, hidden, xa, xb, *g_messages = run_remote(
         route_kernel, "route", 1,
         [mixed_in, wo_full, xt, small, small_t, own_prev, own_routes, hot, g_rows],
         [
-            out((2, head_cols, rows)), out((width, rows), F32), out((8, width + 16, CAPACITY)),
+            out((2, head_cols, rows)), out((width, rows), F32), out((EARLY, width + 16, CAPACITY)),
+            out((8 - EARLY, width + 16, CAPACITY)),
             *[out((2, 3, width, CAPACITY))] * 4,
         ],
         [
@@ -1501,11 +1534,12 @@
             vm((4, 3, width, CAPACITY), BF), sems(8), sems(8), sems(4),
         ],
     )
-    x_all = lax.all_gather(xs, "ctx")
-    g_more = [g_messages[0]] + [flip_plane(g_messages[j], 4 * (j // 2) + j % 2) for j in (1, 2, 3)]
-
-    done = expert_call(jnp.stack([z, f]).astype(jnp.int32), xs[None], gs[None], w_exp, wt_exp)
+    xa_all = lax.all_gather(xa, "ctx")
+    g_more = [g_messages[0]] + [flip_plane(g_messages[j], 4 * (j // 2) + j % 2) for j in (1, 2)]
+
+    done = expert_call(jnp.stack([z, f]).astype(jnp.int32), xa[None], xb[None], gs[None], w_exp, wt_exp)
     ysend, rsend, held = done[0], done[1], done[2:]
+    ysend, g_more[1], g_more[2] = lax.optimization_barrier((ysend, g_more[1], g_more[2]))
     layer_own, grad_prev_t, dm_in, og, d_hidden = run_remote(
         return_kernel, "give_back", 2,
         [ysend, rsend, hidden, small, small_t, own_prev, own_routes, gyt, hot, wo_full, mixed],
@@ -1518,7 +1552,11 @@
             vm((width, rows), BF), vm((width, rows), BF), sems(8), sems(8), sems(8), sems(4), sems(2),
         ],
     )
-    others = jnp.stack([jnp.bitwise_xor(z, d) for d in (1, 2, 3)] + [f]).astype(jnp.int32)
+    far, xb, dm_in = lax.optimization_barrier((g_messages[3], xb, dm_in))
+    xb, xa_all = lax.optimization_barrier((xb, xa_all))
+    xb_all = lax.all_gather(xb, "ctx")
+    g_more.append(flip_plane(far, 5))
+    others = jnp.stack([jnp.bitwise_xor(z, d) for d in (1, 2, 3)] + [f, z % 2]).astype(jnp.int32)
 
     back = run(
         attn_back_kernel, "attention_backward", scalars, [blocks, mixed_lse, dm_in],
@@ -1530,25 +1568,23 @@
         flops=3 * 11 * 512 * 512 * 64 * 10,
     )
     back_in = [back[0]] + [flip_ctx(back[d], d) for d in (1, 2, 3)]
-    held = more_call(others, x_all, g_more, wt_exp, held)
+    held = more_call(others, xa_all, xb_all, g_more, wt_exp, held)
     *back_in, first = lax.optimization_barrier((*back_in, held[0]))
     held = [first, *held[1:]]
     other = flip_tp(layer_own)
-    dn, gq = run(
-        dproj_kernel, "d_projection", scalars, [*back_in, w_full, normed_one_t, cos, sin, tokens],
-        [out((2, rows, width)), out((4, 592, head_cols))],
-        scratch=[pltpu.VMEM((4, 3, rows // 2, head_cols), BF)],
-    )
     parts, cols = 4, 256
     tall = lambda v: v.reshape(4, 2, 1024, 1024)
     bx, bg, ba, bp, bu = held
-    gin, dn_other, att, outg, small_f, line_f = run_remote(
-        finish_kernel, "finish", 5, [bx, bg, tall(bp), tall(bu), tall(ba), dn, gq, og],
+    gin, dn, dn_other, att, outg, small_f, line_f = run_remote(
+        finish_kernel, "finish", 5, [
+            bx, bg, tall(bp), tall(bu), tall(ba), *back_in, w_full, normed_one_t, cos, sin, tokens, og,
+        ],
         [
-            out((parts, 8, 3, 192, cols)), out((2, rows, width)), out((592, head_cols), F32), out((192, 512), F32),
+            out((parts, 8, 3, 192, cols)), out((2, rows, width)), out((2, rows, width)), out((592, head_cols), F32), out((192, 512), F32),
             out((192, 128), F32), out((8, head_cols), F32),
         ],
         [
+            vm((4, 592, head_cols), BF), vm((4, 3, rows // 2, head_cols), BF),
             vm((4, width, 1024), BF), vm((4, width, 1024), BF), vm((2, 2, cols, 1024), BF),
             vm((2, width, cols), F32), vm((9, 8, 192, cols), BF),
             vm((2, 592, head_cols), BF), vm((2, 192, 512), BF), vm((2, 592, head_cols), BF), vm((2, 192, 512), BF),
@@ -1557,19 +1593,13 @@
             vm((2, 192, 128), F32), vm((2, 8, head_cols), F32),
             sems(4), pltpu.SemaphoreType.DMA((2,)), sems(72), pltpu.SemaphoreType.DMA((9,)), sems(12), sems(8), sems(3),
         ],
-        vmem=60, hbm_ins=(0, 1, 2, 3, 4, 5), hbm_outs=(0, 1),
-    )
-    grad_gu, grad_down = place_call(me[None].astype(jnp.int32), gin)
-    layer_out, grad_tokens, grad_prev, grad_gains, grad_qkv, grad_out, grad_gate, grad_const = run(
-        last_kernel, "last", scalars,
-        [
-            tokens, gain_one_row, d_hidden, dn, dn_other, att, outg, small_f, line_f, layer_own, other,
-            grad_prev_t,
-        ],
-        [
-            out((2, rows, width)), out((2, rows, width), F32), out((2, rows, NEXP), F32), out((2, 192), F32),
-            out((3, 192, head_cols), F32), out((192, head_cols), F32), out((192, 16), F32), out((NCONST, 192), F32),
-        ],
+        vmem=61, hbm_ins=(0, 1, 2, 3, 4), hbm_outs=(0, 2),
+    )
+    (
+        grad_gu, grad_down, layer_out, grad_tokens, grad_prev, grad_gains, grad_qkv, grad_out, grad_gate, grad_const,
+    ) = last_call(
+        jnp.stack([me, x]).astype(jnp.int32), gin, tokens, gain_one_row, d_hidden, dn, dn_other, att, outg, small_f,
+        line_f, layer_own, other, grad_prev_t,
     )
     return (
         layer_out, grad_tokens, grad_prev, grad_gains, grad_qkv, grad_out, grad_gate, grad_const,

time: 613 us -> 589 us (0.961)
  Pallas kernels: 553 us -> 537 us
  starting transfers between devices: 15.3 us -> 8.49 us
    pallas_call x3 -> x1, Pallas kernels: 48.7 us -> 30.4 us  [run(): pl.pallas_call(body, out_shape=tuple(outs), in_specs=[SCALARS] + [WHOLE]...]
    pallas_call x1, Pallas kernels: 7.16 us -> 18.5 us  [last_call(): pl.pallas_call(last_body, out_shape=(out((NFFN, 2, 192, cols * parts), F3...]
    pallas_call x1, Pallas kernels: 46.4 us -> 40.2 us  [more_call(): pl.pallas_call(more_body, out_shape=tuple((out(h.shape) for h in held)),...]
    ppermute x3, starting transfers between devices: 10.8 us -> 4.63 us  [flip_ctx(): return lax.ppermute(v, 'ctx', [(i, i ^ k) for i in range(4)])]
  transfers between devices with their start and end apart: 9 -> 10, of which waited for: 0 -> 0; matrix products, arithmetic and copies ran while one was open for 1% -> 2% of each run, Pallas kernels for 81% -> 81%
where the time goes in v5:
time: 589 us; the launch traced here: 579 us
  Pallas kernels  537 us (91%)
  between operations  14.5 us (2%)
  local copies, waits for them, and re-layouts  12.8 us (2%)
  starting transfers between devices  8.49 us (1%)
    pallas_call x5, Pallas kernels, run_remote(): pl.pallas_call(body, out_shape=tuple(outs), in_specs=[HBM if i in hbm_ins...  413 us
    pallas_call x1, Pallas kernels, more_call(): pl.pallas_call(more_body, out_shape=tuple((out(h.shape) for h in held)),...  40.2 us
    pallas_call x1, Pallas kernels, expert_call(): pl.pallas_call(expert_body, out_shape=tuple(packet + [wide] * 2 + [high]...  34.6 us
    pallas_call x1, Pallas kernels, run(): pl.pallas_call(body, out_shape=tuple(outs), in_specs=[SCALARS] + [WHOLE]...  30.4 us
    pallas_call x1, Pallas kernels, last_call(): pl.pallas_call(last_body, out_shape=(out((NFFN, 2, 192, cols * parts), F3...  18.5 us
  transfers between devices with their start and end apart: 10, of which 0 were waited for; matrix products, arithmetic and copies ran while one was open for 2% of the time, Pallas kernels for 81%

profile of v5, /device:TPU:0, one launch (start us, length us, event | category | flops | bytes accessed | tf_op | source)
XLA Modules:
  0.0 578.7 jit_solution(12470455916435673700)
XLA Ops:
  7.2 0.0 copy-start
  7.2 0.0 all-gather.7.cloned.1.call-start
  7.2 1.3 fusion.3
  8.5 1.2 dynamic-slice_bitcast_fusion
  9.8 0.9 fusion.1
  10.7 0.0 all-gather.7.cloned.1.call-update
  10.7 0.0 all-gather.9.cloned.1.call-start
  10.8 0.1 copy.42
  11.0 0.6 pad.12.smallp
  11.6 40.6 %gather.1 = (bf16[1024,512]{1,0:T(8,128)(2,1)}, bf16[768,512]{1,0:T(8,128)(2,1)}, bf16[8,768,128]{2,1,0:T(8,128)(2,1)}, bf16[3,768,384]{2,1,0:T(8,128)(2,1)}, bf...) custom-call(bf16[3,192,384]{2,1,0:T(8,128)(2,1)} %qkv.1, ...), custom_call_target="tpu_custom_call" | custom-call | flops 1024 | bytes 1024 | tf_op jit(solution)/shard_map/gather/pallas_call | solution.py:1424
  52.2 0.6 dynamic_slice.15.prefix_ref
  52.8 1.0 fusion.2
  53.8 1.3 pad_maximum_fusion
  55.1 117.3 %attend.1 = (bf16[768,1024]{1,0:T(8,128)(2,1)}, bf16[768,512]{1,0:T(8,128)(2,1)}, bf16[4,3,256,384]{3,2,1,0:T(8,128)(2,1)}, bf16[4,192,512]{2,1,0:T(8,128)(2,1)}...) custom-call(s32[1]{0:T(128)} %dynamic_slice.15.prefix_ref, ...), custom_call_target="tpu_custom_call" | custom-call | flops 1024 | bytes 1024 | tf_op jit(solution)/shard_map/attend/pallas_call | solution.py:1424
  172.4 0.6 pad.13.prev
  173.1 48.4 %route.1 = (bf16[2,384,512]{2,1,0:T(8,128)(2,1)}, f32[768,512]{1,0:T(8,128)}, bf16[6,784,128]{2,1,0:T(8,128)(2,1)}, bf16[2,784,128]{2,1,0:T(8,128)(2,1)}, bf16[2...) custom-call(bf16[4,192,512]{2,1,0:T(8,128)(2,1)} %get-tuple-element., ...), custom_call_target="tpu_custom_call" | custom-call | flops 1024 | bytes 1024 | tf_op jit(solution)/shard_map/route/pallas_call | solution.py:1424
  221.5 0.0 all-gather.9.cloned.1.call-update
  221.5 0.0 all-gather.11.cloned.1.call-start
  221.6 0.6 collective-permute-start
  222.2 0.6 collective-permute-start.1
  222.8 0.6 pad_add_fusion.1.sc
  223.3 34.6 %experts_own.1 = (bf16[8,784,128]{2,1,0:T(8,128)(2,1)}, bf16[8,768,128]{2,1,0:T(8,128)(2,1)}, bf16[4,768,1024]{2,1,0:T(8,128)(2,1)}, bf16[4,768,1024]{2,1,0:T(8,...) custom-call(s32[2]{0:T(128)} %pad_add_fusion.1.sc, ...), custom_call_target="tpu_custom_call" | custom-call | flops 1024 | bytes 1024 | tf_op jit(solution)/shard_map/experts_own/pallas_call | solution.py:644
  257.9 0.0 collective-permute-done.g1
  258.0 70.0 %give_back.1 = (bf16[512,768]{1,0:T(8,128)(2,1)}, f32[2,16,512]{2,1,0:T(8,128)}, bf16[4,192,512]{2,1,0:T(8,128)(2,1)}, bf16[4,192,512]{2,1,0:T(8,128)(2,1)}, bf16[2,512,768]{2,1,0:T(8,128)(2,1)}) custom-call(bf16[8,784,128]{2,1,0:T(8,128)(2,1)} %get-tuple-element.109.ysend, bf16[8,768,128]{2,1,0:T(8,128)(2,1)} %get-tuple-element.110.rsend, ...), custom_call_target="tpu_custom_call" | custom-call | flops 1024 | bytes 1024 | tf_op jit(solution)/shard_map/give_back/pallas_call | solution.py:1424
  328.0 0.0 all-gather.9.cloned.1.call-done
  328.0 0.0 all-gather.11.cloned.1.call-update
  328.1 2.3 collective-permute-start.5
  330.4 0.2 collective-permute-start.6
  330.6 1.2 stack.46.sc
  331.8 30.4 %attention_backward.1 = (bf16[3,256,384]{2,1,0:T(8,128)(2,1)}, bf16[3,256,384]{2,1,0:T(8,128)(2,1)}, bf16[3,256,384]{2,1,0:T(8,128)(2,1)}, bf16[3,256,384]{2,1,0:T(8,128)(2,1)}) custom-call(s32[5]{0:T(128)} %stack.46.sc, bf16[4,3,256,384]{3,2,1,0:T(8,128)(2,1)} %get-tuple-element.93.blocks, f32[3,72,2048]{2,1,0:T(8,128)} %get-tuple-element.94.m_ref, ...), custom_call_target="tpu_custom_call" | custom-call | flops 1024 | bytes 1024 | tf_op jit(solution)/shard_map/attention_backward/pallas_call | solution.py:451
  362.2 2.3 collective-permute-start.2
  364.5 1.7 collective-permute-start.3
  366.2 0.6 collective-permute-start.4
  366.9 1.3 slice.3.gain
  368.2 0.6 stack.52.sc
  368.8 0.7 pad_add_fusion.sc
  369.5 1.0 copy-done.4
  370.5 40.2 %experts_more.1 = (bf16[4,768,1024]{2,1,0:T(8,128)(2,1)}, bf16[4,768,1024]{2,1,0:T(8,128)(2,1)}, bf16[4,2048,1024]{2,1,0:T(8,128)(2,1)}, bf16[4,2048,1024]{2,1,0:T(8,128)(2,1)}, bf16[4,2048,1024]{2,1,0:T(8,128)(2,1)}) custom-call(s32[5]{0:T(128)} %stack.52.sc, ...), custom_call_target="tpu_custom_call", output_to_operand_aliasing={{0}: (8, {}), {1}: (9, {}), {2}: (10, {}), {3}: (11, {}), {... | custom-call | flops 1024 | bytes 1024 | tf_op jit(solution)/shard_map/experts_more/pallas_call | solution.py:620
  410.7 0.0 copy-start.6
  410.7 0.0 collective-permute-done.3.b2
  410.7 0.0 copy-start.7
  410.7 0.8 copy-done.6
  411.5 0.2 copy-done.7
  411.7 137.1 %finish.1 = (bf16[4,8,3,192,256]{4,3,2,1,0:T(8,128)(2,1)}, bf16[2,512,768]{2,1,0:T(8,128)(2,1)}, bf16[2,512,768]{2,1,0:T(8,128)(2,1)}, f32[592,384]{1,0:T(8,128)...) custom-call(bf16[4,768,1024]{2,1,0:T(8,128)(2,1)} %get-tuple-element.133.bx, ...), custom_call_target="tpu_custom_call" | custom-call | flops 1024 | bytes 1024 | tf_op jit(solution)/shard_map/finish/pallas_call | solution.py:1424
  548.9 0.9 copy-done.5
  549.8 18.5 %last.1 = (f32[8,2,192,1024]{3,2,1,0:T(8,128)}, f32[8,192,1024]{2,1,0:T(8,128)}, bf16[2,512,768]{2,1,0:T(8,128)(2,1)}, f32[2,512,768]{2,1,0:T(8,128)}, f32[2,512...) custom-call(s32[2]{0:T(128)} %pad_add_fusion.sc, ...), custom_call_target="tpu_custom_call" | custom-call | flops 1024 | bytes 1024 | tf_op jit(solution)/shard_map/last/pallas_call | solution.py:938
  568.3 1.9 copy.45
  570.2 1.6 copy.46
  (29 shorter events, 0.1 us)
Async XLA Ops:
  7.2 165.2 %copy-start = (f32[2,512,12]{1,0,2:T(2,128)S(1)}, f32[2,512,12]{1,0,2:T(2,128)}, u32[]{:S(2)}) copy-start(f32[2,512,12]{1,0,2:T(2,128)} %param.13) | copy-start | bytes 147460
  7.2 165.9 %all-gather.7.cloned.1.call-start = ((), (), s32[]{:S(2)}) async-start(), calls=%async_computation | async-start | bytes 4055040 | tf_op jit(solution)/shard_map/all_gather | solution.py:1474
  8.5 2.3 copy-start.8
  8.5 2.3 copy-start.9
  8.5 2.3 copy-start.10
  10.7 317.3 %all-gather.9.cloned.1.call-start = ((), (), s32[]{:S(2)}) async-start(), calls=%async_computation.1 | async-start | bytes 6021120 | tf_op jit(solution)/shard_map/all_gather | solution.py:1537
  11.6 40.6 %copy-start.11 = (s32[2]{0:T(128)S(1)}, s32[2]{0:T(128)}, u32[]{:S(2)}) copy-start(s32[2]{0:T(128)} %param.15) | copy-start | bytes 28
  221.5 147.9 %all-gather.11.cloned.1.call-start = ((), (), s32[]{:S(2)}) async-start(), calls=%async_computation.2 | async-start | bytes 2007040 | tf_op jit(solution)/shard_map/all_gather | solution.py:1557
  221.6 36.4 %collective-permute-start = (bf16[2,3,768,128]{3,2,1,0:T(8,128)(2,1)}, bf16[2,3,768,128]{3,2,1,0:T(8,128)(2,1)S(1)}, u32[]{:S(2)}, u32[]{:S(2)}) collective-permute-start(bf16[2,3,768,128]{3,2,1,0:T(8,128)(2,1)} %get-tuple-element.107), channel_id=1, source_target_pairs={{0,1},{1,0},{8,9},{9,8},{16,17},{17,16},{24,25},{25,24},{2,3},{3,2... | collective-permute-start | bytes 3538952 | tf_op jit(solution)/shard_map/ppermute | solution.py:1464
  222.2 35.8 %collective-permute-start.1 = (bf16[2,3,768,128]{3,2,1,0:T(8,128)(2,1)}, bf16[2,3,768,128]{3,2,1,0:T(8,128)(2,1)S(1)}, u32[]{:S(2)}, u32[]{:S(2)}) collective-permute-start(bf16[2,3,768,128]{3,2,1,0:T(8,128)(2,1)} %get-tuple-element.108), channel_id=1, source_target_pairs={{0,16},{1,17},{8,24},{9,25},{16,0},{17,1},{24,8},{25,9},{2,18},{3,... | collective-permute-start | bytes 3538952 | tf_op jit(solution)/shard_map/ppermute | solution.py:1464
  257.9 70.0 %copy-start.2 = (bf16[2,3,768,128]{3,2,1,0:T(8,128)(2,1)}, bf16[2,3,768,128]{3,2,1,0:T(8,128)(2,1)S(1)}, u32[]{:S(2)}) copy-start(bf16[2,3,768,128]{3,2,1,0:T(8,128)(2,1)S(1)} %collective-permute-done.g1) | copy-start | bytes 3538948
  258.0 70.0 %copy-start.3 = (bf16[2,3,768,128]{3,2,1,0:T(8,128)(2,1)}, bf16[2,3,768,128]{3,2,1,0:T(8,128)(2,1)S(1)}, u32[]{:S(2)}) copy-start(bf16[2,3,768,128]{3,2,1,0:T(8,128)(2,1)S(1)} %collective-permute-done.1.g2) | copy-start | bytes 3538948
  328.1 41.4 %collective-permute-start.5 = (bf16[2,3,768,128]{3,2,1,0:T(8,128)(2,1)}, bf16[2,3,768,128]{3,2,1,0:T(8,128)(2,1)S(1)}, u32[]{:S(2)}, u32[]{:S(2)}) collective-permute-start(bf16[2,3,768,128]{3,2,1,0:T(8,128)(2,1)} %get-tuple-element.126), channel_id=1, source_target_pairs={{0,17},{1,16},{8,25},{9,24},{16,1},{17,0},{24,9},{25,8},{2,19},{3,... | collective-permute-start | bytes 3538952 | tf_op jit(solution)/shard_map/ppermute | solution.py:1464
  330.4 218.5 %collective-permute-start.6 = (bf16[512,768]{1,0:T(8,128)(2,1)}, bf16[512,768]{1,0:T(8,128)(2,1)S(1)}, u32[]{:S(2)}, u32[]{:S(2)}) collective-permute-start(bf16[512,768]{1,0:T(8,128)(2,1)} %get-tuple-element.152.layer_own), channel_id=1, source_target_pairs={{0,1},{1,0},{2,3},{3,2},{4,5},{5,4},{6,7},{7,6},{8,9},{9,8},{10,11... | collective-permute-start | bytes 2359304 | tf_op jit(solution)/shard_map/ppermute | solution.py:1458
  362.2 48.5 %collective-permute-start.2 = (bf16[3,256,384]{2,1,0:T(8,128)(2,1)}, bf16[3,256,384]{2,1,0:T(8,128)(2,1)S(1)}, u32[]{:S(2)}, u32[]{:S(2)}) collective-permute-start(bf16[3,256,384]{2,1,0:T(8,128)(2,1)} %get-tuple-element.117), channel_id=1, source_target_pairs={{0,2},{2,0},{4,6},{6,4},{1,3},{3,1},{5,7},{7,5},{8,10},{10,8},{12,... | collective-permute-start | bytes 1769480 | tf_op jit(solution)/shard_map/ppermute | solution.py:1461
  364.5 46.2 %collective-permute-start.3 = (bf16[3,256,384]{2,1,0:T(8,128)(2,1)}, bf16[3,256,384]{2,1,0:T(8,128)(2,1)S(1)}, u32[]{:S(2)}, u32[]{:S(2)}) collective-permute-start(bf16[3,256,384]{2,1,0:T(8,128)(2,1)} %get-tuple-element.118), channel_id=1, source_target_pairs={{0,4},{2,6},{4,0},{6,2},{1,5},{3,7},{5,1},{7,3},{8,12},{10,14},{12... | collective-permute-start | bytes 1769480 | tf_op jit(solution)/shard_map/ppermute | solution.py:1461
  366.2 44.5 %collective-permute-start.4 = (bf16[3,256,384]{2,1,0:T(8,128)(2,1)}, bf16[3,256,384]{2,1,0:T(8,128)(2,1)}, u32[]{:S(2)}, u32[]{:S(2)}) collective-permute-start(bf16[3,256,384]{2,1,0:T(8,128)(2,1)} %get-tuple-element.119), channel_id=1, source_target_pairs={{0,6},{2,4},{4,2},{6,0},{1,7},{3,5},{5,3},{7,1},{8,14},{10,12},{12... | collective-permute-start | bytes 1769480 | tf_op jit(solution)/shard_map/ppermute | solution.py:1461
  369.5 1.0 copy-start.4
  410.7 0.8 copy-start.6
  410.7 1.0 copy-start.7
  548.9 0.9 copy-start.5
  549.8 21.9 %copy-start.1 = (f32[2,512,12]{1,0,2:T(2,128)S(1)}, f32[2,512,12]{1,0,2:T(2,128)}, u32[]{:S(2)}) copy-start(f32[2,512,12]{1,0,2:T(2,128)} %param.13) | copy-start | bytes 147460
Sparse Core Ops, SparseCore 0:
  10.8 90.7 all-gather.6
  221.6 105.8 all-gather.8
  329.1 36.6 all-gather.10

commit v6 on v5

--- a/solution.py
+++ b/solution.py
@@ -686,11 +686,11 @@
     def tile_copy(part, m, p):
         src = (bp, bu, ba)[m]
         return pltpu.make_async_copy(
-            src.at[p, :, pl.ds(pl.multiple_of(part * cols, cols), cols), :], tiles.at[p % 2], tile_sems.at[p % 2]
+            src.at[p, :, pl.ds(pl.multiple_of(part * cols, cols), cols), :], tiles.at[p], tile_sems.at[p]
         )
 
     plan = [(parity, m) for m in range(3)] + [(part, m) for part in (2, 3) for m in range(3)]
-    for c in [tile_copy(*plan[0], 0)] + loads:
+    for c in [tile_copy(*plan[0], p) for p in range(planes)] + loads:
         c.start()
     def plus(a, b):
         return a.astype(F32) + b.astype(F32)
@@ -791,21 +791,12 @@
 
         def plane_step(p, carry, number=number, part=part, m=m, rows_s=rows_s, at=at):
             tile_copy(part, m, p).wait()
-
-            @pl.when(p < planes - 1)
-            def _():
-                tile_copy(part, m, p + 1).start()
-
-            if number + 1 < len(plan):
-
-                @pl.when(p == planes - 1)
-                def _():
-                    tile_copy(*plan[number + 1], 0).start()
-
             if number in (0, 2):
                 pltpu.make_async_copy((bx, bg)[at].at[p], rows_s.at[p], xg_sems.at[at, p]).wait()
             for xh in range(2):
-                acc[xh] += mm_nt(rows_s[p], tiles[p % 2, xh])
+                acc[xh] += mm_nt(rows_s[p], tiles[p, xh])
+            if number + 1 < len(plan):
+                tile_copy(*plan[number + 1], p).start()
             return carry
 
         lax.fori_loop(0, planes, plane_step, 0)
@@ -818,18 +809,22 @@
                 sent[-1].append(to_plane(k, src, dst, send_sems, number * 8 + k))
             else:
                 sent[-1].append(pltpu.make_async_copy(src, dst, own_sems.at[number]))
-            sent[-1][-1].start()
+            if number not in (3, 4):
+                sent[-1][-1].start()
         if number == 2:
             overs.append(hand_over(0))
             project_back()
             overs.append(hand_over(1))
         if number == 3:
             overs.append(hand_over(2))
-        if number > 4:
+        if number in (3, 4, 7, 8):
             for c in steps:
                 c.wait()
-            steps = after(number - 5)
+            steps = after((3, 4, 7, 8).index(number))
             for c in steps:
+                c.start()
+        if number == 4:
+            for c in sent[3] + sent[4]:
                 c.start()
     for c in steps:
         c.wait()
@@ -912,12 +907,12 @@
     @pl.when(step == 0)
     def _():
         for s in range(2):
-            gprev[s] = gprev_t[s].T[:, 0:NEXP]
+            gprev[:, s, :] = gprev_t[s, 0:NEXP, :]
         for c in range(3):
             gq[c] = att[c * 192 : (c + 1) * 192, :]
         go[...] = outg[:, 0:384]
-        ggate[...] = small_f[:, 0:16]
         turned = small_f[...].T
+        ggate[...] = turned[0:16]
         gconst[...] = turned[16:18]
         gains[...] = jnp.concatenate([line_f[0:1, 0:192], turned[18:19]], axis=0)
 
@@ -932,8 +927,8 @@
     flat = pl.BlockSpec((some, width), lambda k, s: (k % 4, 0))
     whole = lambda shape: pl.BlockSpec(shape, lambda k, s: (0,) * len(shape))
     small = [
-        out((seqs, rows, NEXP), F32), out((2, 192), F32), out((3, 192, head_cols), F32), out((192, head_cols), F32),
-        out((192, 16), F32), out((NCONST, 192), F32),
+        out((NEXP, seqs, rows), F32), out((2, 192), F32), out((3, 192, head_cols), F32), out((192, head_cols), F32),
+        out((16, 192), F32), out((NCONST, 192), F32),
     ]
     return pl.pallas_call(
         last_body,
@@ -1585,13 +1580,13 @@
         ],
         [
             vm((4, 592, head_cols), BF), vm((4, 3, rows // 2, head_cols), BF),
-            vm((4, width, 1024), BF), vm((4, width, 1024), BF), vm((2, 2, cols, 1024), BF),
+            vm((4, width, 1024), BF), vm((4, width, 1024), BF), vm((4, 2, cols, 1024), BF),
             vm((2, width, cols), F32), vm((9, 8, 192, cols), BF),
             vm((2, 592, head_cols), BF), vm((2, 192, 512), BF), vm((2, 592, head_cols), BF), vm((2, 192, 512), BF),
             vm((592, head_cols), BF), vm((192, 512), BF), vm((592, head_cols), BF), vm((192, 512), BF),
             vm((592, head_cols), BF), vm((192, 512), BF), vm((592, head_cols), BF), vm((192, 512), BF),
             vm((2, 192, 128), F32), vm((2, 8, head_cols), F32),
-            sems(4), pltpu.SemaphoreType.DMA((2,)), sems(72), pltpu.SemaphoreType.DMA((9,)), sems(12), sems(8), sems(3),
+            sems(4), pltpu.SemaphoreType.DMA((4,)), sems(72), pltpu.SemaphoreType.DMA((9,)), sems(12), sems(8), sems(3),
         ],
         vmem=61, hbm_ins=(0, 1, 2, 3, 4), hbm_outs=(0, 2),
     )
@@ -1601,6 +1596,8 @@
         jnp.stack([me, x]).astype(jnp.int32), gin, tokens, gain_one_row, d_hidden, dn, dn_other, att, outg, small_f,
         line_f, layer_own, other, grad_prev_t,
     )
+    grad_prev = jnp.transpose(grad_prev, (1, 2, 0))
+    grad_gate = grad_gate.T
     return (
         layer_out, grad_tokens, grad_prev, grad_gains, grad_qkv, grad_out, grad_gate, grad_const,
         grad_gu, grad_down,

time: 589 us -> 581 us (0.986)
  transfers between devices with their start and end apart: 10 -> 10, of which waited for: 0 -> 0; matrix products, arithmetic and copies ran while one was open for 2% -> 2% of each run, Pallas kernels for 81% -> 82%
where the time goes in v6:
time: 581 us; the launch traced here: 572 us
  Pallas kernels  534 us (92%)
  between operations  14.5 us (2%)
  local copies, waits for them, and re-layouts  9.38 us (2%)
  starting transfers between devices  8.49 us (1%)
    pallas_call x5, Pallas kernels, run_remote(): pl.pallas_call(body, out_shape=tuple(outs), in_specs=[HBM if i in hbm_ins...  410 us
    pallas_call x1, Pallas kernels, more_call(): pl.pallas_call(more_body, out_shape=tuple((out(h.shape) for h in held)),...  40.2 us
    pallas_call x1, Pallas kernels, expert_call(): pl.pallas_call(expert_body, out_shape=tuple(packet + [wide] * 2 + [high]...  34.6 us
    pallas_call x1, Pallas kernels, run(): pl.pallas_call(body, out_shape=tuple(outs), in_specs=[SCALARS] + [WHOLE]...  30.4 us
    pallas_call x1, Pallas kernels, last_call(): pl.pallas_call(last_body, out_shape=(out((NFFN, 2, 192, cols * parts), F3...  18.3 us
  transfers between devices with their start and end apart: 10, of which 0 were waited for; matrix products, arithmetic and copies ran while one was open for 2% of the time, Pallas kernels for 82%

profile of v6, /device:TPU:0, one launch (start us, length us, event | category | flops | bytes accessed | tf_op | source)
XLA Modules:
  0.0 572.0 jit_solution(9873455030588264538)
XLA Ops:
  7.2 0.0 copy-start
  7.2 0.0 all-gather.7.cloned.1.call-start
  7.2 1.3 fusion.3
  8.5 1.2 dynamic-slice_bitcast_fusion
  9.8 0.9 fusion.1
  10.7 0.0 all-gather.7.cloned.1.call-update
  10.7 0.0 all-gather.9.cloned.1.call-start
  10.8 0.1 copy.36
  11.0 0.6 pad.12.smallp
  11.6 40.6 %gather.1 = (bf16[1024,512]{1,0:T(8,128)(2,1)}, bf16[768,512]{1,0:T(8,128)(2,1)}, bf16[8,768,128]{2,1,0:T(8,128)(2,1)}, bf16[3,768,384]{2,1,0:T(8,128)(2,1)}, bf...) custom-call(bf16[3,192,384]{2,1,0:T(8,128)(2,1)} %qkv.1, ...), custom_call_target="tpu_custom_call" | custom-call | flops 1024 | bytes 1024 | tf_op jit(solution)/shard_map/gather/pallas_call | solution.py:1419
  52.2 0.6 dynamic_slice.15.prefix_ref
  52.8 1.0 fusion.2
  53.8 1.3 pad_maximum_fusion
  55.1 117.3 %attend.1 = (bf16[768,1024]{1,0:T(8,128)(2,1)}, bf16[768,512]{1,0:T(8,128)(2,1)}, bf16[4,3,256,384]{3,2,1,0:T(8,128)(2,1)}, bf16[4,192,512]{2,1,0:T(8,128)(2,1)}...) custom-call(s32[1]{0:T(128)} %dynamic_slice.15.prefix_ref, ...), custom_call_target="tpu_custom_call" | custom-call | flops 1024 | bytes 1024 | tf_op jit(solution)/shard_map/attend/pallas_call | solution.py:1419
  172.4 0.6 pad.13.prev
  173.1 48.4 %route.1 = (bf16[2,384,512]{2,1,0:T(8,128)(2,1)}, f32[768,512]{1,0:T(8,128)}, bf16[6,784,128]{2,1,0:T(8,128)(2,1)}, bf16[2,784,128]{2,1,0:T(8,128)(2,1)}, bf16[2...) custom-call(bf16[4,192,512]{2,1,0:T(8,128)(2,1)} %get-tuple-element., ...), custom_call_target="tpu_custom_call" | custom-call | flops 1024 | bytes 1024 | tf_op jit(solution)/shard_map/route/pallas_call | solution.py:1419
  221.5 0.0 all-gather.9.cloned.1.call-update
  221.5 0.0 all-gather.11.cloned.1.call-start
  221.6 0.6 collective-permute-start
  222.2 0.6 collective-permute-start.1
  222.8 0.6 pad_add_fusion.1.sc
  223.3 34.6 %experts_own.1 = (bf16[8,784,128]{2,1,0:T(8,128)(2,1)}, bf16[8,768,128]{2,1,0:T(8,128)(2,1)}, bf16[4,768,1024]{2,1,0:T(8,128)(2,1)}, bf16[4,768,1024]{2,1,0:T(8,...) custom-call(s32[2]{0:T(128)} %pad_add_fusion.1.sc, ...), custom_call_target="tpu_custom_call" | custom-call | flops 1024 | bytes 1024 | tf_op jit(solution)/shard_map/experts_own/pallas_call | solution.py:644
  257.9 0.0 collective-permute-done.g1
  258.0 0.0 collective-permute-done.1.g2
  258.0 70.0 %give_back.1 = (bf16[512,768]{1,0:T(8,128)(2,1)}, f32[2,16,512]{2,1,0:T(8,128)}, bf16[4,192,512]{2,1,0:T(8,128)(2,1)}, bf16[4,192,512]{2,1,0:T(8,128)(2,1)}, bf16[2,512,768]{2,1,0:T(8,128)(2,1)}) custom-call(bf16[8,784,128]{2,1,0:T(8,128)(2,1)} %get-tuple-element.109.ysend, bf16[8,768,128]{2,1,0:T(8,128)(2,1)} %get-tuple-element.110.rsend, ...), custom_call_target="tpu_custom_call" | custom-call | flops 1024 | bytes 1024 | tf_op jit(solution)/shard_map/give_back/pallas_call | solution.py:1419
  328.0 0.0 all-gather.9.cloned.1.call-done
  328.0 0.0 all-gather.11.cloned.1.call-update
  328.1 2.3 collective-permute-start.5
  330.4 0.2 collective-permute-start.6
  330.6 1.2 stack.46.sc
  331.8 30.4 %attention_backward.1 = (bf16[3,256,384]{2,1,0:T(8,128)(2,1)}, bf16[3,256,384]{2,1,0:T(8,128)(2,1)}, bf16[3,256,384]{2,1,0:T(8,128)(2,1)}, bf16[3,256,384]{2,1,0:T(8,128)(2,1)}) custom-call(s32[5]{0:T(128)} %stack.46.sc, bf16[4,3,256,384]{3,2,1,0:T(8,128)(2,1)} %get-tuple-element.93.blocks, f32[3,72,2048]{2,1,0:T(8,128)} %get-tuple-element.94.m_ref, ...), custom_call_target="tpu_custom_call" | custom-call | flops 1024 | bytes 1024 | tf_op jit(solution)/shard_map/attention_backward/pallas_call | solution.py:451
  362.2 2.3 collective-permute-start.2
  364.5 1.7 collective-permute-start.3
  366.2 0.6 collective-permute-start.4
  366.9 1.3 slice.3.gain
  368.2 0.6 stack.52.sc
  368.8 0.7 pad_add_fusion.sc
  369.5 1.0 copy-done.4
  370.5 40.2 %experts_more.1 = (bf16[4,768,1024]{2,1,0:T(8,128)(2,1)}, bf16[4,768,1024]{2,1,0:T(8,128)(2,1)}, bf16[4,2048,1024]{2,1,0:T(8,128)(2,1)}, bf16[4,2048,1024]{2,1,0:T(8,128)(2,1)}, bf16[4,2048,1024]{2,1,0:T(8,128)(2,1)}) custom-call(s32[5]{0:T(128)} %stack.52.sc, ...), custom_call_target="tpu_custom_call", output_to_operand_aliasing={{0}: (8, {}), {1}: (9, {}), {2}: (10, {}), {3}: (11, {}), {... | custom-call | flops 1024 | bytes 1024 | tf_op jit(solution)/shard_map/experts_more/pallas_call | solution.py:620
  410.7 0.0 copy-start.6
  410.7 0.0 copy-start.7
  410.7 0.0 collective-permute-done.4.b3
  410.7 0.8 copy-done.6
  411.5 0.2 copy-done.7
  411.7 134.1 %finish.1 = (bf16[4,8,3,192,256]{4,3,2,1,0:T(8,128)(2,1)}, bf16[2,512,768]{2,1,0:T(8,128)(2,1)}, bf16[2,512,768]{2,1,0:T(8,128)(2,1)}, f32[592,384]{1,0:T(8,128)...) custom-call(bf16[4,768,1024]{2,1,0:T(8,128)(2,1)} %get-tuple-element.133.bx, ...), custom_call_target="tpu_custom_call" | custom-call | flops 1024 | bytes 1024 | tf_op jit(solution)/shard_map/finish/pallas_call | solution.py:1419
  545.8 0.0 collective-permute-done.6.layer_other
  545.8 0.9 copy-done.5
  546.8 18.3 %last.1 = (f32[8,2,192,1024]{3,2,1,0:T(8,128)}, f32[8,192,1024]{2,1,0:T(8,128)}, bf16[2,512,768]{2,1,0:T(8,128)(2,1)}, f32[2,512,768]{2,1,0:T(8,128)}, f32[12,2,...) custom-call(s32[2]{0:T(128)} %pad_add_fusion.sc, ...), custom_call_target="tpu_custom_call" | custom-call | flops 1024 | bytes 1024 | tf_op jit(solution)/shard_map/last/pallas_call | solution.py:933
  (27 shorter events, 0.1 us)
Async XLA Ops:
  7.2 165.2 %copy-start = (f32[2,512,12]{1,0,2:T(2,128)S(1)}, f32[2,512,12]{1,0,2:T(2,128)}, u32[]{:S(2)}) copy-start(f32[2,512,12]{1,0,2:T(2,128)} %param.13) | copy-start | bytes 147460
  7.2 165.9 %all-gather.7.cloned.1.call-start = ((), (), s32[]{:S(2)}) async-start(), calls=%async_computation | async-start | bytes 4055040 | tf_op jit(solution)/shard_map/all_gather | solution.py:1469
  8.5 2.3 copy-start.8
  8.5 2.3 copy-start.9
  8.5 2.3 copy-start.10
  10.7 317.3 %all-gather.9.cloned.1.call-start = ((), (), s32[]{:S(2)}) async-start(), calls=%async_computation.1 | async-start | bytes 6021120 | tf_op jit(solution)/shard_map/all_gather | solution.py:1532
  11.6 40.6 %copy-start.11 = (s32[2]{0:T(128)S(1)}, s32[2]{0:T(128)}, u32[]{:S(2)}) copy-start(s32[2]{0:T(128)} %param.15) | copy-start | bytes 28
  221.5 148.0 %all-gather.11.cloned.1.call-start = ((), (), s32[]{:S(2)}) async-start(), calls=%async_computation.2 | async-start | bytes 2007040 | tf_op jit(solution)/shard_map/all_gather | solution.py:1552
  221.6 36.4 %collective-permute-start = (bf16[2,3,768,128]{3,2,1,0:T(8,128)(2,1)}, bf16[2,3,768,128]{3,2,1,0:T(8,128)(2,1)S(1)}, u32[]{:S(2)}, u32[]{:S(2)}) collective-permute-start(bf16[2,3,768,128]{3,2,1,0:T(8,128)(2,1)} %get-tuple-element.107), channel_id=1, source_target_pairs={{0,1},{1,0},{8,9},{9,8},{16,17},{17,16},{24,25},{25,24},{2,3},{3,2... | collective-permute-start | bytes 3538952 | tf_op jit(solution)/shard_map/ppermute | solution.py:1459
  222.2 35.8 %collective-permute-start.1 = (bf16[2,3,768,128]{3,2,1,0:T(8,128)(2,1)}, bf16[2,3,768,128]{3,2,1,0:T(8,128)(2,1)S(1)}, u32[]{:S(2)}, u32[]{:S(2)}) collective-permute-start(bf16[2,3,768,128]{3,2,1,0:T(8,128)(2,1)} %get-tuple-element.108), channel_id=1, source_target_pairs={{0,16},{1,17},{8,24},{9,25},{16,0},{17,1},{24,8},{25,9},{2,18},{3,... | collective-permute-start | bytes 3538952 | tf_op jit(solution)/shard_map/ppermute | solution.py:1459
  257.9 70.0 %copy-start.2 = (bf16[2,3,768,128]{3,2,1,0:T(8,128)(2,1)}, bf16[2,3,768,128]{3,2,1,0:T(8,128)(2,1)S(1)}, u32[]{:S(2)}) copy-start(bf16[2,3,768,128]{3,2,1,0:T(8,128)(2,1)S(1)} %collective-permute-done.g1) | copy-start | bytes 3538948
  258.0 70.0 %copy-start.3 = (bf16[2,3,768,128]{3,2,1,0:T(8,128)(2,1)}, bf16[2,3,768,128]{3,2,1,0:T(8,128)(2,1)S(1)}, u32[]{:S(2)}) copy-start(bf16[2,3,768,128]{3,2,1,0:T(8,128)(2,1)S(1)} %collective-permute-done.1.g2) | copy-start | bytes 3538948
  328.1 41.4 %collective-permute-start.5 = (bf16[2,3,768,128]{3,2,1,0:T(8,128)(2,1)}, bf16[2,3,768,128]{3,2,1,0:T(8,128)(2,1)S(1)}, u32[]{:S(2)}, u32[]{:S(2)}) collective-permute-start(bf16[2,3,768,128]{3,2,1,0:T(8,128)(2,1)} %get-tuple-element.126), channel_id=1, source_target_pairs={{0,17},{1,16},{8,25},{9,24},{16,1},{17,0},{24,9},{25,8},{2,19},{3,... | collective-permute-start | bytes 3538952 | tf_op jit(solution)/shard_map/ppermute | solution.py:1459
  330.4 215.4 %collective-permute-start.6 = (bf16[512,768]{1,0:T(8,128)(2,1)}, bf16[512,768]{1,0:T(8,128)(2,1)S(1)}, u32[]{:S(2)}, u32[]{:S(2)}) collective-permute-start(bf16[512,768]{1,0:T(8,128)(2,1)} %get-tuple-element.152.layer_own), channel_id=1, source_target_pairs={{0,1},{1,0},{2,3},{3,2},{4,5},{5,4},{6,7},{7,6},{8,9},{9,8},{10,11... | collective-permute-start | bytes 2359304 | tf_op jit(solution)/shard_map/ppermute | solution.py:1453
  362.2 48.5 %collective-permute-start.2 = (bf16[3,256,384]{2,1,0:T(8,128)(2,1)}, bf16[3,256,384]{2,1,0:T(8,128)(2,1)S(1)}, u32[]{:S(2)}, u32[]{:S(2)}) collective-permute-start(bf16[3,256,384]{2,1,0:T(8,128)(2,1)} %get-tuple-element.117), channel_id=1, source_target_pairs={{0,2},{2,0},{4,6},{6,4},{1,3},{3,1},{5,7},{7,5},{8,10},{10,8},{12,... | collective-permute-start | bytes 1769480 | tf_op jit(solution)/shard_map/ppermute | solution.py:1456
  364.5 46.2 %collective-permute-start.3 = (bf16[3,256,384]{2,1,0:T(8,128)(2,1)}, bf16[3,256,384]{2,1,0:T(8,128)(2,1)S(1)}, u32[]{:S(2)}, u32[]{:S(2)}) collective-permute-start(bf16[3,256,384]{2,1,0:T(8,128)(2,1)} %get-tuple-element.118), channel_id=1, source_target_pairs={{0,4},{2,6},{4,0},{6,2},{1,5},{3,7},{5,1},{7,3},{8,12},{10,14},{12... | collective-permute-start | bytes 1769480 | tf_op jit(solution)/shard_map/ppermute | solution.py:1456
  366.2 44.5 %collective-permute-start.4 = (bf16[3,256,384]{2,1,0:T(8,128)(2,1)}, bf16[3,256,384]{2,1,0:T(8,128)(2,1)}, u32[]{:S(2)}, u32[]{:S(2)}) collective-permute-start(bf16[3,256,384]{2,1,0:T(8,128)(2,1)} %get-tuple-element.119), channel_id=1, source_target_pairs={{0,6},{2,4},{4,2},{6,0},{1,7},{3,5},{5,3},{7,1},{8,14},{10,12},{12... | collective-permute-start | bytes 1769480 | tf_op jit(solution)/shard_map/ppermute | solution.py:1456
  369.5 1.0 copy-start.4
  410.7 0.8 copy-start.6
  410.7 1.0 copy-start.7
  545.8 0.9 copy-start.5
  546.8 18.3 %copy-start.1 = (f32[2,512,12]{1,0,2:T(2,128)S(1)}, f32[2,512,12]{1,0,2:T(2,128)}, u32[]{:S(2)}) copy-start(f32[2,512,12]{1,0,2:T(2,128)} %param.13) | copy-start | bytes 147460
Sparse Core Ops, SparseCore 0:
  10.8 90.7 all-gather.6
  221.6 105.8 all-gather.8
  329.1 36.6 all-gather.10

commit v7 on v6

--- a/solution.py
+++ b/solution.py
@@ -894,15 +894,17 @@
     parts, cols = block.shape[0], block.shape[4]
     for part in range(parts):
         at = slice(part * cols, (part + 1) * cols)
-        gu[0, 0, :, at] = block[part, 0, 0].astype(F32)
-        gu[0, 1, :, at] = block[part, 0, 1].astype(F32)
-        dn[0, :, at] = block[part, 0, 2].astype(F32)
+        for k in range(2):
+            e = jnp.bitwise_xor(jnp.bitwise_and(sc[0], 1), k)
+            gu[e, 0, :, at] = block[part, k, 0].astype(F32)
+            gu[e, 1, :, at] = block[part, k, 1].astype(F32)
+            dn[e, :, at] = block[part, k, 2].astype(F32)
     v = tokens[0].astype(F32)
     inverse = lax.rsqrt(jnp.mean(v * v, axis=-1, keepdims=True) + epsilon)
     u = (own[0].astype(F32) + recv[0].astype(F32)) * gain[...]
     mean = jnp.mean(u * v, axis=-1, keepdims=True)
     o_ref[0] = dh[0].astype(F32) + inverse * u - v * (inverse * inverse * inverse * mean)
-    layer[0] = jnp.where(step // 4 == sc[1], layer_own[...].astype(F32), layer_other[...].astype(F32)).astype(BF)
+    layer[0] = jnp.where(step // 2 == sc[1], layer_own[...].astype(F32), layer_other[...].astype(F32)).astype(BF)
 
     @pl.when(step == 0)
     def _():
@@ -921,10 +923,10 @@
     parts, cols = gin.shape[0], gin.shape[4]
     seqs, rows, width = tokens.shape
     head_cols = att.shape[1]
-    some = rows // 4
-    xor = lambda k, s: jnp.bitwise_xor(k, s[0])
-    row = pl.BlockSpec((1, some, width), lambda k, s: (k // 4, k % 4, 0))
-    flat = pl.BlockSpec((some, width), lambda k, s: (k % 4, 0))
+    some = rows // 2
+    xor = lambda k, s: jnp.bitwise_xor(k, s[0] // 2)
+    row = pl.BlockSpec((1, some, width), lambda k, s: (k // 2, k % 2, 0))
+    flat = pl.BlockSpec((some, width), lambda k, s: (k % 2, 0))
     whole = lambda shape: pl.BlockSpec(shape, lambda k, s: (0,) * len(shape))
     small = [
         out((NEXP, seqs, rows), F32), out((2, 192), F32), out((3, 192, head_cols), F32), out((192, head_cols), F32),
@@ -937,15 +939,15 @@
             out(tokens.shape, F32), *small,
         ),
         grid_spec=pltpu.PrefetchScalarGridSpec(
-            num_scalar_prefetch=1, grid=(NFFN,),
-            in_specs=[pl.BlockSpec((parts, 1, 3, 192, cols), lambda k, s: (0, k, 0, 0, 0)), row, whole(gain.shape)]
+            num_scalar_prefetch=1, grid=(NFFN // 2,),
+            in_specs=[pl.BlockSpec((parts, 2, 3, 192, cols), lambda k, s: (0, k, 0, 0, 0)), row, whole(gain.shape)]
             + [row] * 3
             + [whole(a.shape) for a in (att, outg, small_f, line_f)]
             + [flat] * 2
             + [whole(gprev_t.shape)],
             out_specs=(
-                pl.BlockSpec((1, 2, 192, cols * parts), lambda k, s: (xor(k, s), 0, 0, 0)),
-                pl.BlockSpec((1, 192, cols * parts), lambda k, s: (xor(k, s), 0, 0)),
+                pl.BlockSpec((2, 2, 192, cols * parts), lambda k, s: (xor(k, s), 0, 0, 0)),
+                pl.BlockSpec((2, 192, cols * parts), lambda k, s: (xor(k, s), 0, 0)),
                 row, row, *[whole(a.shape) for a in small],
             ),
         ),

time: 581 us -> 579 us (level)
  no operation moved by 1% of the time
where the time goes in v7:
time: 579 us; the launch traced here: 570 us
  Pallas kernels  532 us (92%)
  between operations  14.5 us (3%)
  local copies, waits for them, and re-layouts  9.38 us (2%)
  starting transfers between devices  8.49 us (1%)
    pallas_call x5, Pallas kernels, run_remote(): pl.pallas_call(body, out_shape=tuple(outs), in_specs=[HBM if i in hbm_ins...  410 us
    pallas_call x1, Pallas kernels, more_call(): pl.pallas_call(more_body, out_shape=tuple((out(h.shape) for h in held)),...  40.2 us
    pallas_call x1, Pallas kernels, expert_call(): pl.pallas_call(expert_body, out_shape=tuple(packet + [wide] * 2 + [high]...  34.6 us
    pallas_call x1, Pallas kernels, run(): pl.pallas_call(body, out_shape=tuple(outs), in_specs=[SCALARS] + [WHOLE]...  30.4 us
    pallas_call x1, Pallas kernels, last_call(): pl.pallas_call(last_body, out_shape=(out((NFFN, 2, 192, cols * parts), F3...  16.3 us
  transfers between devices with their start and end apart: 10, of which 0 were waited for; matrix products, arithmetic and copies ran while one was open for 2% of the time, Pallas kernels for 82%

profile of v7, /device:TPU:0, one launch (start us, length us, event | category | flops | bytes accessed | tf_op | source)
XLA Modules:
  0.0 570.0 jit_solution(14605392513085458962)
XLA Ops:
  7.2 0.0 copy-start
  7.2 0.0 all-gather.7.cloned.1.call-start
  7.2 1.3 fusion.3
  8.5 1.2 dynamic-slice_bitcast_fusion
  9.8 0.9 fusion.1
  10.7 0.0 all-gather.7.cloned.1.call-update
  10.7 0.0 all-gather.9.cloned.1.call-start
  10.8 0.1 copy.36
  11.0 0.6 pad.12.smallp
  11.6 40.6 %gather.1 = (bf16[1024,512]{1,0:T(8,128)(2,1)}, bf16[768,512]{1,0:T(8,128)(2,1)}, bf16[8,768,128]{2,1,0:T(8,128)(2,1)}, bf16[3,768,384]{2,1,0:T(8,128)(2,1)}, bf...) custom-call(bf16[3,192,384]{2,1,0:T(8,128)(2,1)} %qkv.1, ...), custom_call_target="tpu_custom_call" | custom-call | flops 1024 | bytes 1024 | tf_op jit(solution)/shard_map/gather/pallas_call | solution.py:1421
  52.2 0.6 dynamic_slice.15.prefix_ref
  52.8 1.0 fusion.2
  53.8 1.3 pad_maximum_fusion
  55.1 117.3 %attend.1 = (bf16[768,1024]{1,0:T(8,128)(2,1)}, bf16[768,512]{1,0:T(8,128)(2,1)}, bf16[4,3,256,384]{3,2,1,0:T(8,128)(2,1)}, bf16[4,192,512]{2,1,0:T(8,128)(2,1)}...) custom-call(s32[1]{0:T(128)} %dynamic_slice.15.prefix_ref, ...), custom_call_target="tpu_custom_call" | custom-call | flops 1024 | bytes 1024 | tf_op jit(solution)/shard_map/attend/pallas_call | solution.py:1421
  172.4 0.6 pad.13.prev
  173.1 48.4 %route.1 = (bf16[2,384,512]{2,1,0:T(8,128)(2,1)}, f32[768,512]{1,0:T(8,128)}, bf16[6,784,128]{2,1,0:T(8,128)(2,1)}, bf16[2,784,128]{2,1,0:T(8,128)(2,1)}, bf16[2...) custom-call(bf16[4,192,512]{2,1,0:T(8,128)(2,1)} %get-tuple-element., ...), custom_call_target="tpu_custom_call" | custom-call | flops 1024 | bytes 1024 | tf_op jit(solution)/shard_map/route/pallas_call | solution.py:1421
  221.5 0.0 all-gather.9.cloned.1.call-update
  221.5 0.0 all-gather.11.cloned.1.call-start
  221.6 0.6 collective-permute-start
  222.2 0.6 collective-permute-start.1
  222.8 0.6 pad_add_fusion.1.sc
  223.3 34.6 %experts_own.1 = (bf16[8,784,128]{2,1,0:T(8,128)(2,1)}, bf16[8,768,128]{2,1,0:T(8,128)(2,1)}, bf16[4,768,1024]{2,1,0:T(8,128)(2,1)}, bf16[4,768,1024]{2,1,0:T(8,...) custom-call(s32[2]{0:T(128)} %pad_add_fusion.1.sc, ...), custom_call_target="tpu_custom_call" | custom-call | flops 1024 | bytes 1024 | tf_op jit(solution)/shard_map/experts_own/pallas_call | solution.py:644
  257.9 0.0 collective-permute-done.g1
  258.0 0.0 collective-permute-done.1.g2
  258.0 70.0 %give_back.1 = (bf16[512,768]{1,0:T(8,128)(2,1)}, f32[2,16,512]{2,1,0:T(8,128)}, bf16[4,192,512]{2,1,0:T(8,128)(2,1)}, bf16[4,192,512]{2,1,0:T(8,128)(2,1)}, bf16[2,512,768]{2,1,0:T(8,128)(2,1)}) custom-call(bf16[8,784,128]{2,1,0:T(8,128)(2,1)} %get-tuple-element.109.ysend, bf16[8,768,128]{2,1,0:T(8,128)(2,1)} %get-tuple-element.110.rsend, ...), custom_call_target="tpu_custom_call" | custom-call | flops 1024 | bytes 1024 | tf_op jit(solution)/shard_map/give_back/pallas_call | solution.py:1421
  328.0 0.0 all-gather.9.cloned.1.call-done
  328.0 0.0 all-gather.11.cloned.1.call-update
  328.1 2.3 collective-permute-start.5
  330.4 0.2 collective-permute-start.6
  330.6 1.2 stack.46.sc
  331.8 30.4 %attention_backward.1 = (bf16[3,256,384]{2,1,0:T(8,128)(2,1)}, bf16[3,256,384]{2,1,0:T(8,128)(2,1)}, bf16[3,256,384]{2,1,0:T(8,128)(2,1)}, bf16[3,256,384]{2,1,0:T(8,128)(2,1)}) custom-call(s32[5]{0:T(128)} %stack.46.sc, bf16[4,3,256,384]{3,2,1,0:T(8,128)(2,1)} %get-tuple-element.93.blocks, f32[3,72,2048]{2,1,0:T(8,128)} %get-tuple-element.94.m_ref, ...), custom_call_target="tpu_custom_call" | custom-call | flops 1024 | bytes 1024 | tf_op jit(solution)/shard_map/attention_backward/pallas_call | solution.py:451
  362.2 2.3 collective-permute-start.2
  364.5 1.7 collective-permute-start.3
  366.2 0.6 collective-permute-start.4
  366.9 1.3 slice.3.gain
  368.2 0.6 stack.52.sc
  368.8 0.7 pad_add_fusion.sc
  369.5 1.0 copy-done.4
  370.5 40.2 %experts_more.1 = (bf16[4,768,1024]{2,1,0:T(8,128)(2,1)}, bf16[4,768,1024]{2,1,0:T(8,128)(2,1)}, bf16[4,2048,1024]{2,1,0:T(8,128)(2,1)}, bf16[4,2048,1024]{2,1,0:T(8,128)(2,1)}, bf16[4,2048,1024]{2,1,0:T(8,128)(2,1)}) custom-call(s32[5]{0:T(128)} %stack.52.sc, ...), custom_call_target="tpu_custom_call", output_to_operand_aliasing={{0}: (8, {}), {1}: (9, {}), {2}: (10, {}), {3}: (11, {}), {... | custom-call | flops 1024 | bytes 1024 | tf_op jit(solution)/shard_map/experts_more/pallas_call | solution.py:620
  410.7 0.0 copy-start.6
  410.7 0.0 copy-start.7
  410.7 0.0 collective-permute-done.4.b3
  410.7 0.8 copy-done.6
  411.5 0.2 copy-done.7
  411.7 134.1 %finish.1 = (bf16[4,8,3,192,256]{4,3,2,1,0:T(8,128)(2,1)}, bf16[2,512,768]{2,1,0:T(8,128)(2,1)}, bf16[2,512,768]{2,1,0:T(8,128)(2,1)}, f32[592,384]{1,0:T(8,128)...) custom-call(bf16[4,768,1024]{2,1,0:T(8,128)(2,1)} %get-tuple-element.133.bx, ...), custom_call_target="tpu_custom_call" | custom-call | flops 1024 | bytes 1024 | tf_op jit(solution)/shard_map/finish/pallas_call | solution.py:1421
  545.8 0.0 collective-permute-done.6.layer_other
  545.8 0.9 copy-done.5
  546.8 16.3 %last.1 = (f32[8,2,192,1024]{3,2,1,0:T(8,128)}, f32[8,192,1024]{2,1,0:T(8,128)}, bf16[2,512,768]{2,1,0:T(8,128)(2,1)}, f32[2,512,768]{2,1,0:T(8,128)}, f32[12,2,...) custom-call(s32[2]{0:T(128)} %pad_add_fusion.sc, ...), custom_call_target="tpu_custom_call" | custom-call | flops 1024 | bytes 1024 | tf_op jit(solution)/shard_map/last/pallas_call | solution.py:935
  (27 shorter events, 0.1 us)
Async XLA Ops:
  7.2 165.2 %copy-start = (f32[2,512,12]{1,0,2:T(2,128)S(1)}, f32[2,512,12]{1,0,2:T(2,128)}, u32[]{:S(2)}) copy-start(f32[2,512,12]{1,0,2:T(2,128)} %param.13) | copy-start | bytes 147460
  7.2 165.9 %all-gather.7.cloned.1.call-start = ((), (), s32[]{:S(2)}) async-start(), calls=%async_computation | async-start | bytes 4055040 | tf_op jit(solution)/shard_map/all_gather | solution.py:1471
  8.5 2.3 copy-start.8
  8.5 2.3 copy-start.9
  8.5 2.3 copy-start.10
  10.7 317.3 %all-gather.9.cloned.1.call-start = ((), (), s32[]{:S(2)}) async-start(), calls=%async_computation.1 | async-start | bytes 6021120 | tf_op jit(solution)/shard_map/all_gather | solution.py:1534
  11.6 40.6 %copy-start.11 = (s32[2]{0:T(128)S(1)}, s32[2]{0:T(128)}, u32[]{:S(2)}) copy-start(s32[2]{0:T(128)} %param.15) | copy-start | bytes 28
  221.5 148.0 %all-gather.11.cloned.1.call-start = ((), (), s32[]{:S(2)}) async-start(), calls=%async_computation.2 | async-start | bytes 2007040 | tf_op jit(solution)/shard_map/all_gather | solution.py:1554
  221.6 36.4 %collective-permute-start = (bf16[2,3,768,128]{3,2,1,0:T(8,128)(2,1)}, bf16[2,3,768,128]{3,2,1,0:T(8,128)(2,1)S(1)}, u32[]{:S(2)}, u32[]{:S(2)}) collective-permute-start(bf16[2,3,768,128]{3,2,1,0:T(8,128)(2,1)} %get-tuple-element.107), channel_id=1, source_target_pairs={{0,1},{1,0},{8,9},{9,8},{16,17},{17,16},{24,25},{25,24},{2,3},{3,2... | collective-permute-start | bytes 3538952 | tf_op jit(solution)/shard_map/ppermute | solution.py:1461
  222.2 35.8 %collective-permute-start.1 = (bf16[2,3,768,128]{3,2,1,0:T(8,128)(2,1)}, bf16[2,3,768,128]{3,2,1,0:T(8,128)(2,1)S(1)}, u32[]{:S(2)}, u32[]{:S(2)}) collective-permute-start(bf16[2,3,768,128]{3,2,1,0:T(8,128)(2,1)} %get-tuple-element.108), channel_id=1, source_target_pairs={{0,16},{1,17},{8,24},{9,25},{16,0},{17,1},{24,8},{25,9},{2,18},{3,... | collective-permute-start | bytes 3538952 | tf_op jit(solution)/shard_map/ppermute | solution.py:1461
  257.9 70.0 %copy-start.2 = (bf16[2,3,768,128]{3,2,1,0:T(8,128)(2,1)}, bf16[2,3,768,128]{3,2,1,0:T(8,128)(2,1)S(1)}, u32[]{:S(2)}) copy-start(bf16[2,3,768,128]{3,2,1,0:T(8,128)(2,1)S(1)} %collective-permute-done.g1) | copy-start | bytes 3538948
  258.0 70.0 %copy-start.3 = (bf16[2,3,768,128]{3,2,1,0:T(8,128)(2,1)}, bf16[2,3,768,128]{3,2,1,0:T(8,128)(2,1)S(1)}, u32[]{:S(2)}) copy-start(bf16[2,3,768,128]{3,2,1,0:T(8,128)(2,1)S(1)} %collective-permute-done.1.g2) | copy-start | bytes 3538948
  328.1 41.4 %collective-permute-start.5 = (bf16[2,3,768,128]{3,2,1,0:T(8,128)(2,1)}, bf16[2,3,768,128]{3,2,1,0:T(8,128)(2,1)S(1)}, u32[]{:S(2)}, u32[]{:S(2)}) collective-permute-start(bf16[2,3,768,128]{3,2,1,0:T(8,128)(2,1)} %get-tuple-element.126), channel_id=1, source_target_pairs={{0,17},{1,16},{8,25},{9,24},{16,1},{17,0},{24,9},{25,8},{2,19},{3,... | collective-permute-start | bytes 3538952 | tf_op jit(solution)/shard_map/ppermute | solution.py:1461
  330.4 215.4 %collective-permute-start.6 = (bf16[512,768]{1,0:T(8,128)(2,1)}, bf16[512,768]{1,0:T(8,128)(2,1)S(1)}, u32[]{:S(2)}, u32[]{:S(2)}) collective-permute-start(bf16[512,768]{1,0:T(8,128)(2,1)} %get-tuple-element.152.layer_own), channel_id=1, source_target_pairs={{0,1},{1,0},{2,3},{3,2},{4,5},{5,4},{6,7},{7,6},{8,9},{9,8},{10,11... | collective-permute-start | bytes 2359304 | tf_op jit(solution)/shard_map/ppermute | solution.py:1455
  362.2 48.5 %collective-permute-start.2 = (bf16[3,256,384]{2,1,0:T(8,128)(2,1)}, bf16[3,256,384]{2,1,0:T(8,128)(2,1)S(1)}, u32[]{:S(2)}, u32[]{:S(2)}) collective-permute-start(bf16[3,256,384]{2,1,0:T(8,128)(2,1)} %get-tuple-element.117), channel_id=1, source_target_pairs={{0,2},{2,0},{4,6},{6,4},{1,3},{3,1},{5,7},{7,5},{8,10},{10,8},{12,... | collective-permute-start | bytes 1769480 | tf_op jit(solution)/shard_map/ppermute | solution.py:1458
  364.5 46.2 %collective-permute-start.3 = (bf16[3,256,384]{2,1,0:T(8,128)(2,1)}, bf16[3,256,384]{2,1,0:T(8,128)(2,1)S(1)}, u32[]{:S(2)}, u32[]{:S(2)}) collective-permute-start(bf16[3,256,384]{2,1,0:T(8,128)(2,1)} %get-tuple-element.118), channel_id=1, source_target_pairs={{0,4},{2,6},{4,0},{6,2},{1,5},{3,7},{5,1},{7,3},{8,12},{10,14},{12... | collective-permute-start | bytes 1769480 | tf_op jit(solution)/shard_map/ppermute | solution.py:1458
  366.2 44.5 %collective-permute-start.4 = (bf16[3,256,384]{2,1,0:T(8,128)(2,1)}, bf16[3,256,384]{2,1,0:T(8,128)(2,1)}, u32[]{:S(2)}, u32[]{:S(2)}) collective-permute-start(bf16[3,256,384]{2,1,0:T(8,128)(2,1)} %get-tuple-element.119), channel_id=1, source_target_pairs={{0,6},{2,4},{4,2},{6,0},{1,7},{3,5},{5,3},{7,1},{8,14},{10,12},{12... | collective-permute-start | bytes 1769480 | tf_op jit(solution)/shard_map/ppermute | solution.py:1458
  369.5 1.0 copy-start.4
  410.7 0.8 copy-start.6
  410.7 1.0 copy-start.7
  545.8 0.9 copy-start.5
  546.8 16.3 %copy-start.1 = (f32[2,512,12]{1,0,2:T(2,128)S(1)}, f32[2,512,12]{1,0,2:T(2,128)}, u32[]{:S(2)}) copy-start(f32[2,512,12]{1,0,2:T(2,128)} %param.13) | copy-start | bytes 147460
Sparse Core Ops, SparseCore 0:
  10.8 90.7 all-gather.6
  221.6 105.8 all-gather.8
  329.1 36.6 all-gather.10

commit v8 on v7

--- a/solution.py
+++ b/solution.py
@@ -637,7 +637,7 @@
 
 
 def expert_call(plane, xa, xb, gs, w, wt):
-    tile, n_ctx = 512, 4
+    tile, n_ctx = 256, 4
     slots, width = 8 * CAPACITY, w.shape[1]
     packet = [out((8, width + 16, CAPACITY)), out((8, width, CAPACITY))]
     wide, high = out((n_ctx, width, slots)), out((n_ctx, w.shape[2], slots))
@@ -817,10 +817,10 @@
             overs.append(hand_over(1))
         if number == 3:
             overs.append(hand_over(2))
-        if number in (3, 4, 7, 8):
+        for stage in {3: (0,), 4: (1,), 8: (2, 3)}.get(number, ()):
             for c in steps:
                 c.wait()
-            steps = after((3, 4, 7, 8).index(number))
+            steps = after(stage)
             for c in steps:
                 c.start()
         if number == 4:

time: 579 us -> 579 us (level)
  transfers between devices with their start and end apart: 10 -> 10, of which waited for: 0 -> 1; matrix products, arithmetic and copies ran while one was open for 2% -> 2% of each run, Pallas kernels for 82% -> 82%
where the time goes in v8:
time: 579 us; the launch traced here: 570 us
  Pallas kernels  531 us (92%)
  between operations  14.5 us (3%)
  local copies, waits for them, and re-layouts  9.38 us (2%)
  starting transfers between devices  8.92 us (2%)
    pallas_call x5, Pallas kernels, run_remote(): pl.pallas_call(body, out_shape=tuple(outs), in_specs=[HBM if i in hbm_ins...  411 us
    pallas_call x1, Pallas kernels, more_call(): pl.pallas_call(more_body, out_shape=tuple((out(h.shape) for h in held)),...  40.2 us
    pallas_call x1, Pallas kernels, expert_call(): pl.pallas_call(expert_body, out_shape=tuple(packet + [wide] * 2 + [high]...  33.1 us
    pallas_call x1, Pallas kernels, run(): pl.pallas_call(body, out_shape=tuple(outs), in_specs=[SCALARS] + [WHOLE]...  30.4 us
    pallas_call x1, Pallas kernels, last_call(): pl.pallas_call(last_body, out_shape=(out((NFFN, 2, 192, cols * parts), F3...  16.3 us
  transfers between devices with their start and end apart: 10, of which 1 were waited for; matrix products, arithmetic and copies ran while one was open for 2% of the time, Pallas kernels for 82%

profile of v8, /device:TPU:0, one launch (start us, length us, event | category | flops | bytes accessed | tf_op | source)
XLA Modules:
  0.0 570.2 jit_solution(4401990437928514119)
XLA Ops:
  7.2 0.0 copy-start
  7.2 0.0 all-gather.7.cloned.1.call-start
  7.2 1.3 fusion.3
  8.5 1.2 dynamic-slice_bitcast_fusion
  9.8 0.9 fusion.1
  10.7 0.0 all-gather.7.cloned.1.call-update
  10.7 0.0 all-gather.9.cloned.1.call-start
  10.8 0.1 copy.36
  11.0 0.6 pad.12.smallp
  11.6 40.6 %gather.1 = (bf16[1024,512]{1,0:T(8,128)(2,1)}, bf16[768,512]{1,0:T(8,128)(2,1)}, bf16[8,768,128]{2,1,0:T(8,128)(2,1)}, bf16[3,768,384]{2,1,0:T(8,128)(2,1)}, bf...) custom-call(bf16[3,192,384]{2,1,0:T(8,128)(2,1)} %qkv.1, ...), custom_call_target="tpu_custom_call" | custom-call | flops 1024 | bytes 1024 | tf_op jit(solution)/shard_map/gather/pallas_call | solution.py:1421
  52.2 0.6 dynamic_slice.15.prefix_ref
  52.8 1.0 fusion.2
  53.8 1.3 pad_maximum_fusion
  55.1 117.3 %attend.1 = (bf16[768,1024]{1,0:T(8,128)(2,1)}, bf16[768,512]{1,0:T(8,128)(2,1)}, bf16[4,3,256,384]{3,2,1,0:T(8,128)(2,1)}, bf16[4,192,512]{2,1,0:T(8,128)(2,1)}...) custom-call(s32[1]{0:T(128)} %dynamic_slice.15.prefix_ref, ...), custom_call_target="tpu_custom_call" | custom-call | flops 1024 | bytes 1024 | tf_op jit(solution)/shard_map/attend/pallas_call | solution.py:1421
  172.4 0.6 pad.13.prev
  173.1 48.4 %route.1 = (bf16[2,384,512]{2,1,0:T(8,128)(2,1)}, f32[768,512]{1,0:T(8,128)}, bf16[6,784,128]{2,1,0:T(8,128)(2,1)}, bf16[2,784,128]{2,1,0:T(8,128)(2,1)}, bf16[2...) custom-call(bf16[4,192,512]{2,1,0:T(8,128)(2,1)} %get-tuple-element., ...), custom_call_target="tpu_custom_call" | custom-call | flops 1024 | bytes 1024 | tf_op jit(solution)/shard_map/route/pallas_call | solution.py:1421
  221.5 0.0 all-gather.9.cloned.1.call-update
  221.5 0.0 all-gather.11.cloned.1.call-start
  221.6 0.6 collective-permute-start
  222.2 0.6 collective-permute-start.1
  222.8 0.6 pad_add_fusion.1.sc
  223.3 33.1 %experts_own.1 = (bf16[8,784,128]{2,1,0:T(8,128)(2,1)}, bf16[8,768,128]{2,1,0:T(8,128)(2,1)}, bf16[4,768,1024]{2,1,0:T(8,128)(2,1)}, bf16[4,768,1024]{2,1,0:T(8,...) custom-call(s32[2]{0:T(128)} %pad_add_fusion.1.sc, ...), custom_call_target="tpu_custom_call" | custom-call | flops 1024 | bytes 1024 | tf_op jit(solution)/shard_map/experts_own/pallas_call | solution.py:644
  256.4 0.0 collective-permute-done.g1
  256.4 0.0 collective-permute-done.1.g2
  256.5 70.0 %give_back.1 = (bf16[512,768]{1,0:T(8,128)(2,1)}, f32[2,16,512]{2,1,0:T(8,128)}, bf16[4,192,512]{2,1,0:T(8,128)(2,1)}, bf16[4,192,512]{2,1,0:T(8,128)(2,1)}, bf16[2,512,768]{2,1,0:T(8,128)(2,1)}) custom-call(bf16[8,784,128]{2,1,0:T(8,128)(2,1)} %get-tuple-element.109.ysend, bf16[8,768,128]{2,1,0:T(8,128)(2,1)} %get-tuple-element.110.rsend, ...), custom_call_target="tpu_custom_call" | custom-call | flops 1024 | bytes 1024 | tf_op jit(solution)/shard_map/give_back/pallas_call | solution.py:1421
  326.4 1.1 all-gather.9.cloned.1.call-done
  327.5 0.0 all-gather.11.cloned.1.call-update
  327.6 1.2 collective-permute-start.5
  328.8 1.8 collective-permute-start.6
  330.6 1.2 stack.46.sc
  331.8 30.4 %attention_backward.1 = (bf16[3,256,384]{2,1,0:T(8,128)(2,1)}, bf16[3,256,384]{2,1,0:T(8,128)(2,1)}, bf16[3,256,384]{2,1,0:T(8,128)(2,1)}, bf16[3,256,384]{2,1,0:T(8,128)(2,1)}) custom-call(s32[5]{0:T(128)} %stack.46.sc, bf16[4,3,256,384]{3,2,1,0:T(8,128)(2,1)} %get-tuple-element.93.blocks, f32[3,72,2048]{2,1,0:T(8,128)} %get-tuple-element.94.m_ref, ...), custom_call_target="tpu_custom_call" | custom-call | flops 1024 | bytes 1024 | tf_op jit(solution)/shard_map/attention_backward/pallas_call | solution.py:451
  362.2 2.2 collective-permute-start.2
  364.5 1.3 collective-permute-start.3
  365.7 1.1 collective-permute-start.4
  366.8 1.3 slice.3.gain
  368.2 0.6 stack.52.sc
  368.8 0.7 pad_add_fusion.sc
  369.4 0.0 collective-permute-done.5.g3
  369.4 1.0 copy-done.4
  370.4 40.2 %experts_more.1 = (bf16[4,768,1024]{2,1,0:T(8,128)(2,1)}, bf16[4,768,1024]{2,1,0:T(8,128)(2,1)}, bf16[4,2048,1024]{2,1,0:T(8,128)(2,1)}, bf16[4,2048,1024]{2,1,0:T(8,128)(2,1)}, bf16[4,2048,1024]{2,1,0:T(8,128)(2,1)}) custom-call(s32[5]{0:T(128)} %stack.52.sc, ...), custom_call_target="tpu_custom_call", output_to_operand_aliasing={{0}: (8, {}), {1}: (9, {}), {2}: (10, {}), {3}: (11, {}), {... | custom-call | flops 1024 | bytes 1024 | tf_op jit(solution)/shard_map/experts_more/pallas_call | solution.py:620
  410.7 0.0 copy-start.6
  410.7 0.0 collective-permute-done.3.b2
  410.7 0.0 copy-start.7
  410.7 0.8 copy-done.6
  411.5 0.2 copy-done.7
  411.7 134.3 %finish.1 = (bf16[4,8,3,192,256]{4,3,2,1,0:T(8,128)(2,1)}, bf16[2,512,768]{2,1,0:T(8,128)(2,1)}, bf16[2,512,768]{2,1,0:T(8,128)(2,1)}, f32[592,384]{1,0:T(8,128)...) custom-call(bf16[4,768,1024]{2,1,0:T(8,128)(2,1)} %get-tuple-element.133.bx, ...), custom_call_target="tpu_custom_call" | custom-call | flops 1024 | bytes 1024 | tf_op jit(solution)/shard_map/finish/pallas_call | solution.py:1421
  546.0 0.9 copy-done.5
  547.0 16.3 %last.1 = (f32[8,2,192,1024]{3,2,1,0:T(8,128)}, f32[8,192,1024]{2,1,0:T(8,128)}, bf16[2,512,768]{2,1,0:T(8,128)(2,1)}, f32[2,512,768]{2,1,0:T(8,128)}, f32[12,2,...) custom-call(s32[2]{0:T(128)} %pad_add_fusion.sc, ...), custom_call_target="tpu_custom_call" | custom-call | flops 1024 | bytes 1024 | tf_op jit(solution)/shard_map/last/pallas_call | solution.py:935
  (27 shorter events, 0.1 us)
Async XLA Ops:
  7.2 165.2 %copy-start = (f32[2,512,12]{1,0,2:T(2,128)S(1)}, f32[2,512,12]{1,0,2:T(2,128)}, u32[]{:S(2)}) copy-start(f32[2,512,12]{1,0,2:T(2,128)} %param.13) | copy-start | bytes 147460
  7.2 165.9 %all-gather.7.cloned.1.call-start = ((), (), s32[]{:S(2)}) async-start(), calls=%async_computation | async-start | bytes 4055040 | tf_op jit(solution)/shard_map/all_gather | solution.py:1471
  8.5 2.3 copy-start.8
  8.5 2.3 copy-start.9
  8.5 2.3 copy-start.10
  10.7 316.8 %all-gather.9.cloned.1.call-start = ((), (), s32[]{:S(2)}) async-start(), calls=%async_computation.1 | async-start | bytes 6021120 | tf_op jit(solution)/shard_map/all_gather | solution.py:1534
  11.6 40.6 %copy-start.11 = (s32[2]{0:T(128)S(1)}, s32[2]{0:T(128)}, u32[]{:S(2)}) copy-start(s32[2]{0:T(128)} %param.15) | copy-start | bytes 28
  221.5 147.9 %all-gather.11.cloned.1.call-start = ((), (), s32[]{:S(2)}) async-start(), calls=%async_computation.2 | async-start | bytes 2007040 | tf_op jit(solution)/shard_map/all_gather | solution.py:1554
  221.6 34.8 %collective-permute-start = (bf16[2,3,768,128]{3,2,1,0:T(8,128)(2,1)}, bf16[2,3,768,128]{3,2,1,0:T(8,128)(2,1)S(1)}, u32[]{:S(2)}, u32[]{:S(2)}) collective-permute-start(bf16[2,3,768,128]{3,2,1,0:T(8,128)(2,1)} %get-tuple-element.107), channel_id=1, source_target_pairs={{0,1},{1,0},{8,9},{9,8},{16,17},{17,16},{24,25},{25,24},{2,3},{3,2... | collective-permute-start | bytes 3538952 | tf_op jit(solution)/shard_map/ppermute | solution.py:1461
  222.2 34.2 %collective-permute-start.1 = (bf16[2,3,768,128]{3,2,1,0:T(8,128)(2,1)}, bf16[2,3,768,128]{3,2,1,0:T(8,128)(2,1)S(1)}, u32[]{:S(2)}, u32[]{:S(2)}) collective-permute-start(bf16[2,3,768,128]{3,2,1,0:T(8,128)(2,1)} %get-tuple-element.108), channel_id=1, source_target_pairs={{0,16},{1,17},{8,24},{9,25},{16,0},{17,1},{24,8},{25,9},{2,18},{3,... | collective-permute-start | bytes 3538952 | tf_op jit(solution)/shard_map/ppermute | solution.py:1461
  256.4 70.0 %copy-start.2 = (bf16[2,3,768,128]{3,2,1,0:T(8,128)(2,1)}, bf16[2,3,768,128]{3,2,1,0:T(8,128)(2,1)S(1)}, u32[]{:S(2)}) copy-start(bf16[2,3,768,128]{3,2,1,0:T(8,128)(2,1)S(1)} %collective-permute-done.g1) | copy-start | bytes 3538948
  256.4 70.0 %copy-start.3 = (bf16[2,3,768,128]{3,2,1,0:T(8,128)(2,1)}, bf16[2,3,768,128]{3,2,1,0:T(8,128)(2,1)S(1)}, u32[]{:S(2)}) copy-start(bf16[2,3,768,128]{3,2,1,0:T(8,128)(2,1)S(1)} %collective-permute-done.1.g2) | copy-start | bytes 3538948
  327.6 41.9 %collective-permute-start.5 = (bf16[2,3,768,128]{3,2,1,0:T(8,128)(2,1)}, bf16[2,3,768,128]{3,2,1,0:T(8,128)(2,1)S(1)}, u32[]{:S(2)}, u32[]{:S(2)}) collective-permute-start(bf16[2,3,768,128]{3,2,1,0:T(8,128)(2,1)} %get-tuple-element.126), channel_id=1, source_target_pairs={{0,17},{1,16},{8,25},{9,24},{16,1},{17,0},{24,9},{25,8},{2,19},{3,... | collective-permute-start | bytes 3538952 | tf_op jit(solution)/shard_map/ppermute | solution.py:1461
  328.8 217.2 %collective-permute-start.6 = (bf16[512,768]{1,0:T(8,128)(2,1)}, bf16[512,768]{1,0:T(8,128)(2,1)S(1)}, u32[]{:S(2)}, u32[]{:S(2)}) collective-permute-start(bf16[512,768]{1,0:T(8,128)(2,1)} %get-tuple-element.152.layer_own), channel_id=1, source_target_pairs={{0,1},{1,0},{2,3},{3,2},{4,5},{5,4},{6,7},{7,6},{8,9},{9,8},{10,11... | collective-permute-start | bytes 2359304 | tf_op jit(solution)/shard_map/ppermute | solution.py:1455
  362.2 48.4 %collective-permute-start.2 = (bf16[3,256,384]{2,1,0:T(8,128)(2,1)}, bf16[3,256,384]{2,1,0:T(8,128)(2,1)S(1)}, u32[]{:S(2)}, u32[]{:S(2)}) collective-permute-start(bf16[3,256,384]{2,1,0:T(8,128)(2,1)} %get-tuple-element.117), channel_id=1, source_target_pairs={{0,2},{2,0},{4,6},{6,4},{1,3},{3,1},{5,7},{7,5},{8,10},{10,8},{12,... | collective-permute-start | bytes 1769480 | tf_op jit(solution)/shard_map/ppermute | solution.py:1458
  364.5 46.2 %collective-permute-start.3 = (bf16[3,256,384]{2,1,0:T(8,128)(2,1)}, bf16[3,256,384]{2,1,0:T(8,128)(2,1)S(1)}, u32[]{:S(2)}, u32[]{:S(2)}) collective-permute-start(bf16[3,256,384]{2,1,0:T(8,128)(2,1)} %get-tuple-element.118), channel_id=1, source_target_pairs={{0,4},{2,6},{4,0},{6,2},{1,5},{3,7},{5,1},{7,3},{8,12},{10,14},{12... | collective-permute-start | bytes 1769480 | tf_op jit(solution)/shard_map/ppermute | solution.py:1458
  365.7 45.0 %collective-permute-start.4 = (bf16[3,256,384]{2,1,0:T(8,128)(2,1)}, bf16[3,256,384]{2,1,0:T(8,128)(2,1)}, u32[]{:S(2)}, u32[]{:S(2)}) collective-permute-start(bf16[3,256,384]{2,1,0:T(8,128)(2,1)} %get-tuple-element.119), channel_id=1, source_target_pairs={{0,6},{2,4},{4,2},{6,0},{1,7},{3,5},{5,3},{7,1},{8,14},{10,12},{12... | collective-permute-start | bytes 1769480 | tf_op jit(solution)/shard_map/ppermute | solution.py:1458
  369.4 1.0 copy-start.4
  410.7 0.8 copy-start.6
  410.7 1.0 copy-start.7
  546.0 0.9 copy-start.5
  547.0 16.3 %copy-start.1 = (f32[2,512,12]{1,0,2:T(2,128)S(1)}, f32[2,512,12]{1,0,2:T(2,128)}, u32[]{:S(2)}) copy-start(f32[2,512,12]{1,0,2:T(2,128)} %param.13) | copy-start | bytes 147460
Sparse Core Ops, SparseCore 0:
  10.8 90.7 all-gather.6
  221.6 105.8 all-gather.8
  329.1 36.5 all-gather.10
